TPU v7x, 32 devices: a whole 2x2x4 slice. The times are simulated.
32 devices in a mesh: section: 4 (over y, x), rows: 8 (over z, core).
Axes of the slice: x: 2, y: 2, z: 4, core: 2. Of those that a mesh axis runs over, the one named last changes fastest.
Arguments:
- activations: bfloat16 [32, 16, 64, 128], P('section', 'rows'), may hold values from -48 to 48
- first_cache: bfloat16 [2, 16, 64, 128], P(None, 'rows'), may hold values from -4 to 4
- second_cache: bfloat16 [2, 16, 64, 128], P(None, 'rows'), may hold values from -4 to 4
- norm1_scale: float32 [128], replicated, may hold values from 0.1 to 1.9
- norm1_shift: float32 [128], replicated, may hold values from -3 to 3
- conv1_weight: bfloat16 [3, 3, 3, 128, 128], replicated, may hold values from -0.109375 to 0.109375
- conv1_bias: float32 [128], replicated, may hold values from -5 to 5
- norm2_scale: float32 [128], replicated, may hold values from 0.1 to 1.9
- norm2_shift: float32 [128], replicated, may hold values from -3 to 3
- conv2_weight: bfloat16 [3, 3, 3, 128, 128], replicated, may hold values from -0.109375 to 0.109375
- conv2_bias: float32 [128], replicated, may hold values from -3 to 3
Outputs:
- block_output: bfloat16 [32, 16, 64, 128], P('section', 'rows')
All inputs are finite; a program needn't handle non-finite values.
Results may differ from a plain program's by a relative error of at most 0.007.
Values may be sent and summed in bfloat16 or wider, within the bound.
No kernel may reach another device: no remote copies, remote signals or barrier semaphores. Data moves between devices by JAX's collectives and lax.ppermute only.
A program may use at most 64 MiB of HBM per device.

v0:
```python
import jax
import jax.numpy as jnp
from jax import lax
from jax.sharding import PartitionSpec as P

GROUPS = 32


epsilon = 1e-06


def from_behind(block, axis, distance):
    devices = range(lax.axis_size(axis))
    route = [(i - distance, i) for i in devices if i - distance in devices]
    return lax.ppermute(block, axis, route)


def extended(block, sides, width):
    for axis, dim in sides:
        count = lax.axis_size(axis)
        forward = [(i, i + 1) for i in range(count - 1)]
        backward = [(target, source) for source, target in forward]
        low = lax.ppermute(
            lax.slice_in_dim(block, block.shape[dim] - width, None, axis=dim), axis, forward
        )
        high = lax.ppermute(lax.slice_in_dim(block, 0, width, axis=dim), axis, backward)
        block = jnp.concatenate([low, block, high], axis=dim)
    return block


def group_moments(values):
    frames, row_count, columns, channels = values.shape
    grouped = values.reshape(frames * row_count * columns, GROUPS, channels // GROUPS)
    cells_total = frames * row_count * columns * (channels // GROUPS) * lax.axis_size("rows")
    totals, squares = lax.psum(
        (jnp.sum(grouped, axis=(0, 2)), jnp.sum(grouped * grouped, axis=(0, 2))), "rows"
    )
    average = totals / cells_total
    spread = squares / cells_total - average * average
    return (average, spread)


def apply_norm(values, average, spread, scale, shift):
    frames, row_count, columns, channels = values.shape
    grouped = values.reshape(frames, row_count, columns, GROUPS, channels // GROUPS)
    normal = (grouped - average[:, None]) / jnp.sqrt(spread[:, None] + epsilon)
    normal = normal.reshape(frames, row_count, columns, channels)
    return jax.nn.silu(normal * scale + shift).astype(jnp.bfloat16)


def causal_conv(source, weight, bias):
    frames = source.shape[0] - 2
    row_count = source.shape[1] - 2
    columns = source.shape[2]
    padded = jnp.pad(source, ((0, 0), (0, 0), (1, 1), (0, 0)))
    totals = jnp.zeros((frames, row_count, columns, weight.shape[-1]), jnp.float32)
    for frame_tap in range(3):
        for row_tap in range(3):
            for col_tap in range(3):
                piece = padded[
                    frame_tap : frame_tap + frames,
                    row_tap : row_tap + row_count,
                    col_tap : col_tap + columns,
                ]
                totals = totals + jnp.einsum(
                    "fhwc,cd->fhwd",
                    piece,
                    weight[frame_tap, row_tap, col_tap],
                    preferred_element_type=jnp.float32,
                )
    return totals + bias


def on_device(
    activations,
    first_cache,
    second_cache,
    norm1_scale,
    norm1_shift,
    conv1_weight,
    conv1_bias,
    norm2_scale,
    norm2_shift,
    conv2_weight,
    conv2_bias,
):
    at_start = lax.axis_index("section") == 0
    own_rows = activations.astype(jnp.float32)
    average, spread = group_moments(own_rows)
    entry_block = apply_norm(own_rows, average, spread, norm1_scale, norm1_shift)
    received = from_behind(entry_block[-2:], "section", 1)
    joined = jnp.concatenate([jnp.where(at_start, first_cache, received), entry_block], 0)
    padded = extended(joined, (("rows", 1),), 1)
    middle = causal_conv(padded, conv1_weight, conv1_bias).astype(jnp.bfloat16)
    middle_full = middle.astype(jnp.float32)
    average_two, spread_two = group_moments(middle_full)
    second = apply_norm(middle_full, average_two, spread_two, norm2_scale, norm2_shift)
    received_two = from_behind(second[-2:], "section", 1)
    joined_two = jnp.concatenate([jnp.where(at_start, second_cache, received_two), second], 0)
    padded_two = extended(joined_two, (("rows", 1),), 1)
    final = causal_conv(padded_two, conv2_weight, conv2_bias)
    return (own_rows + final).astype(jnp.bfloat16)


def solution(mesh):
    in_specs = (
        P("section", "rows", None, None),
        P(None, "rows", None, None),
        P(None, "rows", None, None),
        P(),
        P(),
        P(),
        P(),
        P(),
        P(),
        P(),
        P(),
    )
    out_specs = P("section", "rows", None, None)
    return jax.shard_map(
        on_device, mesh=mesh, in_specs=in_specs, out_specs=out_specs, check_vma=False
    )
```

profile of v0, /device:TPU:5, one launch (start us, length us, event | category | flops | bytes accessed | tf_op | source)
XLA Modules:
  0.0 76.0 jit_solution(5771964932719686660)
XLA Ops:
  0.0 1.1 %convert_reduce_fusion = (f32[128]{0:T(128)S(1)}, f32[128]{0:T(128)S(1)}) fusion(bf16[8,2,64,128]{3,2,1,0:T(8,128)(2,1)} %param.11), kind=kLoop, calls=%fused_computation.63 | loop fusion | flops 524032 | bytes 263168 | tf_op jit(solution)/shard_map/reduce_sum | solution.py:36
  1.6 13.8 %all-reduce.3 = (f32[32]{0:T(128)S(1)}, f32[32]{0:T(128)S(1)}) all-reduce(f32[32]{0:T(128)S(1)} %reduce_sum.54, f32[32]{0:T(128)S(1)} %reduce_sum.51), channel_id=1, replica_groups=mesh['section'=4,'rows'=8] {'rows'}, use_global_device_ids=true, to_apply=%region_5.6 | all-reduce | flops 64 | bytes 512 | tf_op jit(solution)/shard_map/psum | solution.py:35
  15.8 1.2 %multiply_convert_fusion.1 = bf16[8,2,64,128]{3,2,1,0:T(8,128)(2,1)S(1)} fusion(bf16[8,2,64,128]{3,2,1,0:T(8,128)(2,1)} %param.11, f32[128]{0:T(128)} %param.15, f32[128]{0:T(128)} %param.14, f32[128]{0:T(128)S(1)} %div.48, f32[128]{0:T(128)S(1)} %sub.33), kind=kLoop, calls=%fused_computation.82 | loop fusion | flops 1310720 | bytes 526336 | tf_op jit(solution)/shard_map/convert_element_type | solution.py:48
  17.0 3.1 %collective-permute-start = (bf16[2,2,64,128]{3,2,1,0:T(8,128)(2,1)S(1)}, bf16[2,2,64,128]{3,2,1,0:T(8,128)(2,1)S(1)}, u32[]{:S(2)}, u32[]{:S(2)}) collective-permute-start(bf16[2,2,64,128]{3,2,1,0:T(8,128)(2,1)S(1)} %slice.486), channel_id=1, source_target_pairs={{0,8},{8,16},{16,24},{1,9},{9,17},{17,25},{2,10},{10,18},{18,26},{... | collective-permute-start | bytes 196616 | tf_op jit(solution)/shard_map/ppermute | solution.py:15
  20.1 2.8 %collective-permute-done = bf16[2,2,64,128]{3,2,1,0:T(8,128)(2,1)S(1)} collective-permute-done((bf16[2,2,64,128]{3,2,1,0:T(8,128)(2,1)S(1)}, bf16[2,2,64,128]{3,2,1,0:T(8,128)(2,1)S(1)}, u32[]{:S(2)}, u32[]{:S(2)}) %collective-permute-start) | collective-permute-done | bytes 65568 | tf_op jit(solution)/shard_map/ppermute | solution.py:15
  22.9 4.1 %collective-permute-start.1 = (bf16[10,1,64,128]{3,2,1,0:T(8,128)(2,1)S(1)}, bf16[10,1,64,128]{3,2,1,0:T(8,128)(2,1)S(1)}, u32[]{:S(2)}, u32[]{:S(2)}) collective-permute-start(bf16[10,1,64,128]{3,2,1,0:T(8,128)(2,1)S(1)} %get-tuple-element.15), channel_id=1, source_target_pairs={{0,1},{1,2},{2,3},{3,4},{4,5},{5,6},{6,7},{8,9},{9,10},{10,11},{11... | collective-permute-start | bytes 491528 | tf_op jit(solution)/shard_map/ppermute | solution.py:23
  27.1 3.7 %collective-permute-start.2 = (bf16[10,1,64,128]{3,2,1,0:T(8,128)(2,1)S(1)}, bf16[10,1,64,128]{3,2,1,0:T(8,128)(2,1)S(1)}, u32[]{:S(2)}, u32[]{:S(2)}) collective-permute-start(bf16[10,1,64,128]{3,2,1,0:T(8,128)(2,1)S(1)} %get-tuple-element.16), channel_id=1, source_target_pairs={{1,0},{2,1},{3,2},{4,3},{5,4},{6,5},{7,6},{9,8},{10,9},{11,10},{12... | collective-permute-start | bytes 491528 | tf_op jit(solution)/shard_map/ppermute | solution.py:26
  31.0 0.2 fusion.102
  31.2 2.5 %collective-permute-done.2 = bf16[10,1,64,128]{3,2,1,0:T(8,128)(2,1)S(1)} collective-permute-done((bf16[10,1,64,128]{3,2,1,0:T(8,128)(2,1)S(1)}, bf16[10,1,64,128]{3,2,1,0:T(8,128)(2,1)S(1)}, u32[]{:S(2)}, u32[]{:S(2)}) %collective-permute-start.2) | collective-permute-done | bytes 163872 | tf_op jit(solution)/shard_map/ppermute | solution.py:26
  33.7 0.3 fusion.42
  34.0 0.2 fusion.94
  34.2 0.2 fusion.91
  34.4 0.2 fusion.88
  34.7 0.2 fusion.85
  34.9 0.2 fusion.82
  35.1 0.2 fusion.79
  35.3 0.2 fusion.74
  35.5 0.2 fusion.170
  35.8 0.2 convolution_add_fusion.23
  36.0 0.2 convolution_add_fusion.22
  36.2 0.2 fusion.2
  36.4 0.2 fusion.163
  36.6 0.2 fusion.4
  37.1 0.2 fusion.6
  37.3 0.2 fusion.8
  37.7 0.2 fusion.10
  38.0 0.2 fusion.148
  38.2 0.2 fusion.12
  38.4 0.2 convolution_add_fusion.15
  38.6 0.2 convolution_add_fusion.14
  38.8 0.2 convolution_add_fusion.13
  39.1 0.2 fusion.141
  39.3 0.4 copy-done.5
  39.7 0.3 fusion.231
  40.5 11.4 %all-reduce.2 = (f32[32]{0:T(128)S(1)}, f32[32]{0:T(128)S(1)}) all-reduce(f32[32]{0:T(128)S(1)} %reduce_sum.75, f32[32]{0:T(128)S(1)} %reduce_sum.72), channel_id=1, replica_groups=mesh['section'=4,'rows'=8] {'rows'}, use_global_device_ids=true, to_apply=%region_11.12 | all-reduce | flops 64 | bytes 512 | tf_op jit(solution)/shard_map/psum | solution.py:35
  52.5 2.4 %collective-permute-start.3 = (bf16[2,2,64,128]{3,2,1,0:T(8,128)(2,1)S(1)}, bf16[2,2,64,128]{3,2,1,0:T(8,128)(2,1)S(1)}, u32[]{:S(2)}, u32[]{:S(2)}) collective-permute-start(bf16[2,2,64,128]{3,2,1,0:T(8,128)(2,1)S(1)} %slice.509), channel_id=1, source_target_pairs={{0,8},{8,16},{16,24},{1,9},{9,17},{17,25},{2,10},{10,18},{18,26},{... | collective-permute-start | bytes 196616 | tf_op jit(solution)/shard_map/ppermute | solution.py:15
  54.9 3.7 %collective-permute-done.3 = bf16[2,2,64,128]{3,2,1,0:T(8,128)(2,1)S(1)} collective-permute-done((bf16[2,2,64,128]{3,2,1,0:T(8,128)(2,1)S(1)}, bf16[2,2,64,128]{3,2,1,0:T(8,128)(2,1)S(1)}, u32[]{:S(2)}, u32[]{:S(2)}) %collective-permute-start.3) | collective-permute-done | bytes 65568 | tf_op jit(solution)/shard_map/ppermute | solution.py:15
  58.6 3.4 %collective-permute-start.4 = (bf16[10,1,64,128]{3,2,1,0:T(8,128)(2,1)S(1)}, bf16[10,1,64,128]{3,2,1,0:T(8,128)(2,1)S(1)}, u32[]{:S(2)}, u32[]{:S(2)}) collective-permute-start(bf16[10,1,64,128]{3,2,1,0:T(8,128)(2,1)S(1)} %get-tuple-element.13), channel_id=1, source_target_pairs={{0,1},{1,2},{2,3},{3,4},{4,5},{5,6},{6,7},{8,9},{9,10},{10,11},{11... | collective-permute-start | bytes 491528 | tf_op jit(solution)/shard_map/ppermute | solution.py:23
  62.0 3.7 %collective-permute-start.5 = (bf16[10,1,64,128]{3,2,1,0:T(8,128)(2,1)S(1)}, bf16[10,1,64,128]{3,2,1,0:T(8,128)(2,1)S(1)}, u32[]{:S(2)}, u32[]{:S(2)}) collective-permute-start(bf16[10,1,64,128]{3,2,1,0:T(8,128)(2,1)S(1)} %get-tuple-element.14), channel_id=1, source_target_pairs={{1,0},{2,1},{3,2},{4,3},{5,4},{6,5},{7,6},{9,8},{10,9},{11,10},{12... | collective-permute-start | bytes 491528 | tf_op jit(solution)/shard_map/ppermute | solution.py:26
  65.7 0.2 fusion.99
  66.1 2.5 %collective-permute-done.5 = bf16[10,1,64,128]{3,2,1,0:T(8,128)(2,1)S(1)} collective-permute-done((bf16[10,1,64,128]{3,2,1,0:T(8,128)(2,1)S(1)}, bf16[10,1,64,128]{3,2,1,0:T(8,128)(2,1)S(1)}, u32[]{:S(2)}, u32[]{:S(2)}) %collective-permute-start.5) | collective-permute-done | bytes 163872 | tf_op jit(solution)/shard_map/ppermute | solution.py:26
  68.7 0.3 select_maximum_fusion
  69.0 0.2 fusion.69
  69.2 0.2 fusion.66
  69.4 0.2 fusion.63
  69.6 0.2 fusion.60
  69.8 0.2 fusion.57
  70.1 0.2 fusion.54
  70.3 0.2 fusion.49
  70.5 0.2 fusion.137
  70.7 0.2 convolution_add_fusion.11
  70.9 0.2 convolution_add_fusion.10
  71.2 0.2 fusion.17
  71.6 0.2 fusion.19
  71.8 0.2 fusion.126
  72.0 0.2 fusion.21
  72.3 0.2 fusion.23
  72.7 0.2 fusion.25
  73.2 0.2 fusion.27
  73.4 0.2 convolution_add_fusion.3
  73.6 0.2 convolution_add_fusion.2
  73.8 0.2 convolution_add_fusion.1
  74.3 0.7 copy-done
  75.0 1.0 %fusion.34 = bf16[8,2,64,128]{3,2,1,0:T(8,128)(2,1)} fusion(f32[8,2,64,128]{3,2,1,0:T(8,128)S(1)} %fusion.49, f32[8,2,64,128]{3,2,1,0:T(8,128)S(1)} %fusion.108, f32[8,2,64,128]{3,2,1,0:T(8,128)S(1)} %convolution_add_fusion.1, bf16[8,2,64,128]{3,2,1,0:T(8,128)(2,1)S(1)} %copy-done, bf16[10,4,66,128]{3,2,1,0:T(8,128)(2,1)S(1)} %select_maximum_fusion, ...), kind=kOutput, calls=%fused_computation.60 | convolution fusion | flops 34471936 | bytes 2392576 | tf_op jit(solution)/shard_map/fhwc,cd->fhwd/dot_general | solution.py:65
  (51 shorter events, 3.5 us)
Async XLA Ops:
  0.0 22.9 %copy-start.3 = (bf16[2,2,64,128]{3,2,1,0:T(8,128)(2,1)S(1)}, bf16[2,2,64,128]{3,2,1,0:T(8,128)(2,1)}, u32[]{:S(2)}) copy-start(bf16[2,2,64,128]{3,2,1,0:T(8,128)(2,1)} %param.12) | copy-start | bytes 196612
  1.1 29.7 %copy-start.1 = (bf16[3,3,3,128,128]{4,3,2,1,0:T(8,128)(2,1)S(1)}, bf16[3,3,3,128,128]{4,3,2,1,0:T(8,128)(2,1)}, u32[]{:S(2)}) copy-start(bf16[3,3,3,128,128]{4,3,2,1,0:T(8,128)(2,1)} %param.16) | copy-start | bytes 2654212
  17.0 5.9 %collective-permute-start = (bf16[2,2,64,128]{3,2,1,0:T(8,128)(2,1)S(1)}, bf16[2,2,64,128]{3,2,1,0:T(8,128)(2,1)S(1)}, u32[]{:S(2)}, u32[]{:S(2)}) collective-permute-start(bf16[2,2,64,128]{3,2,1,0:T(8,128)(2,1)S(1)} %slice.486), channel_id=1, source_target_pairs={{0,8},{8,16},{16,24},{1,9},{9,17},{17,25},{2,10},{10,18},{18,26},{... | collective-permute-start | bytes 196616 | tf_op jit(solution)/shard_map/ppermute | solution.py:15
  22.9 8.3 %collective-permute-start.1 = (bf16[10,1,64,128]{3,2,1,0:T(8,128)(2,1)S(1)}, bf16[10,1,64,128]{3,2,1,0:T(8,128)(2,1)S(1)}, u32[]{:S(2)}, u32[]{:S(2)}) collective-permute-start(bf16[10,1,64,128]{3,2,1,0:T(8,128)(2,1)S(1)} %get-tuple-element.15), channel_id=1, source_target_pairs={{0,1},{1,2},{2,3},{3,4},{4,5},{5,6},{6,7},{8,9},{9,10},{10,11},{11... | collective-permute-start | bytes 491528 | tf_op jit(solution)/shard_map/ppermute | solution.py:23
  27.1 6.6 %collective-permute-start.2 = (bf16[10,1,64,128]{3,2,1,0:T(8,128)(2,1)S(1)}, bf16[10,1,64,128]{3,2,1,0:T(8,128)(2,1)S(1)}, u32[]{:S(2)}, u32[]{:S(2)}) collective-permute-start(bf16[10,1,64,128]{3,2,1,0:T(8,128)(2,1)S(1)} %get-tuple-element.16), channel_id=1, source_target_pairs={{1,0},{2,1},{3,2},{4,3},{5,4},{6,5},{7,6},{9,8},{10,9},{11,10},{12... | collective-permute-start | bytes 491528 | tf_op jit(solution)/shard_map/ppermute | solution.py:26
  39.1 0.7 copy-start.5
  39.7 12.5 %copy-start.6 = (f32[128]{0:T(128)S(1)}, f32[128]{0:T(128)}, u32[]{:S(2)}) copy-start(f32[128]{0:T(128)} %param.19) | copy-start | bytes 1540
  39.7 12.6 %copy-start.7 = (f32[128]{0:T(128)S(1)}, f32[128]{0:T(128)}, u32[]{:S(2)}) copy-start(f32[128]{0:T(128)} %param.18) | copy-start | bytes 1540
  40.0 18.5 %copy-start.4 = (bf16[2,2,64,128]{3,2,1,0:T(8,128)(2,1)S(1)}, bf16[2,2,64,128]{3,2,1,0:T(8,128)(2,1)}, u32[]{:S(2)}) copy-start(bf16[2,2,64,128]{3,2,1,0:T(8,128)(2,1)} %param.13) | copy-start | bytes 196612
  52.3 13.4 %copy-start.2 = (bf16[3,3,3,128,128]{4,3,2,1,0:T(8,128)(2,1)S(1)}, bf16[3,3,3,128,128]{4,3,2,1,0:T(8,128)(2,1)}, u32[]{:S(2)}) copy-start(bf16[3,3,3,128,128]{4,3,2,1,0:T(8,128)(2,1)} %param.20) | copy-start | bytes 2654212
  52.5 6.0 %collective-permute-start.3 = (bf16[2,2,64,128]{3,2,1,0:T(8,128)(2,1)S(1)}, bf16[2,2,64,128]{3,2,1,0:T(8,128)(2,1)S(1)}, u32[]{:S(2)}, u32[]{:S(2)}) collective-permute-start(bf16[2,2,64,128]{3,2,1,0:T(8,128)(2,1)S(1)} %slice.509), channel_id=1, source_target_pairs={{0,8},{8,16},{16,24},{1,9},{9,17},{17,25},{2,10},{10,18},{18,26},{... | collective-permute-start | bytes 196616 | tf_op jit(solution)/shard_map/ppermute | solution.py:15
  58.6 7.5 %collective-permute-start.4 = (bf16[10,1,64,128]{3,2,1,0:T(8,128)(2,1)S(1)}, bf16[10,1,64,128]{3,2,1,0:T(8,128)(2,1)S(1)}, u32[]{:S(2)}, u32[]{:S(2)}) collective-permute-start(bf16[10,1,64,128]{3,2,1,0:T(8,128)(2,1)S(1)} %get-tuple-element.13), channel_id=1, source_target_pairs={{0,1},{1,2},{2,3},{3,4},{4,5},{5,6},{6,7},{8,9},{9,10},{10,11},{11... | collective-permute-start | bytes 491528 | tf_op jit(solution)/shard_map/ppermute | solution.py:23
  62.0 6.6 %collective-permute-start.5 = (bf16[10,1,64,128]{3,2,1,0:T(8,128)(2,1)S(1)}, bf16[10,1,64,128]{3,2,1,0:T(8,128)(2,1)S(1)}, u32[]{:S(2)}, u32[]{:S(2)}) collective-permute-start(bf16[10,1,64,128]{3,2,1,0:T(8,128)(2,1)S(1)} %get-tuple-element.14), channel_id=1, source_target_pairs={{1,0},{2,1},{3,2},{4,3},{5,4},{6,5},{7,6},{9,8},{10,9},{11,10},{12... | collective-permute-start | bytes 491528 | tf_op jit(solution)/shard_map/ppermute | solution.py:26
  74.1 1.0 %copy-start = (bf16[8,2,64,128]{3,2,1,0:T(8,128)(2,1)S(1)}, bf16[8,2,64,128]{3,2,1,0:T(8,128)(2,1)}, u32[]{:S(2)}) copy-start(bf16[8,2,64,128]{3,2,1,0:T(8,128)(2,1)} %param.11) | copy-start | bytes 786436
  74.1 0.9 %copy-start.8 = (f32[128]{0:T(128)S(1)}, f32[128]{0:T(128)}, u32[]{:S(2)}) copy-start(f32[128]{0:T(128)} %param.21) | copy-start | bytes 1540
where the time goes:
time: 76.3 us; the launch traced here: 76 us
  blocking collectives  25.2 us (33%)
  starting transfers between devices  20.4 us (27%)
  matrix products  12.4 us (16%)
  waiting for transfers between devices  11.4 us (15%)
  other arithmetic  3.68 us (5%)
  local copies, waits for them, and re-layouts  2.32 us (3%)
    psum x2, blocking collectives, group_moments(): lax.psum((jnp.sum(grouped, axis=(0, 2)), jnp.sum(grouped * grouped, axis=...  25.2 us
    dot_general x54, matrix products, causal_conv(): jnp.einsum('fhwc,cd->fhwd', piece, weight[frame_tap, row_tap, col_tap], p...  12.4 us
    ppermute x2, starting transfers between devices, extended(): lax.ppermute(lax.slice_in_dim(block, block.shape[dim] - width, None, axis...  7.53 us
    ppermute x2, starting transfers between devices, extended(): lax.ppermute(lax.slice_in_dim(block, 0, width, axis=dim), axis, backward)  7.39 us
    ppermute x2, waiting for transfers between devices, from_behind(): return lax.ppermute(block, axis, route)  6.43 us
    ppermute x2, starting transfers between devices, from_behind(): return lax.ppermute(block, axis, route)  5.5 us
    ppermute x2, waiting for transfers between devices, extended(): lax.ppermute(lax.slice_in_dim(block, 0, width, axis=dim), axis, backward)  4.98 us
  transfers between devices with their start and end apart: 6, of which 4 were waited for; matrix products, arithmetic and copies ran while one was open for 1% of the time, Pallas kernels for 0%

commit v1 on v0

--- a/solution.py
+++ b/solution.py
@@ -32,9 +32,12 @@
     frames, row_count, columns, channels = values.shape
     grouped = values.reshape(frames * row_count * columns, GROUPS, channels // GROUPS)
     cells_total = frames * row_count * columns * (channels // GROUPS) * lax.axis_size("rows")
-    totals, squares = lax.psum(
-        (jnp.sum(grouped, axis=(0, 2)), jnp.sum(grouped * grouped, axis=(0, 2))), "rows"
+    partial = jnp.concatenate(
+        [jnp.sum(grouped, axis=(0, 2)), jnp.sum(grouped * grouped, axis=(0, 2))]
     )
+    everyone = jnp.broadcast_to(partial, (lax.axis_size("rows"), 2 * GROUPS))
+    received = lax.all_to_all(everyone, "rows", 0, 0, tiled=True)
+    totals, squares = jnp.split(jnp.sum(received, axis=0), 2)
     average = totals / cells_total
     spread = squares / cells_total - average * average
     return (average, spread)

time: 76.3 us -> 68.7 us (0.900)
  blocking collectives: 25.2 us -> 16.8 us
  waiting for transfers between devices: 11.4 us -> 15 us
  starting transfers between devices: 20.4 us -> 17.2 us
    psum x2 -> x0, blocking collectives: 25.2 us -> none  [group_moments(): lax.psum((jnp.sum(grouped, axis=(0, 2)), jnp.sum(grouped * grouped, axis=...]
    all_to_all x0 -> x2, blocking collectives: none -> 16.8 us  [group_moments(): received = lax.all_to_all(everyone, 'rows', 0, 0, tiled=True)]
    ppermute x2, starting transfers between devices: 7.39 us -> 3.84 us  [extended(): lax.ppermute(lax.slice_in_dim(block, 0, width, axis=dim), axis, backward)]
    ppermute x2, waiting for transfers between devices: 4.98 us -> 8.52 us  [extended(): lax.ppermute(lax.slice_in_dim(block, 0, width, axis=dim), axis, backward)]
where the time goes in v1:
time: 68.7 us; the launch traced here: 68.3 us
  starting transfers between devices  17.2 us (25%)
  blocking collectives  16.8 us (24%)
  waiting for transfers between devices  15 us (22%)
  matrix products  12.4 us (18%)
  other arithmetic  4 us (6%)
  local copies, waits for them, and re-layouts  2.33 us (3%)
    all_to_all x2, blocking collectives, group_moments(): received = lax.all_to_all(everyone, 'rows', 0, 0, tiled=True)  16.8 us
    dot_general x54, matrix products, causal_conv(): jnp.einsum('fhwc,cd->fhwd', piece, weight[frame_tap, row_tap, col_tap], p...  12.4 us
    ppermute x2, waiting for transfers between devices, extended(): lax.ppermute(lax.slice_in_dim(block, 0, width, axis=dim), axis, backward)  8.52 us
    ppermute x2, starting transfers between devices, extended(): lax.ppermute(lax.slice_in_dim(block, block.shape[dim] - width, None, axis...  7.88 us
    ppermute x2, waiting for transfers between devices, from_behind(): return lax.ppermute(block, axis, route)  6.45 us
    ppermute x2, starting transfers between devices, from_behind(): return lax.ppermute(block, axis, route)  5.47 us
    ppermute x2, starting transfers between devices, extended(): lax.ppermute(lax.slice_in_dim(block, 0, width, axis=dim), axis, backward)  3.84 us
  transfers between devices with their start and end apart: 6, of which 4 were waited for; matrix products, arithmetic and copies ran while one was open for 1% of the time, Pallas kernels for 0%

profile of v1, /device:TPU:5, one launch (start us, length us, event | category | flops | bytes accessed | tf_op | source)
XLA Modules:
  0.0 68.3 jit_solution(17909542897754440108)
XLA Ops:
  0.0 1.1 %convert_reduce_fusion = (f32[128]{0:T(128)S(1)}, f32[128]{0:T(128)S(1)}) fusion(bf16[8,2,64,128]{3,2,1,0:T(8,128)(2,1)} %param.11), kind=kLoop, calls=%fused_computation.63 | loop fusion | flops 524032 | bytes 263168 | tf_op jit(solution)/shard_map/reduce_sum | solution.py:36
  1.7 10.2 %all_to_all.12 = f32[8,1,64]{2,1,0:T(1,128)S(1)} all-to-all(f32[8,1,64]{2,1,0:T(1,128)S(1)} %broadcast_in_dim.4), channel_id=1, replica_groups=mesh['section'=4,'rows'=8] {'rows'}, dimensions={0} | all-to-all | bytes 4096 | tf_op jit(solution)/shard_map/all_to_all | solution.py:39
  12.3 1.2 %multiply_convert_fusion.1 = bf16[8,2,64,128]{3,2,1,0:T(8,128)(2,1)S(1)} fusion(bf16[8,2,64,128]{3,2,1,0:T(8,128)(2,1)} %param.11, f32[128]{0:T(128)} %param.15, f32[128]{0:T(128)} %param.14, f32[128]{0:T(128)S(1)} %div.48, f32[128]{0:T(128)S(1)} %sub.33), kind=kLoop, calls=%fused_computation.82 | loop fusion | flops 1310720 | bytes 526336 | tf_op jit(solution)/shard_map/convert_element_type | solution.py:51
  13.5 3.1 %collective-permute-start = (bf16[2,2,64,128]{3,2,1,0:T(8,128)(2,1)S(1)}, bf16[2,2,64,128]{3,2,1,0:T(8,128)(2,1)S(1)}, u32[]{:S(2)}, u32[]{:S(2)}) collective-permute-start(bf16[2,2,64,128]{3,2,1,0:T(8,128)(2,1)S(1)} %slice.486), channel_id=1, source_target_pairs={{0,8},{8,16},{16,24},{1,9},{9,17},{17,25},{2,10},{10,18},{18,26},{... | collective-permute-start | bytes 196616 | tf_op jit(solution)/shard_map/ppermute | solution.py:15
  16.7 2.8 %collective-permute-done = bf16[2,2,64,128]{3,2,1,0:T(8,128)(2,1)S(1)} collective-permute-done((bf16[2,2,64,128]{3,2,1,0:T(8,128)(2,1)S(1)}, bf16[2,2,64,128]{3,2,1,0:T(8,128)(2,1)S(1)}, u32[]{:S(2)}, u32[]{:S(2)}) %collective-permute-start) | collective-permute-done | bytes 65568 | tf_op jit(solution)/shard_map/ppermute | solution.py:15
  19.5 3.9 %collective-permute-start.1 = (bf16[10,1,64,128]{3,2,1,0:T(8,128)(2,1)S(1)}, bf16[10,1,64,128]{3,2,1,0:T(8,128)(2,1)S(1)}, u32[]{:S(2)}, u32[]{:S(2)}) collective-permute-start(bf16[10,1,64,128]{3,2,1,0:T(8,128)(2,1)S(1)} %get-tuple-element.11), channel_id=1, source_target_pairs={{0,1},{1,2},{2,3},{3,4},{4,5},{5,6},{6,7},{8,9},{9,10},{10,11},{11... | collective-permute-start | bytes 491528 | tf_op jit(solution)/shard_map/ppermute | solution.py:23
  23.4 1.9 %collective-permute-start.2 = (bf16[10,1,64,128]{3,2,1,0:T(8,128)(2,1)S(1)}, bf16[10,1,64,128]{3,2,1,0:T(8,128)(2,1)S(1)}, u32[]{:S(2)}, u32[]{:S(2)}) collective-permute-start(bf16[10,1,64,128]{3,2,1,0:T(8,128)(2,1)S(1)} %get-tuple-element.12), channel_id=1, source_target_pairs={{1,0},{2,1},{3,2},{4,3},{5,4},{6,5},{7,6},{9,8},{10,9},{11,10},{12... | collective-permute-start | bytes 491528 | tf_op jit(solution)/shard_map/ppermute | solution.py:26
  25.6 0.2 fusion.102
  25.8 4.3 %collective-permute-done.2 = bf16[10,1,64,128]{3,2,1,0:T(8,128)(2,1)S(1)} collective-permute-done((bf16[10,1,64,128]{3,2,1,0:T(8,128)(2,1)S(1)}, bf16[10,1,64,128]{3,2,1,0:T(8,128)(2,1)S(1)}, u32[]{:S(2)}, u32[]{:S(2)}) %collective-permute-start.2) | collective-permute-done | bytes 163872 | tf_op jit(solution)/shard_map/ppermute | solution.py:26
  30.1 0.3 fusion.42
  30.4 0.2 fusion.94
  30.6 0.2 fusion.91
  30.8 0.2 fusion.88
  31.1 0.2 fusion.85
  31.3 0.2 fusion.82
  31.5 0.2 fusion.79
  31.7 0.2 fusion.74
  31.9 0.2 fusion.170
  32.1 0.2 convolution_add_fusion.23
  32.4 0.2 convolution_add_fusion.22
  32.6 0.2 fusion.2
  33.0 0.2 fusion.4
  33.5 0.2 fusion.6
  33.7 0.2 fusion.8
  34.1 0.2 fusion.10
  34.4 0.2 fusion.148
  34.6 0.2 fusion.12
  34.8 0.2 convolution_add_fusion.15
  35.0 0.2 convolution_add_fusion.14
  35.2 0.2 convolution_add_fusion.13
  35.5 0.2 fusion.141
  35.7 0.4 copy-done.5
  36.1 0.3 fusion.231
  37.0 6.6 %all_to_all.13 = f32[8,1,64]{2,1,0:T(1,128)S(1)} all-to-all(f32[8,1,64]{2,1,0:T(1,128)S(1)} %broadcast_in_dim.5), channel_id=1, replica_groups=mesh['section'=4,'rows'=8] {'rows'}, dimensions={0} | all-to-all | bytes 4096 | tf_op jit(solution)/shard_map/all_to_all | solution.py:39
  44.3 2.4 %collective-permute-start.3 = (bf16[2,2,64,128]{3,2,1,0:T(8,128)(2,1)S(1)}, bf16[2,2,64,128]{3,2,1,0:T(8,128)(2,1)S(1)}, u32[]{:S(2)}, u32[]{:S(2)}) collective-permute-start(bf16[2,2,64,128]{3,2,1,0:T(8,128)(2,1)S(1)} %slice.509), channel_id=1, source_target_pairs={{0,8},{8,16},{16,24},{1,9},{9,17},{17,25},{2,10},{10,18},{18,26},{... | collective-permute-start | bytes 196616 | tf_op jit(solution)/shard_map/ppermute | solution.py:15
  46.6 3.7 %collective-permute-done.3 = bf16[2,2,64,128]{3,2,1,0:T(8,128)(2,1)S(1)} collective-permute-done((bf16[2,2,64,128]{3,2,1,0:T(8,128)(2,1)S(1)}, bf16[2,2,64,128]{3,2,1,0:T(8,128)(2,1)S(1)}, u32[]{:S(2)}, u32[]{:S(2)}) %collective-permute-start.3) | collective-permute-done | bytes 65568 | tf_op jit(solution)/shard_map/ppermute | solution.py:15
  50.4 3.9 %collective-permute-start.4 = (bf16[10,1,64,128]{3,2,1,0:T(8,128)(2,1)S(1)}, bf16[10,1,64,128]{3,2,1,0:T(8,128)(2,1)S(1)}, u32[]{:S(2)}, u32[]{:S(2)}) collective-permute-start(bf16[10,1,64,128]{3,2,1,0:T(8,128)(2,1)S(1)} %get-tuple-element.9), channel_id=1, source_target_pairs={{0,1},{1,2},{2,3},{3,4},{4,5},{5,6},{6,7},{8,9},{9,10},{10,11},{11... | collective-permute-start | bytes 491528 | tf_op jit(solution)/shard_map/ppermute | solution.py:23
  54.3 1.9 %collective-permute-start.5 = (bf16[10,1,64,128]{3,2,1,0:T(8,128)(2,1)S(1)}, bf16[10,1,64,128]{3,2,1,0:T(8,128)(2,1)S(1)}, u32[]{:S(2)}, u32[]{:S(2)}) collective-permute-start(bf16[10,1,64,128]{3,2,1,0:T(8,128)(2,1)S(1)} %get-tuple-element.10), channel_id=1, source_target_pairs={{1,0},{2,1},{3,2},{4,3},{5,4},{6,5},{7,6},{9,8},{10,9},{11,10},{12... | collective-permute-start | bytes 491528 | tf_op jit(solution)/shard_map/ppermute | solution.py:26
  56.3 0.2 fusion.99
  56.5 0.2 fusion.100
  56.7 4.3 %collective-permute-done.5 = bf16[10,1,64,128]{3,2,1,0:T(8,128)(2,1)S(1)} collective-permute-done((bf16[10,1,64,128]{3,2,1,0:T(8,128)(2,1)S(1)}, bf16[10,1,64,128]{3,2,1,0:T(8,128)(2,1)S(1)}, u32[]{:S(2)}, u32[]{:S(2)}) %collective-permute-start.5) | collective-permute-done | bytes 163872 | tf_op jit(solution)/shard_map/ppermute | solution.py:26
  61.0 0.3 select_maximum_fusion
  61.3 0.2 fusion.69
  61.5 0.2 fusion.66
  61.7 0.2 fusion.63
  61.9 0.2 fusion.60
  62.1 0.2 fusion.57
  62.4 0.2 fusion.54
  62.6 0.2 fusion.49
  62.8 0.2 fusion.137
  63.0 0.2 convolution_add_fusion.11
  63.2 0.2 convolution_add_fusion.10
  63.5 0.2 fusion.17
  63.9 0.2 fusion.19
  64.1 0.2 fusion.126
  64.3 0.2 fusion.21
  64.6 0.2 fusion.23
  65.0 0.2 fusion.25
  65.5 0.2 fusion.27
  65.7 0.2 convolution_add_fusion.3
  65.9 0.2 convolution_add_fusion.2
  66.1 0.2 convolution_add_fusion.1
  66.6 0.7 %copy-done = bf16[8,2,64,128]{3,2,1,0:T(8,128)(2,1)S(1)} copy-done((bf16[8,2,64,128]{3,2,1,0:T(8,128)(2,1)S(1)}, bf16[8,2,64,128]{3,2,1,0:T(8,128)(2,1)}, u32[]{:S(2)}) %copy-start) | copy-done | bytes 262168
  67.3 1.0 %fusion.34 = bf16[8,2,64,128]{3,2,1,0:T(8,128)(2,1)} fusion(f32[8,2,64,128]{3,2,1,0:T(8,128)S(1)} %fusion.49, f32[8,2,64,128]{3,2,1,0:T(8,128)S(1)} %fusion.108, f32[8,2,64,128]{3,2,1,0:T(8,128)S(1)} %convolution_add_fusion.1, bf16[8,2,64,128]{3,2,1,0:T(8,128)(2,1)S(1)} %copy-done, bf16[10,4,66,128]{3,2,1,0:T(8,128)(2,1)S(1)} %select_maximum_fusion, ...), kind=kOutput, calls=%fused_computation.60 | convolution fusion | flops 34471936 | bytes 2392576 | tf_op jit(solution)/shard_map/fhwc,cd->fhwd/dot_general | solution.py:68
  (57 shorter events, 3.9 us)
Async XLA Ops:
  0.0 19.4 %copy-start.3 = (bf16[2,2,64,128]{3,2,1,0:T(8,128)(2,1)S(1)}, bf16[2,2,64,128]{3,2,1,0:T(8,128)(2,1)}, u32[]{:S(2)}) copy-start(bf16[2,2,64,128]{3,2,1,0:T(8,128)(2,1)} %param.12) | copy-start | bytes 196612
  1.1 24.2 %copy-start.1 = (bf16[3,3,3,128,128]{4,3,2,1,0:T(8,128)(2,1)S(1)}, bf16[3,3,3,128,128]{4,3,2,1,0:T(8,128)(2,1)}, u32[]{:S(2)}) copy-start(bf16[3,3,3,128,128]{4,3,2,1,0:T(8,128)(2,1)} %param.16) | copy-start | bytes 2654212
  13.5 5.9 %collective-permute-start = (bf16[2,2,64,128]{3,2,1,0:T(8,128)(2,1)S(1)}, bf16[2,2,64,128]{3,2,1,0:T(8,128)(2,1)S(1)}, u32[]{:S(2)}, u32[]{:S(2)}) collective-permute-start(bf16[2,2,64,128]{3,2,1,0:T(8,128)(2,1)S(1)} %slice.486), channel_id=1, source_target_pairs={{0,8},{8,16},{16,24},{1,9},{9,17},{17,25},{2,10},{10,18},{18,26},{... | collective-permute-start | bytes 196616 | tf_op jit(solution)/shard_map/ppermute | solution.py:15
  19.5 6.3 %collective-permute-start.1 = (bf16[10,1,64,128]{3,2,1,0:T(8,128)(2,1)S(1)}, bf16[10,1,64,128]{3,2,1,0:T(8,128)(2,1)S(1)}, u32[]{:S(2)}, u32[]{:S(2)}) collective-permute-start(bf16[10,1,64,128]{3,2,1,0:T(8,128)(2,1)S(1)} %get-tuple-element.11), channel_id=1, source_target_pairs={{0,1},{1,2},{2,3},{3,4},{4,5},{5,6},{6,7},{8,9},{9,10},{10,11},{11... | collective-permute-start | bytes 491528 | tf_op jit(solution)/shard_map/ppermute | solution.py:23
  23.4 6.6 %collective-permute-start.2 = (bf16[10,1,64,128]{3,2,1,0:T(8,128)(2,1)S(1)}, bf16[10,1,64,128]{3,2,1,0:T(8,128)(2,1)S(1)}, u32[]{:S(2)}, u32[]{:S(2)}) collective-permute-start(bf16[10,1,64,128]{3,2,1,0:T(8,128)(2,1)S(1)} %get-tuple-element.12), channel_id=1, source_target_pairs={{1,0},{2,1},{3,2},{4,3},{5,4},{6,5},{7,6},{9,8},{10,9},{11,10},{12... | collective-permute-start | bytes 491528 | tf_op jit(solution)/shard_map/ppermute | solution.py:26
  35.5 0.7 copy-start.5
  36.1 7.9 %copy-start.6 = (f32[128]{0:T(128)S(1)}, f32[128]{0:T(128)}, u32[]{:S(2)}) copy-start(f32[128]{0:T(128)} %param.19) | copy-start | bytes 1540
  36.1 7.9 %copy-start.7 = (f32[128]{0:T(128)S(1)}, f32[128]{0:T(128)}, u32[]{:S(2)}) copy-start(f32[128]{0:T(128)} %param.18) | copy-start | bytes 1540
  36.4 13.9 %copy-start.4 = (bf16[2,2,64,128]{3,2,1,0:T(8,128)(2,1)S(1)}, bf16[2,2,64,128]{3,2,1,0:T(8,128)(2,1)}, u32[]{:S(2)}) copy-start(bf16[2,2,64,128]{3,2,1,0:T(8,128)(2,1)} %param.13) | copy-start | bytes 196612
  44.1 12.2 %copy-start.2 = (bf16[3,3,3,128,128]{4,3,2,1,0:T(8,128)(2,1)S(1)}, bf16[3,3,3,128,128]{4,3,2,1,0:T(8,128)(2,1)}, u32[]{:S(2)}) copy-start(bf16[3,3,3,128,128]{4,3,2,1,0:T(8,128)(2,1)} %param.20) | copy-start | bytes 2654212
  44.3 6.0 %collective-permute-start.3 = (bf16[2,2,64,128]{3,2,1,0:T(8,128)(2,1)S(1)}, bf16[2,2,64,128]{3,2,1,0:T(8,128)(2,1)S(1)}, u32[]{:S(2)}, u32[]{:S(2)}) collective-permute-start(bf16[2,2,64,128]{3,2,1,0:T(8,128)(2,1)S(1)} %slice.509), channel_id=1, source_target_pairs={{0,8},{8,16},{16,24},{1,9},{9,17},{17,25},{2,10},{10,18},{18,26},{... | collective-permute-start | bytes 196616 | tf_op jit(solution)/shard_map/ppermute | solution.py:15
  50.4 6.3 %collective-permute-start.4 = (bf16[10,1,64,128]{3,2,1,0:T(8,128)(2,1)S(1)}, bf16[10,1,64,128]{3,2,1,0:T(8,128)(2,1)S(1)}, u32[]{:S(2)}, u32[]{:S(2)}) collective-permute-start(bf16[10,1,64,128]{3,2,1,0:T(8,128)(2,1)S(1)} %get-tuple-element.9), channel_id=1, source_target_pairs={{0,1},{1,2},{2,3},{3,4},{4,5},{5,6},{6,7},{8,9},{9,10},{10,11},{11... | collective-permute-start | bytes 491528 | tf_op jit(solution)/shard_map/ppermute | solution.py:23
  54.3 6.6 %collective-permute-start.5 = (bf16[10,1,64,128]{3,2,1,0:T(8,128)(2,1)S(1)}, bf16[10,1,64,128]{3,2,1,0:T(8,128)(2,1)S(1)}, u32[]{:S(2)}, u32[]{:S(2)}) collective-permute-start(bf16[10,1,64,128]{3,2,1,0:T(8,128)(2,1)S(1)} %get-tuple-element.10), channel_id=1, source_target_pairs={{1,0},{2,1},{3,2},{4,3},{5,4},{6,5},{7,6},{9,8},{10,9},{11,10},{12... | collective-permute-start | bytes 491528 | tf_op jit(solution)/shard_map/ppermute | solution.py:26
  66.4 1.0 %copy-start = (bf16[8,2,64,128]{3,2,1,0:T(8,128)(2,1)S(1)}, bf16[8,2,64,128]{3,2,1,0:T(8,128)(2,1)}, u32[]{:S(2)}) copy-start(bf16[8,2,64,128]{3,2,1,0:T(8,128)(2,1)} %param.11) | copy-start | bytes 786436
  66.4 0.9 %copy-start.8 = (f32[128]{0:T(128)S(1)}, f32[128]{0:T(128)}, u32[]{:S(2)}) copy-start(f32[128]{0:T(128)} %param.21) | copy-start | bytes 1540

commit v2 on v1

--- a/solution.py
+++ b/solution.py
@@ -35,9 +35,12 @@
     partial = jnp.concatenate(
         [jnp.sum(grouped, axis=(0, 2)), jnp.sum(grouped * grouped, axis=(0, 2))]
     )
-    everyone = jnp.broadcast_to(partial, (lax.axis_size("rows"), 2 * GROUPS))
-    received = lax.all_to_all(everyone, "rows", 0, 0, tiled=True)
-    totals, squares = jnp.split(jnp.sum(received, axis=0), 2)
+    count = lax.axis_size("rows")
+    step = 1
+    while step < count:
+        partial = partial + lax.ppermute(partial, "rows", [(i, i ^ step) for i in range(count)])
+        step *= 2
+    totals, squares = jnp.split(partial, 2)
     average = totals / cells_total
     spread = squares / cells_total - average * average
     return (average, spread)

time: 68.7 us -> 71.6 us (1.042)
  the two profiles are of different devices: /device:TPU:5 before, /device:TPU:13 now
where the time goes in v2:
time: 71.6 us; the launch traced here: 71.3 us
  starting transfers between devices  27.3 us (38%)
  waiting for transfers between devices  24.6 us (34%)
  matrix products  12.3 us (17%)
  other arithmetic  4.13 us (6%)
  local copies, waits for them, and re-layouts  2.33 us (3%)
    ppermute x2, starting transfers between devices, extended(): lax.ppermute(lax.slice_in_dim(block, block.shape[dim] - width, None, axis...  13.6 us
    dot_general x54, matrix products, causal_conv(): jnp.einsum('fhwc,cd->fhwd', piece, weight[frame_tap, row_tap, col_tap], p...  12.3 us
    ppermute x6, waiting for transfers between devices, group_moments(): lax.ppermute(partial, 'rows', [(i, i ^ step) for i in range(count)])  9.59 us
    ppermute x2, waiting for transfers between devices, extended(): lax.ppermute(lax.slice_in_dim(block, 0, width, axis=dim), axis, backward)  8.54 us
    ppermute x2, waiting for transfers between devices, from_behind(): return lax.ppermute(block, axis, route)  6.42 us
    ppermute x2, starting transfers between devices, from_behind(): return lax.ppermute(block, axis, route)  5.51 us
    ppermute x6, starting transfers between devices, group_moments(): lax.ppermute(partial, 'rows', [(i, i ^ step) for i in range(count)])  4.4 us
    ppermute x2, starting transfers between devices, extended(): lax.ppermute(lax.slice_in_dim(block, 0, width, axis=dim), axis, backward)  3.84 us
  transfers between devices with their start and end apart: 12, of which 10 were waited for; matrix products, arithmetic and copies ran while one was open for 1% of the time, Pallas kernels for 0%

profile of v2, /device:TPU:13, one launch (start us, length us, event | category | flops | bytes accessed | tf_op | source)
XLA Modules:
  0.0 71.3 jit_solution(10906696647471063213)
XLA Ops:
  0.0 1.1 %convert_reduce_fusion = (f32[128]{0:T(128)S(1)}, f32[128]{0:T(128)S(1)}) fusion(bf16[8,2,64,128]{3,2,1,0:T(8,128)(2,1)} %param.11), kind=kLoop, calls=%fused_computation.63 | loop fusion | flops 524032 | bytes 263168 | tf_op jit(solution)/shard_map/reduce_sum | solution.py:36
  1.7 0.7 collective-permute-start
  2.3 0.8 %collective-permute-done = f32[64]{0:T(128)S(1)} collective-permute-done((f32[64]{0:T(128)S(1)}, f32[64]{0:T(128)S(1)}, u32[]{:S(2)}, u32[]{:S(2)}) %collective-permute-start) | collective-permute-done | bytes 288 | tf_op jit(solution)/shard_map/ppermute | solution.py:41
  3.4 2.2 %collective-permute-done.1 = f32[64]{0:T(128)S(1)} collective-permute-done((f32[64]{0:T(128)S(1)}, f32[64]{0:T(128)S(1)}, u32[]{:S(2)}, u32[]{:S(2)}) %collective-permute-start.1) | collective-permute-done | bytes 288 | tf_op jit(solution)/shard_map/ppermute | solution.py:41
  5.6 2.3 %collective-permute-start.2 = (f32[64]{0:T(128)S(1)}, f32[64]{0:T(128)S(1)}, u32[]{:S(2)}, u32[]{:S(2)}) collective-permute-start(f32[64]{0:T(128)S(1)} %add.229), channel_id=1, source_target_pairs={{0,4},{1,5},{2,6},{3,7},{4,0},{5,1},{6,2},{7,3},{8,12},{9,13},{10,... | collective-permute-start | bytes 776 | tf_op jit(solution)/shard_map/ppermute | solution.py:41
  7.9 1.0 %collective-permute-done.2 = f32[64]{0:T(128)S(1)} collective-permute-done((f32[64]{0:T(128)S(1)}, f32[64]{0:T(128)S(1)}, u32[]{:S(2)}, u32[]{:S(2)}) %collective-permute-start.2) | collective-permute-done | bytes 288 | tf_op jit(solution)/shard_map/ppermute | solution.py:41
  9.4 1.2 %multiply_convert_fusion.1 = bf16[8,2,64,128]{3,2,1,0:T(8,128)(2,1)S(1)} fusion(bf16[8,2,64,128]{3,2,1,0:T(8,128)(2,1)} %param.11, f32[128]{0:T(128)} %param.15, f32[128]{0:T(128)} %param.14, f32[128]{0:T(128)S(1)} %div.48, f32[128]{0:T(128)S(1)} %sub.33), kind=kLoop, calls=%fused_computation.82 | loop fusion | flops 1310720 | bytes 526336 | tf_op jit(solution)/shard_map/convert_element_type | solution.py:54
  10.6 3.1 %collective-permute-start.3 = (bf16[2,2,64,128]{3,2,1,0:T(8,128)(2,1)S(1)}, bf16[2,2,64,128]{3,2,1,0:T(8,128)(2,1)S(1)}, u32[]{:S(2)}, u32[]{:S(2)}) collective-permute-start(bf16[2,2,64,128]{3,2,1,0:T(8,128)(2,1)S(1)} %slice.486), channel_id=1, source_target_pairs={{0,8},{8,16},{16,24},{1,9},{9,17},{17,25},{2,10},{10,18},{18,26},{... | collective-permute-start | bytes 196616 | tf_op jit(solution)/shard_map/ppermute | solution.py:15
  13.7 2.8 %collective-permute-done.3 = bf16[2,2,64,128]{3,2,1,0:T(8,128)(2,1)S(1)} collective-permute-done((bf16[2,2,64,128]{3,2,1,0:T(8,128)(2,1)S(1)}, bf16[2,2,64,128]{3,2,1,0:T(8,128)(2,1)S(1)}, u32[]{:S(2)}, u32[]{:S(2)}) %collective-permute-start.3) | collective-permute-done | bytes 65568 | tf_op jit(solution)/shard_map/ppermute | solution.py:15
  16.5 6.8 %collective-permute-start.4 = (bf16[10,1,64,128]{3,2,1,0:T(8,128)(2,1)S(1)}, bf16[10,1,64,128]{3,2,1,0:T(8,128)(2,1)S(1)}, u32[]{:S(2)}, u32[]{:S(2)}) collective-permute-start(bf16[10,1,64,128]{3,2,1,0:T(8,128)(2,1)S(1)} %get-tuple-element.11), channel_id=1, source_target_pairs={{0,1},{1,2},{2,3},{3,4},{4,5},{5,6},{6,7},{8,9},{9,10},{10,11},{11... | collective-permute-start | bytes 491528 | tf_op jit(solution)/shard_map/ppermute | solution.py:23
  23.4 1.9 %collective-permute-start.5 = (bf16[10,1,64,128]{3,2,1,0:T(8,128)(2,1)S(1)}, bf16[10,1,64,128]{3,2,1,0:T(8,128)(2,1)S(1)}, u32[]{:S(2)}, u32[]{:S(2)}) collective-permute-start(bf16[10,1,64,128]{3,2,1,0:T(8,128)(2,1)S(1)} %get-tuple-element.12), channel_id=1, source_target_pairs={{1,0},{2,1},{3,2},{4,3},{5,4},{6,5},{7,6},{9,8},{10,9},{11,10},{12... | collective-permute-start | bytes 491528 | tf_op jit(solution)/shard_map/ppermute | solution.py:26
  25.5 0.2 fusion.102
  25.8 4.3 %collective-permute-done.5 = bf16[10,1,64,128]{3,2,1,0:T(8,128)(2,1)S(1)} collective-permute-done((bf16[10,1,64,128]{3,2,1,0:T(8,128)(2,1)S(1)}, bf16[10,1,64,128]{3,2,1,0:T(8,128)(2,1)S(1)}, u32[]{:S(2)}, u32[]{:S(2)}) %collective-permute-start.5) | collective-permute-done | bytes 163872 | tf_op jit(solution)/shard_map/ppermute | solution.py:26
  30.0 0.3 fusion.42
  30.3 0.2 fusion.94
  30.6 0.2 fusion.91
  30.8 0.2 fusion.88
  31.0 0.2 fusion.85
  31.2 0.2 fusion.82
  31.4 0.2 fusion.79
  31.6 0.2 fusion.74
  32.1 0.2 convolution_add_fusion.23
  32.3 0.2 convolution_add_fusion.22
  32.5 0.2 fusion.2
  32.7 0.2 fusion.163
  33.0 0.2 fusion.4
  33.4 0.2 fusion.6
  33.6 0.2 fusion.8
  33.9 0.2 fusion.152
  34.1 0.2 fusion.10
  34.5 0.2 fusion.12
  35.2 0.2 convolution_add_fusion.13
  35.6 0.4 copy-done.5
  36.0 0.3 fusion.231
  36.9 1.1 %collective-permute-done.6 = f32[64]{0:T(128)S(1)} collective-permute-done((f32[64]{0:T(128)S(1)}, f32[64]{0:T(128)S(1)}, u32[]{:S(2)}, u32[]{:S(2)}) %collective-permute-start.6) | collective-permute-done | bytes 288 | tf_op jit(solution)/shard_map/ppermute | solution.py:41
  38.3 2.2 %collective-permute-done.7 = f32[64]{0:T(128)S(1)} collective-permute-done((f32[64]{0:T(128)S(1)}, f32[64]{0:T(128)S(1)}, u32[]{:S(2)}, u32[]{:S(2)}) %collective-permute-start.7) | collective-permute-done | bytes 288 | tf_op jit(solution)/shard_map/ppermute | solution.py:41
  40.5 1.0 %collective-permute-start.8 = (f32[64]{0:T(128)S(1)}, f32[64]{0:T(128)S(1)}, u32[]{:S(2)}, u32[]{:S(2)}) collective-permute-start(f32[64]{0:T(128)S(1)} %add.264), channel_id=1, source_target_pairs={{0,4},{1,5},{2,6},{3,7},{4,0},{5,1},{6,2},{7,3},{8,12},{9,13},{10,... | collective-permute-start | bytes 776 | tf_op jit(solution)/shard_map/ppermute | solution.py:41
  41.5 2.3 %collective-permute-done.8 = f32[64]{0:T(128)S(1)} collective-permute-done((f32[64]{0:T(128)S(1)}, f32[64]{0:T(128)S(1)}, u32[]{:S(2)}, u32[]{:S(2)}) %collective-permute-start.8) | collective-permute-done | bytes 288 | tf_op jit(solution)/shard_map/ppermute | solution.py:41
  44.5 2.4 %collective-permute-start.9 = (bf16[2,2,64,128]{3,2,1,0:T(8,128)(2,1)S(1)}, bf16[2,2,64,128]{3,2,1,0:T(8,128)(2,1)S(1)}, u32[]{:S(2)}, u32[]{:S(2)}) collective-permute-start(bf16[2,2,64,128]{3,2,1,0:T(8,128)(2,1)S(1)} %slice.509), channel_id=1, source_target_pairs={{0,8},{8,16},{16,24},{1,9},{9,17},{17,25},{2,10},{10,18},{18,26},{... | collective-permute-start | bytes 196616 | tf_op jit(solution)/shard_map/ppermute | solution.py:15
  46.9 3.6 %collective-permute-done.9 = bf16[2,2,64,128]{3,2,1,0:T(8,128)(2,1)S(1)} collective-permute-done((bf16[2,2,64,128]{3,2,1,0:T(8,128)(2,1)S(1)}, bf16[2,2,64,128]{3,2,1,0:T(8,128)(2,1)S(1)}, u32[]{:S(2)}, u32[]{:S(2)}) %collective-permute-start.9) | collective-permute-done | bytes 65568 | tf_op jit(solution)/shard_map/ppermute | solution.py:15
  50.6 6.7 %collective-permute-start.10 = (bf16[10,1,64,128]{3,2,1,0:T(8,128)(2,1)S(1)}, bf16[10,1,64,128]{3,2,1,0:T(8,128)(2,1)S(1)}, u32[]{:S(2)}, u32[]{:S(2)}) collective-permute-start(bf16[10,1,64,128]{3,2,1,0:T(8,128)(2,1)S(1)} %get-tuple-element.9), channel_id=1, source_target_pairs={{0,1},{1,2},{2,3},{3,4},{4,5},{5,6},{6,7},{8,9},{9,10},{10,11},{11... | collective-permute-start | bytes 491528 | tf_op jit(solution)/shard_map/ppermute | solution.py:23
  57.3 1.9 %collective-permute-start.11 = (bf16[10,1,64,128]{3,2,1,0:T(8,128)(2,1)S(1)}, bf16[10,1,64,128]{3,2,1,0:T(8,128)(2,1)S(1)}, u32[]{:S(2)}, u32[]{:S(2)}) collective-permute-start(bf16[10,1,64,128]{3,2,1,0:T(8,128)(2,1)S(1)} %get-tuple-element.10), channel_id=1, source_target_pairs={{1,0},{2,1},{3,2},{4,3},{5,4},{6,5},{7,6},{9,8},{10,9},{11,10},{12... | collective-permute-start | bytes 491528 | tf_op jit(solution)/shard_map/ppermute | solution.py:26
  59.7 4.3 %collective-permute-done.11 = bf16[10,1,64,128]{3,2,1,0:T(8,128)(2,1)S(1)} collective-permute-done((bf16[10,1,64,128]{3,2,1,0:T(8,128)(2,1)S(1)}, bf16[10,1,64,128]{3,2,1,0:T(8,128)(2,1)S(1)}, u32[]{:S(2)}, u32[]{:S(2)}) %collective-permute-start.11) | collective-permute-done | bytes 163872 | tf_op jit(solution)/shard_map/ppermute | solution.py:26
  63.9 0.3 select_maximum_fusion
  64.3 0.2 fusion.69
  64.5 0.2 fusion.66
  64.7 0.2 fusion.63
  64.9 0.2 fusion.60
  65.1 0.2 fusion.57
  65.4 0.2 fusion.54
  65.6 0.2 fusion.49
  66.0 0.2 convolution_add_fusion.11
  66.2 0.2 convolution_add_fusion.10
  66.5 0.2 fusion.17
  66.9 0.2 fusion.19
  67.3 0.2 fusion.21
  67.5 0.2 fusion.23
  68.0 0.2 fusion.25
  68.4 0.2 fusion.27
  68.7 0.2 convolution_add_fusion.3
  68.9 0.2 convolution_add_fusion.2
  69.1 0.2 convolution_add_fusion.1
  69.6 0.7 %copy-done = bf16[8,2,64,128]{3,2,1,0:T(8,128)(2,1)S(1)} copy-done((bf16[8,2,64,128]{3,2,1,0:T(8,128)(2,1)S(1)}, bf16[8,2,64,128]{3,2,1,0:T(8,128)(2,1)}, u32[]{:S(2)}) %copy-start) | copy-done | bytes 262168
  70.3 1.0 %fusion.34 = bf16[8,2,64,128]{3,2,1,0:T(8,128)(2,1)} fusion(f32[8,2,64,128]{3,2,1,0:T(8,128)S(1)} %fusion.49, f32[8,2,64,128]{3,2,1,0:T(8,128)S(1)} %fusion.108, f32[8,2,64,128]{3,2,1,0:T(8,128)S(1)} %convolution_add_fusion.1, bf16[8,2,64,128]{3,2,1,0:T(8,128)(2,1)S(1)} %copy-done, bf16[10,4,66,128]{3,2,1,0:T(8,128)(2,1)S(1)} %select_maximum_fusion, ...), kind=kOutput, calls=%fused_computation.60 | convolution fusion | flops 34471936 | bytes 2392576 | tf_op jit(solution)/shard_map/fhwc,cd->fhwd/dot_general | solution.py:71
  (69 shorter events, 5.8 us)
Async XLA Ops:
  0.0 16.5 %copy-start.3 = (bf16[2,2,64,128]{3,2,1,0:T(8,128)(2,1)S(1)}, bf16[2,2,64,128]{3,2,1,0:T(8,128)(2,1)}, u32[]{:S(2)}) copy-start(bf16[2,2,64,128]{3,2,1,0:T(8,128)(2,1)} %param.12) | copy-start | bytes 196612
  1.1 24.2 %copy-start.1 = (bf16[3,3,3,128,128]{4,3,2,1,0:T(8,128)(2,1)S(1)}, bf16[3,3,3,128,128]{4,3,2,1,0:T(8,128)(2,1)}, u32[]{:S(2)}) copy-start(bf16[3,3,3,128,128]{4,3,2,1,0:T(8,128)(2,1)} %param.16) | copy-start | bytes 2654212
  1.7 1.5 %collective-permute-start = (f32[64]{0:T(128)S(1)}, f32[64]{0:T(128)S(1)}, u32[]{:S(2)}, u32[]{:S(2)}) collective-permute-start(f32[64]{0:T(128)S(1)} %pad_maximum_fusion.8), channel_id=1, source_target_pairs={{0,1},{1,0},{2,3},{3,2},{4,5},{5,4},{6,7},{7,6},{8,9},{9,8},{10,11... | collective-permute-start | bytes 776 | tf_op jit(solution)/shard_map/ppermute | solution.py:41
  3.2 2.4 %collective-permute-start.1 = (f32[64]{0:T(128)S(1)}, f32[64]{0:T(128)S(1)}, u32[]{:S(2)}, u32[]{:S(2)}) collective-permute-start(f32[64]{0:T(128)S(1)} %fusion.235), channel_id=1, source_target_pairs={{0,2},{1,3},{2,0},{3,1},{4,6},{5,7},{6,4},{7,5},{8,10},{9,11},{10,... | collective-permute-start | bytes 776 | tf_op jit(solution)/shard_map/ppermute | solution.py:41
  5.6 3.3 %collective-permute-start.2 = (f32[64]{0:T(128)S(1)}, f32[64]{0:T(128)S(1)}, u32[]{:S(2)}, u32[]{:S(2)}) collective-permute-start(f32[64]{0:T(128)S(1)} %add.229), channel_id=1, source_target_pairs={{0,4},{1,5},{2,6},{3,7},{4,0},{5,1},{6,2},{7,3},{8,12},{9,13},{10,... | collective-permute-start | bytes 776 | tf_op jit(solution)/shard_map/ppermute | solution.py:41
  10.6 5.9 %collective-permute-start.3 = (bf16[2,2,64,128]{3,2,1,0:T(8,128)(2,1)S(1)}, bf16[2,2,64,128]{3,2,1,0:T(8,128)(2,1)S(1)}, u32[]{:S(2)}, u32[]{:S(2)}) collective-permute-start(bf16[2,2,64,128]{3,2,1,0:T(8,128)(2,1)S(1)} %slice.486), channel_id=1, source_target_pairs={{0,8},{8,16},{16,24},{1,9},{9,17},{17,25},{2,10},{10,18},{18,26},{... | collective-permute-start | bytes 196616 | tf_op jit(solution)/shard_map/ppermute | solution.py:15
  16.5 9.2 %collective-permute-start.4 = (bf16[10,1,64,128]{3,2,1,0:T(8,128)(2,1)S(1)}, bf16[10,1,64,128]{3,2,1,0:T(8,128)(2,1)S(1)}, u32[]{:S(2)}, u32[]{:S(2)}) collective-permute-start(bf16[10,1,64,128]{3,2,1,0:T(8,128)(2,1)S(1)} %get-tuple-element.11), channel_id=1, source_target_pairs={{0,1},{1,2},{2,3},{3,4},{4,5},{5,6},{6,7},{8,9},{9,10},{10,11},{11... | collective-permute-start | bytes 491528 | tf_op jit(solution)/shard_map/ppermute | solution.py:23
  23.4 6.6 %collective-permute-start.5 = (bf16[10,1,64,128]{3,2,1,0:T(8,128)(2,1)S(1)}, bf16[10,1,64,128]{3,2,1,0:T(8,128)(2,1)S(1)}, u32[]{:S(2)}, u32[]{:S(2)}) collective-permute-start(bf16[10,1,64,128]{3,2,1,0:T(8,128)(2,1)S(1)} %get-tuple-element.12), channel_id=1, source_target_pairs={{1,0},{2,1},{3,2},{4,3},{5,4},{6,5},{7,6},{9,8},{10,9},{11,10},{12... | collective-permute-start | bytes 491528 | tf_op jit(solution)/shard_map/ppermute | solution.py:26
  35.4 0.7 copy-start.5
  36.0 8.2 %copy-start.6 = (f32[128]{0:T(128)S(1)}, f32[128]{0:T(128)}, u32[]{:S(2)}) copy-start(f32[128]{0:T(128)} %param.19) | copy-start | bytes 1540
  36.0 8.2 %copy-start.7 = (f32[128]{0:T(128)S(1)}, f32[128]{0:T(128)}, u32[]{:S(2)}) copy-start(f32[128]{0:T(128)} %param.18) | copy-start | bytes 1540
  36.3 14.2 %copy-start.4 = (bf16[2,2,64,128]{3,2,1,0:T(8,128)(2,1)S(1)}, bf16[2,2,64,128]{3,2,1,0:T(8,128)(2,1)}, u32[]{:S(2)}) copy-start(bf16[2,2,64,128]{3,2,1,0:T(8,128)(2,1)} %param.13) | copy-start | bytes 196612
  36.9 1.1 %collective-permute-start.6 = (f32[64]{0:T(128)S(1)}, f32[64]{0:T(128)S(1)}, u32[]{:S(2)}, u32[]{:S(2)}) collective-permute-start(f32[64]{0:T(128)S(1)} %pad_maximum_fusion.9), channel_id=1, source_target_pairs={{0,1},{1,0},{2,3},{3,2},{4,5},{5,4},{6,7},{7,6},{8,9},{9,8},{10,11... | collective-permute-start | bytes 776 | tf_op jit(solution)/shard_map/ppermute | solution.py:41
  38.1 2.4 %collective-permute-start.7 = (f32[64]{0:T(128)S(1)}, f32[64]{0:T(128)S(1)}, u32[]{:S(2)}, u32[]{:S(2)}) collective-permute-start(f32[64]{0:T(128)S(1)} %fusion.234), channel_id=1, source_target_pairs={{0,2},{1,3},{2,0},{3,1},{4,6},{5,7},{6,4},{7,5},{8,10},{9,11},{10,... | collective-permute-start | bytes 776 | tf_op jit(solution)/shard_map/ppermute | solution.py:41
  40.5 3.3 %collective-permute-start.8 = (f32[64]{0:T(128)S(1)}, f32[64]{0:T(128)S(1)}, u32[]{:S(2)}, u32[]{:S(2)}) collective-permute-start(f32[64]{0:T(128)S(1)} %add.264), channel_id=1, source_target_pairs={{0,4},{1,5},{2,6},{3,7},{4,0},{5,1},{6,2},{7,3},{8,12},{9,13},{10,... | collective-permute-start | bytes 776 | tf_op jit(solution)/shard_map/ppermute | solution.py:41
  44.2 15.0 %copy-start.2 = (bf16[3,3,3,128,128]{4,3,2,1,0:T(8,128)(2,1)S(1)}, bf16[3,3,3,128,128]{4,3,2,1,0:T(8,128)(2,1)}, u32[]{:S(2)}) copy-start(bf16[3,3,3,128,128]{4,3,2,1,0:T(8,128)(2,1)} %param.20) | copy-start | bytes 2654212
  44.5 6.0 %collective-permute-start.9 = (bf16[2,2,64,128]{3,2,1,0:T(8,128)(2,1)S(1)}, bf16[2,2,64,128]{3,2,1,0:T(8,128)(2,1)S(1)}, u32[]{:S(2)}, u32[]{:S(2)}) collective-permute-start(bf16[2,2,64,128]{3,2,1,0:T(8,128)(2,1)S(1)} %slice.509), channel_id=1, source_target_pairs={{0,8},{8,16},{16,24},{1,9},{9,17},{17,25},{2,10},{10,18},{18,26},{... | collective-permute-start | bytes 196616 | tf_op jit(solution)/shard_map/ppermute | solution.py:15
  50.6 9.1 %collective-permute-start.10 = (bf16[10,1,64,128]{3,2,1,0:T(8,128)(2,1)S(1)}, bf16[10,1,64,128]{3,2,1,0:T(8,128)(2,1)S(1)}, u32[]{:S(2)}, u32[]{:S(2)}) collective-permute-start(bf16[10,1,64,128]{3,2,1,0:T(8,128)(2,1)S(1)} %get-tuple-element.9), channel_id=1, source_target_pairs={{0,1},{1,2},{2,3},{3,4},{4,5},{5,6},{6,7},{8,9},{9,10},{10,11},{11... | collective-permute-start | bytes 491528 | tf_op jit(solution)/shard_map/ppermute | solution.py:23
  57.3 6.6 %collective-permute-start.11 = (bf16[10,1,64,128]{3,2,1,0:T(8,128)(2,1)S(1)}, bf16[10,1,64,128]{3,2,1,0:T(8,128)(2,1)S(1)}, u32[]{:S(2)}, u32[]{:S(2)}) collective-permute-start(bf16[10,1,64,128]{3,2,1,0:T(8,128)(2,1)S(1)} %get-tuple-element.10), channel_id=1, source_target_pairs={{1,0},{2,1},{3,2},{4,3},{5,4},{6,5},{7,6},{9,8},{10,9},{11,10},{12... | collective-permute-start | bytes 491528 | tf_op jit(solution)/shard_map/ppermute | solution.py:26
  69.3 1.0 %copy-start = (bf16[8,2,64,128]{3,2,1,0:T(8,128)(2,1)S(1)}, bf16[8,2,64,128]{3,2,1,0:T(8,128)(2,1)}, u32[]{:S(2)}) copy-start(bf16[8,2,64,128]{3,2,1,0:T(8,128)(2,1)} %param.11) | copy-start | bytes 786436
  69.4 0.9 %copy-start.8 = (f32[128]{0:T(128)S(1)}, f32[128]{0:T(128)}, u32[]{:S(2)}) copy-start(f32[128]{0:T(128)} %param.21) | copy-start | bytes 1540

commit v3 on v1

--- a/solution.py
+++ b/solution.py
@@ -35,8 +35,7 @@
     partial = jnp.concatenate(
         [jnp.sum(grouped, axis=(0, 2)), jnp.sum(grouped * grouped, axis=(0, 2))]
     )
-    everyone = jnp.broadcast_to(partial, (lax.axis_size("rows"), 2 * GROUPS))
-    received = lax.all_to_all(everyone, "rows", 0, 0, tiled=True)
+    received = lax.all_gather(partial, "rows")
     totals, squares = jnp.split(jnp.sum(received, axis=0), 2)
     average = totals / cells_total
     spread = squares / cells_total - average * average

time: 68.7 us -> 79 us (1.15)
  blocking collectives: 16.8 us -> 25.2 us
  waiting for transfers between devices: 15 us -> 11.4 us
  starting transfers between devices: 17.2 us -> 20.4 us
  local copies, waits for them, and re-layouts: 2.33 us -> 3.76 us
    unnamed x0 -> x2, blocking collectives: none -> 25.2 us
    all_to_all x2 -> x0, blocking collectives: 16.8 us -> none  [group_moments(): received = lax.all_to_all(everyone, 'rows', 0, 0, tiled=True)]
    ppermute x2, starting transfers between devices: 3.84 us -> 7.39 us  [extended(): lax.ppermute(lax.slice_in_dim(block, 0, width, axis=dim), axis, backward)]
    ppermute x2, waiting for transfers between devices: 8.52 us -> 4.98 us  [extended(): lax.ppermute(lax.slice_in_dim(block, 0, width, axis=dim), axis, backward)]
    unnamed x18 -> x21, local copies, waits for them, and re-layouts: 1.19 us -> 2.48 us
where the time goes in v3:
time: 79 us; the launch traced here: 78.6 us
  blocking collectives  25.2 us (32%)
  starting transfers between devices  20.4 us (26%)
  matrix products  12.4 us (16%)
  waiting for transfers between devices  11.4 us (14%)
  other arithmetic  4.2 us (5%)
  local copies, waits for them, and re-layouts  3.76 us (5%)
  between operations  1.26 us (2%)
    unnamed x2, blocking collectives  25.2 us
    dot_general x54, matrix products, causal_conv(): jnp.einsum('fhwc,cd->fhwd', piece, weight[frame_tap, row_tap, col_tap], p...  12.4 us
    ppermute x2, starting transfers between devices, extended(): lax.ppermute(lax.slice_in_dim(block, block.shape[dim] - width, None, axis...  7.51 us
    ppermute x2, starting transfers between devices, extended(): lax.ppermute(lax.slice_in_dim(block, 0, width, axis=dim), axis, backward)  7.39 us
    ppermute x2, waiting for transfers between devices, from_behind(): return lax.ppermute(block, axis, route)  6.45 us
    ppermute x2, starting transfers between devices, from_behind(): return lax.ppermute(block, axis, route)  5.48 us
    ppermute x2, waiting for transfers between devices, extended(): lax.ppermute(lax.slice_in_dim(block, 0, width, axis=dim), axis, backward)  4.98 us
    unnamed x21, local copies, waits for them, and re-layouts  2.48 us
  transfers between devices with their start and end apart: 6, of which 4 were waited for; matrix products, arithmetic and copies ran while one was open for 1% of the time, Pallas kernels for 0%

profile of v3, /device:TPU:5, one launch (start us, length us, event | category | flops | bytes accessed | tf_op | source)
XLA Modules:
  0.0 78.6 jit_solution(155762476115640561)
XLA Ops:
  0.0 1.1 %convert_reduce_fusion = (f32[128]{0:T(128)S(1)}, f32[128]{0:T(128)S(1)}) fusion(bf16[8,2,64,128]{3,2,1,0:T(8,128)(2,1)} %param.11), kind=kLoop, calls=%fused_computation.63 | loop fusion | flops 524032 | bytes 263168 | tf_op jit(solution)/shard_map/reduce_sum | solution.py:36
  1.4 1.3 %dynamic-slice = u32[1]{0:T(128)} dynamic-slice(u32[32]{0:T(128)} %constant.32, u32[]{:T(128)S(6)} %add.275), dynamic_slice_sizes={1} | dynamic-slice | bytes 12
  3.7 13.8 %all-reduce.2 = f32[512]{0:T(512)S(1)} all-reduce(f32[512]{0:T(512)S(1)} %maximum_dynamic-update-slice_fusion), channel_id=2, replica_groups=mesh['section'=4,'rows'=8] {'rows'}, use_global_device_ids=true, to_apply=%add.2 | all-reduce | flops 512 | bytes 4096
  18.0 1.2 %multiply_convert_fusion.1 = bf16[8,2,64,128]{3,2,1,0:T(8,128)(2,1)S(1)} fusion(bf16[8,2,64,128]{3,2,1,0:T(8,128)(2,1)} %param.11, f32[128]{0:T(128)} %param.15, f32[128]{0:T(128)} %param.14, f32[128]{0:T(128)S(1)} %div.48, f32[128]{0:T(128)S(1)} %sub.33), kind=kLoop, calls=%fused_computation.82 | loop fusion | flops 1310720 | bytes 526336 | tf_op jit(solution)/shard_map/convert_element_type | solution.py:50
  19.2 3.1 %collective-permute-start = (bf16[2,2,64,128]{3,2,1,0:T(8,128)(2,1)S(1)}, bf16[2,2,64,128]{3,2,1,0:T(8,128)(2,1)S(1)}, u32[]{:S(2)}, u32[]{:S(2)}) collective-permute-start(bf16[2,2,64,128]{3,2,1,0:T(8,128)(2,1)S(1)} %slice.486), channel_id=1, source_target_pairs={{0,8},{8,16},{16,24},{1,9},{9,17},{17,25},{2,10},{10,18},{18,26},{... | collective-permute-start | bytes 196616 | tf_op jit(solution)/shard_map/ppermute | solution.py:15
  22.4 2.8 %collective-permute-done = bf16[2,2,64,128]{3,2,1,0:T(8,128)(2,1)S(1)} collective-permute-done((bf16[2,2,64,128]{3,2,1,0:T(8,128)(2,1)S(1)}, bf16[2,2,64,128]{3,2,1,0:T(8,128)(2,1)S(1)}, u32[]{:S(2)}, u32[]{:S(2)}) %collective-permute-start) | collective-permute-done | bytes 65568 | tf_op jit(solution)/shard_map/ppermute | solution.py:15
  25.2 4.1 %collective-permute-start.1 = (bf16[10,1,64,128]{3,2,1,0:T(8,128)(2,1)S(1)}, bf16[10,1,64,128]{3,2,1,0:T(8,128)(2,1)S(1)}, u32[]{:S(2)}, u32[]{:S(2)}) collective-permute-start(bf16[10,1,64,128]{3,2,1,0:T(8,128)(2,1)S(1)} %get-tuple-element.11), channel_id=1, source_target_pairs={{0,1},{1,2},{2,3},{3,4},{4,5},{5,6},{6,7},{8,9},{9,10},{10,11},{11... | collective-permute-start | bytes 491528 | tf_op jit(solution)/shard_map/ppermute | solution.py:23
  29.3 3.7 %collective-permute-start.2 = (bf16[10,1,64,128]{3,2,1,0:T(8,128)(2,1)S(1)}, bf16[10,1,64,128]{3,2,1,0:T(8,128)(2,1)S(1)}, u32[]{:S(2)}, u32[]{:S(2)}) collective-permute-start(bf16[10,1,64,128]{3,2,1,0:T(8,128)(2,1)S(1)} %get-tuple-element.12), channel_id=1, source_target_pairs={{1,0},{2,1},{3,2},{4,3},{5,4},{6,5},{7,6},{9,8},{10,9},{11,10},{12... | collective-permute-start | bytes 491528 | tf_op jit(solution)/shard_map/ppermute | solution.py:26
  33.3 0.2 fusion.102
  33.5 2.5 %collective-permute-done.2 = bf16[10,1,64,128]{3,2,1,0:T(8,128)(2,1)S(1)} collective-permute-done((bf16[10,1,64,128]{3,2,1,0:T(8,128)(2,1)S(1)}, bf16[10,1,64,128]{3,2,1,0:T(8,128)(2,1)S(1)}, u32[]{:S(2)}, u32[]{:S(2)}) %collective-permute-start.2) | collective-permute-done | bytes 163872 | tf_op jit(solution)/shard_map/ppermute | solution.py:26
  36.0 0.3 fusion.42
  36.3 0.2 fusion.94
  36.5 0.2 fusion.91
  36.7 0.2 fusion.88
  36.9 0.2 fusion.85
  37.2 0.2 fusion.82
  37.4 0.2 fusion.79
  37.6 0.2 fusion.74
  37.8 0.2 fusion.170
  38.0 0.2 convolution_add_fusion.23
  38.2 0.2 convolution_add_fusion.22
  38.5 0.2 fusion.2
  38.9 0.2 fusion.4
  39.3 0.2 fusion.6
  39.6 0.2 fusion.8
  40.0 0.2 fusion.10
  40.2 0.2 fusion.148
  40.5 0.2 fusion.12
  40.7 0.2 convolution_add_fusion.15
  40.9 0.2 convolution_add_fusion.14
  41.1 0.2 convolution_add_fusion.13
  41.4 0.2 fusion.141
  41.6 0.4 copy-done.5
  42.0 0.3 fusion.231
  42.9 11.4 %all-reduce.3 = f32[512]{0:T(512)S(1)} all-reduce(f32[512]{0:T(512)S(1)} %maximum_dynamic-update-slice_fusion.1), channel_id=3, replica_groups=mesh['section'=4,'rows'=8] {'rows'}, use_global_device_ids=true, to_apply=%add.3 | all-reduce | flops 512 | bytes 4096
  55.1 2.4 %collective-permute-start.3 = (bf16[2,2,64,128]{3,2,1,0:T(8,128)(2,1)S(1)}, bf16[2,2,64,128]{3,2,1,0:T(8,128)(2,1)S(1)}, u32[]{:S(2)}, u32[]{:S(2)}) collective-permute-start(bf16[2,2,64,128]{3,2,1,0:T(8,128)(2,1)S(1)} %slice.509), channel_id=1, source_target_pairs={{0,8},{8,16},{16,24},{1,9},{9,17},{17,25},{2,10},{10,18},{18,26},{... | collective-permute-start | bytes 196616 | tf_op jit(solution)/shard_map/ppermute | solution.py:15
  57.5 3.7 %collective-permute-done.3 = bf16[2,2,64,128]{3,2,1,0:T(8,128)(2,1)S(1)} collective-permute-done((bf16[2,2,64,128]{3,2,1,0:T(8,128)(2,1)S(1)}, bf16[2,2,64,128]{3,2,1,0:T(8,128)(2,1)S(1)}, u32[]{:S(2)}, u32[]{:S(2)}) %collective-permute-start.3) | collective-permute-done | bytes 65568 | tf_op jit(solution)/shard_map/ppermute | solution.py:15
  61.2 3.4 %collective-permute-start.4 = (bf16[10,1,64,128]{3,2,1,0:T(8,128)(2,1)S(1)}, bf16[10,1,64,128]{3,2,1,0:T(8,128)(2,1)S(1)}, u32[]{:S(2)}, u32[]{:S(2)}) collective-permute-start(bf16[10,1,64,128]{3,2,1,0:T(8,128)(2,1)S(1)} %get-tuple-element.9), channel_id=1, source_target_pairs={{0,1},{1,2},{2,3},{3,4},{4,5},{5,6},{6,7},{8,9},{9,10},{10,11},{11... | collective-permute-start | bytes 491528 | tf_op jit(solution)/shard_map/ppermute | solution.py:23
  64.6 3.7 %collective-permute-start.5 = (bf16[10,1,64,128]{3,2,1,0:T(8,128)(2,1)S(1)}, bf16[10,1,64,128]{3,2,1,0:T(8,128)(2,1)S(1)}, u32[]{:S(2)}, u32[]{:S(2)}) collective-permute-start(bf16[10,1,64,128]{3,2,1,0:T(8,128)(2,1)S(1)} %get-tuple-element.10), channel_id=1, source_target_pairs={{1,0},{2,1},{3,2},{4,3},{5,4},{6,5},{7,6},{9,8},{10,9},{11,10},{12... | collective-permute-start | bytes 491528 | tf_op jit(solution)/shard_map/ppermute | solution.py:26
  68.5 0.2 fusion.100
  68.7 2.5 %collective-permute-done.5 = bf16[10,1,64,128]{3,2,1,0:T(8,128)(2,1)S(1)} collective-permute-done((bf16[10,1,64,128]{3,2,1,0:T(8,128)(2,1)S(1)}, bf16[10,1,64,128]{3,2,1,0:T(8,128)(2,1)S(1)}, u32[]{:S(2)}, u32[]{:S(2)}) %collective-permute-start.5) | collective-permute-done | bytes 163872 | tf_op jit(solution)/shard_map/ppermute | solution.py:26
  71.3 0.3 select_maximum_fusion
  71.6 0.2 fusion.69
  71.8 0.2 fusion.66
  72.0 0.2 fusion.63
  72.2 0.2 fusion.60
  72.4 0.2 fusion.57
  72.7 0.2 fusion.54
  72.9 0.2 fusion.49
  73.1 0.2 fusion.137
  73.3 0.2 convolution_add_fusion.11
  73.5 0.2 convolution_add_fusion.10
  73.8 0.2 fusion.17
  74.2 0.2 fusion.19
  74.4 0.2 fusion.126
  74.6 0.2 fusion.21
  74.9 0.2 fusion.23
  75.3 0.2 fusion.25
  75.8 0.2 fusion.27
  76.0 0.2 convolution_add_fusion.3
  76.2 0.2 convolution_add_fusion.2
  76.5 0.2 convolution_add_fusion.1
  76.9 0.7 copy-done
  77.6 1.0 %fusion.34 = bf16[8,2,64,128]{3,2,1,0:T(8,128)(2,1)} fusion(f32[8,2,64,128]{3,2,1,0:T(8,128)S(1)} %fusion.49, f32[8,2,64,128]{3,2,1,0:T(8,128)S(1)} %fusion.108, f32[8,2,64,128]{3,2,1,0:T(8,128)S(1)} %convolution_add_fusion.1, bf16[8,2,64,128]{3,2,1,0:T(8,128)(2,1)S(1)} %copy-done, bf16[10,4,66,128]{3,2,1,0:T(8,128)(2,1)S(1)} %select_maximum_fusion, ...), kind=kOutput, calls=%fused_computation.60 | convolution fusion | flops 34471936 | bytes 2392576 | tf_op jit(solution)/shard_map/fhwc,cd->fhwd/dot_general | solution.py:67
  (60 shorter events, 4.4 us)
Async XLA Ops:
  0.0 25.1 %copy-start.3 = (bf16[2,2,64,128]{3,2,1,0:T(8,128)(2,1)S(1)}, bf16[2,2,64,128]{3,2,1,0:T(8,128)(2,1)}, u32[]{:S(2)}) copy-start(bf16[2,2,64,128]{3,2,1,0:T(8,128)(2,1)} %param.12) | copy-start | bytes 196612
  1.1 31.9 %copy-start.1 = (bf16[3,3,3,128,128]{4,3,2,1,0:T(8,128)(2,1)S(1)}, bf16[3,3,3,128,128]{4,3,2,1,0:T(8,128)(2,1)}, u32[]{:S(2)}) copy-start(bf16[3,3,3,128,128]{4,3,2,1,0:T(8,128)(2,1)} %param.16) | copy-start | bytes 2654212
  19.2 5.9 %collective-permute-start = (bf16[2,2,64,128]{3,2,1,0:T(8,128)(2,1)S(1)}, bf16[2,2,64,128]{3,2,1,0:T(8,128)(2,1)S(1)}, u32[]{:S(2)}, u32[]{:S(2)}) collective-permute-start(bf16[2,2,64,128]{3,2,1,0:T(8,128)(2,1)S(1)} %slice.486), channel_id=1, source_target_pairs={{0,8},{8,16},{16,24},{1,9},{9,17},{17,25},{2,10},{10,18},{18,26},{... | collective-permute-start | bytes 196616 | tf_op jit(solution)/shard_map/ppermute | solution.py:15
  25.2 8.3 %collective-permute-start.1 = (bf16[10,1,64,128]{3,2,1,0:T(8,128)(2,1)S(1)}, bf16[10,1,64,128]{3,2,1,0:T(8,128)(2,1)S(1)}, u32[]{:S(2)}, u32[]{:S(2)}) collective-permute-start(bf16[10,1,64,128]{3,2,1,0:T(8,128)(2,1)S(1)} %get-tuple-element.11), channel_id=1, source_target_pairs={{0,1},{1,2},{2,3},{3,4},{4,5},{5,6},{6,7},{8,9},{9,10},{10,11},{11... | collective-permute-start | bytes 491528 | tf_op jit(solution)/shard_map/ppermute | solution.py:23
  29.3 6.6 %collective-permute-start.2 = (bf16[10,1,64,128]{3,2,1,0:T(8,128)(2,1)S(1)}, bf16[10,1,64,128]{3,2,1,0:T(8,128)(2,1)S(1)}, u32[]{:S(2)}, u32[]{:S(2)}) collective-permute-start(bf16[10,1,64,128]{3,2,1,0:T(8,128)(2,1)S(1)} %get-tuple-element.12), channel_id=1, source_target_pairs={{1,0},{2,1},{3,2},{4,3},{5,4},{6,5},{7,6},{9,8},{10,9},{11,10},{12... | collective-permute-start | bytes 491528 | tf_op jit(solution)/shard_map/ppermute | solution.py:26
  41.3 0.7 copy-start.5
  42.0 12.9 %copy-start.6 = (f32[128]{0:T(128)S(1)}, f32[128]{0:T(128)}, u32[]{:S(2)}) copy-start(f32[128]{0:T(128)} %param.19) | copy-start | bytes 1540
  42.0 12.9 %copy-start.7 = (f32[128]{0:T(128)S(1)}, f32[128]{0:T(128)}, u32[]{:S(2)}) copy-start(f32[128]{0:T(128)} %param.18) | copy-start | bytes 1540
  42.3 18.9 %copy-start.4 = (bf16[2,2,64,128]{3,2,1,0:T(8,128)(2,1)S(1)}, bf16[2,2,64,128]{3,2,1,0:T(8,128)(2,1)}, u32[]{:S(2)}) copy-start(bf16[2,2,64,128]{3,2,1,0:T(8,128)(2,1)} %param.13) | copy-start | bytes 196612
  54.9 13.4 %copy-start.2 = (bf16[3,3,3,128,128]{4,3,2,1,0:T(8,128)(2,1)S(1)}, bf16[3,3,3,128,128]{4,3,2,1,0:T(8,128)(2,1)}, u32[]{:S(2)}) copy-start(bf16[3,3,3,128,128]{4,3,2,1,0:T(8,128)(2,1)} %param.20) | copy-start | bytes 2654212
  55.1 6.0 %collective-permute-start.3 = (bf16[2,2,64,128]{3,2,1,0:T(8,128)(2,1)S(1)}, bf16[2,2,64,128]{3,2,1,0:T(8,128)(2,1)S(1)}, u32[]{:S(2)}, u32[]{:S(2)}) collective-permute-start(bf16[2,2,64,128]{3,2,1,0:T(8,128)(2,1)S(1)} %slice.509), channel_id=1, source_target_pairs={{0,8},{8,16},{16,24},{1,9},{9,17},{17,25},{2,10},{10,18},{18,26},{... | collective-permute-start | bytes 196616 | tf_op jit(solution)/shard_map/ppermute | solution.py:15
  61.2 7.5 %collective-permute-start.4 = (bf16[10,1,64,128]{3,2,1,0:T(8,128)(2,1)S(1)}, bf16[10,1,64,128]{3,2,1,0:T(8,128)(2,1)S(1)}, u32[]{:S(2)}, u32[]{:S(2)}) collective-permute-start(bf16[10,1,64,128]{3,2,1,0:T(8,128)(2,1)S(1)} %get-tuple-element.9), channel_id=1, source_target_pairs={{0,1},{1,2},{2,3},{3,4},{4,5},{5,6},{6,7},{8,9},{9,10},{10,11},{11... | collective-permute-start | bytes 491528 | tf_op jit(solution)/shard_map/ppermute | solution.py:23
  64.6 6.6 %collective-permute-start.5 = (bf16[10,1,64,128]{3,2,1,0:T(8,128)(2,1)S(1)}, bf16[10,1,64,128]{3,2,1,0:T(8,128)(2,1)S(1)}, u32[]{:S(2)}, u32[]{:S(2)}) collective-permute-start(bf16[10,1,64,128]{3,2,1,0:T(8,128)(2,1)S(1)} %get-tuple-element.10), channel_id=1, source_target_pairs={{1,0},{2,1},{3,2},{4,3},{5,4},{6,5},{7,6},{9,8},{10,9},{11,10},{12... | collective-permute-start | bytes 491528 | tf_op jit(solution)/shard_map/ppermute | solution.py:26
  76.7 1.0 %copy-start = (bf16[8,2,64,128]{3,2,1,0:T(8,128)(2,1)S(1)}, bf16[8,2,64,128]{3,2,1,0:T(8,128)(2,1)}, u32[]{:S(2)}) copy-start(bf16[8,2,64,128]{3,2,1,0:T(8,128)(2,1)} %param.11) | copy-start | bytes 786436
  76.7 0.9 %copy-start.8 = (f32[128]{0:T(128)S(1)}, f32[128]{0:T(128)}, u32[]{:S(2)}) copy-start(f32[128]{0:T(128)} %param.21) | copy-start | bytes 1540

commit v4 on v0

v4 whole, which is shorter than its diff:
```python
import functools

import functools

import jax
import jax.numpy as jnp
from jax import lax
from jax.experimental import pallas as pl
from jax.experimental.pallas import tpu as pltpu
from jax.sharding import PartitionSpec as P

GROUPS = 32
SPAN_HALO = 4

epsilon = 1e-06


def moments(blocks):
    cells = sum(block.shape[0] for block in blocks)
    total = sum(jnp.sum(block, axis=0, keepdims=True) for block in blocks)
    mean = total * (1.0 / cells)
    centred = sum(
        jnp.sum((block - mean) * (block - mean), axis=0, keepdims=True) for block in blocks
    )
    return jnp.concatenate([total, centred], axis=1)


def group_sum(values, width):
    lanes = values.shape[-1]
    lane = lax.broadcasted_iota(jnp.int32, values.shape, values.ndim - 1)
    step = 1
    while step < width:
        up = pltpu.roll(values, lanes - step, values.ndim - 1)
        down = pltpu.roll(values, step, values.ndim - 1)
        values = values + jnp.where((lane // step) % 2 == 0, up, down)
        step *= 2
    return values


def affine(stats, cells, scale, shift):
    channels = scale.shape[-1]
    width = channels // GROUPS
    totals, centred = stats[:, 0, :channels], stats[:, 0, channels:]
    count = cells * width * stats.shape[0]
    average = group_sum(jnp.sum(totals, axis=0, keepdims=True), width) * (1.0 / count)
    away = totals * (1.0 / cells) - average
    inner = jnp.sum(centred + cells * (away * away), axis=0, keepdims=True)
    spread = group_sum(inner, width) * (1.0 / count)
    slope = 0.5 * scale / jnp.sqrt(spread + epsilon)
    return slope, 0.5 * shift - average * slope


def activate(values, slope, offset):
    half = values.astype(jnp.float32) * slope + offset
    return half + half * jnp.tanh(half)


def pair_conv(field, row, frames, weight_ref):
    columns, channels = field.shape[2], field.shape[3]
    pieces, blocks = [], []
    nothing = jnp.zeros((channels, channels), jnp.bfloat16)
    for frame_tap in range(3):
        for line in range(4):
            piece = field[frame_tap : frame_tap + frames, row + line]
            pieces.append(piece.reshape(frames * columns, channels))
            blocks.append(
                jnp.concatenate(
                    [
                        weight_ref[frame_tap, line - out, col_tap]
                        if 0 <= line - out <= 2
                        else nothing
                        for col_tap in range(3)
                        for out in range(2)
                    ],
                    axis=1,
                )
            )
    product = jnp.dot(
        jnp.concatenate(pieces, axis=1),
        jnp.concatenate(blocks, axis=0),
        preferred_element_type=jnp.float32,
    )
    cells = frames * columns
    column = lax.broadcasted_iota(jnp.int32, (cells, channels), 0) % columns
    results = []
    for out in range(2):
        left, centre, right = (
            product[:, (2 * tap + out) * channels : (2 * tap + out + 1) * channels]
            for tap in range(3)
        )
        left = jnp.where(column == 0, 0.0, pltpu.roll(left, 1, 0))
        right = jnp.where(column == columns - 1, 0.0, pltpu.roll(right, cells - 1, 0))
        results.append(left + centre + right)
    return results


def stats_kernel(own_ref, stats_ref):
    own = own_ref[...].astype(jnp.float32)
    packed = moments([own.reshape(-1, own.shape[-1])])
    stats_ref[...] = jnp.broadcast_to(packed[None], stats_ref.shape)


def first_kernel(
    row_count, place, own_ref, near_ref, far_ref, stats_ref, scale_ref, shift_ref, weight_ref, bias_ref,
    middle_ref, sums_ref, field
):
    section, row_at = place[0], place[1]
    frames, lines, columns, channels = own_ref.shape
    inner = frames - SPAN_HALO
    cells = inner * lines * columns
    scale, shift = scale_ref[...], shift_ref[...]
    mine = stats_ref[pl.ds(section * row_count, row_count)]
    before = stats_ref[pl.ds(jnp.maximum(section - 1, 0) * row_count, row_count)]
    slope, offset = affine(mine, cells, scale, shift)
    slope_before, offset_before = affine(before, cells, scale, shift)
    even = row_at % 2 == 0
    at_start = section == 0
    for line in range(3 * lines):
        side, local = divmod(line, lines)
        if side == 1:
            block = own_ref[:, local]
        else:
            near_side = even if side == 2 else jnp.logical_not(even)
            block = jnp.where(near_side, near_ref[:, local], far_ref[:, local])
        halo, body = block[:SPAN_HALO], block[SPAN_HALO:]
        behind = activate(halo, slope_before, offset_before).astype(jnp.bfloat16)
        behind = jnp.where(at_start, halo, behind)
        ahead = activate(body, slope, offset).astype(jnp.bfloat16)
        if side != 1:
            outside = row_at == 0 if side == 0 else row_at == row_count - 1
            behind = jnp.where(outside, jnp.zeros_like(behind), behind)
            ahead = jnp.where(outside, jnp.zeros_like(ahead), ahead)
        field[:SPAN_HALO, line] = behind
        field[SPAN_HALO:, line] = ahead
    bias = bias_ref[...]
    kept = []
    spare = SPAN_HALO - 2
    for pair in range((lines + 2) // 2):
        results = pair_conv(field, 2 * pair, inner + 2, weight_ref)
        for out in range(2):
            line = 2 * pair + out
            rounded = (results[out] + bias).astype(jnp.bfloat16)
            rounded = rounded.reshape(inner + 2, columns, channels)
            middle_ref[:2, line] = jnp.where(at_start, field[:spare, line + lines - 1], rounded[:2])
            middle_ref[2:, line] = rounded[2:]
            if 1 <= line <= lines:
                kept.append(rounded[2:].astype(jnp.float32).reshape(-1, channels))
    sums_ref[...] = jnp.broadcast_to(moments(kept)[None], sums_ref.shape)


def second_kernel(
    row_count, place, middle_ref, stats_ref, scale_ref, shift_ref, weight_ref, bias_ref, own_ref,
    out_ref, field
):
    section, row_at = place[0], place[1]
    frames, lines, columns, channels = own_ref.shape
    cells = frames * lines * columns
    scale, shift = scale_ref[...], shift_ref[...]
    mine = stats_ref[pl.ds(section * row_count, row_count)]
    before = stats_ref[pl.ds(jnp.maximum(section - 1, 0) * row_count, row_count)]
    slope, offset = affine(mine, cells, scale, shift)
    slope_before, offset_before = affine(before, cells, scale, shift)
    at_start = section == 0
    for line in range(lines + 2):
        halo, body = middle_ref[:2, line], middle_ref[2:, line]
        behind = activate(halo, slope_before, offset_before).astype(jnp.bfloat16)
        behind = jnp.where(at_start, halo, behind)
        ahead = activate(body, slope, offset).astype(jnp.bfloat16)
        if line == 0 or line == lines + 1:
            outside = row_at == 0 if line == 0 else row_at == row_count - 1
            behind = jnp.where(outside, jnp.zeros_like(behind), behind)
            ahead = jnp.where(outside, jnp.zeros_like(ahead), ahead)
        field[:2, line] = behind
        field[2:, line] = ahead
    bias = bias_ref[...]
    for pair in range(lines // 2):
        results = pair_conv(field, 2 * pair, frames, weight_ref)
        for out in range(2):
            line = 2 * pair + out
            result = (results[out] + bias).reshape(frames, columns, channels)
            out_ref[:, line] = (result + own_ref[:, line].astype(jnp.float32)).astype(jnp.bfloat16)


def call(kernel, out_shape, scratch, operands, scalars=True, flops=0):
    specs = [pl.BlockSpec(memory_space=pltpu.VMEM)] * len(operands)
    if scalars:
        specs[0] = pl.BlockSpec(memory_space=pltpu.SMEM)
    return pl.pallas_call(
        kernel,
        out_shape=out_shape,
        in_specs=specs,
        out_specs=jax.tree.map(lambda _: pl.BlockSpec(memory_space=pltpu.VMEM), out_shape),
        scratch_shapes=scratch,
        compiler_params=pltpu.CompilerParams(vmem_limit_bytes=40 * 2**20),
        cost_estimate=pl.CostEstimate(flops=flops, bytes_accessed=2**20, transcendentals=0),
    )(*operands)


def on_device(
    activations,
    first_cache,
    second_cache,
    norm1_scale,
    norm1_shift,
    conv1_weight,
    conv1_bias,
    norm2_scale,
    norm2_shift,
    conv2_weight,
    conv2_bias,
):
    frames, lines, columns, channels = activations.shape
    sections, row_count = lax.axis_size("section"), lax.axis_size("rows")
    everyone = sections * row_count
    section, row_at = lax.axis_index("section"), lax.axis_index("rows")
    place = jnp.stack([section, row_at]).astype(jnp.int32)
    stats_shape = jax.ShapeDtypeStruct((everyone, 1, 2 * channels), jnp.float32)

    def flat(vector):
        return vector.reshape(1, channels)

    def exchange(stats):
        return lax.all_to_all(stats, ("section", "rows"), 0, 0, tiled=True)

    ring = [(i, (i + 1) % sections) for i in range(sections)]
    near = [(i, i ^ 1) for i in range(row_count)]
    far = [(0, 0)] + [(i, i + 1 if i % 2 else i - 1) for i in range(1, row_count - 1)]
    far = far + [(row_count - 1, row_count - 1)]

    received = lax.ppermute(activations[-SPAN_HALO:], "section", ring)
    sums = call(stats_kernel, stats_shape, [], (activations,), scalars=False)
    caches = jnp.concatenate([second_cache, first_cache], axis=0)
    halo = jnp.where(section == 0, caches, received)
    own = jnp.concatenate([halo, activations], axis=0)
    own, sums = lax.optimization_barrier((own, sums))
    from_near = lax.ppermute(own, "rows", near)
    from_far = lax.ppermute(own, "rows", far)
    stats = exchange(sums)
    middle, sums_two = call(
        functools.partial(first_kernel, row_count),
        (
            jax.ShapeDtypeStruct((frames + 2, lines + 2, columns, channels), jnp.bfloat16),
            stats_shape,
        ),
        [pltpu.VMEM((frames + SPAN_HALO, 3 * lines, columns, channels), jnp.bfloat16)],
        (
            place, own, from_near, from_far, stats, flat(norm1_scale), flat(norm1_shift),
            conv1_weight, flat(conv1_bias),
        ),
        flops=10**9,
    )
    stats_two = exchange(sums_two)
    return call(
        functools.partial(second_kernel, row_count),
        jax.ShapeDtypeStruct(activations.shape, jnp.bfloat16),
        [pltpu.VMEM((frames + 2, lines + 2, columns, channels), jnp.bfloat16)],
        (
            place, middle, stats_two, flat(norm2_scale), flat(norm2_shift), conv2_weight,
            flat(conv2_bias), activations,
        ),
        flops=10**9,
    )


def solution(mesh):
    in_specs = (
        P("section", "rows", None, None),
        P(None, "rows", None, None),
        P(None, "rows", None, None),
        P(),
        P(),
        P(),
        P(),
        P(),
        P(),
        P(),
        P(),
    )
    out_specs = P("section", "rows", None, None)
    return jax.shard_map(
        on_device, mesh=mesh, in_specs=in_specs, out_specs=out_specs, check_vma=False
    )
```

time: 76.3 us -> 42.5 us (0.56)
  the two profiles are of different devices: /device:TPU:5 before, /device:TPU:0 now
where the time goes in v4:
time: 42.5 us; the launch traced here: 42.2 us
  starting transfers between devices  10.8 us (25%)
  waiting for transfers between devices  10.7 us (25%)
  blocking collectives  8.93 us (21%)
  Pallas kernels  8.33 us (20%)
  local copies, waits for them, and re-layouts  2.36 us (6%)
  other arithmetic  1.01 us (2%)
    all_to_all x1, blocking collectives, exchange(): return lax.all_to_all(stats, ('section', 'rows'), 0, 0, tiled=True)  8.93 us
    pallas_call x3, Pallas kernels, call(): pl.pallas_call(kernel, out_shape=out_shape, in_specs=specs, out_specs=jax...  8.33 us
    all_to_all x1, waiting for transfers between devices, exchange(): return lax.all_to_all(stats, ('section', 'rows'), 0, 0, tiled=True)  7.16 us
    all_to_all x1, starting transfers between devices, exchange(): return lax.all_to_all(stats, ('section', 'rows'), 0, 0, tiled=True)  3.94 us
    ppermute x1, waiting for transfers between devices, on_device(): received = lax.ppermute(activations[-SPAN_HALO:], 'section', ring)  3.54 us
    ppermute x1, starting transfers between devices, on_device(): from_near = lax.ppermute(own, 'rows', near)  3.17 us
    ppermute x1, starting transfers between devices, on_device(): received = lax.ppermute(activations[-SPAN_HALO:], 'section', ring)  2.99 us
    unnamed x18, local copies, waits for them, and re-layouts  1.35 us
  transfers between devices with their start and end apart: 4, of which 2 were waited for; matrix products, arithmetic and copies ran while one was open for 0% of the time, Pallas kernels for 2%

profile of v4, /device:TPU:0, one launch (start us, length us, event | category | flops | bytes accessed | tf_op | source)
XLA Modules:
  0.0 42.2 jit_solution(2114203386541876170)
XLA Ops:
  0.0 0.0 copy-start
  0.0 0.0 copy-start.1
  0.0 1.0 %slice.3 = bf16[4,2,64,128]{3,2,1,0:T(8,128)(2,1)S(1)} slice(bf16[8,2,64,128]{3,2,1,0:T(8,128)(2,1)} %own_ref.3), slice={[4:8], [0:2], [0:64], [0:128]} | slice | bytes 262144 | tf_op jit(solution)/shard_map/slice | solution.py:230
  1.0 3.0 %collective-permute-start = (bf16[4,2,64,128]{3,2,1,0:T(8,128)(2,1)S(1)}, bf16[4,2,64,128]{3,2,1,0:T(8,128)(2,1)S(1)}, u32[]{:S(2)}, u32[]{:S(2)}) collective-permute-start(bf16[4,2,64,128]{3,2,1,0:T(8,128)(2,1)S(1)} %slice.3), channel_id=1, source_target_pairs={{0,8},{8,16},{16,24},{24,0},{1,9},{9,17},{17,25},{25,1},{2,10},{10... | collective-permute-start | bytes 393224 | tf_op jit(solution)/shard_map/ppermute | solution.py:230
  4.0 0.0 copy-done
  4.0 0.9 %shard_map.109 = f32[32,1,256]{2,1,0:T(1,128)} custom-call(bf16[8,2,64,128]{3,2,1,0:T(8,128)(2,1)S(1)} %copy-done), custom_call_target="tpu_custom_call" | custom-call | bytes 1048576 | tf_op jit(solution)/shard_map/pallas_call | solution.py:188
  4.9 3.5 %collective-permute-done = bf16[4,2,64,128]{3,2,1,0:T(8,128)(2,1)S(1)} collective-permute-done((bf16[4,2,64,128]{3,2,1,0:T(8,128)(2,1)S(1)}, bf16[4,2,64,128]{3,2,1,0:T(8,128)(2,1)S(1)}, u32[]{:S(2)}, u32[]{:S(2)}) %collective-permute-start) | collective-permute-done | bytes 131104 | tf_op jit(solution)/shard_map/ppermute | solution.py:230
  8.5 0.9 %maximum_select_fusion = bf16[4,2,64,128]{3,2,1,0:T(8,128)(2,1)S(1)} fusion(bf16[4,2,64,128]{3,2,1,0:T(8,128)(2,1)S(1)} %collective-permute-done, bf16[2,2,64,128]{3,2,1,0:T(8,128)(2,1)} %param.12, bf16[2,2,64,128]{3,2,1,0:T(8,128)(2,1)} %param.13, pred[]{:T(512)S(6)} %eq.3), kind=kLoop, calls=%fused_computation.1 | loop fusion | flops 131072 | bytes 393217 | tf_op jit(solution)/shard_map/jit(_where)/select_n | solution.py:233
  9.4 0.7 %collective-permute-start.2 = (bf16[12,2,64,128]{3,2,1,0:T(8,128)(2,1)S(1)}, bf16[12,2,64,128]{3,2,1,0:T(8,128)(2,1)S(1)}, u32[]{:S(2)}, u32[]{:S(2)}) collective-permute-start(bf16[12,2,64,128]{3,2,1,0:T(8,128)(2,1)S(1)} %pad_maximum_fusion.own_ref), channel_id=1, source_target_pairs={{0,0},{1,2},{2,1},{3,4},{4,3},{5,6},{6,5},{7,7},{8,8},{9,10},{10,9... | collective-permute-start | bytes 1179656 | tf_op jit(solution)/shard_map/ppermute | solution.py:237
  10.1 3.2 %collective-permute-start.1 = (bf16[12,2,64,128]{3,2,1,0:T(8,128)(2,1)S(1)}, bf16[12,2,64,128]{3,2,1,0:T(8,128)(2,1)S(1)}, u32[]{:S(2)}, u32[]{:S(2)}) collective-permute-start(bf16[12,2,64,128]{3,2,1,0:T(8,128)(2,1)S(1)} %pad_maximum_fusion.own_ref), channel_id=1, source_target_pairs={{0,1},{1,0},{2,3},{3,2},{4,5},{5,4},{6,7},{7,6},{8,9},{9,8},{10,11... | collective-permute-start | bytes 1179656 | tf_op jit(solution)/shard_map/ppermute | solution.py:236
  13.3 3.9 %all-to-all-start = ((f32[32,1,256]{2,1,0:T(1,128)}), f32[32,1,256]{2,1,0:T(1,128)S(1)}, u32[]{:S(2)}, u32[]{:S(2)}) async-start(f32[32,1,256]{2,1,0:T(1,128)} %shard_map.109), calls=%async_computation | async-start | bytes 65536 | tf_op jit(solution)/shard_map/all_to_all | solution.py:223
  17.2 0.1 pad_add_fusion.place
  17.3 7.2 %all-to-all-done.stats_ref = f32[32,1,256]{2,1,0:T(1,128)S(1)} async-done(((f32[32,1,256]{2,1,0:T(1,128)}), f32[32,1,256]{2,1,0:T(1,128)S(1)}, u32[]{:S(2)}, u32[]{:S(2)}) %all-to-all-start) | async-done | bytes 32800 | tf_op jit(solution)/shard_map/all_to_all | solution.py:223
  24.4 0.0 collective-permute-done.2.far_ref
  24.5 0.0 collective-permute-done.1.near_ref
  24.5 0.0 copy-start.3
  24.5 0.0 copy-start.4
  24.5 0.0 copy-start.5
  24.5 0.0 copy-done.1
  24.5 0.6 %copy-done.3 = f32[128]{0:T(128)S(1)} copy-done((f32[128]{0:T(128)S(1)}, f32[128]{0:T(128)}, u32[]{:S(2)}) %copy-start.3) | copy-done | bytes 536
  25.1 0.0 copy-done.4
  25.1 0.0 copy-done.5
  25.1 0.0 copy-start.2
  25.1 4.3 %shard_map.110 = (bf16[10,4,64,128]{3,2,1,0:T(8,128)(2,1)S(1)}, f32[32,1,256]{2,1,0:T(1,128)S(1)}) custom-call(s32[2]{0:T(128)S(1)} %pad_add_fusion.place, bf16[12,2,64,128]{3,2,1,0:T(8,128)(2,1)S(1)} %pad_maximum_fusion.own_ref, bf16[12,2,64,128]{3,2,1,0:T(8,128)(2,1)S(1)} %collective-permute-done.1.near_ref, ...), custom_call_target="tpu_custom_call" | custom-call | flops 1000000000 | bytes 1048576 | tf_op jit(solution)/shard_map/pallas_call | solution.py:188
  29.4 8.9 %all_to_all.10.stats_ref = f32[32,1,256]{2,1,0:T(1,128)S(1)} all-to-all(f32[32,1,256]{2,1,0:T(1,128)S(1)} %get-tuple-element.12), channel_id=1, replica_groups=mesh['section'=4,'rows'=8] {'section','rows'}, dimensions={0} | all-to-all | bytes 65536 | tf_op jit(solution)/shard_map/all_to_all | solution.py:223
  38.4 0.0 copy-start.6
  38.4 0.0 copy-start.7
  38.4 0.0 copy-start.8
  38.4 0.0 copy-done.2
  38.4 0.6 %copy-done.6 = f32[128]{0:T(128)S(1)} copy-done((f32[128]{0:T(128)S(1)}, f32[128]{0:T(128)}, u32[]{:S(2)}) %copy-start.6) | copy-done | bytes 536
  39.0 0.0 copy-done.7
  39.0 0.0 copy-done.8
  39.1 3.1 %shard_map.111 = bf16[8,2,64,128]{3,2,1,0:T(8,128)(2,1)} custom-call(s32[2]{0:T(128)S(1)} %pad_add_fusion.place, bf16[10,4,64,128]{3,2,1,0:T(8,128)(2,1)S(1)} %get-tuple-element.11.middle_ref, f32[32,1,256]{2,1,0:T(1,128)S(1)} %all_to_all.10.stats_ref, f32[1,128]{1,0:T(1,128)S(1)} %bitcast.11, f32[1,128]{1,0:T(1,128)S(1)} %bitcast.12, ...), custom_call_target="tpu_custom_call" | custom-call | flops 1000000000 | bytes 1048576 | tf_op jit(solution)/shard_map/pallas_call | solution.py:188
  (1 shorter events, 0.0 us)
Async XLA Ops:
  0.0 4.0 %copy-start = (bf16[8,2,64,128]{3,2,1,0:T(8,128)(2,1)S(1)}, bf16[8,2,64,128]{3,2,1,0:T(8,128)(2,1)}, u32[]{:S(2)}) copy-start(bf16[8,2,64,128]{3,2,1,0:T(8,128)(2,1)} %own_ref.3) | copy-start | bytes 786436
  0.0 24.5 %copy-start.1 = (bf16[3,3,3,128,128]{4,3,2,1,0:T(8,128)(2,1)S(1)}, bf16[3,3,3,128,128]{4,3,2,1,0:T(8,128)(2,1)}, u32[]{:S(2)}) copy-start(bf16[3,3,3,128,128]{4,3,2,1,0:T(8,128)(2,1)} %weight_ref.2) | copy-start | bytes 2654212
  1.0 7.4 %collective-permute-start = (bf16[4,2,64,128]{3,2,1,0:T(8,128)(2,1)S(1)}, bf16[4,2,64,128]{3,2,1,0:T(8,128)(2,1)S(1)}, u32[]{:S(2)}, u32[]{:S(2)}) collective-permute-start(bf16[4,2,64,128]{3,2,1,0:T(8,128)(2,1)S(1)} %slice.3), channel_id=1, source_target_pairs={{0,8},{8,16},{16,24},{24,0},{1,9},{9,17},{17,25},{25,1},{2,10},{10... | collective-permute-start | bytes 393224 | tf_op jit(solution)/shard_map/ppermute | solution.py:230
  9.4 15.1 %collective-permute-start.2 = (bf16[12,2,64,128]{3,2,1,0:T(8,128)(2,1)S(1)}, bf16[12,2,64,128]{3,2,1,0:T(8,128)(2,1)S(1)}, u32[]{:S(2)}, u32[]{:S(2)}) collective-permute-start(bf16[12,2,64,128]{3,2,1,0:T(8,128)(2,1)S(1)} %pad_maximum_fusion.own_ref), channel_id=1, source_target_pairs={{0,0},{1,2},{2,1},{3,4},{4,3},{5,6},{6,5},{7,7},{8,8},{9,10},{10,9... | collective-permute-start | bytes 1179656 | tf_op jit(solution)/shard_map/ppermute | solution.py:237
  10.1 14.4 %collective-permute-start.1 = (bf16[12,2,64,128]{3,2,1,0:T(8,128)(2,1)S(1)}, bf16[12,2,64,128]{3,2,1,0:T(8,128)(2,1)S(1)}, u32[]{:S(2)}, u32[]{:S(2)}) collective-permute-start(bf16[12,2,64,128]{3,2,1,0:T(8,128)(2,1)S(1)} %pad_maximum_fusion.own_ref), channel_id=1, source_target_pairs={{0,1},{1,0},{2,3},{3,2},{4,5},{5,4},{6,7},{7,6},{8,9},{9,8},{10,11... | collective-permute-start | bytes 1179656 | tf_op jit(solution)/shard_map/ppermute | solution.py:236
  13.3 11.2 %all-to-all-start = ((f32[32,1,256]{2,1,0:T(1,128)}), f32[32,1,256]{2,1,0:T(1,128)S(1)}, u32[]{:S(2)}, u32[]{:S(2)}) async-start(f32[32,1,256]{2,1,0:T(1,128)} %shard_map.109), calls=%async_computation | async-start | bytes 65536 | tf_op jit(solution)/shard_map/all_to_all | solution.py:223
  24.5 0.7 %copy-start.3 = (f32[128]{0:T(128)S(1)}, f32[128]{0:T(128)}, u32[]{:S(2)}) copy-start(f32[128]{0:T(128)} %param.14) | copy-start | bytes 1540
  24.5 0.7 %copy-start.4 = (f32[128]{0:T(128)S(1)}, f32[128]{0:T(128)}, u32[]{:S(2)}) copy-start(f32[128]{0:T(128)} %param.15) | copy-start | bytes 1540
  24.5 0.7 %copy-start.5 = (f32[128]{0:T(128)S(1)}, f32[128]{0:T(128)}, u32[]{:S(2)}) copy-start(f32[128]{0:T(128)} %param.17) | copy-start | bytes 1540
  25.1 13.2 %copy-start.2 = (bf16[3,3,3,128,128]{4,3,2,1,0:T(8,128)(2,1)S(1)}, bf16[3,3,3,128,128]{4,3,2,1,0:T(8,128)(2,1)}, u32[]{:S(2)}) copy-start(bf16[3,3,3,128,128]{4,3,2,1,0:T(8,128)(2,1)} %weight_ref.3) | copy-start | bytes 2654212
  38.4 0.7 %copy-start.6 = (f32[128]{0:T(128)S(1)}, f32[128]{0:T(128)}, u32[]{:S(2)}) copy-start(f32[128]{0:T(128)} %param.18) | copy-start | bytes 1540
  38.4 0.7 %copy-start.7 = (f32[128]{0:T(128)S(1)}, f32[128]{0:T(128)}, u32[]{:S(2)}) copy-start(f32[128]{0:T(128)} %param.19) | copy-start | bytes 1540
  38.4 0.7 %copy-start.8 = (f32[128]{0:T(128)S(1)}, f32[128]{0:T(128)}, u32[]{:S(2)}) copy-start(f32[128]{0:T(128)} %param.21) | copy-start | bytes 1540

commit v5 on v4

--- a/solution.py
+++ b/solution.py
@@ -13,16 +13,6 @@
 SPAN_HALO = 4
 
 epsilon = 1e-06
-
-
-def moments(blocks):
-    cells = sum(block.shape[0] for block in blocks)
-    total = sum(jnp.sum(block, axis=0, keepdims=True) for block in blocks)
-    mean = total * (1.0 / cells)
-    centred = sum(
-        jnp.sum((block - mean) * (block - mean), axis=0, keepdims=True) for block in blocks
-    )
-    return jnp.concatenate([total, centred], axis=1)
 
 
 def group_sum(values, width):
@@ -37,16 +27,32 @@
     return values
 
 
+def moments(blocks):
+    channels = blocks[0].shape[1]
+    width = channels // GROUPS
+    cells = sum(block.shape[0] for block in blocks) * width
+    total = group_sum(sum(jnp.sum(block, axis=0, keepdims=True) for block in blocks), width)
+    mean = total * (1.0 / cells)
+    centred = group_sum(
+        sum(jnp.sum((block - mean) * (block - mean), axis=0, keepdims=True) for block in blocks),
+        width,
+    )
+    lane = lax.broadcasted_iota(jnp.int32, total.shape, 1)
+    return jnp.where(lane % width == 0, total, centred)
+
+
 def affine(stats, cells, scale, shift):
-    channels = scale.shape[-1]
+    devices, _, channels = stats.shape
     width = channels // GROUPS
-    totals, centred = stats[:, 0, :channels], stats[:, 0, channels:]
-    count = cells * width * stats.shape[0]
-    average = group_sum(jnp.sum(totals, axis=0, keepdims=True), width) * (1.0 / count)
+    stats = stats.reshape(devices, channels)
+    lane = lax.broadcasted_iota(jnp.int32, stats.shape, 1) % width
+    totals = group_sum(jnp.where(lane == 0, stats, 0.0), width)
+    centred = group_sum(jnp.where(lane == 1, stats, 0.0), width)
+    cells = cells * width
+    average = jnp.sum(totals, axis=0, keepdims=True) * (1.0 / (cells * devices))
     away = totals * (1.0 / cells) - average
     inner = jnp.sum(centred + cells * (away * away), axis=0, keepdims=True)
-    spread = group_sum(inner, width) * (1.0 / count)
-    slope = 0.5 * scale / jnp.sqrt(spread + epsilon)
+    slope = 0.5 * scale / jnp.sqrt(inner * (1.0 / (cells * devices)) + epsilon)
     return slope, 0.5 * shift - average * slope
 
 
@@ -94,21 +100,62 @@
     return results
 
 
-def stats_kernel(own_ref, stats_ref):
-    own = own_ref[...].astype(jnp.float32)
+def prepare_kernel(
+    place, own_ref, second_cache_ref, first_cache_ref, *rest
+):
+    *vector_refs, stats_ref, halo_ref, vectors_ref, copied, sems = rest
+    last = place[0] == place[2] - 1
+    frames = own_ref.shape[0]
+    load = pltpu.make_async_copy(own_ref, copied, sems.at[0])
+    load.start()
+    tail = pltpu.make_async_copy(own_ref.at[frames - SPAN_HALO :], halo_ref, sems.at[1])
+    spare = SPAN_HALO - 2
+    older = pltpu.make_async_copy(second_cache_ref, halo_ref.at[:spare], sems.at[2])
+    newer = pltpu.make_async_copy(first_cache_ref, halo_ref.at[spare:], sems.at[3])
+
+    @pl.when(last)
+    def _():
+        older.start()
+        newer.start()
+
+    @pl.when(jnp.logical_not(last))
+    def _():
+        tail.start()
+
+    vector_loads = [
+        pltpu.make_async_copy(vector_ref, vectors_ref.at[index], sems.at[4 + index])
+        for index, vector_ref in enumerate(vector_refs)
+    ]
+    for vector_load in vector_loads:
+        vector_load.start()
+    load.wait()
+    own = copied[...].astype(jnp.float32)
     packed = moments([own.reshape(-1, own.shape[-1])])
     stats_ref[...] = jnp.broadcast_to(packed[None], stats_ref.shape)
 
+    for vector_load in vector_loads:
+        vector_load.wait()
+
+    @pl.when(last)
+    def _():
+        older.wait()
+        newer.wait()
+
+    @pl.when(jnp.logical_not(last))
+    def _():
+        tail.wait()
+
 
 def first_kernel(
-    row_count, place, own_ref, near_ref, far_ref, stats_ref, scale_ref, shift_ref, weight_ref, bias_ref,
-    middle_ref, sums_ref, field
+    row_count, place, own_ref, near_ref, far_ref, halo_ref, halo_near_ref, halo_far_ref,
+    stats_ref, vectors_ref, far_weight_ref, middle_ref, sums_ref, field, weight_ref, sem
 ):
+    load = pltpu.make_async_copy(far_weight_ref, weight_ref, sem)
+    load.start()
     section, row_at = place[0], place[1]
-    frames, lines, columns, channels = own_ref.shape
-    inner = frames - SPAN_HALO
+    inner, lines, columns, channels = own_ref.shape
     cells = inner * lines * columns
-    scale, shift = scale_ref[...], shift_ref[...]
+    scale, shift = vectors_ref[0], vectors_ref[1]
     mine = stats_ref[pl.ds(section * row_count, row_count)]
     before = stats_ref[pl.ds(jnp.maximum(section - 1, 0) * row_count, row_count)]
     slope, offset = affine(mine, cells, scale, shift)
@@ -118,11 +165,11 @@
     for line in range(3 * lines):
         side, local = divmod(line, lines)
         if side == 1:
-            block = own_ref[:, local]
+            halo, body = halo_ref[:, local], own_ref[:, local]
         else:
             near_side = even if side == 2 else jnp.logical_not(even)
-            block = jnp.where(near_side, near_ref[:, local], far_ref[:, local])
-        halo, body = block[:SPAN_HALO], block[SPAN_HALO:]
+            halo = jnp.where(near_side, halo_near_ref[:, local], halo_far_ref[:, local])
+            body = jnp.where(near_side, near_ref[:, local], far_ref[:, local])
         behind = activate(halo, slope_before, offset_before).astype(jnp.bfloat16)
         behind = jnp.where(at_start, halo, behind)
         ahead = activate(body, slope, offset).astype(jnp.bfloat16)
@@ -132,7 +179,8 @@
             ahead = jnp.where(outside, jnp.zeros_like(ahead), ahead)
         field[:SPAN_HALO, line] = behind
         field[SPAN_HALO:, line] = ahead
-    bias = bias_ref[...]
+    load.wait()
+    bias = vectors_ref[2]
     kept = []
     spare = SPAN_HALO - 2
     for pair in range((lines + 2) // 2):
@@ -149,13 +197,15 @@
 
 
 def second_kernel(
-    row_count, place, middle_ref, stats_ref, scale_ref, shift_ref, weight_ref, bias_ref, own_ref,
-    out_ref, field
+    row_count, place, middle_ref, stats_ref, vectors_ref, far_weight_ref, own_ref, out_ref,
+    field, weight_ref, sem
 ):
+    load = pltpu.make_async_copy(far_weight_ref, weight_ref, sem)
+    load.start()
     section, row_at = place[0], place[1]
     frames, lines, columns, channels = own_ref.shape
     cells = frames * lines * columns
-    scale, shift = scale_ref[...], shift_ref[...]
+    scale, shift = vectors_ref[3], vectors_ref[4]
     mine = stats_ref[pl.ds(section * row_count, row_count)]
     before = stats_ref[pl.ds(jnp.maximum(section - 1, 0) * row_count, row_count)]
     slope, offset = affine(mine, cells, scale, shift)
@@ -172,7 +222,8 @@
             ahead = jnp.where(outside, jnp.zeros_like(ahead), ahead)
         field[:2, line] = behind
         field[2:, line] = ahead
-    bias = bias_ref[...]
+    load.wait()
+    bias = vectors_ref[5]
     for pair in range(lines // 2):
         results = pair_conv(field, 2 * pair, frames, weight_ref)
         for out in range(2):
@@ -181,15 +232,20 @@
             out_ref[:, line] = (result + own_ref[:, line].astype(jnp.float32)).astype(jnp.bfloat16)
 
 
-def call(kernel, out_shape, scratch, operands, scalars=True, flops=0):
-    specs = [pl.BlockSpec(memory_space=pltpu.VMEM)] * len(operands)
-    if scalars:
-        specs[0] = pl.BlockSpec(memory_space=pltpu.SMEM)
+def call(kernel, out_shape, scratch, operands, in_place=(), flops=0):
+    vmem = pl.BlockSpec(memory_space=pltpu.VMEM)
+    specs = [pl.BlockSpec(memory_space=pltpu.SMEM)] + [vmem] * (len(operands) - 1)
+    for index in in_place:
+        specs[index] = pl.BlockSpec(memory_space=pltpu.HBM)
+    operands = [
+        pltpu.with_memory_space_constraint(operand, pltpu.HBM) if index in in_place else operand
+        for index, operand in enumerate(operands)
+    ]
     return pl.pallas_call(
         kernel,
         out_shape=out_shape,
         in_specs=specs,
-        out_specs=jax.tree.map(lambda _: pl.BlockSpec(memory_space=pltpu.VMEM), out_shape),
+        out_specs=jax.tree.map(lambda _: vmem, out_shape),
         scratch_shapes=scratch,
         compiler_params=pltpu.CompilerParams(vmem_limit_bytes=40 * 2**20),
         cost_estimate=pl.CostEstimate(flops=flops, bytes_accessed=2**20, transcendentals=0),
@@ -213,28 +269,45 @@
     sections, row_count = lax.axis_size("section"), lax.axis_size("rows")
     everyone = sections * row_count
     section, row_at = lax.axis_index("section"), lax.axis_index("rows")
-    place = jnp.stack([section, row_at]).astype(jnp.int32)
-    stats_shape = jax.ShapeDtypeStruct((everyone, 1, 2 * channels), jnp.float32)
-
-    def flat(vector):
-        return vector.reshape(1, channels)
+    place = jnp.stack([section, row_at, jnp.int32(sections)]).astype(jnp.int32)
+    stats_shape = jax.ShapeDtypeStruct((everyone, 1, channels), jnp.float32)
+    vectors = (norm1_scale, norm1_shift, conv1_bias, norm2_scale, norm2_shift, conv2_bias)
 
     def exchange(stats):
         return lax.all_to_all(stats, ("section", "rows"), 0, 0, tiled=True)
 
-    ring = [(i, (i + 1) % sections) for i in range(sections)]
-    near = [(i, i ^ 1) for i in range(row_count)]
-    far = [(0, 0)] + [(i, i + 1 if i % 2 else i - 1) for i in range(1, row_count - 1)]
-    far = far + [(row_count - 1, row_count - 1)]
-
-    received = lax.ppermute(activations[-SPAN_HALO:], "section", ring)
-    sums = call(stats_kernel, stats_shape, [], (activations,), scalars=False)
-    caches = jnp.concatenate([second_cache, first_cache], axis=0)
-    halo = jnp.where(section == 0, caches, received)
-    own = jnp.concatenate([halo, activations], axis=0)
-    own, sums = lax.optimization_barrier((own, sums))
-    from_near = lax.ppermute(own, "rows", near)
-    from_far = lax.ppermute(own, "rows", far)
+    weight_scratch = [
+        pltpu.VMEM(conv1_weight.shape, jnp.bfloat16), pltpu.SemaphoreType.DMA
+    ]
+    near = [i ^ 1 for i in range(row_count)]
+    far = [0] + [i + 1 if i % 2 else i - 1 for i in range(1, row_count - 1)] + [row_count - 1]
+
+    def across(block, partner):
+        return lax.ppermute(block, "rows", list(enumerate(partner)))
+
+    def onward(block, partner):
+        route = [
+            (at * row_count + row, (at + 1) % sections * row_count + partner[row])
+            for at in range(sections)
+            for row in range(row_count)
+        ]
+        return lax.ppermute(block, ("section", "rows"), route)
+
+    sums, halo, packed, own = call(
+        prepare_kernel,
+        (
+            stats_shape,
+            jax.ShapeDtypeStruct((SPAN_HALO, lines, columns, channels), jnp.bfloat16),
+            jax.ShapeDtypeStruct((len(vectors), 1, channels), jnp.float32),
+            jax.ShapeDtypeStruct(activations.shape, jnp.bfloat16),
+        ),
+        [pltpu.SemaphoreType.DMA((4 + len(vectors),))],
+        (place, activations, second_cache, first_cache)
+        + tuple(vector.reshape(1, channels) for vector in vectors),
+        in_place=range(1, 4 + len(vectors)),
+    )
+    beside = [across(activations, near), across(activations, far)]
+    behind = [onward(halo, partner) for partner in (range(row_count), near, far)]
     stats = exchange(sums)
     middle, sums_two = call(
         functools.partial(first_kernel, row_count),
@@ -242,22 +315,20 @@
             jax.ShapeDtypeStruct((frames + 2, lines + 2, columns, channels), jnp.bfloat16),
             stats_shape,
         ),
-        [pltpu.VMEM((frames + SPAN_HALO, 3 * lines, columns, channels), jnp.bfloat16)],
-        (
-            place, own, from_near, from_far, stats, flat(norm1_scale), flat(norm1_shift),
-            conv1_weight, flat(conv1_bias),
-        ),
+        [pltpu.VMEM((frames + SPAN_HALO, 3 * lines, columns, channels), jnp.bfloat16)]
+        + weight_scratch,
+        (place, own, *beside, *behind, stats, packed, conv1_weight),
+        in_place=(9,),
         flops=10**9,
     )
     stats_two = exchange(sums_two)
     return call(
         functools.partial(second_kernel, row_count),
         jax.ShapeDtypeStruct(activations.shape, jnp.bfloat16),
-        [pltpu.VMEM((frames + 2, lines + 2, columns, channels), jnp.bfloat16)],
-        (
-            place, middle, stats_two, flat(norm2_scale), flat(norm2_shift), conv2_weight,
-            flat(conv2_bias), activations,
-        ),
+        [pltpu.VMEM((frames + 2, lines + 2, columns, channels), jnp.bfloat16)]
+        + weight_scratch,
+        (place, middle, stats_two, packed, conv2_weight, own),
+        in_place=(4,),
         flops=10**9,
     )
 

time: 42.5 us -> 41.2 us (0.969)
  waiting for transfers between devices: 10.7 us -> 0.01 us
  blocking collectives: 8.93 us -> 19.1 us
  Pallas kernels: 8.33 us -> 11.3 us
  local copies, waits for them, and re-layouts: 2.36 us -> 0 us
  other arithmetic: 1.01 us -> 0.08 us
    all_to_all x1 -> x2, blocking collectives: 8.93 us -> 19.1 us  [exchange(): return lax.all_to_all(stats, ('section', 'rows'), 0, 0, tiled=True)]
    all_to_all x1 -> x0, waiting for transfers between devices: 7.16 us -> none  [exchange(): return lax.all_to_all(stats, ('section', 'rows'), 0, 0, tiled=True)]
    all_to_all x1 -> x0, starting transfers between devices: 3.94 us -> none  [exchange(): return lax.all_to_all(stats, ('section', 'rows'), 0, 0, tiled=True)]
    ppermute x3 -> x5, waiting for transfers between devices: 3.54 us -> 0.01 us  [the longest x3 0.01 us: onward(): return lax.ppermute(block, ('section', 'rows'), route)]
    ppermute x3 -> x5, starting transfers between devices: 6.85 us -> 10.4 us  [the longest x3 5.26 us: onward(): return lax.ppermute(block, ('section', 'rows'), route)]
    pallas_call x3, Pallas kernels: 8.33 us -> 11.3 us  [call(): pl.pallas_call(kernel, out_shape=out_shape, in_specs=specs, out_specs=jax...]
    unnamed x18 -> x0, local copies, waits for them, and re-layouts: 1.35 us -> none
    slice x1 -> x0, local copies, waits for them, and re-layouts: 1.01 us -> none  [on_device(): received = lax.ppermute(activations[-SPAN_HALO:], 'section', ring)]
  transfers between devices with their start and end apart: 4 -> 5, of which waited for: 2 -> 0; matrix products, arithmetic and copies ran while one was open for 0% -> 0% of each run, Pallas kernels for 2% -> 5%
where the time goes in v5:
time: 41.2 us; the launch traced here: 40.9 us
  blocking collectives  19.1 us (46%)
  Pallas kernels  11.3 us (27%)
  starting transfers between devices  10.4 us (25%)
    all_to_all x2, blocking collectives, exchange(): return lax.all_to_all(stats, ('section', 'rows'), 0, 0, tiled=True)  19.1 us
    pallas_call x3, Pallas kernels, call(): pl.pallas_call(kernel, out_shape=out_shape, in_specs=specs, out_specs=jax...  11.3 us
    ppermute x3, starting transfers between devices, onward(): return lax.ppermute(block, ('section', 'rows'), route)  5.26 us
    ppermute x2, starting transfers between devices, across(): return lax.ppermute(block, 'rows', list(enumerate(partner)))  5.11 us
  transfers between devices with their start and end apart: 5, of which 0 were waited for; matrix products, arithmetic and copies ran while one was open for 0% of the time, Pallas kernels for 5%

profile of v5, /device:TPU:0, one launch (start us, length us, event | category | flops | bytes accessed | tf_op | source)
XLA Modules:
  0.0 40.9 jit_solution(2747680841461123896)
XLA Ops:
  0.0 1.6 %collective-permute-start.1 = (bf16[8,2,64,128]{3,2,1,0:T(8,128)(2,1)}, bf16[8,2,64,128]{3,2,1,0:T(8,128)(2,1)S(1)}, u32[]{:S(2)}, u32[]{:S(2)}) collective-permute-start(bf16[8,2,64,128]{3,2,1,0:T(8,128)(2,1)} %own_ref.1), channel_id=1, source_target_pairs={{0,0},{1,2},{2,1},{3,4},{4,3},{5,6},{6,5},{7,7},{8,8},{9,10},{10,9... | collective-permute-start | bytes 786440 | tf_op jit(solution)/shard_map/ppermute | solution.py:286
  1.6 3.5 %collective-permute-start = (bf16[8,2,64,128]{3,2,1,0:T(8,128)(2,1)}, bf16[8,2,64,128]{3,2,1,0:T(8,128)(2,1)S(1)}, u32[]{:S(2)}, u32[]{:S(2)}) collective-permute-start(bf16[8,2,64,128]{3,2,1,0:T(8,128)(2,1)} %own_ref.1), channel_id=1, source_target_pairs={{0,1},{1,0},{2,3},{3,2},{4,5},{5,4},{6,7},{7,6},{8,9},{9,8},{10,11... | collective-permute-start | bytes 786440 | tf_op jit(solution)/shard_map/ppermute | solution.py:286
  5.1 0.1 pad_add_fusion.place
  5.2 2.2 %shard_map.109 = (f32[32,1,128]{2,1,0:T(1,128)S(1)}, bf16[4,2,64,128]{3,2,1,0:T(8,128)(2,1)S(1)}, f32[6,1,128]{2,1,0:T(1,128)S(1)}, bf16[8,2,64,128]{3,2,1,0:T(8,128)(2,1)S(1)}) custom-call(s32[3]{0:T(128)S(1)} %pad_add_fusion.place, bf16[8,2,64,128]{3,2,1,0:T(8,128)(2,1)} %own_ref.1, bf16[2,2,64,128]{3,2,1,0:T(8,128)(2,1)} %second_cache_ref.1, ...), custom_call_target="tpu_custom_call" | custom-call | bytes 1048576 | tf_op jit(solution)/shard_map/pallas_call | solution.py:244
  7.4 1.5 %collective-permute-start.4 = (bf16[4,2,64,128]{3,2,1,0:T(8,128)(2,1)S(1)}, bf16[4,2,64,128]{3,2,1,0:T(8,128)(2,1)S(1)}, u32[]{:S(2)}, u32[]{:S(2)}) collective-permute-start(bf16[4,2,64,128]{3,2,1,0:T(8,128)(2,1)S(1)} %get-tuple-element.12), channel_id=1, source_target_pairs={{0,8},{1,10},{2,9},{3,12},{4,11},{5,14},{6,13},{7,15},{8,16},{9,18... | collective-permute-start | bytes 393224 | tf_op jit(solution)/shard_map/ppermute | solution.py:294
  8.9 2.2 %collective-permute-start.3 = (bf16[4,2,64,128]{3,2,1,0:T(8,128)(2,1)S(1)}, bf16[4,2,64,128]{3,2,1,0:T(8,128)(2,1)S(1)}, u32[]{:S(2)}, u32[]{:S(2)}) collective-permute-start(bf16[4,2,64,128]{3,2,1,0:T(8,128)(2,1)S(1)} %get-tuple-element.12), channel_id=1, source_target_pairs={{0,9},{1,8},{2,11},{3,10},{4,13},{5,12},{6,15},{7,14},{8,17},{9,16... | collective-permute-start | bytes 393224 | tf_op jit(solution)/shard_map/ppermute | solution.py:294
  11.1 1.5 %collective-permute-start.2 = (bf16[4,2,64,128]{3,2,1,0:T(8,128)(2,1)S(1)}, bf16[4,2,64,128]{3,2,1,0:T(8,128)(2,1)S(1)}, u32[]{:S(2)}, u32[]{:S(2)}) collective-permute-start(bf16[4,2,64,128]{3,2,1,0:T(8,128)(2,1)S(1)} %get-tuple-element.12), channel_id=1, source_target_pairs={{0,8},{1,9},{2,10},{3,11},{4,12},{5,13},{6,14},{7,15},{8,16},{9,17... | collective-permute-start | bytes 393224 | tf_op jit(solution)/shard_map/ppermute | solution.py:294
  12.6 10.0 %all_to_all.10.stats_ref = f32[32,1,128]{2,1,0:T(1,128)S(1)} all-to-all(f32[32,1,128]{2,1,0:T(1,128)S(1)} %get-tuple-element.13), channel_id=1, replica_groups=mesh['section'=4,'rows'=8] {'section','rows'}, dimensions={0} | all-to-all | bytes 32768 | tf_op jit(solution)/shard_map/all_to_all | solution.py:277
  22.6 0.0 collective-permute-done.4.halo_far_ref
  22.6 0.0 collective-permute-done.3.halo_near_ref
  22.6 0.0 collective-permute-done.2.halo_ref
  22.6 0.0 collective-permute-done.1.far_ref
  22.6 0.0 collective-permute-done.near_ref
  22.7 5.3 %shard_map.110 = (bf16[10,4,64,128]{3,2,1,0:T(8,128)(2,1)S(1)}, f32[32,1,128]{2,1,0:T(1,128)S(1)}) custom-call(s32[3]{0:T(128)S(1)} %pad_add_fusion.place, bf16[8,2,64,128]{3,2,1,0:T(8,128)(2,1)S(1)} %get-tuple-element.11.own_ref, bf16[8,2,64,128]{3,2,1,0:T(8,128)(2,1)S(1)} %collective-permute-done.near_ref, ...), custom_call_target="tpu_custom_call" | custom-call | flops 1000000000 | bytes 1048576 | tf_op jit(solution)/shard_map/pallas_call | solution.py:244
  28.0 9.1 %all_to_all.11.stats_ref = f32[32,1,128]{2,1,0:T(1,128)S(1)} all-to-all(f32[32,1,128]{2,1,0:T(1,128)S(1)} %get-tuple-element.16), channel_id=1, replica_groups=mesh['section'=4,'rows'=8] {'section','rows'}, dimensions={0} | all-to-all | bytes 32768 | tf_op jit(solution)/shard_map/all_to_all | solution.py:277
  37.1 3.8 %shard_map.111 = bf16[8,2,64,128]{3,2,1,0:T(8,128)(2,1)} custom-call(s32[3]{0:T(128)S(1)} %pad_add_fusion.place, bf16[10,4,64,128]{3,2,1,0:T(8,128)(2,1)S(1)} %get-tuple-element.15.middle_ref, f32[32,1,128]{2,1,0:T(1,128)S(1)} %all_to_all.11.stats_ref, f32[6,1,128]{2,1,0:T(1,128)S(1)} %get-tuple-element.14.vectors_ref, ...), custom_call_target="tpu_custom_call" | custom-call | flops 1000000000 | bytes 1048576 | tf_op jit(solution)/shard_map/pallas_call | solution.py:244
Async XLA Ops:
  0.0 22.6 %collective-permute-start.1 = (bf16[8,2,64,128]{3,2,1,0:T(8,128)(2,1)}, bf16[8,2,64,128]{3,2,1,0:T(8,128)(2,1)S(1)}, u32[]{:S(2)}, u32[]{:S(2)}) collective-permute-start(bf16[8,2,64,128]{3,2,1,0:T(8,128)(2,1)} %own_ref.1), channel_id=1, source_target_pairs={{0,0},{1,2},{2,1},{3,4},{4,3},{5,6},{6,5},{7,7},{8,8},{9,10},{10,9... | collective-permute-start | bytes 786440 | tf_op jit(solution)/shard_map/ppermute | solution.py:286
  1.6 21.0 %collective-permute-start = (bf16[8,2,64,128]{3,2,1,0:T(8,128)(2,1)}, bf16[8,2,64,128]{3,2,1,0:T(8,128)(2,1)S(1)}, u32[]{:S(2)}, u32[]{:S(2)}) collective-permute-start(bf16[8,2,64,128]{3,2,1,0:T(8,128)(2,1)} %own_ref.1), channel_id=1, source_target_pairs={{0,1},{1,0},{2,3},{3,2},{4,5},{5,4},{6,7},{7,6},{8,9},{9,8},{10,11... | collective-permute-start | bytes 786440 | tf_op jit(solution)/shard_map/ppermute | solution.py:286
  7.4 15.3 %collective-permute-start.4 = (bf16[4,2,64,128]{3,2,1,0:T(8,128)(2,1)S(1)}, bf16[4,2,64,128]{3,2,1,0:T(8,128)(2,1)S(1)}, u32[]{:S(2)}, u32[]{:S(2)}) collective-permute-start(bf16[4,2,64,128]{3,2,1,0:T(8,128)(2,1)S(1)} %get-tuple-element.12), channel_id=1, source_target_pairs={{0,8},{1,10},{2,9},{3,12},{4,11},{5,14},{6,13},{7,15},{8,16},{9,18... | collective-permute-start | bytes 393224 | tf_op jit(solution)/shard_map/ppermute | solution.py:294
  8.9 13.7 %collective-permute-start.3 = (bf16[4,2,64,128]{3,2,1,0:T(8,128)(2,1)S(1)}, bf16[4,2,64,128]{3,2,1,0:T(8,128)(2,1)S(1)}, u32[]{:S(2)}, u32[]{:S(2)}) collective-permute-start(bf16[4,2,64,128]{3,2,1,0:T(8,128)(2,1)S(1)} %get-tuple-element.12), channel_id=1, source_target_pairs={{0,9},{1,8},{2,11},{3,10},{4,13},{5,12},{6,15},{7,14},{8,17},{9,16... | collective-permute-start | bytes 393224 | tf_op jit(solution)/shard_map/ppermute | solution.py:294
  11.1 11.5 %collective-permute-start.2 = (bf16[4,2,64,128]{3,2,1,0:T(8,128)(2,1)S(1)}, bf16[4,2,64,128]{3,2,1,0:T(8,128)(2,1)S(1)}, u32[]{:S(2)}, u32[]{:S(2)}) collective-permute-start(bf16[4,2,64,128]{3,2,1,0:T(8,128)(2,1)S(1)} %get-tuple-element.12), channel_id=1, source_target_pairs={{0,8},{1,9},{2,10},{3,11},{4,12},{5,13},{6,14},{7,15},{8,16},{9,17... | collective-permute-start | bytes 393224 | tf_op jit(solution)/shard_map/ppermute | solution.py:294

commit v6 on v5

--- a/solution.py
+++ b/solution.py
@@ -1,6 +1,8 @@
 import functools
+import itertools
 
 import functools
+import itertools
 
 import jax
 import jax.numpy as jnp
@@ -11,6 +13,7 @@
 
 GROUPS = 32
 SPAN_HALO = 4
+PARTS = 4
 
 epsilon = 1e-06
 
@@ -28,31 +31,28 @@
 
 
 def moments(blocks):
-    channels = blocks[0].shape[1]
+    first = next(blocks)
+    pivot = jnp.sum(first, axis=0, keepdims=True) * (1.0 / first.shape[0])
+    cells, total, squares = 0, 0.0, 0.0
+    for block in itertools.chain([first], blocks):
+        away = block - pivot
+        cells += block.shape[0]
+        total = total + jnp.sum(away, axis=0, keepdims=True)
+        squares = squares + jnp.sum(away * away, axis=0, keepdims=True)
+    shift = total * (1.0 / cells)
+    return jnp.concatenate([(pivot + shift) * cells, squares - total * shift], axis=1)
+
+
+def affine(stats, cells, scale, shift):
+    devices, channels = stats.shape[0], scale.shape[-1]
     width = channels // GROUPS
-    cells = sum(block.shape[0] for block in blocks) * width
-    total = group_sum(sum(jnp.sum(block, axis=0, keepdims=True) for block in blocks), width)
-    mean = total * (1.0 / cells)
-    centred = group_sum(
-        sum(jnp.sum((block - mean) * (block - mean), axis=0, keepdims=True) for block in blocks),
-        width,
-    )
-    lane = lax.broadcasted_iota(jnp.int32, total.shape, 1)
-    return jnp.where(lane % width == 0, total, centred)
-
-
-def affine(stats, cells, scale, shift):
-    devices, _, channels = stats.shape
-    width = channels // GROUPS
-    stats = stats.reshape(devices, channels)
-    lane = lax.broadcasted_iota(jnp.int32, stats.shape, 1) % width
-    totals = group_sum(jnp.where(lane == 0, stats, 0.0), width)
-    centred = group_sum(jnp.where(lane == 1, stats, 0.0), width)
-    cells = cells * width
-    average = jnp.sum(totals, axis=0, keepdims=True) * (1.0 / (cells * devices))
+    totals, centred = stats[:, :channels], stats[:, channels:]
+    count = cells * width * devices
+    average = group_sum(jnp.sum(totals, axis=0, keepdims=True), width) * (1.0 / count)
     away = totals * (1.0 / cells) - average
     inner = jnp.sum(centred + cells * (away * away), axis=0, keepdims=True)
-    slope = 0.5 * scale / jnp.sqrt(inner * (1.0 / (cells * devices)) + epsilon)
+    spread = group_sum(inner, width) * (1.0 / count)
+    slope = 0.5 * scale / jnp.sqrt(spread + epsilon)
     return slope, 0.5 * shift - average * slope
 
 
@@ -101,17 +101,26 @@
 
 
 def prepare_kernel(
-    place, own_ref, second_cache_ref, first_cache_ref, *rest
+    place, own_ref, second_cache_ref, first_cache_ref, weight_ref, *rest
 ):
-    *vector_refs, stats_ref, halo_ref, vectors_ref, copied, sems = rest
+    *vector_refs, stats_ref, halo_ref, vectors_ref, copied, weight_copy, sems = rest
     last = place[0] == place[2] - 1
     frames = own_ref.shape[0]
-    load = pltpu.make_async_copy(own_ref, copied, sems.at[0])
-    load.start()
-    tail = pltpu.make_async_copy(own_ref.at[frames - SPAN_HALO :], halo_ref, sems.at[1])
+    part = frames // PARTS
+    loads = [
+        pltpu.make_async_copy(
+            own_ref.at[pl.ds(index * part, part)],
+            copied.at[pl.ds(index * part, part)],
+            sems.at[3 + index],
+        )
+        for index in range(PARTS)
+    ]
+    for load in loads:
+        load.start()
+    tail = pltpu.make_async_copy(own_ref.at[frames - SPAN_HALO :], halo_ref, sems.at[0])
     spare = SPAN_HALO - 2
-    older = pltpu.make_async_copy(second_cache_ref, halo_ref.at[:spare], sems.at[2])
-    newer = pltpu.make_async_copy(first_cache_ref, halo_ref.at[spare:], sems.at[3])
+    older = pltpu.make_async_copy(second_cache_ref, halo_ref.at[:spare], sems.at[1])
+    newer = pltpu.make_async_copy(first_cache_ref, halo_ref.at[spare:], sems.at[2])
 
     @pl.when(last)
     def _():
@@ -122,19 +131,25 @@
     def _():
         tail.start()
 
-    vector_loads = [
-        pltpu.make_async_copy(vector_ref, vectors_ref.at[index], sems.at[4 + index])
+    late_loads = [
+        pltpu.make_async_copy(vector_ref, vectors_ref.at[index], sems.at[3 + PARTS + index])
         for index, vector_ref in enumerate(vector_refs)
     ]
-    for vector_load in vector_loads:
-        vector_load.start()
-    load.wait()
-    own = copied[...].astype(jnp.float32)
-    packed = moments([own.reshape(-1, own.shape[-1])])
-    stats_ref[...] = jnp.broadcast_to(packed[None], stats_ref.shape)
-
-    for vector_load in vector_loads:
-        vector_load.wait()
+    late_loads.append(
+        pltpu.make_async_copy(weight_ref, weight_copy, sems.at[3 + PARTS + len(vector_refs)])
+    )
+    for late_load in late_loads:
+        late_load.start()
+
+    def arriving():
+        for index, load in enumerate(loads):
+            load.wait()
+            block = copied[index * part : (index + 1) * part].astype(jnp.float32)
+            yield block.reshape(-1, block.shape[-1])
+
+    stats_ref[...] = moments(arriving())
+    for late_load in late_loads:
+        late_load.wait()
 
     @pl.when(last)
     def _():
@@ -148,16 +163,13 @@
 
 def first_kernel(
     row_count, place, own_ref, near_ref, far_ref, halo_ref, halo_near_ref, halo_far_ref,
-    stats_ref, vectors_ref, far_weight_ref, middle_ref, sums_ref, field, weight_ref, sem
+    stats_ref, vectors_ref, weight_ref, middle_ref, sums_ref, field
 ):
-    load = pltpu.make_async_copy(far_weight_ref, weight_ref, sem)
-    load.start()
     section, row_at = place[0], place[1]
     inner, lines, columns, channels = own_ref.shape
     cells = inner * lines * columns
     scale, shift = vectors_ref[0], vectors_ref[1]
-    mine = stats_ref[pl.ds(section * row_count, row_count)]
-    before = stats_ref[pl.ds(jnp.maximum(section - 1, 0) * row_count, row_count)]
+    mine, before = stats_ref[:, 0], stats_ref[:, 1]
     slope, offset = affine(mine, cells, scale, shift)
     slope_before, offset_before = affine(before, cells, scale, shift)
     even = row_at % 2 == 0
@@ -179,7 +191,6 @@
             ahead = jnp.where(outside, jnp.zeros_like(ahead), ahead)
         field[:SPAN_HALO, line] = behind
         field[SPAN_HALO:, line] = ahead
-    load.wait()
     bias = vectors_ref[2]
     kept = []
     spare = SPAN_HALO - 2
@@ -193,21 +204,18 @@
             middle_ref[2:, line] = rounded[2:]
             if 1 <= line <= lines:
                 kept.append(rounded[2:].astype(jnp.float32).reshape(-1, channels))
-    sums_ref[...] = jnp.broadcast_to(moments(kept)[None], sums_ref.shape)
+    sums_ref[...] = jnp.broadcast_to(moments(iter(kept))[None], sums_ref.shape)
 
 
 def second_kernel(
-    row_count, place, middle_ref, stats_ref, vectors_ref, far_weight_ref, own_ref, out_ref,
-    field, weight_ref, sem
+    row_count, place, middle_ref, stats_ref, vectors_ref, weight_ref, own_ref, out_ref, field
 ):
-    load = pltpu.make_async_copy(far_weight_ref, weight_ref, sem)
-    load.start()
     section, row_at = place[0], place[1]
     frames, lines, columns, channels = own_ref.shape
     cells = frames * lines * columns
     scale, shift = vectors_ref[3], vectors_ref[4]
-    mine = stats_ref[pl.ds(section * row_count, row_count)]
-    before = stats_ref[pl.ds(jnp.maximum(section - 1, 0) * row_count, row_count)]
+    mine = stats_ref[pl.ds(section * row_count, row_count), 0]
+    before = stats_ref[pl.ds(jnp.maximum(section - 1, 0) * row_count, row_count), 0]
     slope, offset = affine(mine, cells, scale, shift)
     slope_before, offset_before = affine(before, cells, scale, shift)
     at_start = section == 0
@@ -222,7 +230,6 @@
             ahead = jnp.where(outside, jnp.zeros_like(ahead), ahead)
         field[:2, line] = behind
         field[2:, line] = ahead
-    load.wait()
     bias = vectors_ref[5]
     for pair in range(lines // 2):
         results = pair_conv(field, 2 * pair, frames, weight_ref)
@@ -270,15 +277,9 @@
     everyone = sections * row_count
     section, row_at = lax.axis_index("section"), lax.axis_index("rows")
     place = jnp.stack([section, row_at, jnp.int32(sections)]).astype(jnp.int32)
-    stats_shape = jax.ShapeDtypeStruct((everyone, 1, channels), jnp.float32)
+    stats_shape = jax.ShapeDtypeStruct((everyone, 1, 2 * channels), jnp.float32)
     vectors = (norm1_scale, norm1_shift, conv1_bias, norm2_scale, norm2_shift, conv2_bias)
 
-    def exchange(stats):
-        return lax.all_to_all(stats, ("section", "rows"), 0, 0, tiled=True)
-
-    weight_scratch = [
-        pltpu.VMEM(conv1_weight.shape, jnp.bfloat16), pltpu.SemaphoreType.DMA
-    ]
     near = [i ^ 1 for i in range(row_count)]
     far = [0] + [i + 1 if i % 2 else i - 1 for i in range(1, row_count - 1)] + [row_count - 1]
 
@@ -293,42 +294,42 @@
         ]
         return lax.ppermute(block, ("section", "rows"), route)
 
-    sums, halo, packed, own = call(
+    sums, halo, packed, own, weight = call(
         prepare_kernel,
         (
-            stats_shape,
+            jax.ShapeDtypeStruct((1, 2 * channels), jnp.float32),
             jax.ShapeDtypeStruct((SPAN_HALO, lines, columns, channels), jnp.bfloat16),
             jax.ShapeDtypeStruct((len(vectors), 1, channels), jnp.float32),
             jax.ShapeDtypeStruct(activations.shape, jnp.bfloat16),
+            jax.ShapeDtypeStruct(conv1_weight.shape, jnp.bfloat16),
         ),
-        [pltpu.SemaphoreType.DMA((4 + len(vectors),))],
-        (place, activations, second_cache, first_cache)
+        [pltpu.SemaphoreType.DMA((4 + PARTS + len(vectors),))],
+        (place, activations, second_cache, first_cache, conv1_weight)
         + tuple(vector.reshape(1, channels) for vector in vectors),
-        in_place=range(1, 4 + len(vectors)),
+        in_place=range(1, 5 + len(vectors)),
     )
     beside = [across(activations, near), across(activations, far)]
     behind = [onward(halo, partner) for partner in (range(row_count), near, far)]
-    stats = exchange(sums)
+    ring = [(at, (at + 1) % sections) for at in range(sections)]
+    both = jnp.stack([sums, lax.ppermute(sums, "section", ring)], axis=1)
+    both = jnp.broadcast_to(both, (row_count,) + both.shape[1:])
+    stats = lax.all_to_all(both, "rows", 0, 0, tiled=True)
     middle, sums_two = call(
         functools.partial(first_kernel, row_count),
         (
             jax.ShapeDtypeStruct((frames + 2, lines + 2, columns, channels), jnp.bfloat16),
             stats_shape,
         ),
-        [pltpu.VMEM((frames + SPAN_HALO, 3 * lines, columns, channels), jnp.bfloat16)]
-        + weight_scratch,
-        (place, own, *beside, *behind, stats, packed, conv1_weight),
-        in_place=(9,),
+        [pltpu.VMEM((frames + SPAN_HALO, 3 * lines, columns, channels), jnp.bfloat16)],
+        (place, own, *beside, *behind, stats, packed, weight),
         flops=10**9,
     )
-    stats_two = exchange(sums_two)
+    stats_two = lax.all_to_all(sums_two, ("section", "rows"), 0, 0, tiled=True)
     return call(
         functools.partial(second_kernel, row_count),
         jax.ShapeDtypeStruct(activations.shape, jnp.bfloat16),
-        [pltpu.VMEM((frames + 2, lines + 2, columns, channels), jnp.bfloat16)]
-        + weight_scratch,
+        [pltpu.VMEM((frames + 2, lines + 2, columns, channels), jnp.bfloat16)],
         (place, middle, stats_two, packed, conv2_weight, own),
-        in_place=(4,),
         flops=10**9,
     )
 

time: 41.2 us -> 39.8 us (0.966)
  Pallas kernels: 11.3 us -> 9.52 us
    pallas_call x3, Pallas kernels: 11.3 us -> 9.52 us  [call(): pl.pallas_call(kernel, out_shape=out_shape, in_specs=specs, out_specs=jax...]
    ppermute x0 -> x1, starting transfers between devices: none -> 1.54 us  [on_device(): both = jnp.stack([sums, lax.ppermute(sums, 'section', ring)], axis=1)]
    ppermute x3, starting transfers between devices: 5.26 us -> 4.19 us  [onward(): return lax.ppermute(block, ('section', 'rows'), route)]
  transfers between devices with their start and end apart: 5 -> 6, of which waited for: 0 -> 0; matrix products, arithmetic and copies ran while one was open for 0% -> 0% of each run, Pallas kernels for 5% -> 5%
where the time goes in v6:
time: 39.8 us; the launch traced here: 39.5 us
  blocking collectives  19 us (48%)
  starting transfers between devices  10.8 us (27%)
  Pallas kernels  9.52 us (24%)
    all_to_all x1, blocking collectives, on_device(): stats_two = lax.all_to_all(sums_two, ('section', 'rows'), 0, 0, tiled=True)  10.3 us
    pallas_call x3, Pallas kernels, call(): pl.pallas_call(kernel, out_shape=out_shape, in_specs=specs, out_specs=jax...  9.52 us
    all_to_all x1, blocking collectives, on_device(): stats = lax.all_to_all(both, 'rows', 0, 0, tiled=True)  8.69 us
    ppermute x2, starting transfers between devices, across(): return lax.ppermute(block, 'rows', list(enumerate(partner)))  5.11 us
    ppermute x3, starting transfers between devices, onward(): return lax.ppermute(block, ('section', 'rows'), route)  4.19 us
    ppermute x1, starting transfers between devices, on_device(): both = jnp.stack([sums, lax.ppermute(sums, 'section', ring)], axis=1)  1.54 us
  transfers between devices with their start and end apart: 6, of which 0 were waited for; matrix products, arithmetic and copies ran while one was open for 0% of the time, Pallas kernels for 5%

profile of v6, /device:TPU:0, one launch (start us, length us, event | category | flops | bytes accessed | tf_op | source)
XLA Modules:
  0.0 39.5 jit_solution(10383699482952400695)
XLA Ops:
  0.0 1.6 %collective-permute-start.1 = (bf16[8,2,64,128]{3,2,1,0:T(8,128)(2,1)}, bf16[8,2,64,128]{3,2,1,0:T(8,128)(2,1)S(1)}, u32[]{:S(2)}, u32[]{:S(2)}) collective-permute-start(bf16[8,2,64,128]{3,2,1,0:T(8,128)(2,1)} %own_ref.1), channel_id=1, source_target_pairs={{0,0},{1,2},{2,1},{3,4},{4,3},{5,6},{6,5},{7,7},{8,8},{9,10},{10,9... | collective-permute-start | bytes 786440 | tf_op jit(solution)/shard_map/ppermute | solution.py:287
  1.6 3.5 %collective-permute-start = (bf16[8,2,64,128]{3,2,1,0:T(8,128)(2,1)}, bf16[8,2,64,128]{3,2,1,0:T(8,128)(2,1)S(1)}, u32[]{:S(2)}, u32[]{:S(2)}) collective-permute-start(bf16[8,2,64,128]{3,2,1,0:T(8,128)(2,1)} %own_ref.1), channel_id=1, source_target_pairs={{0,1},{1,0},{2,3},{3,2},{4,5},{5,4},{6,7},{7,6},{8,9},{9,8},{10,11... | collective-permute-start | bytes 786440 | tf_op jit(solution)/shard_map/ppermute | solution.py:287
  5.1 0.1 pad_add_fusion.place
  5.2 2.1 %shard_map.109 = (f32[1,256]{1,0:T(1,128)S(1)}, bf16[4,2,64,128]{3,2,1,0:T(8,128)(2,1)S(1)}, f32[6,1,128]{2,1,0:T(1,128)S(1)}, bf16[8,2,64,128]{3,2,1,0:T(8,128)(2,1)S(1)}, bf16[3,3,3,128,128]{4,3,2,1,0:T(8,128)(2,1)S(1)}) custom-call(s32[3]{0:T(128)S(1)} %pad_add_fusion.place, bf16[8,2,64,128]{3,2,1,0:T(8,128)(2,1)} %own_ref.1, ...), custom_call_target="tpu_custom_call" | custom-call | bytes 1048576 | tf_op jit(solution)/shard_map/pallas_call | solution.py:251
  7.3 1.5 %collective-permute-start.5 = (f32[1,256]{1,0:T(1,128)S(1)}, f32[1,256]{1,0:T(1,128)S(1)}, u32[]{:S(2)}, u32[]{:S(2)}) collective-permute-start(f32[1,256]{1,0:T(1,128)S(1)} %get-tuple-element.14), channel_id=1, source_target_pairs={{0,8},{8,16},{16,24},{24,0},{1,9},{9,17},{17,25},{25,1},{2,10},{10... | collective-permute-start | bytes 3080 | tf_op jit(solution)/shard_map/ppermute | solution.py:314
  8.8 1.5 %collective-permute-start.4 = (bf16[4,2,64,128]{3,2,1,0:T(8,128)(2,1)S(1)}, bf16[4,2,64,128]{3,2,1,0:T(8,128)(2,1)S(1)}, u32[]{:S(2)}, u32[]{:S(2)}) collective-permute-start(bf16[4,2,64,128]{3,2,1,0:T(8,128)(2,1)S(1)} %get-tuple-element.13), channel_id=1, source_target_pairs={{0,8},{1,10},{2,9},{3,12},{4,11},{5,14},{6,13},{7,15},{8,16},{9,18... | collective-permute-start | bytes 393224 | tf_op jit(solution)/shard_map/ppermute | solution.py:295
  10.3 2.2 %collective-permute-start.3 = (bf16[4,2,64,128]{3,2,1,0:T(8,128)(2,1)S(1)}, bf16[4,2,64,128]{3,2,1,0:T(8,128)(2,1)S(1)}, u32[]{:S(2)}, u32[]{:S(2)}) collective-permute-start(bf16[4,2,64,128]{3,2,1,0:T(8,128)(2,1)S(1)} %get-tuple-element.13), channel_id=1, source_target_pairs={{0,9},{1,8},{2,11},{3,10},{4,13},{5,12},{6,15},{7,14},{8,17},{9,16... | collective-permute-start | bytes 393224 | tf_op jit(solution)/shard_map/ppermute | solution.py:295
  12.6 0.0 collective-permute-done.5
  12.6 0.5 %collective-permute-start.2 = (bf16[4,2,64,128]{3,2,1,0:T(8,128)(2,1)S(1)}, bf16[4,2,64,128]{3,2,1,0:T(8,128)(2,1)S(1)}, u32[]{:S(2)}, u32[]{:S(2)}) collective-permute-start(bf16[4,2,64,128]{3,2,1,0:T(8,128)(2,1)S(1)} %get-tuple-element.13), channel_id=1, source_target_pairs={{0,8},{1,9},{2,10},{3,11},{4,12},{5,13},{6,14},{7,15},{8,16},{9,17... | collective-permute-start | bytes 393224 | tf_op jit(solution)/shard_map/ppermute | solution.py:295
  13.1 8.7 %all_to_all.10.stats_ref = f32[8,2,256]{2,1,0:T(2,128)S(1)} all-to-all(f32[8,2,256]{2,1,0:T(2,128)S(1)} %broadcast_in_dim.8), channel_id=1, replica_groups=mesh['section'=4,'rows'=8] {'rows'}, dimensions={0} | all-to-all | bytes 32768 | tf_op jit(solution)/shard_map/all_to_all | solution.py:316
  21.7 0.0 collective-permute-done.4.halo_far_ref
  21.8 0.0 collective-permute-done.3.halo_near_ref
  21.8 0.0 collective-permute-done.2.halo_ref
  21.8 0.0 collective-permute-done.1.far_ref
  21.8 0.0 collective-permute-done.near_ref
  21.8 0.0 copy-start
  21.8 4.3 %shard_map.110 = (bf16[10,4,64,128]{3,2,1,0:T(8,128)(2,1)S(1)}, f32[32,1,256]{2,1,0:T(1,128)S(1)}) custom-call(s32[3]{0:T(128)S(1)} %pad_add_fusion.place, bf16[8,2,64,128]{3,2,1,0:T(8,128)(2,1)S(1)} %get-tuple-element.12.own_ref, bf16[8,2,64,128]{3,2,1,0:T(8,128)(2,1)S(1)} %collective-permute-done.near_ref, ...), custom_call_target="tpu_custom_call" | custom-call | flops 1000000000 | bytes 1048576 | tf_op jit(solution)/shard_map/pallas_call | solution.py:251
  26.1 10.3 %all_to_all.11.stats_ref = f32[32,1,256]{2,1,0:T(1,128)S(1)} all-to-all(f32[32,1,256]{2,1,0:T(1,128)S(1)} %get-tuple-element.18), channel_id=1, replica_groups=mesh['section'=4,'rows'=8] {'section','rows'}, dimensions={0} | all-to-all | bytes 65536 | tf_op jit(solution)/shard_map/all_to_all | solution.py:327
  36.4 0.0 copy-done
  36.4 3.1 %shard_map.111 = bf16[8,2,64,128]{3,2,1,0:T(8,128)(2,1)} custom-call(s32[3]{0:T(128)S(1)} %pad_add_fusion.place, bf16[10,4,64,128]{3,2,1,0:T(8,128)(2,1)S(1)} %get-tuple-element.17.middle_ref, f32[32,1,256]{2,1,0:T(1,128)S(1)} %all_to_all.11.stats_ref, f32[6,1,128]{2,1,0:T(1,128)S(1)} %get-tuple-element.15.vectors_ref, ...), custom_call_target="tpu_custom_call" | custom-call | flops 1000000000 | bytes 1048576 | tf_op jit(solution)/shard_map/pallas_call | solution.py:251
  (2 shorter events, 0.0 us)
Async XLA Ops:
  0.0 21.8 %collective-permute-start.1 = (bf16[8,2,64,128]{3,2,1,0:T(8,128)(2,1)}, bf16[8,2,64,128]{3,2,1,0:T(8,128)(2,1)S(1)}, u32[]{:S(2)}, u32[]{:S(2)}) collective-permute-start(bf16[8,2,64,128]{3,2,1,0:T(8,128)(2,1)} %own_ref.1), channel_id=1, source_target_pairs={{0,0},{1,2},{2,1},{3,4},{4,3},{5,6},{6,5},{7,7},{8,8},{9,10},{10,9... | collective-permute-start | bytes 786440 | tf_op jit(solution)/shard_map/ppermute | solution.py:287
  1.6 20.2 %collective-permute-start = (bf16[8,2,64,128]{3,2,1,0:T(8,128)(2,1)}, bf16[8,2,64,128]{3,2,1,0:T(8,128)(2,1)S(1)}, u32[]{:S(2)}, u32[]{:S(2)}) collective-permute-start(bf16[8,2,64,128]{3,2,1,0:T(8,128)(2,1)} %own_ref.1), channel_id=1, source_target_pairs={{0,1},{1,0},{2,3},{3,2},{4,5},{5,4},{6,7},{7,6},{8,9},{9,8},{10,11... | collective-permute-start | bytes 786440 | tf_op jit(solution)/shard_map/ppermute | solution.py:287
  7.3 5.3 %collective-permute-start.5 = (f32[1,256]{1,0:T(1,128)S(1)}, f32[1,256]{1,0:T(1,128)S(1)}, u32[]{:S(2)}, u32[]{:S(2)}) collective-permute-start(f32[1,256]{1,0:T(1,128)S(1)} %get-tuple-element.14), channel_id=1, source_target_pairs={{0,8},{8,16},{16,24},{24,0},{1,9},{9,17},{17,25},{25,1},{2,10},{10... | collective-permute-start | bytes 3080 | tf_op jit(solution)/shard_map/ppermute | solution.py:314
  8.8 12.9 %collective-permute-start.4 = (bf16[4,2,64,128]{3,2,1,0:T(8,128)(2,1)S(1)}, bf16[4,2,64,128]{3,2,1,0:T(8,128)(2,1)S(1)}, u32[]{:S(2)}, u32[]{:S(2)}) collective-permute-start(bf16[4,2,64,128]{3,2,1,0:T(8,128)(2,1)S(1)} %get-tuple-element.13), channel_id=1, source_target_pairs={{0,8},{1,10},{2,9},{3,12},{4,11},{5,14},{6,13},{7,15},{8,16},{9,18... | collective-permute-start | bytes 393224 | tf_op jit(solution)/shard_map/ppermute | solution.py:295
  10.3 11.4 %collective-permute-start.3 = (bf16[4,2,64,128]{3,2,1,0:T(8,128)(2,1)S(1)}, bf16[4,2,64,128]{3,2,1,0:T(8,128)(2,1)S(1)}, u32[]{:S(2)}, u32[]{:S(2)}) collective-permute-start(bf16[4,2,64,128]{3,2,1,0:T(8,128)(2,1)S(1)} %get-tuple-element.13), channel_id=1, source_target_pairs={{0,9},{1,8},{2,11},{3,10},{4,13},{5,12},{6,15},{7,14},{8,17},{9,16... | collective-permute-start | bytes 393224 | tf_op jit(solution)/shard_map/ppermute | solution.py:295
  12.6 9.2 %collective-permute-start.2 = (bf16[4,2,64,128]{3,2,1,0:T(8,128)(2,1)S(1)}, bf16[4,2,64,128]{3,2,1,0:T(8,128)(2,1)S(1)}, u32[]{:S(2)}, u32[]{:S(2)}) collective-permute-start(bf16[4,2,64,128]{3,2,1,0:T(8,128)(2,1)S(1)} %get-tuple-element.13), channel_id=1, source_target_pairs={{0,8},{1,9},{2,10},{3,11},{4,12},{5,13},{6,14},{7,15},{8,16},{9,17... | collective-permute-start | bytes 393224 | tf_op jit(solution)/shard_map/ppermute | solution.py:295
  21.8 14.6 %copy-start = (bf16[3,3,3,128,128]{4,3,2,1,0:T(8,128)(2,1)S(1)}, bf16[3,3,3,128,128]{4,3,2,1,0:T(8,128)(2,1)}, u32[]{:S(2)}) copy-start(bf16[3,3,3,128,128]{4,3,2,1,0:T(8,128)(2,1)} %weight_ref.3) | copy-start | bytes 2654212

commit v7 on v6

--- a/solution.py
+++ b/solution.py
@@ -286,14 +286,7 @@
     def across(block, partner):
         return lax.ppermute(block, "rows", list(enumerate(partner)))
 
-    def onward(block, partner):
-        route = [
-            (at * row_count + row, (at + 1) % sections * row_count + partner[row])
-            for at in range(sections)
-            for row in range(row_count)
-        ]
-        return lax.ppermute(block, ("section", "rows"), route)
-
+    ring = [(at, (at + 1) % sections) for at in range(sections)]
     sums, halo, packed, own, weight = call(
         prepare_kernel,
         (
@@ -309,8 +302,8 @@
         in_place=range(1, 5 + len(vectors)),
     )
     beside = [across(activations, near), across(activations, far)]
-    behind = [onward(halo, partner) for partner in (range(row_count), near, far)]
-    ring = [(at, (at + 1) % sections) for at in range(sections)]
+    behind = [lax.ppermute(halo, "section", ring)]
+    behind += [across(behind[0], near), across(behind[0], far)]
     both = jnp.stack([sums, lax.ppermute(sums, "section", ring)], axis=1)
     both = jnp.broadcast_to(both, (row_count,) + both.shape[1:])
     stats = lax.all_to_all(both, "rows", 0, 0, tiled=True)

time: 39.8 us -> 39.5 us (level)
  blocking collectives: 19 us -> 17.8 us
  starting transfers between devices: 10.8 us -> 11.8 us
    ppermute x2 -> x4, starting transfers between devices: 5.11 us -> 7.31 us  [across(): return lax.ppermute(block, 'rows', list(enumerate(partner)))]
    all_to_all x1, blocking collectives: 10.3 us -> 8.99 us  [on_device(): stats_two = lax.all_to_all(sums_two, ('section', 'rows'), 0, 0, tiled=True)]
    ppermute x3 -> x1, starting transfers between devices: 4.19 us -> 2.99 us  [on_device(): behind = [lax.ppermute(halo, 'section', ring)]]
  transfers between devices with their start and end apart: 6 -> 6, of which waited for: 0 -> 0; matrix products, arithmetic and copies ran while one was open for 0% -> 0% of each run, Pallas kernels for 5% -> 0%
where the time goes in v7:
time: 39.5 us; the launch traced here: 39.3 us
  blocking collectives  17.8 us (45%)
  starting transfers between devices  11.8 us (30%)
  Pallas kernels  9.52 us (24%)
    pallas_call x3, Pallas kernels, call(): pl.pallas_call(kernel, out_shape=out_shape, in_specs=specs, out_specs=jax...  9.52 us
    all_to_all x1, blocking collectives, on_device(): stats_two = lax.all_to_all(sums_two, ('section', 'rows'), 0, 0, tiled=True)  8.99 us
    all_to_all x1, blocking collectives, on_device(): stats = lax.all_to_all(both, 'rows', 0, 0, tiled=True)  8.8 us
    ppermute x4, starting transfers between devices, across(): return lax.ppermute(block, 'rows', list(enumerate(partner)))  7.31 us
    ppermute x1, starting transfers between devices, on_device(): behind = [lax.ppermute(halo, 'section', ring)]  2.99 us
    ppermute x1, starting transfers between devices, on_device(): both = jnp.stack([sums, lax.ppermute(sums, 'section', ring)], axis=1)  1.49 us
  transfers between devices with their start and end apart: 6, of which 0 were waited for; matrix products, arithmetic and copies ran while one was open for 0% of the time, Pallas kernels for 0%

profile of v7, /device:TPU:0, one launch (start us, length us, event | category | flops | bytes accessed | tf_op | source)
XLA Modules:
  0.0 39.3 jit_solution(7532644751895185095)
XLA Ops:
  0.0 0.1 pad_add_fusion.place
  0.1 0.0 copy-start.1
  0.1 2.1 %shard_map.109 = (f32[1,256]{1,0:T(1,128)S(1)}, bf16[4,2,64,128]{3,2,1,0:T(8,128)(2,1)S(1)}, f32[6,1,128]{2,1,0:T(1,128)S(1)}, bf16[8,2,64,128]{3,2,1,0:T(8,128)(2,1)S(1)}, bf16[3,3,3,128,128]{4,3,2,1,0:T(8,128)(2,1)S(1)}) custom-call(s32[3]{0:T(128)S(1)} %pad_add_fusion.place, bf16[8,2,64,128]{3,2,1,0:T(8,128)(2,1)} %own_ref.1, ...), custom_call_target="tpu_custom_call" | custom-call | bytes 1048576 | tf_op jit(solution)/shard_map/pallas_call | solution.py:251
  2.2 3.0 %collective-permute-start.2 = (bf16[4,2,64,128]{3,2,1,0:T(8,128)(2,1)S(1)}, bf16[4,2,64,128]{3,2,1,0:T(8,128)(2,1)S(1)}, u32[]{:S(2)}, u32[]{:S(2)}) collective-permute-start(bf16[4,2,64,128]{3,2,1,0:T(8,128)(2,1)S(1)} %get-tuple-element.13), channel_id=1, source_target_pairs={{0,8},{8,16},{16,24},{24,0},{1,9},{9,17},{17,25},{25,1},{2,10},{10... | collective-permute-start | bytes 393224 | tf_op jit(solution)/shard_map/ppermute | solution.py:305
  5.2 0.0 copy-done.1
  5.2 0.7 %collective-permute-start.1 = (bf16[8,2,64,128]{3,2,1,0:T(8,128)(2,1)S(1)}, bf16[8,2,64,128]{3,2,1,0:T(8,128)(2,1)S(1)}, u32[]{:S(2)}, u32[]{:S(2)}) collective-permute-start(bf16[8,2,64,128]{3,2,1,0:T(8,128)(2,1)S(1)} %copy-done.1), channel_id=1, source_target_pairs={{0,0},{1,2},{2,1},{3,4},{4,3},{5,6},{6,5},{7,7},{8,8},{9,10},{10,9... | collective-permute-start | bytes 786440 | tf_op jit(solution)/shard_map/ppermute | solution.py:287
  5.9 3.0 %collective-permute-start = (bf16[8,2,64,128]{3,2,1,0:T(8,128)(2,1)S(1)}, bf16[8,2,64,128]{3,2,1,0:T(8,128)(2,1)S(1)}, u32[]{:S(2)}, u32[]{:S(2)}) collective-permute-start(bf16[8,2,64,128]{3,2,1,0:T(8,128)(2,1)S(1)} %copy-done.1), channel_id=1, source_target_pairs={{0,1},{1,0},{2,3},{3,2},{4,5},{5,4},{6,7},{7,6},{8,9},{9,8},{10,11... | collective-permute-start | bytes 786440 | tf_op jit(solution)/shard_map/ppermute | solution.py:287
  8.8 1.5 %collective-permute-start.5 = (f32[1,256]{1,0:T(1,128)S(1)}, f32[1,256]{1,0:T(1,128)S(1)}, u32[]{:S(2)}, u32[]{:S(2)}) collective-permute-start(f32[1,256]{1,0:T(1,128)S(1)} %get-tuple-element.14), channel_id=1, source_target_pairs={{0,8},{8,16},{16,24},{24,0},{1,9},{9,17},{17,25},{25,1},{2,10},{10... | collective-permute-start | bytes 3080 | tf_op jit(solution)/shard_map/ppermute | solution.py:307
  10.3 0.0 collective-permute-done.2.halo_ref
  10.3 0.7 %collective-permute-start.4 = (bf16[4,2,64,128]{3,2,1,0:T(8,128)(2,1)S(1)}, bf16[4,2,64,128]{3,2,1,0:T(8,128)(2,1)S(1)}, u32[]{:S(2)}, u32[]{:S(2)}) collective-permute-start(bf16[4,2,64,128]{3,2,1,0:T(8,128)(2,1)S(1)} %collective-permute-done.2.halo_ref), channel_id=1, source_target_pairs={{0,0},{1,2},{2,1},{3,4},{4,3},{5,6},{6,5},{7,7},{8,8},{9,10},{10,9... | collective-permute-start | bytes 393224 | tf_op jit(solution)/shard_map/ppermute | solution.py:287
  11.0 3.0 %collective-permute-start.3 = (bf16[4,2,64,128]{3,2,1,0:T(8,128)(2,1)S(1)}, bf16[4,2,64,128]{3,2,1,0:T(8,128)(2,1)S(1)}, u32[]{:S(2)}, u32[]{:S(2)}) collective-permute-start(bf16[4,2,64,128]{3,2,1,0:T(8,128)(2,1)S(1)} %collective-permute-done.2.halo_ref), channel_id=1, source_target_pairs={{0,1},{1,0},{2,3},{3,2},{4,5},{5,4},{6,7},{7,6},{8,9},{9,8},{10,11... | collective-permute-start | bytes 393224 | tf_op jit(solution)/shard_map/ppermute | solution.py:287
  14.0 0.0 collective-permute-done.5
  14.0 8.8 %all_to_all.10.stats_ref = f32[8,2,256]{2,1,0:T(2,128)S(1)} all-to-all(f32[8,2,256]{2,1,0:T(2,128)S(1)} %broadcast_in_dim.8), channel_id=1, replica_groups=mesh['section'=4,'rows'=8] {'rows'}, dimensions={0} | all-to-all | bytes 32768 | tf_op jit(solution)/shard_map/all_to_all | solution.py:309
  22.8 0.0 collective-permute-done.1.far_ref
  22.8 0.0 collective-permute-done.near_ref
  22.8 0.0 collective-permute-done.4.halo_far_ref
  22.8 0.0 collective-permute-done.3.halo_near_ref
  22.9 0.0 copy-start
  22.9 4.3 %shard_map.110 = (bf16[10,4,64,128]{3,2,1,0:T(8,128)(2,1)S(1)}, f32[32,1,256]{2,1,0:T(1,128)S(1)}) custom-call(s32[3]{0:T(128)S(1)} %pad_add_fusion.place, bf16[8,2,64,128]{3,2,1,0:T(8,128)(2,1)S(1)} %get-tuple-element.12.own_ref, bf16[8,2,64,128]{3,2,1,0:T(8,128)(2,1)S(1)} %collective-permute-done.near_ref, ...), custom_call_target="tpu_custom_call" | custom-call | flops 1000000000 | bytes 1048576 | tf_op jit(solution)/shard_map/pallas_call | solution.py:251
  27.1 9.0 %all_to_all.11.stats_ref = f32[32,1,256]{2,1,0:T(1,128)S(1)} all-to-all(f32[32,1,256]{2,1,0:T(1,128)S(1)} %get-tuple-element.18), channel_id=1, replica_groups=mesh['section'=4,'rows'=8] {'section','rows'}, dimensions={0} | all-to-all | bytes 65536 | tf_op jit(solution)/shard_map/all_to_all | solution.py:320
  36.1 0.0 copy-done
  36.1 3.1 %shard_map.111 = bf16[8,2,64,128]{3,2,1,0:T(8,128)(2,1)} custom-call(s32[3]{0:T(128)S(1)} %pad_add_fusion.place, bf16[10,4,64,128]{3,2,1,0:T(8,128)(2,1)S(1)} %get-tuple-element.17.middle_ref, f32[32,1,256]{2,1,0:T(1,128)S(1)} %all_to_all.11.stats_ref, f32[6,1,128]{2,1,0:T(1,128)S(1)} %get-tuple-element.15.vectors_ref, ...), custom_call_target="tpu_custom_call" | custom-call | flops 1000000000 | bytes 1048576 | tf_op jit(solution)/shard_map/pallas_call | solution.py:251
  (2 shorter events, 0.0 us)
Async XLA Ops:
  0.1 5.1 %copy-start.1 = (bf16[8,2,64,128]{3,2,1,0:T(8,128)(2,1)S(1)}, bf16[8,2,64,128]{3,2,1,0:T(8,128)(2,1)}, u32[]{:S(2)}) copy-start(bf16[8,2,64,128]{3,2,1,0:T(8,128)(2,1)} %own_ref.1) | copy-start | bytes 786436
  2.2 8.2 %collective-permute-start.2 = (bf16[4,2,64,128]{3,2,1,0:T(8,128)(2,1)S(1)}, bf16[4,2,64,128]{3,2,1,0:T(8,128)(2,1)S(1)}, u32[]{:S(2)}, u32[]{:S(2)}) collective-permute-start(bf16[4,2,64,128]{3,2,1,0:T(8,128)(2,1)S(1)} %get-tuple-element.13), channel_id=1, source_target_pairs={{0,8},{8,16},{16,24},{24,0},{1,9},{9,17},{17,25},{25,1},{2,10},{10... | collective-permute-start | bytes 393224 | tf_op jit(solution)/shard_map/ppermute | solution.py:305
  5.2 17.7 %collective-permute-start.1 = (bf16[8,2,64,128]{3,2,1,0:T(8,128)(2,1)S(1)}, bf16[8,2,64,128]{3,2,1,0:T(8,128)(2,1)S(1)}, u32[]{:S(2)}, u32[]{:S(2)}) collective-permute-start(bf16[8,2,64,128]{3,2,1,0:T(8,128)(2,1)S(1)} %copy-done.1), channel_id=1, source_target_pairs={{0,0},{1,2},{2,1},{3,4},{4,3},{5,6},{6,5},{7,7},{8,8},{9,10},{10,9... | collective-permute-start | bytes 786440 | tf_op jit(solution)/shard_map/ppermute | solution.py:287
  5.9 17.0 %collective-permute-start = (bf16[8,2,64,128]{3,2,1,0:T(8,128)(2,1)S(1)}, bf16[8,2,64,128]{3,2,1,0:T(8,128)(2,1)S(1)}, u32[]{:S(2)}, u32[]{:S(2)}) collective-permute-start(bf16[8,2,64,128]{3,2,1,0:T(8,128)(2,1)S(1)} %copy-done.1), channel_id=1, source_target_pairs={{0,1},{1,0},{2,3},{3,2},{4,5},{5,4},{6,7},{7,6},{8,9},{9,8},{10,11... | collective-permute-start | bytes 786440 | tf_op jit(solution)/shard_map/ppermute | solution.py:287
  8.8 5.2 %collective-permute-start.5 = (f32[1,256]{1,0:T(1,128)S(1)}, f32[1,256]{1,0:T(1,128)S(1)}, u32[]{:S(2)}, u32[]{:S(2)}) collective-permute-start(f32[1,256]{1,0:T(1,128)S(1)} %get-tuple-element.14), channel_id=1, source_target_pairs={{0,8},{8,16},{16,24},{24,0},{1,9},{9,17},{17,25},{25,1},{2,10},{10... | collective-permute-start | bytes 3080 | tf_op jit(solution)/shard_map/ppermute | solution.py:307
  10.3 12.5 %collective-permute-start.4 = (bf16[4,2,64,128]{3,2,1,0:T(8,128)(2,1)S(1)}, bf16[4,2,64,128]{3,2,1,0:T(8,128)(2,1)S(1)}, u32[]{:S(2)}, u32[]{:S(2)}) collective-permute-start(bf16[4,2,64,128]{3,2,1,0:T(8,128)(2,1)S(1)} %collective-permute-done.2.halo_ref), channel_id=1, source_target_pairs={{0,0},{1,2},{2,1},{3,4},{4,3},{5,6},{6,5},{7,7},{8,8},{9,10},{10,9... | collective-permute-start | bytes 393224 | tf_op jit(solution)/shard_map/ppermute | solution.py:287
  11.0 11.8 %collective-permute-start.3 = (bf16[4,2,64,128]{3,2,1,0:T(8,128)(2,1)S(1)}, bf16[4,2,64,128]{3,2,1,0:T(8,128)(2,1)S(1)}, u32[]{:S(2)}, u32[]{:S(2)}) collective-permute-start(bf16[4,2,64,128]{3,2,1,0:T(8,128)(2,1)S(1)} %collective-permute-done.2.halo_ref), channel_id=1, source_target_pairs={{0,1},{1,0},{2,3},{3,2},{4,5},{5,4},{6,7},{7,6},{8,9},{9,8},{10,11... | collective-permute-start | bytes 393224 | tf_op jit(solution)/shard_map/ppermute | solution.py:287
  22.9 13.3 %copy-start = (bf16[3,3,3,128,128]{4,3,2,1,0:T(8,128)(2,1)S(1)}, bf16[3,3,3,128,128]{4,3,2,1,0:T(8,128)(2,1)}, u32[]{:S(2)}) copy-start(bf16[3,3,3,128,128]{4,3,2,1,0:T(8,128)(2,1)} %weight_ref.3) | copy-start | bytes 2654212

commit v8 on v7

--- a/solution.py
+++ b/solution.py
@@ -13,7 +13,6 @@
 
 GROUPS = 32
 SPAN_HALO = 4
-PARTS = 4
 
 epsilon = 1e-06
 
@@ -100,27 +99,14 @@
     return results
 
 
-def prepare_kernel(
-    place, own_ref, second_cache_ref, first_cache_ref, weight_ref, *rest
-):
-    *vector_refs, stats_ref, halo_ref, vectors_ref, copied, weight_copy, sems = rest
-    last = place[0] == place[2] - 1
+def copy_kernel(sections, own_ref, second_cache_ref, first_cache_ref, copied, halo_ref, sems):
+    last = lax.axis_index("section") == sections - 1
     frames = own_ref.shape[0]
-    part = frames // PARTS
-    loads = [
-        pltpu.make_async_copy(
-            own_ref.at[pl.ds(index * part, part)],
-            copied.at[pl.ds(index * part, part)],
-            sems.at[3 + index],
-        )
-        for index in range(PARTS)
-    ]
-    for load in loads:
-        load.start()
+    spare = SPAN_HALO - 2
     tail = pltpu.make_async_copy(own_ref.at[frames - SPAN_HALO :], halo_ref, sems.at[0])
-    spare = SPAN_HALO - 2
     older = pltpu.make_async_copy(second_cache_ref, halo_ref.at[:spare], sems.at[1])
     newer = pltpu.make_async_copy(first_cache_ref, halo_ref.at[spare:], sems.at[2])
+    load = pltpu.make_async_copy(own_ref, copied, sems.at[3])
 
     @pl.when(last)
     def _():
@@ -131,25 +117,7 @@
     def _():
         tail.start()
 
-    late_loads = [
-        pltpu.make_async_copy(vector_ref, vectors_ref.at[index], sems.at[3 + PARTS + index])
-        for index, vector_ref in enumerate(vector_refs)
-    ]
-    late_loads.append(
-        pltpu.make_async_copy(weight_ref, weight_copy, sems.at[3 + PARTS + len(vector_refs)])
-    )
-    for late_load in late_loads:
-        late_load.start()
-
-    def arriving():
-        for index, load in enumerate(loads):
-            load.wait()
-            block = copied[index * part : (index + 1) * part].astype(jnp.float32)
-            yield block.reshape(-1, block.shape[-1])
-
-    stats_ref[...] = moments(arriving())
-    for late_load in late_loads:
-        late_load.wait()
+    load.start()
 
     @pl.when(last)
     def _():
@@ -160,12 +128,30 @@
     def _():
         tail.wait()
 
+    load.wait()
+
+
+def stats_kernel(own_ref, weight_ref, *rest):
+    *vector_refs, stats_ref, vectors_ref, weight_copy, sems = rest
+    loads = [pltpu.make_async_copy(weight_ref, weight_copy, sems.at[0])]
+    loads += [
+        pltpu.make_async_copy(vector_ref, vectors_ref.at[index], sems.at[1 + index])
+        for index, vector_ref in enumerate(vector_refs)
+    ]
+    for load in loads:
+        load.start()
+    channels = own_ref.shape[-1]
+    blocks = (own_ref[frame].astype(jnp.float32) for frame in range(own_ref.shape[0]))
+    stats_ref[...] = moments(block.reshape(-1, channels) for block in blocks)
+    for load in loads:
+        load.wait()
+
 
 def first_kernel(
-    row_count, place, own_ref, near_ref, far_ref, halo_ref, halo_near_ref, halo_far_ref,
+    row_count, own_ref, near_ref, far_ref, halo_ref, halo_near_ref, halo_far_ref,
     stats_ref, vectors_ref, weight_ref, middle_ref, sums_ref, field
 ):
-    section, row_at = place[0], place[1]
+    section, row_at = lax.axis_index("section"), lax.axis_index("rows")
     inner, lines, columns, channels = own_ref.shape
     cells = inner * lines * columns
     scale, shift = vectors_ref[0], vectors_ref[1]
@@ -174,7 +160,8 @@
     slope_before, offset_before = affine(before, cells, scale, shift)
     even = row_at % 2 == 0
     at_start = section == 0
-    for line in range(3 * lines):
+
+    def fill(line):
         side, local = divmod(line, lines)
         if side == 1:
             halo, body = halo_ref[:, local], own_ref[:, local]
@@ -191,10 +178,15 @@
             ahead = jnp.where(outside, jnp.zeros_like(ahead), ahead)
         field[:SPAN_HALO, line] = behind
         field[SPAN_HALO:, line] = ahead
+
     bias = vectors_ref[2]
     kept = []
     spare = SPAN_HALO - 2
+    ready = 0
     for pair in range((lines + 2) // 2):
+        for line in range(ready, 2 * pair + 4):
+            fill(line)
+        ready = 2 * pair + 4
         results = pair_conv(field, 2 * pair, inner + 2, weight_ref)
         for out in range(2):
             line = 2 * pair + out
@@ -208,9 +200,9 @@
 
 
 def second_kernel(
-    row_count, place, middle_ref, stats_ref, vectors_ref, weight_ref, own_ref, out_ref, field
+    row_count, middle_ref, stats_ref, vectors_ref, weight_ref, own_ref, out_ref, field
 ):
-    section, row_at = place[0], place[1]
+    section, row_at = lax.axis_index("section"), lax.axis_index("rows")
     frames, lines, columns, channels = own_ref.shape
     cells = frames * lines * columns
     scale, shift = vectors_ref[3], vectors_ref[4]
@@ -241,7 +233,7 @@
 
 def call(kernel, out_shape, scratch, operands, in_place=(), flops=0):
     vmem = pl.BlockSpec(memory_space=pltpu.VMEM)
-    specs = [pl.BlockSpec(memory_space=pltpu.SMEM)] + [vmem] * (len(operands) - 1)
+    specs = [vmem] * len(operands)
     for index in in_place:
         specs[index] = pl.BlockSpec(memory_space=pltpu.HBM)
     operands = [
@@ -275,8 +267,6 @@
     frames, lines, columns, channels = activations.shape
     sections, row_count = lax.axis_size("section"), lax.axis_size("rows")
     everyone = sections * row_count
-    section, row_at = lax.axis_index("section"), lax.axis_index("rows")
-    place = jnp.stack([section, row_at, jnp.int32(sections)]).astype(jnp.int32)
     stats_shape = jax.ShapeDtypeStruct((everyone, 1, 2 * channels), jnp.float32)
     vectors = (norm1_scale, norm1_shift, conv1_bias, norm2_scale, norm2_shift, conv2_bias)
 
@@ -287,21 +277,28 @@
         return lax.ppermute(block, "rows", list(enumerate(partner)))
 
     ring = [(at, (at + 1) % sections) for at in range(sections)]
-    sums, halo, packed, own, weight = call(
-        prepare_kernel,
+    own, halo = call(
+        functools.partial(copy_kernel, sections),
+        (
+            jax.ShapeDtypeStruct(activations.shape, jnp.bfloat16),
+            jax.ShapeDtypeStruct((SPAN_HALO, lines, columns, channels), jnp.bfloat16),
+        ),
+        [pltpu.SemaphoreType.DMA((4,))],
+        (activations, second_cache, first_cache),
+        in_place=range(3),
+    )
+    sums, packed, weight = call(
+        stats_kernel,
         (
             jax.ShapeDtypeStruct((1, 2 * channels), jnp.float32),
-            jax.ShapeDtypeStruct((SPAN_HALO, lines, columns, channels), jnp.bfloat16),
             jax.ShapeDtypeStruct((len(vectors), 1, channels), jnp.float32),
-            jax.ShapeDtypeStruct(activations.shape, jnp.bfloat16),
             jax.ShapeDtypeStruct(conv1_weight.shape, jnp.bfloat16),
         ),
-        [pltpu.SemaphoreType.DMA((4 + PARTS + len(vectors),))],
-        (place, activations, second_cache, first_cache, conv1_weight)
-        + tuple(vector.reshape(1, channels) for vector in vectors),
-        in_place=range(1, 5 + len(vectors)),
-    )
-    beside = [across(activations, near), across(activations, far)]
+        [pltpu.SemaphoreType.DMA((1 + len(vectors),))],
+        (own, conv1_weight) + tuple(vector.reshape(1, channels) for vector in vectors),
+        in_place=range(1, 2 + len(vectors)),
+    )
+    beside = [across(own, near), across(own, far)]
     behind = [lax.ppermute(halo, "section", ring)]
     behind += [across(behind[0], near), across(behind[0], far)]
     both = jnp.stack([sums, lax.ppermute(sums, "section", ring)], axis=1)
@@ -314,7 +311,7 @@
             stats_shape,
         ),
         [pltpu.VMEM((frames + SPAN_HALO, 3 * lines, columns, channels), jnp.bfloat16)],
-        (place, own, *beside, *behind, stats, packed, weight),
+        (own, *beside, *behind, stats, packed, weight),
         flops=10**9,
     )
     stats_two = lax.all_to_all(sums_two, ("section", "rows"), 0, 0, tiled=True)
@@ -322,7 +319,7 @@
         functools.partial(second_kernel, row_count),
         jax.ShapeDtypeStruct(activations.shape, jnp.bfloat16),
         [pltpu.VMEM((frames + 2, lines + 2, columns, channels), jnp.bfloat16)],
-        (place, middle, stats_two, packed, conv2_weight, own),
+        (middle, stats_two, packed, conv2_weight, own),
         flops=10**9,
     )
 

time: 39.5 us -> 38.4 us (0.972)
  Pallas kernels: 9.52 us -> 8.64 us
    pallas_call x3 -> x4, Pallas kernels: 9.52 us -> 8.64 us  [call(): pl.pallas_call(kernel, out_shape=out_shape, in_specs=specs, out_specs=jax...]
  transfers between devices with their start and end apart: 6 -> 6, of which waited for: 0 -> 0; matrix products, arithmetic and copies ran while one was open for 0% -> 0% of each run, Pallas kernels for 0% -> 3%
where the time goes in v8:
time: 38.4 us; the launch traced here: 38.2 us
  blocking collectives  17.6 us (46%)
  starting transfers between devices  11.8 us (31%)
  Pallas kernels  8.64 us (22%)
    all_to_all x1, blocking collectives, on_device(): stats_two = lax.all_to_all(sums_two, ('section', 'rows'), 0, 0, tiled=True)  8.97 us
    pallas_call x4, Pallas kernels, call(): pl.pallas_call(kernel, out_shape=out_shape, in_specs=specs, out_specs=jax...  8.64 us
    all_to_all x1, blocking collectives, on_device(): stats = lax.all_to_all(both, 'rows', 0, 0, tiled=True)  8.62 us
    ppermute x4, starting transfers between devices, across(): return lax.ppermute(block, 'rows', list(enumerate(partner)))  7.31 us
    ppermute x1, starting transfers between devices, on_device(): behind = [lax.ppermute(halo, 'section', ring)]  2.99 us
    ppermute x1, starting transfers between devices, on_device(): both = jnp.stack([sums, lax.ppermute(sums, 'section', ring)], axis=1)  1.54 us
  transfers between devices with their start and end apart: 6, of which 0 were waited for; matrix products, arithmetic and copies ran while one was open for 0% of the time, Pallas kernels for 3%

profile of v8, /device:TPU:0, one launch (start us, length us, event | category | flops | bytes accessed | tf_op | source)
XLA Modules:
  0.0 38.2 jit_solution(5697239074024083379)
XLA Ops:
  0.0 1.1 %shard_map.109 = (bf16[8,2,64,128]{3,2,1,0:T(8,128)(2,1)S(1)}, bf16[4,2,64,128]{3,2,1,0:T(8,128)(2,1)S(1)}) custom-call(bf16[8,2,64,128]{3,2,1,0:T(8,128)(2,1)} %own_ref.1, bf16[2,2,64,128]{3,2,1,0:T(8,128)(2,1)} %second_cache_ref.1, bf16[2,2,64,128]{3,2,1,0:T(8,128)(2,1)} %first_cache_ref.1), custom_call_target="tpu_custom_call" | custom-call | bytes 1048576 | tf_op jit(solution)/shard_map/pallas_call | solution.py:243
  1.1 3.0 %collective-permute-start.2 = (bf16[4,2,64,128]{3,2,1,0:T(8,128)(2,1)S(1)}, bf16[4,2,64,128]{3,2,1,0:T(8,128)(2,1)S(1)}, u32[]{:S(2)}, u32[]{:S(2)}) collective-permute-start(bf16[4,2,64,128]{3,2,1,0:T(8,128)(2,1)S(1)} %get-tuple-element.13), channel_id=1, source_target_pairs={{0,8},{8,16},{16,24},{24,0},{1,9},{9,17},{17,25},{25,1},{2,10},{10... | collective-permute-start | bytes 393224 | tf_op jit(solution)/shard_map/ppermute | solution.py:302
  4.1 0.7 %collective-permute-start.1 = (bf16[8,2,64,128]{3,2,1,0:T(8,128)(2,1)S(1)}, bf16[8,2,64,128]{3,2,1,0:T(8,128)(2,1)S(1)}, u32[]{:S(2)}, u32[]{:S(2)}) collective-permute-start(bf16[8,2,64,128]{3,2,1,0:T(8,128)(2,1)S(1)} %get-tuple-element.12.own_ref), channel_id=1, source_target_pairs={{0,0},{1,2},{2,1},{3,4},{4,3},{5,6},{6,5},{7,7},{8,8},{9,10},{10,9... | collective-permute-start | bytes 786440 | tf_op jit(solution)/shard_map/ppermute | solution.py:277
  4.7 3.0 %collective-permute-start = (bf16[8,2,64,128]{3,2,1,0:T(8,128)(2,1)S(1)}, bf16[8,2,64,128]{3,2,1,0:T(8,128)(2,1)S(1)}, u32[]{:S(2)}, u32[]{:S(2)}) collective-permute-start(bf16[8,2,64,128]{3,2,1,0:T(8,128)(2,1)S(1)} %get-tuple-element.12.own_ref), channel_id=1, source_target_pairs={{0,1},{1,0},{2,3},{3,2},{4,5},{5,4},{6,7},{7,6},{8,9},{9,8},{10,11... | collective-permute-start | bytes 786440 | tf_op jit(solution)/shard_map/ppermute | solution.py:277
  7.7 1.2 %shard_map.110 = (f32[1,256]{1,0:T(1,128)S(1)}, f32[6,1,128]{2,1,0:T(1,128)S(1)}, bf16[3,3,3,128,128]{4,3,2,1,0:T(8,128)(2,1)S(1)}) custom-call(bf16[8,2,64,128]{3,2,1,0:T(8,128)(2,1)S(1)} %get-tuple-element.12.own_ref, bf16[3,3,3,128,128]{4,3,2,1,0:T(8,128)(2,1)} %weight_ref.2, f32[1,128]{1,0:T(1,128)} %bitcast.12, f32[1,128]{1,0:T(1,128)} %bitcast.13, ...), custom_call_target="tpu_custom_call" | custom-call | bytes 1048576 | tf_op jit(solution)/shard_map/pallas_call | solution.py:243
  9.0 1.5 %collective-permute-start.5 = (f32[1,256]{1,0:T(1,128)S(1)}, f32[1,256]{1,0:T(1,128)S(1)}, u32[]{:S(2)}, u32[]{:S(2)}) collective-permute-start(f32[1,256]{1,0:T(1,128)S(1)} %get-tuple-element.14), channel_id=1, source_target_pairs={{0,8},{8,16},{16,24},{24,0},{1,9},{9,17},{17,25},{25,1},{2,10},{10... | collective-permute-start | bytes 3080 | tf_op jit(solution)/shard_map/ppermute | solution.py:304
  10.5 0.0 collective-permute-done.2.halo_ref
  10.5 0.7 %collective-permute-start.4 = (bf16[4,2,64,128]{3,2,1,0:T(8,128)(2,1)S(1)}, bf16[4,2,64,128]{3,2,1,0:T(8,128)(2,1)S(1)}, u32[]{:S(2)}, u32[]{:S(2)}) collective-permute-start(bf16[4,2,64,128]{3,2,1,0:T(8,128)(2,1)S(1)} %collective-permute-done.2.halo_ref), channel_id=1, source_target_pairs={{0,0},{1,2},{2,1},{3,4},{4,3},{5,6},{6,5},{7,7},{8,8},{9,10},{10,9... | collective-permute-start | bytes 393224 | tf_op jit(solution)/shard_map/ppermute | solution.py:277
  11.2 3.0 %collective-permute-start.3 = (bf16[4,2,64,128]{3,2,1,0:T(8,128)(2,1)S(1)}, bf16[4,2,64,128]{3,2,1,0:T(8,128)(2,1)S(1)}, u32[]{:S(2)}, u32[]{:S(2)}) collective-permute-start(bf16[4,2,64,128]{3,2,1,0:T(8,128)(2,1)S(1)} %collective-permute-done.2.halo_ref), channel_id=1, source_target_pairs={{0,1},{1,0},{2,3},{3,2},{4,5},{5,4},{6,7},{7,6},{8,9},{9,8},{10,11... | collective-permute-start | bytes 393224 | tf_op jit(solution)/shard_map/ppermute | solution.py:277
  14.2 0.0 collective-permute-done.5
  14.2 8.6 %all_to_all.10.stats_ref = f32[8,2,256]{2,1,0:T(2,128)S(1)} all-to-all(f32[8,2,256]{2,1,0:T(2,128)S(1)} %broadcast_in_dim.8), channel_id=1, replica_groups=mesh['section'=4,'rows'=8] {'rows'}, dimensions={0} | all-to-all | bytes 32768 | tf_op jit(solution)/shard_map/all_to_all | solution.py:306
  22.8 0.0 collective-permute-done.4.halo_far_ref
  22.8 0.0 collective-permute-done.3.halo_near_ref
  22.8 0.0 collective-permute-done.1.far_ref
  22.8 0.0 collective-permute-done.near_ref
  22.9 0.0 copy-start
  22.9 3.7 %shard_map.111 = (bf16[10,4,64,128]{3,2,1,0:T(8,128)(2,1)S(1)}, f32[32,1,256]{2,1,0:T(1,128)S(1)}) custom-call(bf16[8,2,64,128]{3,2,1,0:T(8,128)(2,1)S(1)} %get-tuple-element.12.own_ref, bf16[8,2,64,128]{3,2,1,0:T(8,128)(2,1)S(1)} %collective-permute-done.near_ref, bf16[8,2,64,128]{3,2,1,0:T(8,128)(2,1)S(1)} %collective-permute-done.1.far_ref, ...), custom_call_target="tpu_custom_call" | custom-call | flops 1000000000 | bytes 1048576 | tf_op jit(solution)/shard_map/pallas_call | solution.py:243
  26.6 9.0 %all_to_all.11.stats_ref = f32[32,1,256]{2,1,0:T(1,128)S(1)} all-to-all(f32[32,1,256]{2,1,0:T(1,128)S(1)} %get-tuple-element.18), channel_id=1, replica_groups=mesh['section'=4,'rows'=8] {'section','rows'}, dimensions={0} | all-to-all | bytes 65536 | tf_op jit(solution)/shard_map/all_to_all | solution.py:317
  35.6 0.0 copy-done
  35.6 2.6 %shard_map.112 = bf16[8,2,64,128]{3,2,1,0:T(8,128)(2,1)} custom-call(bf16[10,4,64,128]{3,2,1,0:T(8,128)(2,1)S(1)} %get-tuple-element.17.middle_ref, f32[32,1,256]{2,1,0:T(1,128)S(1)} %all_to_all.11.stats_ref, f32[6,1,128]{2,1,0:T(1,128)S(1)} %get-tuple-element.15.vectors_ref, bf16[3,3,3,128,128]{4,3,2,1,0:T(8,128)(2,1)S(1)} %copy-done, ...), custom_call_target="tpu_custom_call" | custom-call | flops 1000000000 | bytes 1048576 | tf_op jit(solution)/shard_map/pallas_call | solution.py:243
  (2 shorter events, 0.0 us)
Async XLA Ops:
  1.1 9.4 %collective-permute-start.2 = (bf16[4,2,64,128]{3,2,1,0:T(8,128)(2,1)S(1)}, bf16[4,2,64,128]{3,2,1,0:T(8,128)(2,1)S(1)}, u32[]{:S(2)}, u32[]{:S(2)}) collective-permute-start(bf16[4,2,64,128]{3,2,1,0:T(8,128)(2,1)S(1)} %get-tuple-element.13), channel_id=1, source_target_pairs={{0,8},{8,16},{16,24},{24,0},{1,9},{9,17},{17,25},{25,1},{2,10},{10... | collective-permute-start | bytes 393224 | tf_op jit(solution)/shard_map/ppermute | solution.py:302
  4.1 18.8 %collective-permute-start.1 = (bf16[8,2,64,128]{3,2,1,0:T(8,128)(2,1)S(1)}, bf16[8,2,64,128]{3,2,1,0:T(8,128)(2,1)S(1)}, u32[]{:S(2)}, u32[]{:S(2)}) collective-permute-start(bf16[8,2,64,128]{3,2,1,0:T(8,128)(2,1)S(1)} %get-tuple-element.12.own_ref), channel_id=1, source_target_pairs={{0,0},{1,2},{2,1},{3,4},{4,3},{5,6},{6,5},{7,7},{8,8},{9,10},{10,9... | collective-permute-start | bytes 786440 | tf_op jit(solution)/shard_map/ppermute | solution.py:277
  4.7 18.1 %collective-permute-start = (bf16[8,2,64,128]{3,2,1,0:T(8,128)(2,1)S(1)}, bf16[8,2,64,128]{3,2,1,0:T(8,128)(2,1)S(1)}, u32[]{:S(2)}, u32[]{:S(2)}) collective-permute-start(bf16[8,2,64,128]{3,2,1,0:T(8,128)(2,1)S(1)} %get-tuple-element.12.own_ref), channel_id=1, source_target_pairs={{0,1},{1,0},{2,3},{3,2},{4,5},{5,4},{6,7},{7,6},{8,9},{9,8},{10,11... | collective-permute-start | bytes 786440 | tf_op jit(solution)/shard_map/ppermute | solution.py:277
  9.0 5.2 %collective-permute-start.5 = (f32[1,256]{1,0:T(1,128)S(1)}, f32[1,256]{1,0:T(1,128)S(1)}, u32[]{:S(2)}, u32[]{:S(2)}) collective-permute-start(f32[1,256]{1,0:T(1,128)S(1)} %get-tuple-element.14), channel_id=1, source_target_pairs={{0,8},{8,16},{16,24},{24,0},{1,9},{9,17},{17,25},{25,1},{2,10},{10... | collective-permute-start | bytes 3080 | tf_op jit(solution)/shard_map/ppermute | solution.py:304
  10.5 12.3 %collective-permute-start.4 = (bf16[4,2,64,128]{3,2,1,0:T(8,128)(2,1)S(1)}, bf16[4,2,64,128]{3,2,1,0:T(8,128)(2,1)S(1)}, u32[]{:S(2)}, u32[]{:S(2)}) collective-permute-start(bf16[4,2,64,128]{3,2,1,0:T(8,128)(2,1)S(1)} %collective-permute-done.2.halo_ref), channel_id=1, source_target_pairs={{0,0},{1,2},{2,1},{3,4},{4,3},{5,6},{6,5},{7,7},{8,8},{9,10},{10,9... | collective-permute-start | bytes 393224 | tf_op jit(solution)/shard_map/ppermute | solution.py:277
  11.2 11.6 %collective-permute-start.3 = (bf16[4,2,64,128]{3,2,1,0:T(8,128)(2,1)S(1)}, bf16[4,2,64,128]{3,2,1,0:T(8,128)(2,1)S(1)}, u32[]{:S(2)}, u32[]{:S(2)}) collective-permute-start(bf16[4,2,64,128]{3,2,1,0:T(8,128)(2,1)S(1)} %collective-permute-done.2.halo_ref), channel_id=1, source_target_pairs={{0,1},{1,0},{2,3},{3,2},{4,5},{5,4},{6,7},{7,6},{8,9},{9,8},{10,11... | collective-permute-start | bytes 393224 | tf_op jit(solution)/shard_map/ppermute | solution.py:277
  22.9 12.7 %copy-start = (bf16[3,3,3,128,128]{4,3,2,1,0:T(8,128)(2,1)S(1)}, bf16[3,3,3,128,128]{4,3,2,1,0:T(8,128)(2,1)}, u32[]{:S(2)}) copy-start(bf16[3,3,3,128,128]{4,3,2,1,0:T(8,128)(2,1)} %weight_ref.3) | copy-start | bytes 2654212

commit v9 on v8

--- a/solution.py
+++ b/solution.py
@@ -148,11 +148,12 @@
 
 
 def first_kernel(
-    row_count, own_ref, near_ref, far_ref, halo_ref, halo_near_ref, halo_far_ref,
-    stats_ref, vectors_ref, weight_ref, middle_ref, sums_ref, field
+    row_count, own_ref, near_ref, far_ref, stats_ref, vectors_ref, weight_ref, middle_ref,
+    sums_ref, field
 ):
     section, row_at = lax.axis_index("section"), lax.axis_index("rows")
-    inner, lines, columns, channels = own_ref.shape
+    frames, lines, columns, channels = own_ref.shape
+    inner = frames - SPAN_HALO
     cells = inner * lines * columns
     scale, shift = vectors_ref[0], vectors_ref[1]
     mine, before = stats_ref[:, 0], stats_ref[:, 1]
@@ -164,11 +165,11 @@
     def fill(line):
         side, local = divmod(line, lines)
         if side == 1:
-            halo, body = halo_ref[:, local], own_ref[:, local]
+            block = own_ref[:, local]
         else:
             near_side = even if side == 2 else jnp.logical_not(even)
-            halo = jnp.where(near_side, halo_near_ref[:, local], halo_far_ref[:, local])
-            body = jnp.where(near_side, near_ref[:, local], far_ref[:, local])
+            block = jnp.where(near_side, near_ref[:, local], far_ref[:, local])
+        halo, body = block[:SPAN_HALO], block[SPAN_HALO:]
         behind = activate(halo, slope_before, offset_before).astype(jnp.bfloat16)
         behind = jnp.where(at_start, halo, behind)
         ahead = activate(body, slope, offset).astype(jnp.bfloat16)
@@ -298,9 +299,7 @@
         (own, conv1_weight) + tuple(vector.reshape(1, channels) for vector in vectors),
         in_place=range(1, 2 + len(vectors)),
     )
-    beside = [across(own, near), across(own, far)]
-    behind = [lax.ppermute(halo, "section", ring)]
-    behind += [across(behind[0], near), across(behind[0], far)]
+    joined = jnp.concatenate([lax.ppermute(halo, "section", ring), own], axis=0)
     both = jnp.stack([sums, lax.ppermute(sums, "section", ring)], axis=1)
     both = jnp.broadcast_to(both, (row_count,) + both.shape[1:])
     stats = lax.all_to_all(both, "rows", 0, 0, tiled=True)
@@ -311,7 +310,7 @@
             stats_shape,
         ),
         [pltpu.VMEM((frames + SPAN_HALO, 3 * lines, columns, channels), jnp.bfloat16)],
-        (own, *beside, *behind, stats, packed, weight),
+        (joined, across(joined, near), across(joined, far), stats, packed, weight),
         flops=10**9,
     )
     stats_two = lax.all_to_all(sums_two, ("section", "rows"), 0, 0, tiled=True)

time: 38.4 us -> 43.1 us (1.12)
  waiting for transfers between devices: 0.02 us -> 8.33 us
  starting transfers between devices: 11.8 us -> 7.5 us
  blocking collectives: 17.6 us -> 18.3 us
    ppermute x1, waiting for transfers between devices: 0.01 us -> 4.45 us  [on_device(): joined = jnp.concatenate([lax.ppermute(halo, 'section', ring), own], axis=0)]
    ppermute x1, waiting for transfers between devices: 0.01 us -> 3.88 us  [on_device(): both = jnp.stack([sums, lax.ppermute(sums, 'section', ring)], axis=1)]
    ppermute x4 -> x2, starting transfers between devices: 7.31 us -> 3.86 us  [across(): return lax.ppermute(block, 'rows', list(enumerate(partner)))]
    ppermute x1, starting transfers between devices: 1.54 us -> 0.64 us  [on_device(): both = jnp.stack([sums, lax.ppermute(sums, 'section', ring)], axis=1)]
    all_to_all x1, blocking collectives: 8.62 us -> 9.32 us  [on_device(): stats = lax.all_to_all(both, 'rows', 0, 0, tiled=True)]
  transfers between devices with their start and end apart: 6 -> 4, of which waited for: 0 -> 2; matrix products, arithmetic and copies ran while one was open for 0% -> 0% of each run, Pallas kernels for 3% -> 3%
where the time goes in v9:
time: 43.1 us; the launch traced here: 42.9 us
  blocking collectives  18.3 us (42%)
  Pallas kernels  8.62 us (20%)
  waiting for transfers between devices  8.33 us (19%)
  starting transfers between devices  7.5 us (17%)
    all_to_all x1, blocking collectives, on_device(): stats = lax.all_to_all(both, 'rows', 0, 0, tiled=True)  9.32 us
    all_to_all x1, blocking collectives, on_device(): stats_two = lax.all_to_all(sums_two, ('section', 'rows'), 0, 0, tiled=True)  8.98 us
    pallas_call x4, Pallas kernels, call(): pl.pallas_call(kernel, out_shape=out_shape, in_specs=specs, out_specs=jax...  8.62 us
    ppermute x1, waiting for transfers between devices, on_device(): joined = jnp.concatenate([lax.ppermute(halo, 'section', ring), own], axis=0)  4.45 us
    ppermute x1, waiting for transfers between devices, on_device(): both = jnp.stack([sums, lax.ppermute(sums, 'section', ring)], axis=1)  3.88 us
    ppermute x2, starting transfers between devices, across(): return lax.ppermute(block, 'rows', list(enumerate(partner)))  3.86 us
    ppermute x1, starting transfers between devices, on_device(): joined = jnp.concatenate([lax.ppermute(halo, 'section', ring), own], axis=0)  2.99 us
  transfers between devices with their start and end apart: 4, of which 2 were waited for; matrix products, arithmetic and copies ran while one was open for 0% of the time, Pallas kernels for 3%

profile of v9, /device:TPU:0, one launch (start us, length us, event | category | flops | bytes accessed | tf_op | source)
XLA Modules:
  0.0 42.9 jit_solution(8790546429942528196)
XLA Ops:
  0.0 1.1 %shard_map.109 = (bf16[8,2,64,128]{3,2,1,0:T(8,128)(2,1)S(1)}, bf16[4,2,64,128]{3,2,1,0:T(8,128)(2,1)S(1)}) custom-call(bf16[8,2,64,128]{3,2,1,0:T(8,128)(2,1)} %own_ref.1, bf16[2,2,64,128]{3,2,1,0:T(8,128)(2,1)} %second_cache_ref.1, bf16[2,2,64,128]{3,2,1,0:T(8,128)(2,1)} %first_cache_ref.1), custom_call_target="tpu_custom_call" | custom-call | bytes 1048576 | tf_op jit(solution)/shard_map/pallas_call | solution.py:244
  1.1 3.0 %collective-permute-start = (bf16[4,2,64,128]{3,2,1,0:T(8,128)(2,1)S(1)}, bf16[4,2,64,128]{3,2,1,0:T(8,128)(2,1)S(1)}, u32[]{:S(2)}, u32[]{:S(2)}) collective-permute-start(bf16[4,2,64,128]{3,2,1,0:T(8,128)(2,1)S(1)} %get-tuple-element.12), channel_id=1, source_target_pairs={{0,8},{8,16},{16,24},{24,0},{1,9},{9,17},{17,25},{25,1},{2,10},{10... | collective-permute-start | bytes 393224 | tf_op jit(solution)/shard_map/ppermute | solution.py:302
  4.1 4.4 %collective-permute-done = bf16[4,2,64,128]{3,2,1,0:T(8,128)(2,1)S(1)} collective-permute-done((bf16[4,2,64,128]{3,2,1,0:T(8,128)(2,1)S(1)}, bf16[4,2,64,128]{3,2,1,0:T(8,128)(2,1)S(1)}, u32[]{:S(2)}, u32[]{:S(2)}) %collective-permute-start) | collective-permute-done | bytes 131104 | tf_op jit(solution)/shard_map/ppermute | solution.py:302
  8.6 0.7 %collective-permute-start.2 = (bf16[12,2,64,128]{3,2,1,0:T(8,128)(2,1)S(1)}, bf16[12,2,64,128]{3,2,1,0:T(8,128)(2,1)S(1)}, u32[]{:S(2)}, u32[]{:S(2)}) collective-permute-start(bf16[12,2,64,128]{3,2,1,0:T(8,128)(2,1)S(1)} %constant_dynamic-update-slice_fusion.own_ref), channel_id=1, source_target_pairs={{0,0},{1,2},{2,1},{3,4},{4,3},{5,6},{6,5},{7,7},{8,8},{9,10},{10,9... | collective-permute-start | bytes 1179656 | tf_op jit(solution)/shard_map/ppermute | solution.py:278
  9.3 3.2 %collective-permute-start.1 = (bf16[12,2,64,128]{3,2,1,0:T(8,128)(2,1)S(1)}, bf16[12,2,64,128]{3,2,1,0:T(8,128)(2,1)S(1)}, u32[]{:S(2)}, u32[]{:S(2)}) collective-permute-start(bf16[12,2,64,128]{3,2,1,0:T(8,128)(2,1)S(1)} %constant_dynamic-update-slice_fusion.own_ref), channel_id=1, source_target_pairs={{0,1},{1,0},{2,3},{3,2},{4,5},{5,4},{6,7},{7,6},{8,9},{9,8},{10,11... | collective-permute-start | bytes 1179656 | tf_op jit(solution)/shard_map/ppermute | solution.py:278
  12.4 1.2 %shard_map.110 = (f32[1,256]{1,0:T(1,128)S(1)}, f32[6,1,128]{2,1,0:T(1,128)S(1)}, bf16[3,3,3,128,128]{4,3,2,1,0:T(8,128)(2,1)S(1)}) custom-call(bf16[8,2,64,128]{3,2,1,0:T(8,128)(2,1)S(1)} %get-tuple-element.13.own_ref, bf16[3,3,3,128,128]{4,3,2,1,0:T(8,128)(2,1)} %weight_ref.2, f32[1,128]{1,0:T(1,128)} %bitcast.12, f32[1,128]{1,0:T(1,128)} %bitcast.13, ...), custom_call_target="tpu_custom_call" | custom-call | bytes 1048576 | tf_op jit(solution)/shard_map/pallas_call | solution.py:244
  13.7 0.6 %collective-permute-start.3 = (f32[1,256]{1,0:T(1,128)S(1)}, f32[1,256]{1,0:T(1,128)S(1)}, u32[]{:S(2)}, u32[]{:S(2)}) collective-permute-start(f32[1,256]{1,0:T(1,128)S(1)} %get-tuple-element.14), channel_id=1, source_target_pairs={{0,8},{8,16},{16,24},{24,0},{1,9},{9,17},{17,25},{25,1},{2,10},{10... | collective-permute-start | bytes 3080 | tf_op jit(solution)/shard_map/ppermute | solution.py:303
  14.3 3.9 %collective-permute-done.3 = f32[1,256]{1,0:T(1,128)S(1)} collective-permute-done((f32[1,256]{1,0:T(1,128)S(1)}, f32[1,256]{1,0:T(1,128)S(1)}, u32[]{:S(2)}, u32[]{:S(2)}) %collective-permute-start.3) | collective-permute-done | bytes 1056 | tf_op jit(solution)/shard_map/ppermute | solution.py:303
  18.2 9.3 %all_to_all.10.stats_ref = f32[8,2,256]{2,1,0:T(2,128)S(1)} all-to-all(f32[8,2,256]{2,1,0:T(2,128)S(1)} %broadcast_in_dim.8), channel_id=1, replica_groups=mesh['section'=4,'rows'=8] {'rows'}, dimensions={0} | all-to-all | bytes 32768 | tf_op jit(solution)/shard_map/all_to_all | solution.py:305
  27.5 0.0 collective-permute-done.2.far_ref
  27.5 0.0 collective-permute-done.1.near_ref
  27.6 0.0 copy-start
  27.6 3.7 %shard_map.111 = (bf16[10,4,64,128]{3,2,1,0:T(8,128)(2,1)S(1)}, f32[32,1,256]{2,1,0:T(1,128)S(1)}) custom-call(bf16[12,2,64,128]{3,2,1,0:T(8,128)(2,1)S(1)} %constant_dynamic-update-slice_fusion.own_ref, bf16[12,2,64,128]{3,2,1,0:T(8,128)(2,1)S(1)} %collective-permute-done.1.near_ref, bf16[12,2,64,128]{3,2,1,0:T(8,128)(2,1)S(1)} %collective-permute-done.2.far_ref, ...), custom_call_target="tpu_custom_call" | custom-call | flops 1000000000 | bytes 1048576 | tf_op jit(solution)/shard_map/pallas_call | solution.py:244
  31.3 9.0 %all_to_all.11.stats_ref = f32[32,1,256]{2,1,0:T(1,128)S(1)} all-to-all(f32[32,1,256]{2,1,0:T(1,128)S(1)} %get-tuple-element.18), channel_id=1, replica_groups=mesh['section'=4,'rows'=8] {'section','rows'}, dimensions={0} | all-to-all | bytes 65536 | tf_op jit(solution)/shard_map/all_to_all | solution.py:316
  40.3 0.0 copy-done
  40.3 2.6 %shard_map.112 = bf16[8,2,64,128]{3,2,1,0:T(8,128)(2,1)} custom-call(bf16[10,4,64,128]{3,2,1,0:T(8,128)(2,1)S(1)} %get-tuple-element.17.middle_ref, f32[32,1,256]{2,1,0:T(1,128)S(1)} %all_to_all.11.stats_ref, f32[6,1,128]{2,1,0:T(1,128)S(1)} %get-tuple-element.15.vectors_ref, bf16[3,3,3,128,128]{4,3,2,1,0:T(8,128)(2,1)S(1)} %copy-done, ...), custom_call_target="tpu_custom_call" | custom-call | flops 1000000000 | bytes 1048576 | tf_op jit(solution)/shard_map/pallas_call | solution.py:244
  (4 shorter events, 0.1 us)
Async XLA Ops:
  1.1 7.4 %collective-permute-start = (bf16[4,2,64,128]{3,2,1,0:T(8,128)(2,1)S(1)}, bf16[4,2,64,128]{3,2,1,0:T(8,128)(2,1)S(1)}, u32[]{:S(2)}, u32[]{:S(2)}) collective-permute-start(bf16[4,2,64,128]{3,2,1,0:T(8,128)(2,1)S(1)} %get-tuple-element.12), channel_id=1, source_target_pairs={{0,8},{8,16},{16,24},{24,0},{1,9},{9,17},{17,25},{25,1},{2,10},{10... | collective-permute-start | bytes 393224 | tf_op jit(solution)/shard_map/ppermute | solution.py:302
  8.6 19.0 %collective-permute-start.2 = (bf16[12,2,64,128]{3,2,1,0:T(8,128)(2,1)S(1)}, bf16[12,2,64,128]{3,2,1,0:T(8,128)(2,1)S(1)}, u32[]{:S(2)}, u32[]{:S(2)}) collective-permute-start(bf16[12,2,64,128]{3,2,1,0:T(8,128)(2,1)S(1)} %constant_dynamic-update-slice_fusion.own_ref), channel_id=1, source_target_pairs={{0,0},{1,2},{2,1},{3,4},{4,3},{5,6},{6,5},{7,7},{8,8},{9,10},{10,9... | collective-permute-start | bytes 1179656 | tf_op jit(solution)/shard_map/ppermute | solution.py:278
  9.3 18.3 %collective-permute-start.1 = (bf16[12,2,64,128]{3,2,1,0:T(8,128)(2,1)S(1)}, bf16[12,2,64,128]{3,2,1,0:T(8,128)(2,1)S(1)}, u32[]{:S(2)}, u32[]{:S(2)}) collective-permute-start(bf16[12,2,64,128]{3,2,1,0:T(8,128)(2,1)S(1)} %constant_dynamic-update-slice_fusion.own_ref), channel_id=1, source_target_pairs={{0,1},{1,0},{2,3},{3,2},{4,5},{5,4},{6,7},{7,6},{8,9},{9,8},{10,11... | collective-permute-start | bytes 1179656 | tf_op jit(solution)/shard_map/ppermute | solution.py:278
  13.7 4.5 %collective-permute-start.3 = (f32[1,256]{1,0:T(1,128)S(1)}, f32[1,256]{1,0:T(1,128)S(1)}, u32[]{:S(2)}, u32[]{:S(2)}) collective-permute-start(f32[1,256]{1,0:T(1,128)S(1)} %get-tuple-element.14), channel_id=1, source_target_pairs={{0,8},{8,16},{16,24},{24,0},{1,9},{9,17},{17,25},{25,1},{2,10},{10... | collective-permute-start | bytes 3080 | tf_op jit(solution)/shard_map/ppermute | solution.py:303
  27.6 12.7 %copy-start = (bf16[3,3,3,128,128]{4,3,2,1,0:T(8,128)(2,1)S(1)}, bf16[3,3,3,128,128]{4,3,2,1,0:T(8,128)(2,1)}, u32[]{:S(2)}) copy-start(bf16[3,3,3,128,128]{4,3,2,1,0:T(8,128)(2,1)} %weight_ref.3) | copy-start | bytes 2654212

commit v10 on v9

--- a/solution.py
+++ b/solution.py
@@ -299,8 +299,11 @@
         (own, conv1_weight) + tuple(vector.reshape(1, channels) for vector in vectors),
         in_place=range(1, 2 + len(vectors)),
     )
-    joined = jnp.concatenate([lax.ppermute(halo, "section", ring), own], axis=0)
-    both = jnp.stack([sums, lax.ppermute(sums, "section", ring)], axis=1)
+    received = lax.ppermute(halo, "section", ring)
+    passed = lax.ppermute(sums, "section", ring)
+    received, sums, passed = lax.optimization_barrier((received, sums, passed))
+    joined = jnp.concatenate([received, own], axis=0)
+    both = jnp.stack([sums, passed], axis=1)
     both = jnp.broadcast_to(both, (row_count,) + both.shape[1:])
     stats = lax.all_to_all(both, "rows", 0, 0, tiled=True)
     middle, sums_two = call(

time: 43.1 us -> 38.4 us (0.89)
  waiting for transfers between devices: 8.33 us -> 2.98 us
  starting transfers between devices: 7.5 us -> 8.2 us
    ppermute x2, waiting for transfers between devices: 8.32 us -> 2.98 us  [the longest x1 2.98 us: on_device(): passed = lax.ppermute(sums, 'section', ring)]
    ppermute x2, starting transfers between devices: 3.63 us -> 4.53 us  [the longest x1 2.99 us: on_device(): received = lax.ppermute(halo, 'section', ring)]
  transfers between devices with their start and end apart: 4 -> 4, of which waited for: 2 -> 1; matrix products, arithmetic and copies ran while one was open for 0% -> 0% of each run, Pallas kernels for 3% -> 3%
where the time goes in v10:
time: 38.4 us; the launch traced here: 38.2 us
  blocking collectives  18.3 us (48%)
  Pallas kernels  8.62 us (22%)
  starting transfers between devices  8.2 us (21%)
  waiting for transfers between devices  2.98 us (8%)
    all_to_all x1, blocking collectives, on_device(): stats = lax.all_to_all(both, 'rows', 0, 0, tiled=True)  9.32 us
    all_to_all x1, blocking collectives, on_device(): stats_two = lax.all_to_all(sums_two, ('section', 'rows'), 0, 0, tiled=True)  8.97 us
    pallas_call x4, Pallas kernels, call(): pl.pallas_call(kernel, out_shape=out_shape, in_specs=specs, out_specs=jax...  8.62 us
    ppermute x2, starting transfers between devices, across(): return lax.ppermute(block, 'rows', list(enumerate(partner)))  3.67 us
    ppermute x1, starting transfers between devices, on_device(): received = lax.ppermute(halo, 'section', ring)  2.99 us
    ppermute x1, waiting for transfers between devices, on_device(): passed = lax.ppermute(sums, 'section', ring)  2.98 us
    ppermute x1, starting transfers between devices, on_device(): passed = lax.ppermute(sums, 'section', ring)  1.54 us
  transfers between devices with their start and end apart: 4, of which 1 were waited for; matrix products, arithmetic and copies ran while one was open for 0% of the time, Pallas kernels for 3%

profile of v10, /device:TPU:0, one launch (start us, length us, event | category | flops | bytes accessed | tf_op | source)
XLA Modules:
  0.0 38.2 jit_solution(16136894522173811554)
XLA Ops:
  0.0 1.1 %shard_map.109 = (bf16[8,2,64,128]{3,2,1,0:T(8,128)(2,1)S(1)}, bf16[4,2,64,128]{3,2,1,0:T(8,128)(2,1)S(1)}) custom-call(bf16[8,2,64,128]{3,2,1,0:T(8,128)(2,1)} %own_ref.1, bf16[2,2,64,128]{3,2,1,0:T(8,128)(2,1)} %second_cache_ref.1, bf16[2,2,64,128]{3,2,1,0:T(8,128)(2,1)} %first_cache_ref.1), custom_call_target="tpu_custom_call" | custom-call | bytes 1048576 | tf_op jit(solution)/shard_map/pallas_call | solution.py:244
  1.1 3.0 %collective-permute-start = (bf16[4,2,64,128]{3,2,1,0:T(8,128)(2,1)S(1)}, bf16[4,2,64,128]{3,2,1,0:T(8,128)(2,1)S(1)}, u32[]{:S(2)}, u32[]{:S(2)}) collective-permute-start(bf16[4,2,64,128]{3,2,1,0:T(8,128)(2,1)S(1)} %get-tuple-element.15), channel_id=1, source_target_pairs={{0,8},{8,16},{16,24},{24,0},{1,9},{9,17},{17,25},{25,1},{2,10},{10... | collective-permute-start | bytes 393224 | tf_op jit(solution)/shard_map/ppermute | solution.py:302
  4.1 1.2 %shard_map.110 = (f32[1,256]{1,0:T(1,128)S(1)}, f32[6,1,128]{2,1,0:T(1,128)S(1)}, bf16[3,3,3,128,128]{4,3,2,1,0:T(8,128)(2,1)S(1)}) custom-call(bf16[8,2,64,128]{3,2,1,0:T(8,128)(2,1)S(1)} %get-tuple-element.16.own_ref, bf16[3,3,3,128,128]{4,3,2,1,0:T(8,128)(2,1)} %weight_ref.2, f32[1,128]{1,0:T(1,128)} %bitcast.12, f32[1,128]{1,0:T(1,128)} %bitcast.13, ...), custom_call_target="tpu_custom_call" | custom-call | bytes 1048576 | tf_op jit(solution)/shard_map/pallas_call | solution.py:244
  5.3 1.5 %collective-permute-start.1 = (f32[1,256]{1,0:T(1,128)S(1)}, f32[1,256]{1,0:T(1,128)S(1)}, u32[]{:S(2)}, u32[]{:S(2)}) collective-permute-start(f32[1,256]{1,0:T(1,128)S(1)} %get-tuple-element.19), channel_id=1, source_target_pairs={{0,8},{8,16},{16,24},{24,0},{1,9},{9,17},{17,25},{25,1},{2,10},{10... | collective-permute-start | bytes 3080 | tf_op jit(solution)/shard_map/ppermute | solution.py:303
  6.9 3.0 %collective-permute-done.1 = f32[1,256]{1,0:T(1,128)S(1)} collective-permute-done((f32[1,256]{1,0:T(1,128)S(1)}, f32[1,256]{1,0:T(1,128)S(1)}, u32[]{:S(2)}, u32[]{:S(2)}) %collective-permute-start.1) | collective-permute-done | bytes 1056 | tf_op jit(solution)/shard_map/ppermute | solution.py:303
  9.8 0.0 collective-permute-done
  9.9 0.7 %collective-permute-start.3 = (bf16[12,2,64,128]{3,2,1,0:T(8,128)(2,1)S(1)}, bf16[12,2,64,128]{3,2,1,0:T(8,128)(2,1)S(1)}, u32[]{:S(2)}, u32[]{:S(2)}) collective-permute-start(bf16[12,2,64,128]{3,2,1,0:T(8,128)(2,1)S(1)} %constant_dynamic-update-slice_fusion.own_ref), channel_id=1, source_target_pairs={{0,0},{1,2},{2,1},{3,4},{4,3},{5,6},{6,5},{7,7},{8,8},{9,10},{10,9... | collective-permute-start | bytes 1179656 | tf_op jit(solution)/shard_map/ppermute | solution.py:278
  10.6 3.0 %collective-permute-start.2 = (bf16[12,2,64,128]{3,2,1,0:T(8,128)(2,1)S(1)}, bf16[12,2,64,128]{3,2,1,0:T(8,128)(2,1)S(1)}, u32[]{:S(2)}, u32[]{:S(2)}) collective-permute-start(bf16[12,2,64,128]{3,2,1,0:T(8,128)(2,1)S(1)} %constant_dynamic-update-slice_fusion.own_ref), channel_id=1, source_target_pairs={{0,1},{1,0},{2,3},{3,2},{4,5},{5,4},{6,7},{7,6},{8,9},{9,8},{10,11... | collective-permute-start | bytes 1179656 | tf_op jit(solution)/shard_map/ppermute | solution.py:278
  13.6 9.3 %all_to_all.10.stats_ref = f32[8,2,256]{2,1,0:T(2,128)S(1)} all-to-all(f32[8,2,256]{2,1,0:T(2,128)S(1)} %broadcast_in_dim.8), channel_id=1, replica_groups=mesh['section'=4,'rows'=8] {'rows'}, dimensions={0} | all-to-all | bytes 32768 | tf_op jit(solution)/shard_map/all_to_all | solution.py:308
  22.9 0.0 collective-permute-done.3.far_ref
  22.9 0.0 collective-permute-done.2.near_ref
  22.9 0.0 copy-start
  22.9 3.7 %shard_map.111 = (bf16[10,4,64,128]{3,2,1,0:T(8,128)(2,1)S(1)}, f32[32,1,256]{2,1,0:T(1,128)S(1)}) custom-call(bf16[12,2,64,128]{3,2,1,0:T(8,128)(2,1)S(1)} %constant_dynamic-update-slice_fusion.own_ref, bf16[12,2,64,128]{3,2,1,0:T(8,128)(2,1)S(1)} %collective-permute-done.2.near_ref, bf16[12,2,64,128]{3,2,1,0:T(8,128)(2,1)S(1)} %collective-permute-done.3.far_ref, ...), custom_call_target="tpu_custom_call" | custom-call | flops 1000000000 | bytes 1048576 | tf_op jit(solution)/shard_map/pallas_call | solution.py:244
  26.6 9.0 %all_to_all.11.stats_ref = f32[32,1,256]{2,1,0:T(1,128)S(1)} all-to-all(f32[32,1,256]{2,1,0:T(1,128)S(1)} %get-tuple-element.24), channel_id=1, replica_groups=mesh['section'=4,'rows'=8] {'section','rows'}, dimensions={0} | all-to-all | bytes 65536 | tf_op jit(solution)/shard_map/all_to_all | solution.py:319
  35.6 0.0 copy-done
  35.6 2.6 %shard_map.112 = bf16[8,2,64,128]{3,2,1,0:T(8,128)(2,1)} custom-call(bf16[10,4,64,128]{3,2,1,0:T(8,128)(2,1)S(1)} %get-tuple-element.23.middle_ref, f32[32,1,256]{2,1,0:T(1,128)S(1)} %all_to_all.11.stats_ref, f32[6,1,128]{2,1,0:T(1,128)S(1)} %get-tuple-element.21.vectors_ref, bf16[3,3,3,128,128]{4,3,2,1,0:T(8,128)(2,1)S(1)} %copy-done, ...), custom_call_target="tpu_custom_call" | custom-call | flops 1000000000 | bytes 1048576 | tf_op jit(solution)/shard_map/pallas_call | solution.py:244
  (4 shorter events, 0.1 us)
Async XLA Ops:
  1.1 8.8 %collective-permute-start = (bf16[4,2,64,128]{3,2,1,0:T(8,128)(2,1)S(1)}, bf16[4,2,64,128]{3,2,1,0:T(8,128)(2,1)S(1)}, u32[]{:S(2)}, u32[]{:S(2)}) collective-permute-start(bf16[4,2,64,128]{3,2,1,0:T(8,128)(2,1)S(1)} %get-tuple-element.15), channel_id=1, source_target_pairs={{0,8},{8,16},{16,24},{24,0},{1,9},{9,17},{17,25},{25,1},{2,10},{10... | collective-permute-start | bytes 393224 | tf_op jit(solution)/shard_map/ppermute | solution.py:302
  5.3 4.5 %collective-permute-start.1 = (f32[1,256]{1,0:T(1,128)S(1)}, f32[1,256]{1,0:T(1,128)S(1)}, u32[]{:S(2)}, u32[]{:S(2)}) collective-permute-start(f32[1,256]{1,0:T(1,128)S(1)} %get-tuple-element.19), channel_id=1, source_target_pairs={{0,8},{8,16},{16,24},{24,0},{1,9},{9,17},{17,25},{25,1},{2,10},{10... | collective-permute-start | bytes 3080 | tf_op jit(solution)/shard_map/ppermute | solution.py:303
  9.9 13.0 %collective-permute-start.3 = (bf16[12,2,64,128]{3,2,1,0:T(8,128)(2,1)S(1)}, bf16[12,2,64,128]{3,2,1,0:T(8,128)(2,1)S(1)}, u32[]{:S(2)}, u32[]{:S(2)}) collective-permute-start(bf16[12,2,64,128]{3,2,1,0:T(8,128)(2,1)S(1)} %constant_dynamic-update-slice_fusion.own_ref), channel_id=1, source_target_pairs={{0,0},{1,2},{2,1},{3,4},{4,3},{5,6},{6,5},{7,7},{8,8},{9,10},{10,9... | collective-permute-start | bytes 1179656 | tf_op jit(solution)/shard_map/ppermute | solution.py:278
  10.6 12.3 %collective-permute-start.2 = (bf16[12,2,64,128]{3,2,1,0:T(8,128)(2,1)S(1)}, bf16[12,2,64,128]{3,2,1,0:T(8,128)(2,1)S(1)}, u32[]{:S(2)}, u32[]{:S(2)}) collective-permute-start(bf16[12,2,64,128]{3,2,1,0:T(8,128)(2,1)S(1)} %constant_dynamic-update-slice_fusion.own_ref), channel_id=1, source_target_pairs={{0,1},{1,0},{2,3},{3,2},{4,5},{5,4},{6,7},{7,6},{8,9},{9,8},{10,11... | collective-permute-start | bytes 1179656 | tf_op jit(solution)/shard_map/ppermute | solution.py:278
  22.9 12.7 %copy-start = (bf16[3,3,3,128,128]{4,3,2,1,0:T(8,128)(2,1)S(1)}, bf16[3,3,3,128,128]{4,3,2,1,0:T(8,128)(2,1)}, u32[]{:S(2)}) copy-start(bf16[3,3,3,128,128]{4,3,2,1,0:T(8,128)(2,1)} %weight_ref.3) | copy-start | bytes 2654212

commit v11 on v9

v11 whole, which is shorter than its diff:
```python
import functools

import functools

import jax
import jax.numpy as jnp
from jax import lax
from jax.experimental import pallas as pl
from jax.experimental.pallas import tpu as pltpu
from jax.sharding import PartitionSpec as P

GROUPS = 32
REACH = 2

epsilon = 1e-06


def moments(blocks):
    pivot = blocks[0][:1]
    cells = sum(block.shape[0] for block in blocks)
    total, squares = 0.0, 0.0
    for block in blocks:
        away = block - pivot
        total = total + jnp.sum(away, axis=0, keepdims=True)
        squares = squares + jnp.sum(away * away, axis=0, keepdims=True)
    shift = total * (1.0 / cells)
    return jnp.concatenate([pivot + shift, squares - total * shift], axis=1)


def affine(stats, cells, scale, shift):
    devices, channels = stats.shape[0], scale.shape[-1]
    means, squares = stats[:, :channels], stats[:, channels:]
    mean = jnp.sum(means, axis=0, keepdims=True) * (1.0 / devices)
    away = means - mean
    square = jnp.sum(squares + cells * (away * away), axis=0, keepdims=True)
    count = cells * devices
    lane = lax.broadcasted_iota(jnp.int32, mean.shape, 1)
    step = 1
    while step < channels // GROUPS:

        def partner(values):
            up = pltpu.roll(values, channels - step, 1)
            return jnp.where((lane // step) % 2 == 0, up, pltpu.roll(values, step, 1))

        away = partner(mean) - mean
        square = square + partner(square) + (0.5 * count) * (away * away)
        mean = mean + 0.5 * away
        count, step = 2 * count, 2 * step
    slope = 0.5 * scale * lax.rsqrt(square * (1.0 / count) + epsilon)
    return slope, 0.5 * shift - mean * slope


def activate(values, slope, offset):
    half = values.astype(jnp.float32) * slope + offset
    return half + half * jnp.tanh(half)


def pair_conv(field, row, frames, weight_ref):
    columns, channels = field.shape[2], field.shape[3]
    pieces, blocks = [], []
    nothing = jnp.zeros((channels, channels), jnp.bfloat16)
    for frame_tap in range(3):
        for line in range(4):
            piece = field[frame_tap : frame_tap + frames, row + line]
            pieces.append(piece.reshape(frames * columns, channels))
            blocks.append(
                jnp.concatenate(
                    [
                        weight_ref[frame_tap, line - out, col_tap]
                        if 0 <= line - out <= 2
                        else nothing
                        for col_tap in range(3)
                        for out in range(2)
                    ],
                    axis=1,
                )
            )
    product = jnp.dot(
        jnp.concatenate(pieces, axis=1),
        jnp.concatenate(blocks, axis=0),
        preferred_element_type=jnp.float32,
    )
    cells = frames * columns
    column = lax.broadcasted_iota(jnp.int32, (cells, channels), 0) % columns
    results = []
    for out in range(2):
        left, centre, right = (
            product[:, (2 * tap + out) * channels : (2 * tap + out + 1) * channels]
            for tap in range(3)
        )
        left = jnp.where(column == 0, 0.0, pltpu.roll(left, 1, 0))
        right = jnp.where(column == columns - 1, 0.0, pltpu.roll(right, cells - 1, 0))
        results.append(left + centre + right)
    return results


def copy_kernel(own_ref, second_cache_ref, first_cache_ref, tail_ref, copied, caches_ref, sems):
    kept = tail_ref.shape[0]
    copies = [
        (own_ref.at[own_ref.shape[0] - kept :], tail_ref),
        (own_ref, copied),
        (second_cache_ref, caches_ref.at[0]),
        (first_cache_ref, caches_ref.at[1]),
    ]
    copies = [
        pltpu.make_async_copy(source, target, sems.at[index])
        for index, (source, target) in enumerate(copies)
    ]
    for copy in copies:
        copy.start()
    for copy in copies:
        copy.wait()


def stats_kernel(own_ref, weight_ref, *rest):
    *vector_refs, stats_ref, vectors_ref, weight_copy, sems = rest
    loads = [pltpu.make_async_copy(weight_ref, weight_copy, sems.at[0])]
    loads += [
        pltpu.make_async_copy(vector_ref, vectors_ref.at[index], sems.at[1 + index])
        for index, vector_ref in enumerate(vector_refs)
    ]
    for load in loads:
        load.start()
    channels = own_ref.shape[-1]
    blocks = [own_ref[frame].astype(jnp.float32) for frame in range(own_ref.shape[0])]
    stats_ref[...] = moments([block.reshape(-1, channels) for block in blocks])
    for load in loads:
        load.wait()


def span_moments(stats_ref, section, row_count):
    chips = row_count // 2
    own = stats_ref[pl.ds(section * chips, chips)]
    return own.reshape(row_count, own.shape[-1])


def first_kernel(
    row_count, own_ref, near_ref, far_ref, stats_ref, vectors_ref, weight_ref, middle_ref,
    tail_ref, cache_ref, sums_ref, field
):
    section, row_at = lax.axis_index("section"), lax.axis_index("rows")
    inner, columns = middle_ref.shape[0], middle_ref.shape[2]
    lines, channels = own_ref.shape[1], own_ref.shape[3]
    cells = inner * lines * columns
    scale, shift = vectors_ref[0], vectors_ref[1]
    mine = span_moments(stats_ref, section, row_count)
    before = span_moments(stats_ref, jnp.maximum(section - 1, 0), row_count)
    slope, offset = affine(mine, cells, scale, shift)
    slope_before, offset_before = affine(before, cells, scale, shift)
    even = row_at % 2 == 0
    at_start = section == 0

    def fill(line):
        side, local = divmod(line, lines)
        if side == 1:
            block = own_ref[:, local]
        else:
            near_side = even if side == 2 else jnp.logical_not(even)
            block = jnp.where(near_side, near_ref[:, local], far_ref[:, local])
        cache, halo, body = block[:REACH], block[REACH : 2 * REACH], block[2 * REACH :]
        behind = activate(halo, slope_before, offset_before).astype(jnp.bfloat16)
        behind = jnp.where(at_start, halo, behind)
        ahead = activate(body, slope, offset).astype(jnp.bfloat16)
        if side != 1:
            outside = row_at == 0 if side == 0 else row_at == row_count - 1
            behind = jnp.where(outside, jnp.zeros_like(behind), behind)
            ahead = jnp.where(outside, jnp.zeros_like(ahead), ahead)
        field[:REACH, line] = behind
        field[REACH:, line] = ahead
        if lines - 1 <= line <= 2 * lines:
            cache_ref[:, line - lines + 1] = cache

    bias = vectors_ref[2]
    kept = []
    ready = 0
    for pair in range((lines + 2) // 2):
        for line in range(ready, 2 * pair + 4):
            fill(line)
        ready = 2 * pair + 4
        results = pair_conv(field, 2 * pair, inner, weight_ref)
        for out in range(2):
            line = 2 * pair + out
            rounded = (results[out] + bias).astype(jnp.bfloat16)
            if 1 <= line <= lines:
                kept.append(rounded.astype(jnp.float32))
            rounded = rounded.reshape(inner, columns, channels)
            middle_ref[:, line] = rounded
            tail_ref[:, line] = rounded[inner - REACH :]
    sums_ref[...] = moments(kept)


def second_kernel(
    row_count, middle_ref, halo_ref, cache_ref, stats_ref, vectors_ref, weight_ref, own_ref,
    out_ref, field
):
    section, row_at = lax.axis_index("section"), lax.axis_index("rows")
    frames, lines, columns, channels = own_ref.shape
    cells = frames * lines * columns
    scale, shift = vectors_ref[3], vectors_ref[4]
    mine = span_moments(stats_ref, section, row_count)
    before = span_moments(stats_ref, jnp.maximum(section - 1, 0), row_count)
    slope, offset = affine(mine, cells, scale, shift)
    slope_before, offset_before = affine(before, cells, scale, shift)
    at_start = section == 0
    for line in range(lines + 2):
        behind = activate(halo_ref[:, line], slope_before, offset_before).astype(jnp.bfloat16)
        behind = jnp.where(at_start, cache_ref[:, line], behind)
        ahead = activate(middle_ref[:, line], slope, offset).astype(jnp.bfloat16)
        if line == 0 or line == lines + 1:
            outside = row_at == 0 if line == 0 else row_at == row_count - 1
            behind = jnp.where(outside, jnp.zeros_like(behind), behind)
            ahead = jnp.where(outside, jnp.zeros_like(ahead), ahead)
        field[:REACH, line] = behind
        field[REACH:, line] = ahead
    bias = vectors_ref[5]
    for pair in range(lines // 2):
        results = pair_conv(field, 2 * pair, frames, weight_ref)
        for out in range(2):
            line = 2 * pair + out
            result = (results[out] + bias).reshape(frames, columns, channels)
            out_ref[:, line] = (result + own_ref[:, line].astype(jnp.float32)).astype(jnp.bfloat16)


def call(kernel, out_shape, scratch, operands, in_place=(), flops=0):
    vmem = pl.BlockSpec(memory_space=pltpu.VMEM)
    specs = [vmem] * len(operands)
    for index in in_place:
        specs[index] = pl.BlockSpec(memory_space=pltpu.HBM)
    operands = [
        pltpu.with_memory_space_constraint(operand, pltpu.HBM) if index in in_place else operand
        for index, operand in enumerate(operands)
    ]
    return pl.pallas_call(
        kernel,
        out_shape=out_shape,
        in_specs=specs,
        out_specs=jax.tree.map(lambda _: vmem, out_shape),
        scratch_shapes=scratch,
        compiler_params=pltpu.CompilerParams(vmem_limit_bytes=40 * 2**20),
        cost_estimate=pl.CostEstimate(flops=flops, bytes_accessed=2**20, transcendentals=0),
    )(*operands)


def on_device(
    activations,
    first_cache,
    second_cache,
    norm1_scale,
    norm1_shift,
    conv1_weight,
    conv1_bias,
    norm2_scale,
    norm2_shift,
    conv2_weight,
    conv2_bias,
):
    frames, lines, columns, channels = activations.shape
    sections, row_count = lax.axis_size("section"), lax.axis_size("rows")
    chips = sections * row_count // 2
    near = [i ^ 1 for i in range(row_count)]
    far = [0] + [i + 1 if i % 2 else i - 1 for i in range(1, row_count - 1)] + [row_count - 1]
    ring = [(at, (at + 1) % sections) for at in range(sections)]
    vectors = (norm1_scale, norm1_shift, conv1_bias, norm2_scale, norm2_shift, conv2_bias)
    wide = (lines + 2, columns, channels)

    def across(block, partner):
        return lax.ppermute(block, "rows", list(enumerate(partner)))

    def with_near(sums):
        return jnp.stack([sums, across(sums, near)], axis=1)

    def exchange(pair):
        same_core = [list(range(core, 2 * chips, 2)) for core in range(2)]
        return lax.all_to_all(
            jnp.broadcast_to(pair, (chips,) + pair.shape[1:]), ("section", "rows"), 0, 0,
            tiled=True, axis_index_groups=same_core,
        )

    def shaped(*shape):
        return jax.ShapeDtypeStruct(shape, jnp.bfloat16)

    sums_shape = jax.ShapeDtypeStruct((1, 2 * channels), jnp.float32)
    tail, own, caches = call(
        copy_kernel,
        (
            shaped(REACH, lines, columns, channels),
            shaped(*activations.shape),
            shaped(2, REACH, lines, columns, channels),
        ),
        [pltpu.SemaphoreType.DMA((4,))],
        (activations, second_cache, first_cache),
        in_place=range(3),
    )
    received = lax.ppermute(tail, "section", ring)
    sums, packed, weight = call(
        stats_kernel,
        (
            sums_shape,
            jax.ShapeDtypeStruct((len(vectors), 1, channels), jnp.float32),
            shaped(*conv1_weight.shape),
        ),
        [pltpu.SemaphoreType.DMA((1 + len(vectors),))],
        (own, conv1_weight) + tuple(vector.reshape(1, channels) for vector in vectors),
        in_place=range(1, 2 + len(vectors)),
    )
    received, pair = lax.optimization_barrier((received, with_near(sums)))
    halo = jnp.where(lax.axis_index("section") == 0, caches[1], received)
    joined = jnp.concatenate([caches[0], halo, own], axis=0)
    middle, tail, cache, sums = call(
        functools.partial(first_kernel, row_count),
        (shaped(frames, *wide), shaped(REACH, *wide), shaped(REACH, *wide), sums_shape),
        [pltpu.VMEM((frames + REACH, 3 * lines, columns, channels), jnp.bfloat16)],
        (joined, across(joined, near), across(joined, far), exchange(pair), packed, weight),
        flops=10**9,
    )
    return call(
        functools.partial(second_kernel, row_count),
        shaped(*activations.shape),
        [pltpu.VMEM((frames + REACH, *wide), jnp.bfloat16)],
        (
            middle, lax.ppermute(tail, "section", ring), cache, exchange(with_near(sums)),
            packed, conv2_weight, own,
        ),
        flops=10**9,
    )


def solution(mesh):
    in_specs = (
        P("section", "rows", None, None),
        P(None, "rows", None, None),
        P(None, "rows", None, None),
        P(),
        P(),
        P(),
        P(),
        P(),
        P(),
        P(),
        P(),
    )
    out_specs = P("section", "rows", None, None)
    return jax.shard_map(
        on_device, mesh=mesh, in_specs=in_specs, out_specs=out_specs, check_vma=False
    )
```

time: 43.1 us -> 41 us (0.951)
  waiting for transfers between devices: 8.33 us -> 2.28 us
  blocking collectives: 18.3 us -> 22.7 us
  Pallas kernels: 8.62 us -> 7.66 us
  starting transfers between devices: 7.5 us -> 7.97 us
    ppermute x2, waiting for transfers between devices: 8.32 us -> 0.74 us  [the longest x1 0.74 us: on_device(): received = lax.ppermute(tail, 'section', ring)]
    all_to_all x2, blocking collectives: 18.3 us -> 22.7 us  [exchange(): lax.all_to_all(jnp.broadcast_to(pair, (chips,) + pair.shape[1:]), ('secti...]
    ppermute x2 -> x4, waiting for transfers between devices: 0.01 us -> 1.54 us  [across(): return lax.ppermute(block, 'rows', list(enumerate(partner)))]
    pallas_call x4, Pallas kernels: 8.62 us -> 7.66 us  [call(): pl.pallas_call(kernel, out_shape=out_shape, in_specs=specs, out_specs=jax...]
    ppermute x2 -> x4, starting transfers between devices: 3.86 us -> 4.28 us  [across(): return lax.ppermute(block, 'rows', list(enumerate(partner)))]
  transfers between devices with their start and end apart: 4 -> 6, of which waited for: 2 -> 3; matrix products, arithmetic and copies ran while one was open for 0% -> 0% of each run, Pallas kernels for 3% -> 3%
where the time goes in v11:
time: 41 us; the launch traced here: 40.8 us
  blocking collectives  22.7 us (55%)
  starting transfers between devices  7.97 us (19%)
  Pallas kernels  7.66 us (19%)
  waiting for transfers between devices  2.28 us (6%)
    all_to_all x2, blocking collectives, exchange(): lax.all_to_all(jnp.broadcast_to(pair, (chips,) + pair.shape[1:]), ('secti...  22.7 us
    pallas_call x4, Pallas kernels, call(): pl.pallas_call(kernel, out_shape=out_shape, in_specs=specs, out_specs=jax...  7.66 us
    ppermute x4, starting transfers between devices, across(): return lax.ppermute(block, 'rows', list(enumerate(partner)))  4.28 us
    ppermute x1, starting transfers between devices, on_device(): received = lax.ppermute(tail, 'section', ring)  2.99 us
    ppermute x4, waiting for transfers between devices, across(): return lax.ppermute(block, 'rows', list(enumerate(partner)))  1.54 us
  transfers between devices with their start and end apart: 6, of which 3 were waited for; matrix products, arithmetic and copies ran while one was open for 0% of the time, Pallas kernels for 3%

profile of v11, /device:TPU:0, one launch (start us, length us, event | category | flops | bytes accessed | tf_op | source)
XLA Modules:
  0.0 40.8 jit_solution(10724909972110881753)
XLA Ops:
  0.0 1.1 %shard_map.109 = (bf16[2,2,64,128]{3,2,1,0:T(8,128)(2,1)S(1)}, bf16[8,2,64,128]{3,2,1,0:T(8,128)(2,1)S(1)}, bf16[2,2,2,64,128]{4,3,2,1,0:T(8,128)(2,1)S(1)}) custom-call(bf16[8,2,64,128]{3,2,1,0:T(8,128)(2,1)} %own_ref.1, bf16[2,2,64,128]{3,2,1,0:T(8,128)(2,1)} %second_cache_ref.1, bf16[2,2,64,128]{3,2,1,0:T(8,128)(2,1)} %first_cache_ref.1), custom_call_target="tpu_custom_call" | custom-call | bytes 1048576 | tf_op jit(solution)/shard_map/pallas_call | solution.py:233
  1.1 3.0 %collective-permute-start = (bf16[2,2,64,128]{3,2,1,0:T(8,128)(2,1)S(1)}, bf16[2,2,64,128]{3,2,1,0:T(8,128)(2,1)S(1)}, u32[]{:S(2)}, u32[]{:S(2)}) collective-permute-start(bf16[2,2,64,128]{3,2,1,0:T(8,128)(2,1)S(1)} %get-tuple-element.18), channel_id=1, source_target_pairs={{0,8},{8,16},{16,24},{24,0},{1,9},{9,17},{17,25},{25,1},{2,10},{10... | collective-permute-start | bytes 196616 | tf_op jit(solution)/shard_map/ppermute | solution.py:294
  4.1 1.2 %shard_map.110 = (f32[1,256]{1,0:T(1,128)S(1)}, f32[6,1,128]{2,1,0:T(1,128)S(1)}, bf16[3,3,3,128,128]{4,3,2,1,0:T(8,128)(2,1)S(1)}) custom-call(bf16[8,2,64,128]{3,2,1,0:T(8,128)(2,1)S(1)} %get-tuple-element.19.own_ref, bf16[3,3,3,128,128]{4,3,2,1,0:T(8,128)(2,1)} %weight_ref.2, f32[1,128]{1,0:T(1,128)} %bitcast.22, f32[1,128]{1,0:T(1,128)} %bitcast.23, ...), custom_call_target="tpu_custom_call" | custom-call | bytes 1048576 | tf_op jit(solution)/shard_map/pallas_call | solution.py:233
  5.3 0.1 collective-permute-start.1
  5.4 1.1 %collective-permute-done.1 = f32[1,256]{1,0:T(1,128)S(1)} collective-permute-done((f32[1,256]{1,0:T(1,128)S(1)}, f32[1,256]{1,0:T(1,128)S(1)}, u32[]{:S(2)}, u32[]{:S(2)}) %collective-permute-start.1) | collective-permute-done | bytes 1056 | tf_op jit(solution)/shard_map/ppermute | solution.py:267
  6.5 0.7 %collective-permute-done = bf16[2,2,64,128]{3,2,1,0:T(8,128)(2,1)S(1)} collective-permute-done((bf16[2,2,64,128]{3,2,1,0:T(8,128)(2,1)S(1)}, bf16[2,2,64,128]{3,2,1,0:T(8,128)(2,1)S(1)}, u32[]{:S(2)}, u32[]{:S(2)}) %collective-permute-start) | collective-permute-done | bytes 65568 | tf_op jit(solution)/shard_map/ppermute | solution.py:294
  7.3 0.7 %collective-permute-start.3 = (bf16[12,2,64,128]{3,2,1,0:T(8,128)(2,1)S(1)}, bf16[12,2,64,128]{3,2,1,0:T(8,128)(2,1)S(1)}, u32[]{:S(2)}, u32[]{:S(2)}) collective-permute-start(bf16[12,2,64,128]{3,2,1,0:T(8,128)(2,1)S(1)} %pad_maximum_fusion.own_ref), channel_id=1, source_target_pairs={{0,0},{1,2},{2,1},{3,4},{4,3},{5,6},{6,5},{7,7},{8,8},{9,10},{10,9... | collective-permute-start | bytes 1179656 | tf_op jit(solution)/shard_map/ppermute | solution.py:267
  8.0 3.5 %collective-permute-start.2 = (bf16[12,2,64,128]{3,2,1,0:T(8,128)(2,1)S(1)}, bf16[12,2,64,128]{3,2,1,0:T(8,128)(2,1)S(1)}, u32[]{:S(2)}, u32[]{:S(2)}) collective-permute-start(bf16[12,2,64,128]{3,2,1,0:T(8,128)(2,1)S(1)} %pad_maximum_fusion.own_ref), channel_id=1, source_target_pairs={{0,1},{1,0},{2,3},{3,2},{4,5},{5,4},{6,7},{7,6},{8,9},{9,8},{10,11... | collective-permute-start | bytes 1179656 | tf_op jit(solution)/shard_map/ppermute | solution.py:267
  11.5 12.1 %all_to_all.10.stats_ref = f32[16,2,256]{2,1,0:T(2,128)S(1)} all-to-all(f32[16,2,256]{2,1,0:T(2,128)S(1)} %broadcast_in_dim.15), channel_id=1, replica_groups={{0,2,4,6,8,10,12,14,16,18,20,22,24,26,28,30},{1,3,5,7,9,11,13,15,17,19,..., dimensions={0} | all-to-all | bytes 65536 | tf_op jit(solution)/shard_map/all_to_all | solution.py:274
  23.6 0.0 collective-permute-done.3.far_ref
  23.6 0.0 collective-permute-done.2.near_ref
  23.6 0.0 copy-start
  23.6 2.9 %shard_map.111 = (bf16[8,4,64,128]{3,2,1,0:T(8,128)(2,1)S(1)}, bf16[2,4,64,128]{3,2,1,0:T(8,128)(2,1)S(1)}, bf16[2,4,64,128]{3,2,1,0:T(8,128)(2,1)S(1)}, f32[1,256]{1,0:T(1,128)S(1)}) custom-call(bf16[12,2,64,128]{3,2,1,0:T(8,128)(2,1)S(1)} %pad_maximum_fusion.own_ref, bf16[12,2,64,128]{3,2,1,0:T(8,128)(2,1)S(1)} %collective-permute-done.2.near_ref, ...), custom_call_target="tpu_custom_call" | custom-call | flops 1000000000 | bytes 1048576 | tf_op jit(solution)/shard_map/pallas_call | solution.py:233
  26.5 0.1 collective-permute-start.5
  26.6 0.7 %collective-permute-start.4 = (bf16[2,4,64,128]{3,2,1,0:T(8,128)(2,1)S(1)}, bf16[2,4,64,128]{3,2,1,0:T(8,128)(2,1)S(1)}, u32[]{:S(2)}, u32[]{:S(2)}) collective-permute-start(bf16[2,4,64,128]{3,2,1,0:T(8,128)(2,1)S(1)} %get-tuple-element.26), channel_id=1, source_target_pairs={{0,8},{8,16},{16,24},{24,0},{1,9},{9,17},{17,25},{25,1},{2,10},{10... | collective-permute-start | bytes 393224 | tf_op jit(solution)/shard_map/ppermute | solution.py:321
  27.3 0.4 %collective-permute-done.5 = f32[1,256]{1,0:T(1,128)S(1)} collective-permute-done((f32[1,256]{1,0:T(1,128)S(1)}, f32[1,256]{1,0:T(1,128)S(1)}, u32[]{:S(2)}, u32[]{:S(2)}) %collective-permute-start.5) | collective-permute-done | bytes 1056 | tf_op jit(solution)/shard_map/ppermute | solution.py:267
  27.7 10.6 %all_to_all.11.stats_ref = f32[16,2,256]{2,1,0:T(2,128)S(1)} all-to-all(f32[16,2,256]{2,1,0:T(2,128)S(1)} %broadcast_in_dim.17), channel_id=1, replica_groups={{0,2,4,6,8,10,12,14,16,18,20,22,24,26,28,30},{1,3,5,7,9,11,13,15,17,19,..., dimensions={0} | all-to-all | bytes 65536 | tf_op jit(solution)/shard_map/all_to_all | solution.py:274
  38.3 0.0 collective-permute-done.4.halo_ref
  38.3 0.0 copy-done
  38.3 2.5 %shard_map.112 = bf16[8,2,64,128]{3,2,1,0:T(8,128)(2,1)} custom-call(bf16[8,4,64,128]{3,2,1,0:T(8,128)(2,1)S(1)} %get-tuple-element.25.middle_ref, bf16[2,4,64,128]{3,2,1,0:T(8,128)(2,1)S(1)} %collective-permute-done.4.halo_ref, bf16[2,4,64,128]{3,2,1,0:T(8,128)(2,1)S(1)} %get-tuple-element.27.cache_ref, f32[16,2,256]{2,1,0:T(2,128)S(1)} %all_to_all.11.stats_ref, ...), custom_call_target="tpu_custom_call" | custom-call | flops 1000000000 | bytes 1048576 | tf_op jit(solution)/shard_map/pallas_call | solution.py:233
  (7 shorter events, 0.1 us)
Async XLA Ops:
  1.1 6.2 %collective-permute-start = (bf16[2,2,64,128]{3,2,1,0:T(8,128)(2,1)S(1)}, bf16[2,2,64,128]{3,2,1,0:T(8,128)(2,1)S(1)}, u32[]{:S(2)}, u32[]{:S(2)}) collective-permute-start(bf16[2,2,64,128]{3,2,1,0:T(8,128)(2,1)S(1)} %get-tuple-element.18), channel_id=1, source_target_pairs={{0,8},{8,16},{16,24},{24,0},{1,9},{9,17},{17,25},{25,1},{2,10},{10... | collective-permute-start | bytes 196616 | tf_op jit(solution)/shard_map/ppermute | solution.py:294
  5.3 1.2 %collective-permute-start.1 = (f32[1,256]{1,0:T(1,128)S(1)}, f32[1,256]{1,0:T(1,128)S(1)}, u32[]{:S(2)}, u32[]{:S(2)}) collective-permute-start(f32[1,256]{1,0:T(1,128)S(1)} %get-tuple-element.20), channel_id=1, source_target_pairs={{0,1},{1,0},{2,3},{3,2},{4,5},{5,4},{6,7},{7,6},{8,9},{9,8},{10,11... | collective-permute-start | bytes 3080 | tf_op jit(solution)/shard_map/ppermute | solution.py:267
  7.3 16.3 %collective-permute-start.3 = (bf16[12,2,64,128]{3,2,1,0:T(8,128)(2,1)S(1)}, bf16[12,2,64,128]{3,2,1,0:T(8,128)(2,1)S(1)}, u32[]{:S(2)}, u32[]{:S(2)}) collective-permute-start(bf16[12,2,64,128]{3,2,1,0:T(8,128)(2,1)S(1)} %pad_maximum_fusion.own_ref), channel_id=1, source_target_pairs={{0,0},{1,2},{2,1},{3,4},{4,3},{5,6},{6,5},{7,7},{8,8},{9,10},{10,9... | collective-permute-start | bytes 1179656 | tf_op jit(solution)/shard_map/ppermute | solution.py:267
  8.0 15.6 %collective-permute-start.2 = (bf16[12,2,64,128]{3,2,1,0:T(8,128)(2,1)S(1)}, bf16[12,2,64,128]{3,2,1,0:T(8,128)(2,1)S(1)}, u32[]{:S(2)}, u32[]{:S(2)}) collective-permute-start(bf16[12,2,64,128]{3,2,1,0:T(8,128)(2,1)S(1)} %pad_maximum_fusion.own_ref), channel_id=1, source_target_pairs={{0,1},{1,0},{2,3},{3,2},{4,5},{5,4},{6,7},{7,6},{8,9},{9,8},{10,11... | collective-permute-start | bytes 1179656 | tf_op jit(solution)/shard_map/ppermute | solution.py:267
  23.6 14.7 %copy-start = (bf16[3,3,3,128,128]{4,3,2,1,0:T(8,128)(2,1)S(1)}, bf16[3,3,3,128,128]{4,3,2,1,0:T(8,128)(2,1)}, u32[]{:S(2)}) copy-start(bf16[3,3,3,128,128]{4,3,2,1,0:T(8,128)(2,1)} %weight_ref.3) | copy-start | bytes 2654212
  26.5 1.2 %collective-permute-start.5 = (f32[1,256]{1,0:T(1,128)S(1)}, f32[1,256]{1,0:T(1,128)S(1)}, u32[]{:S(2)}, u32[]{:S(2)}) collective-permute-start(f32[1,256]{1,0:T(1,128)S(1)} %get-tuple-element.28), channel_id=1, source_target_pairs={{0,1},{1,0},{2,3},{3,2},{4,5},{5,4},{6,7},{7,6},{8,9},{9,8},{10,11... | collective-permute-start | bytes 3080 | tf_op jit(solution)/shard_map/ppermute | solution.py:267
  26.6 11.7 %collective-permute-start.4 = (bf16[2,4,64,128]{3,2,1,0:T(8,128)(2,1)S(1)}, bf16[2,4,64,128]{3,2,1,0:T(8,128)(2,1)S(1)}, u32[]{:S(2)}, u32[]{:S(2)}) collective-permute-start(bf16[2,4,64,128]{3,2,1,0:T(8,128)(2,1)S(1)} %get-tuple-element.26), channel_id=1, source_target_pairs={{0,8},{8,16},{16,24},{24,0},{1,9},{9,17},{17,25},{25,1},{2,10},{10... | collective-permute-start | bytes 393224 | tf_op jit(solution)/shard_map/ppermute | solution.py:321

commit v12 on v11

--- a/solution.py
+++ b/solution.py
@@ -128,25 +128,24 @@
         load.wait()
 
 
-def span_moments(stats_ref, section, row_count):
-    chips = row_count // 2
-    own = stats_ref[pl.ds(section * chips, chips)]
-    return own.reshape(row_count, own.shape[-1])
+def affine_kernel(row_count, cells, which, stats_ref, vectors_ref, affine_ref):
+    section = lax.axis_index("section")
+    scale, shift = vectors_ref[which], vectors_ref[which + 1]
+    for index, span in enumerate((section, jnp.maximum(section - 1, 0))):
+        stats = stats_ref[pl.ds(span * row_count, row_count)]
+        slope, offset = affine(stats.reshape(row_count, stats.shape[-1]), cells, scale, shift)
+        affine_ref[2 * index] = slope
+        affine_ref[2 * index + 1] = offset
 
 
 def first_kernel(
-    row_count, own_ref, near_ref, far_ref, stats_ref, vectors_ref, weight_ref, middle_ref,
+    row_count, own_ref, near_ref, far_ref, affine_ref, vectors_ref, weight_ref, middle_ref,
     tail_ref, cache_ref, sums_ref, field
 ):
     section, row_at = lax.axis_index("section"), lax.axis_index("rows")
     inner, columns = middle_ref.shape[0], middle_ref.shape[2]
     lines, channels = own_ref.shape[1], own_ref.shape[3]
-    cells = inner * lines * columns
-    scale, shift = vectors_ref[0], vectors_ref[1]
-    mine = span_moments(stats_ref, section, row_count)
-    before = span_moments(stats_ref, jnp.maximum(section - 1, 0), row_count)
-    slope, offset = affine(mine, cells, scale, shift)
-    slope_before, offset_before = affine(before, cells, scale, shift)
+    slope, offset, slope_before, offset_before = (affine_ref[row] for row in range(4))
     even = row_at % 2 == 0
     at_start = section == 0
 
@@ -190,17 +189,12 @@
 
 
 def second_kernel(
-    row_count, middle_ref, halo_ref, cache_ref, stats_ref, vectors_ref, weight_ref, own_ref,
+    row_count, middle_ref, halo_ref, cache_ref, affine_ref, vectors_ref, weight_ref, own_ref,
     out_ref, field
 ):
     section, row_at = lax.axis_index("section"), lax.axis_index("rows")
     frames, lines, columns, channels = own_ref.shape
-    cells = frames * lines * columns
-    scale, shift = vectors_ref[3], vectors_ref[4]
-    mine = span_moments(stats_ref, section, row_count)
-    before = span_moments(stats_ref, jnp.maximum(section - 1, 0), row_count)
-    slope, offset = affine(mine, cells, scale, shift)
-    slope_before, offset_before = affine(before, cells, scale, shift)
+    slope, offset, slope_before, offset_before = (affine_ref[row] for row in range(4))
     at_start = section == 0
     for line in range(lines + 2):
         behind = activate(halo_ref[:, line], slope_before, offset_before).astype(jnp.bfloat16)
@@ -256,7 +250,6 @@
 ):
     frames, lines, columns, channels = activations.shape
     sections, row_count = lax.axis_size("section"), lax.axis_size("rows")
-    chips = sections * row_count // 2
     near = [i ^ 1 for i in range(row_count)]
     far = [0] + [i + 1 if i % 2 else i - 1 for i in range(1, row_count - 1)] + [row_count - 1]
     ring = [(at, (at + 1) % sections) for at in range(sections)]
@@ -266,14 +259,15 @@
     def across(block, partner):
         return lax.ppermute(block, "rows", list(enumerate(partner)))
 
-    def with_near(sums):
-        return jnp.stack([sums, across(sums, near)], axis=1)
-
-    def exchange(pair):
-        same_core = [list(range(core, 2 * chips, 2)) for core in range(2)]
-        return lax.all_to_all(
-            jnp.broadcast_to(pair, (chips,) + pair.shape[1:]), ("section", "rows"), 0, 0,
-            tiled=True, axis_index_groups=same_core,
+    def coefficients(sums, which):
+        everyone = jnp.broadcast_to(sums, (sections * row_count,) + sums.shape)
+        stats = lax.all_to_all(everyone, ("section", "rows"), 0, 0, tiled=True)
+        return call(
+            functools.partial(affine_kernel, row_count, frames * lines * columns, which),
+            jax.ShapeDtypeStruct((4, 1, channels), jnp.float32),
+            [],
+            (stats, packed),
+            flops=10**11,
         )
 
     def shaped(*shape):
@@ -303,14 +297,17 @@
         (own, conv1_weight) + tuple(vector.reshape(1, channels) for vector in vectors),
         in_place=range(1, 2 + len(vectors)),
     )
-    received, pair = lax.optimization_barrier((received, with_near(sums)))
+    received, _ = lax.optimization_barrier((received, sums))
     halo = jnp.where(lax.axis_index("section") == 0, caches[1], received)
     joined = jnp.concatenate([caches[0], halo, own], axis=0)
     middle, tail, cache, sums = call(
         functools.partial(first_kernel, row_count),
         (shaped(frames, *wide), shaped(REACH, *wide), shaped(REACH, *wide), sums_shape),
         [pltpu.VMEM((frames + REACH, 3 * lines, columns, channels), jnp.bfloat16)],
-        (joined, across(joined, near), across(joined, far), exchange(pair), packed, weight),
+        (
+            joined, across(joined, near), across(joined, far), coefficients(sums, 0), packed,
+            weight,
+        ),
         flops=10**9,
     )
     return call(
@@ -318,7 +315,7 @@
         shaped(*activations.shape),
         [pltpu.VMEM((frames + REACH, *wide), jnp.bfloat16)],
         (
-            middle, lax.ppermute(tail, "section", ring), cache, exchange(with_near(sums)),
+            middle, lax.ppermute(tail, "section", ring), cache, coefficients(sums, 3),
             packed, conv2_weight, own,
         ),
         flops=10**9,

time: 41 us -> 39.3 us (0.959)
  blocking collectives: 22.7 us -> 0 us
  starting transfers between devices: 7.97 us -> 21.2 us
  waiting for transfers between devices: 2.28 us -> 8.69 us
  local copies, waits for them, and re-layouts: 0.03 us -> 1.28 us
    all_to_all x2 -> x0, blocking collectives: 22.7 us -> none  [exchange(): lax.all_to_all(jnp.broadcast_to(pair, (chips,) + pair.shape[1:]), ('secti...]
    all_to_all x0 -> x2, starting transfers between devices: none -> 12.5 us  [coefficients(): stats = lax.all_to_all(everyone, ('section', 'rows'), 0, 0, tiled=True)]
    all_to_all x0 -> x2, waiting for transfers between devices: none -> 8.68 us  [coefficients(): stats = lax.all_to_all(everyone, ('section', 'rows'), 0, 0, tiled=True)]
    ppermute x4 -> x2, waiting for transfers between devices: 1.54 us -> 0.01 us  [across(): return lax.ppermute(block, 'rows', list(enumerate(partner)))]
    broadcast_in_dim x2, local copies, waits for them, and re-layouts: 0.02 us -> 1.27 us  [coefficients(): everyone = jnp.broadcast_to(sums, (sections * row_count,) + sums.shape)]
    ppermute x1, starting transfers between devices: 0.7 us -> 1.82 us  [on_device(): lax.ppermute(tail, 'section', ring)]
    ppermute x1, waiting for transfers between devices: 0.74 us -> 0.01 us  [on_device(): received = lax.ppermute(tail, 'section', ring)]
    ppermute x4 -> x2, starting transfers between devices: 4.28 us -> 3.86 us  [across(): return lax.ppermute(block, 'rows', list(enumerate(partner)))]
  transfers between devices with their start and end apart: 6 -> 6, of which waited for: 3 -> 2; matrix products, arithmetic and copies ran while one was open for 0% -> 2% of each run, Pallas kernels for 3% -> 4%
where the time goes in v12:
time: 39.3 us; the launch traced here: 39.1 us
  starting transfers between devices  21.2 us (54%)
  waiting for transfers between devices  8.69 us (22%)
  Pallas kernels  7.76 us (20%)
  local copies, waits for them, and re-layouts  1.28 us (3%)
    all_to_all x2, starting transfers between devices, coefficients(): stats = lax.all_to_all(everyone, ('section', 'rows'), 0, 0, tiled=True)  12.5 us
    all_to_all x2, waiting for transfers between devices, coefficients(): stats = lax.all_to_all(everyone, ('section', 'rows'), 0, 0, tiled=True)  8.68 us
    pallas_call x6, Pallas kernels, call(): pl.pallas_call(kernel, out_shape=out_shape, in_specs=specs, out_specs=jax...  7.76 us
    ppermute x2, starting transfers between devices, across(): return lax.ppermute(block, 'rows', list(enumerate(partner)))  3.86 us
    ppermute x1, starting transfers between devices, on_device(): received = lax.ppermute(tail, 'section', ring)  2.99 us
    ppermute x1, starting transfers between devices, on_device(): lax.ppermute(tail, 'section', ring)  1.82 us
    broadcast_in_dim x2, local copies, waits for them, and re-layouts, coefficients(): everyone = jnp.broadcast_to(sums, (sections * row_count,) + sums.shape)  1.27 us
  transfers between devices with their start and end apart: 6, of which 2 were waited for; matrix products, arithmetic and copies ran while one was open for 2% of the time, Pallas kernels for 4%

profile of v12, /device:TPU:0, one launch (start us, length us, event | category | flops | bytes accessed | tf_op | source)
XLA Modules:
  0.0 39.1 jit_solution(9902258006058338203)
XLA Ops:
  0.0 1.1 %shard_map.109 = (bf16[2,2,64,128]{3,2,1,0:T(8,128)(2,1)S(1)}, bf16[8,2,64,128]{3,2,1,0:T(8,128)(2,1)S(1)}, bf16[2,2,2,64,128]{4,3,2,1,0:T(8,128)(2,1)S(1)}) custom-call(bf16[8,2,64,128]{3,2,1,0:T(8,128)(2,1)} %own_ref.1, bf16[2,2,64,128]{3,2,1,0:T(8,128)(2,1)} %second_cache_ref.1, bf16[2,2,64,128]{3,2,1,0:T(8,128)(2,1)} %first_cache_ref.1), custom_call_target="tpu_custom_call" | custom-call | bytes 1048576 | tf_op jit(solution)/shard_map/pallas_call | solution.py:227
  1.1 3.0 %collective-permute-start = (bf16[2,2,64,128]{3,2,1,0:T(8,128)(2,1)S(1)}, bf16[2,2,64,128]{3,2,1,0:T(8,128)(2,1)S(1)}, u32[]{:S(2)}, u32[]{:S(2)}) collective-permute-start(bf16[2,2,64,128]{3,2,1,0:T(8,128)(2,1)S(1)} %get-tuple-element.17), channel_id=1, source_target_pairs={{0,8},{8,16},{16,24},{24,0},{1,9},{9,17},{17,25},{25,1},{2,10},{10... | collective-permute-start | bytes 196616 | tf_op jit(solution)/shard_map/ppermute | solution.py:288
  4.1 1.2 %shard_map.110 = (f32[1,256]{1,0:T(1,128)S(1)}, f32[6,1,128]{2,1,0:T(1,128)S(1)}, bf16[3,3,3,128,128]{4,3,2,1,0:T(8,128)(2,1)S(1)}) custom-call(bf16[8,2,64,128]{3,2,1,0:T(8,128)(2,1)S(1)} %get-tuple-element.18.own_ref, bf16[3,3,3,128,128]{4,3,2,1,0:T(8,128)(2,1)} %weight_ref.2, f32[1,128]{1,0:T(1,128)} %bitcast.14, f32[1,128]{1,0:T(1,128)} %bitcast.15, ...), custom_call_target="tpu_custom_call" | custom-call | bytes 1048576 | tf_op jit(solution)/shard_map/pallas_call | solution.py:227
  5.3 0.6 %broadcast_in_dim.6 = f32[32,1,256]{2,1,0:T(1,128)} broadcast(f32[256]{0:T(256)S(1)} %bitcast.13), dimensions={2} | broadcast | bytes 33792 | tf_op jit(solution)/shard_map/broadcast_in_dim | solution.py:263
  5.9 4.9 %all-to-all-start = ((f32[32,1,256]{2,1,0:T(1,128)}), f32[32,1,256]{2,1,0:T(1,128)S(1)}, u32[]{:S(2)}, u32[]{:S(2)}) async-start(f32[32,1,256]{2,1,0:T(1,128)} %broadcast_in_dim.6), calls=%async_computation | async-start | bytes 65536 | tf_op jit(solution)/shard_map/all_to_all | solution.py:264
  10.9 0.0 collective-permute-done
  11.0 0.7 %collective-permute-start.2 = (bf16[12,2,64,128]{3,2,1,0:T(8,128)(2,1)S(1)}, bf16[12,2,64,128]{3,2,1,0:T(8,128)(2,1)S(1)}, u32[]{:S(2)}, u32[]{:S(2)}) collective-permute-start(bf16[12,2,64,128]{3,2,1,0:T(8,128)(2,1)S(1)} %pad_maximum_fusion.own_ref), channel_id=1, source_target_pairs={{0,0},{1,2},{2,1},{3,4},{4,3},{5,6},{6,5},{7,7},{8,8},{9,10},{10,9... | collective-permute-start | bytes 1179656 | tf_op jit(solution)/shard_map/ppermute | solution.py:260
  11.7 3.2 %collective-permute-start.1 = (bf16[12,2,64,128]{3,2,1,0:T(8,128)(2,1)S(1)}, bf16[12,2,64,128]{3,2,1,0:T(8,128)(2,1)S(1)}, u32[]{:S(2)}, u32[]{:S(2)}) collective-permute-start(bf16[12,2,64,128]{3,2,1,0:T(8,128)(2,1)S(1)} %pad_maximum_fusion.own_ref), channel_id=1, source_target_pairs={{0,1},{1,0},{2,3},{3,2},{4,5},{5,4},{6,7},{7,6},{8,9},{9,8},{10,11... | collective-permute-start | bytes 1179656 | tf_op jit(solution)/shard_map/ppermute | solution.py:260
  14.8 3.3 %all-to-all-done.stats_ref = f32[32,1,256]{2,1,0:T(1,128)S(1)} async-done(((f32[32,1,256]{2,1,0:T(1,128)}), f32[32,1,256]{2,1,0:T(1,128)S(1)}, u32[]{:S(2)}, u32[]{:S(2)}) %all-to-all-start) | async-done | bytes 32800 | tf_op jit(solution)/shard_map/all_to_all | solution.py:264
  18.1 0.2 shard_map.111.affine_ref
  18.3 0.0 collective-permute-done.2.far_ref
  18.3 0.0 collective-permute-done.1.near_ref
  18.3 2.8 %shard_map.112 = (bf16[8,4,64,128]{3,2,1,0:T(8,128)(2,1)S(1)}, bf16[2,4,64,128]{3,2,1,0:T(8,128)(2,1)S(1)}, bf16[2,4,64,128]{3,2,1,0:T(8,128)(2,1)S(1)}, f32[1,256]{1,0:T(1,128)S(1)}) custom-call(bf16[12,2,64,128]{3,2,1,0:T(8,128)(2,1)S(1)} %pad_maximum_fusion.own_ref, bf16[12,2,64,128]{3,2,1,0:T(8,128)(2,1)S(1)} %collective-permute-done.1.near_ref, ...), custom_call_target="tpu_custom_call" | custom-call | flops 1000000000 | bytes 1048576 | tf_op jit(solution)/shard_map/pallas_call | solution.py:227
  21.1 0.6 %broadcast_in_dim.7 = f32[32,1,256]{2,1,0:T(1,128)} broadcast(f32[256]{0:T(256)S(1)} %bitcast.12), dimensions={2} | broadcast | bytes 33792 | tf_op jit(solution)/shard_map/broadcast_in_dim | solution.py:263
  21.7 7.6 %all-to-all-start.1 = ((f32[32,1,256]{2,1,0:T(1,128)}), f32[32,1,256]{2,1,0:T(1,128)S(1)}, u32[]{:S(2)}, u32[]{:S(2)}) async-start(f32[32,1,256]{2,1,0:T(1,128)} %broadcast_in_dim.7), calls=%async_computation.1 | async-start | bytes 65536 | tf_op jit(solution)/shard_map/all_to_all | solution.py:264
  29.3 0.0 copy-start
  29.4 1.8 %collective-permute-start.3 = (bf16[2,4,64,128]{3,2,1,0:T(8,128)(2,1)S(1)}, bf16[2,4,64,128]{3,2,1,0:T(8,128)(2,1)S(1)}, u32[]{:S(2)}, u32[]{:S(2)}) collective-permute-start(bf16[2,4,64,128]{3,2,1,0:T(8,128)(2,1)S(1)} %get-tuple-element.24), channel_id=1, source_target_pairs={{0,8},{8,16},{16,24},{24,0},{1,9},{9,17},{17,25},{25,1},{2,10},{10... | collective-permute-start | bytes 393224 | tf_op jit(solution)/shard_map/ppermute | solution.py:318
  31.2 5.4 %all-to-all-done.1.stats_ref = f32[32,1,256]{2,1,0:T(1,128)S(1)} async-done(((f32[32,1,256]{2,1,0:T(1,128)}), f32[32,1,256]{2,1,0:T(1,128)S(1)}, u32[]{:S(2)}, u32[]{:S(2)}) %all-to-all-start.1) | async-done | bytes 32800 | tf_op jit(solution)/shard_map/all_to_all | solution.py:264
  36.6 0.2 shard_map.113.affine_ref
  36.8 0.0 collective-permute-done.3.halo_ref
  36.8 0.0 copy-done
  36.8 2.3 %shard_map.114 = bf16[8,2,64,128]{3,2,1,0:T(8,128)(2,1)} custom-call(bf16[8,4,64,128]{3,2,1,0:T(8,128)(2,1)S(1)} %get-tuple-element.23.middle_ref, bf16[2,4,64,128]{3,2,1,0:T(8,128)(2,1)S(1)} %collective-permute-done.3.halo_ref, bf16[2,4,64,128]{3,2,1,0:T(8,128)(2,1)S(1)} %get-tuple-element.25.cache_ref, f32[4,1,128]{2,1,0:T(1,128)S(1)} %shard_map.113.affine_ref, ...), custom_call_target="tpu_custom_call" | custom-call | flops 1000000000 | bytes 1048576 | tf_op jit(solution)/shard_map/pallas_call | solution.py:227
  (3 shorter events, 0.1 us)
Async XLA Ops:
  1.1 9.8 %collective-permute-start = (bf16[2,2,64,128]{3,2,1,0:T(8,128)(2,1)S(1)}, bf16[2,2,64,128]{3,2,1,0:T(8,128)(2,1)S(1)}, u32[]{:S(2)}, u32[]{:S(2)}) collective-permute-start(bf16[2,2,64,128]{3,2,1,0:T(8,128)(2,1)S(1)} %get-tuple-element.17), channel_id=1, source_target_pairs={{0,8},{8,16},{16,24},{24,0},{1,9},{9,17},{17,25},{25,1},{2,10},{10... | collective-permute-start | bytes 196616 | tf_op jit(solution)/shard_map/ppermute | solution.py:288
  5.9 12.2 %all-to-all-start = ((f32[32,1,256]{2,1,0:T(1,128)}), f32[32,1,256]{2,1,0:T(1,128)S(1)}, u32[]{:S(2)}, u32[]{:S(2)}) async-start(f32[32,1,256]{2,1,0:T(1,128)} %broadcast_in_dim.6), calls=%async_computation | async-start | bytes 65536 | tf_op jit(solution)/shard_map/all_to_all | solution.py:264
  11.0 7.3 %collective-permute-start.2 = (bf16[12,2,64,128]{3,2,1,0:T(8,128)(2,1)S(1)}, bf16[12,2,64,128]{3,2,1,0:T(8,128)(2,1)S(1)}, u32[]{:S(2)}, u32[]{:S(2)}) collective-permute-start(bf16[12,2,64,128]{3,2,1,0:T(8,128)(2,1)S(1)} %pad_maximum_fusion.own_ref), channel_id=1, source_target_pairs={{0,0},{1,2},{2,1},{3,4},{4,3},{5,6},{6,5},{7,7},{8,8},{9,10},{10,9... | collective-permute-start | bytes 1179656 | tf_op jit(solution)/shard_map/ppermute | solution.py:260
  11.7 6.6 %collective-permute-start.1 = (bf16[12,2,64,128]{3,2,1,0:T(8,128)(2,1)S(1)}, bf16[12,2,64,128]{3,2,1,0:T(8,128)(2,1)S(1)}, u32[]{:S(2)}, u32[]{:S(2)}) collective-permute-start(bf16[12,2,64,128]{3,2,1,0:T(8,128)(2,1)S(1)} %pad_maximum_fusion.own_ref), channel_id=1, source_target_pairs={{0,1},{1,0},{2,3},{3,2},{4,5},{5,4},{6,7},{7,6},{8,9},{9,8},{10,11... | collective-permute-start | bytes 1179656 | tf_op jit(solution)/shard_map/ppermute | solution.py:260
  21.7 14.8 %all-to-all-start.1 = ((f32[32,1,256]{2,1,0:T(1,128)}), f32[32,1,256]{2,1,0:T(1,128)S(1)}, u32[]{:S(2)}, u32[]{:S(2)}) async-start(f32[32,1,256]{2,1,0:T(1,128)} %broadcast_in_dim.7), calls=%async_computation.1 | async-start | bytes 65536 | tf_op jit(solution)/shard_map/all_to_all | solution.py:264
  29.3 7.4 %copy-start = (bf16[3,3,3,128,128]{4,3,2,1,0:T(8,128)(2,1)S(1)}, bf16[3,3,3,128,128]{4,3,2,1,0:T(8,128)(2,1)}, u32[]{:S(2)}) copy-start(bf16[3,3,3,128,128]{4,3,2,1,0:T(8,128)(2,1)} %weight_ref.3) | copy-start | bytes 2654212
  29.4 7.4 %collective-permute-start.3 = (bf16[2,4,64,128]{3,2,1,0:T(8,128)(2,1)S(1)}, bf16[2,4,64,128]{3,2,1,0:T(8,128)(2,1)S(1)}, u32[]{:S(2)}, u32[]{:S(2)}) collective-permute-start(bf16[2,4,64,128]{3,2,1,0:T(8,128)(2,1)S(1)} %get-tuple-element.24), channel_id=1, source_target_pairs={{0,8},{8,16},{16,24},{24,0},{1,9},{9,17},{17,25},{25,1},{2,10},{10... | collective-permute-start | bytes 393224 | tf_op jit(solution)/shard_map/ppermute | solution.py:318

commit v13 on v10

--- a/solution.py
+++ b/solution.py
@@ -1,8 +1,6 @@
 import functools
-import itertools
 
 import functools
-import itertools
 
 import jax
 import jax.numpy as jnp
@@ -17,42 +15,39 @@
 epsilon = 1e-06
 
 
-def group_sum(values, width):
-    lanes = values.shape[-1]
-    lane = lax.broadcasted_iota(jnp.int32, values.shape, values.ndim - 1)
-    step = 1
-    while step < width:
-        up = pltpu.roll(values, lanes - step, values.ndim - 1)
-        down = pltpu.roll(values, step, values.ndim - 1)
-        values = values + jnp.where((lane // step) % 2 == 0, up, down)
-        step *= 2
-    return values
-
-
 def moments(blocks):
-    first = next(blocks)
-    pivot = jnp.sum(first, axis=0, keepdims=True) * (1.0 / first.shape[0])
-    cells, total, squares = 0, 0.0, 0.0
-    for block in itertools.chain([first], blocks):
+    pivot = blocks[0][:1]
+    cells = sum(block.shape[0] for block in blocks)
+    total, squares = 0.0, 0.0
+    for block in blocks:
         away = block - pivot
-        cells += block.shape[0]
         total = total + jnp.sum(away, axis=0, keepdims=True)
         squares = squares + jnp.sum(away * away, axis=0, keepdims=True)
     shift = total * (1.0 / cells)
-    return jnp.concatenate([(pivot + shift) * cells, squares - total * shift], axis=1)
+    return jnp.concatenate([pivot + shift, squares - total * shift], axis=1)
 
 
 def affine(stats, cells, scale, shift):
     devices, channels = stats.shape[0], scale.shape[-1]
-    width = channels // GROUPS
-    totals, centred = stats[:, :channels], stats[:, channels:]
-    count = cells * width * devices
-    average = group_sum(jnp.sum(totals, axis=0, keepdims=True), width) * (1.0 / count)
-    away = totals * (1.0 / cells) - average
-    inner = jnp.sum(centred + cells * (away * away), axis=0, keepdims=True)
-    spread = group_sum(inner, width) * (1.0 / count)
-    slope = 0.5 * scale / jnp.sqrt(spread + epsilon)
-    return slope, 0.5 * shift - average * slope
+    means, squares = stats[:, :channels], stats[:, channels:]
+    mean = jnp.sum(means, axis=0, keepdims=True) * (1.0 / devices)
+    away = means - mean
+    square = jnp.sum(squares + cells * (away * away), axis=0, keepdims=True)
+    count = cells * devices
+    lane = lax.broadcasted_iota(jnp.int32, mean.shape, 1)
+    step = 1
+    while step < channels // GROUPS:
+
+        def partner(values):
+            up = pltpu.roll(values, channels - step, 1)
+            return jnp.where((lane // step) % 2 == 0, up, pltpu.roll(values, step, 1))
+
+        away = partner(mean) - mean
+        square = square + partner(square) + (0.5 * count) * (away * away)
+        mean = mean + 0.5 * away
+        count, step = 2 * count, 2 * step
+    slope = 0.5 * scale * lax.rsqrt(square * (1.0 / count) + epsilon)
+    return slope, 0.5 * shift - mean * slope
 
 
 def activate(values, slope, offset):
@@ -141,24 +136,31 @@
     for load in loads:
         load.start()
     channels = own_ref.shape[-1]
-    blocks = (own_ref[frame].astype(jnp.float32) for frame in range(own_ref.shape[0]))
-    stats_ref[...] = moments(block.reshape(-1, channels) for block in blocks)
+    blocks = [own_ref[frame].astype(jnp.float32) for frame in range(own_ref.shape[0])]
+    packed = moments([block.reshape(-1, channels) for block in blocks])
+    stats_ref[...] = jnp.broadcast_to(packed[None], stats_ref.shape)
     for load in loads:
         load.wait()
 
 
+def affine_kernel(row_count, cells, which, stats_ref, vectors_ref, affine_ref):
+    section = lax.axis_index("section")
+    scale, shift = vectors_ref[which], vectors_ref[which + 1]
+    for index, span in enumerate((section, jnp.maximum(section - 1, 0))):
+        stats = stats_ref[pl.ds(span * row_count, row_count)]
+        slope, offset = affine(stats.reshape(row_count, stats.shape[-1]), cells, scale, shift)
+        affine_ref[2 * index] = slope
+        affine_ref[2 * index + 1] = offset
+
+
 def first_kernel(
-    row_count, own_ref, near_ref, far_ref, stats_ref, vectors_ref, weight_ref, middle_ref,
+    row_count, own_ref, near_ref, far_ref, affine_ref, vectors_ref, weight_ref, middle_ref,
     sums_ref, field
 ):
     section, row_at = lax.axis_index("section"), lax.axis_index("rows")
     frames, lines, columns, channels = own_ref.shape
     inner = frames - SPAN_HALO
-    cells = inner * lines * columns
-    scale, shift = vectors_ref[0], vectors_ref[1]
-    mine, before = stats_ref[:, 0], stats_ref[:, 1]
-    slope, offset = affine(mine, cells, scale, shift)
-    slope_before, offset_before = affine(before, cells, scale, shift)
+    slope, offset, slope_before, offset_before = (affine_ref[row] for row in range(4))
     even = row_at % 2 == 0
     at_start = section == 0
 
@@ -197,20 +199,15 @@
             middle_ref[2:, line] = rounded[2:]
             if 1 <= line <= lines:
                 kept.append(rounded[2:].astype(jnp.float32).reshape(-1, channels))
-    sums_ref[...] = jnp.broadcast_to(moments(iter(kept))[None], sums_ref.shape)
+    sums_ref[...] = jnp.broadcast_to(moments(kept)[None], sums_ref.shape)
 
 
 def second_kernel(
-    row_count, middle_ref, stats_ref, vectors_ref, weight_ref, own_ref, out_ref, field
+    row_count, middle_ref, affine_ref, vectors_ref, weight_ref, own_ref, out_ref, field
 ):
     section, row_at = lax.axis_index("section"), lax.axis_index("rows")
     frames, lines, columns, channels = own_ref.shape
-    cells = frames * lines * columns
-    scale, shift = vectors_ref[3], vectors_ref[4]
-    mine = stats_ref[pl.ds(section * row_count, row_count), 0]
-    before = stats_ref[pl.ds(jnp.maximum(section - 1, 0) * row_count, row_count), 0]
-    slope, offset = affine(mine, cells, scale, shift)
-    slope_before, offset_before = affine(before, cells, scale, shift)
+    slope, offset, slope_before, offset_before = (affine_ref[row] for row in range(4))
     at_start = section == 0
     for line in range(lines + 2):
         halo, body = middle_ref[:2, line], middle_ref[2:, line]
@@ -291,7 +288,7 @@
     sums, packed, weight = call(
         stats_kernel,
         (
-            jax.ShapeDtypeStruct((1, 2 * channels), jnp.float32),
+            stats_shape,
             jax.ShapeDtypeStruct((len(vectors), 1, channels), jnp.float32),
             jax.ShapeDtypeStruct(conv1_weight.shape, jnp.bfloat16),
         ),
@@ -300,28 +297,37 @@
         in_place=range(1, 2 + len(vectors)),
     )
     received = lax.ppermute(halo, "section", ring)
-    passed = lax.ppermute(sums, "section", ring)
-    received, sums, passed = lax.optimization_barrier((received, sums, passed))
+    received, _ = lax.optimization_barrier((received, sums))
     joined = jnp.concatenate([received, own], axis=0)
-    both = jnp.stack([sums, passed], axis=1)
-    both = jnp.broadcast_to(both, (row_count,) + both.shape[1:])
-    stats = lax.all_to_all(both, "rows", 0, 0, tiled=True)
-    middle, sums_two = call(
+
+    def coefficients(sums, which):
+        stats = lax.all_to_all(sums, ("section", "rows"), 0, 0, tiled=True)
+        return call(
+            functools.partial(affine_kernel, row_count, frames * lines * columns, which),
+            jax.ShapeDtypeStruct((4, 1, channels), jnp.float32),
+            [],
+            (stats, packed),
+            flops=10**11,
+        )
+
+    middle, sums = call(
         functools.partial(first_kernel, row_count),
         (
             jax.ShapeDtypeStruct((frames + 2, lines + 2, columns, channels), jnp.bfloat16),
             stats_shape,
         ),
         [pltpu.VMEM((frames + SPAN_HALO, 3 * lines, columns, channels), jnp.bfloat16)],
-        (joined, across(joined, near), across(joined, far), stats, packed, weight),
+        (
+            joined, across(joined, near), across(joined, far), coefficients(sums, 0), packed,
+            weight,
+        ),
         flops=10**9,
     )
-    stats_two = lax.all_to_all(sums_two, ("section", "rows"), 0, 0, tiled=True)
     return call(
         functools.partial(second_kernel, row_count),
         jax.ShapeDtypeStruct(activations.shape, jnp.bfloat16),
         [pltpu.VMEM((frames + 2, lines + 2, columns, channels), jnp.bfloat16)],
-        (middle, stats_two, packed, conv2_weight, own),
+        (middle, coefficients(sums, 3), packed, conv2_weight, own),
         flops=10**9,
     )
 

time: 38.4 us -> 40 us (1.042)
  blocking collectives: 18.3 us -> 14.6 us
  starting transfers between devices: 8.2 us -> 11.8 us
  local copies, waits for them, and re-layouts: 0.06 us -> 1.04 us
    all_to_all x0 -> x1, starting transfers between devices: none -> 4.92 us  [coefficients(): stats = lax.all_to_all(sums, ('section', 'rows'), 0, 0, tiled=True)]
    all_to_all x2 -> x1, blocking collectives: 18.3 us -> 14.6 us  [coefficients(): stats = lax.all_to_all(sums, ('section', 'rows'), 0, 0, tiled=True)]
    all_to_all x0 -> x1, waiting for transfers between devices: none -> 3.29 us  [coefficients(): stats = lax.all_to_all(sums, ('section', 'rows'), 0, 0, tiled=True)]
    ppermute x1 -> x0, waiting for transfers between devices: 2.98 us -> none  [on_device(): passed = lax.ppermute(sums, 'section', ring)]
    ppermute x1 -> x0, starting transfers between devices: 1.54 us -> none  [on_device(): passed = lax.ppermute(sums, 'section', ring)]
    unnamed x3, local copies, waits for them, and re-layouts: 0.01 us -> 1 us
    pallas_call x4 -> x6, Pallas kernels: 8.62 us -> 8.98 us  [call(): pl.pallas_call(kernel, out_shape=out_shape, in_specs=specs, out_specs=jax...]
  transfers between devices with their start and end apart: 4 -> 4, of which waited for: 1 -> 1; matrix products, arithmetic and copies ran while one was open for 0% -> 0% of each run, Pallas kernels for 3% -> 5%
where the time goes in v13:
time: 40 us; the launch traced here: 39.8 us
  blocking collectives  14.6 us (36%)
  starting transfers between devices  11.8 us (30%)
  Pallas kernels  8.98 us (22%)
  waiting for transfers between devices  3.3 us (8%)
  local copies, waits for them, and re-layouts  1.04 us (3%)
    all_to_all x1, blocking collectives, coefficients(): stats = lax.all_to_all(sums, ('section', 'rows'), 0, 0, tiled=True)  14.6 us
    pallas_call x6, Pallas kernels, call(): pl.pallas_call(kernel, out_shape=out_shape, in_specs=specs, out_specs=jax...  8.98 us
    all_to_all x1, starting transfers between devices, coefficients(): stats = lax.all_to_all(sums, ('section', 'rows'), 0, 0, tiled=True)  4.92 us
    ppermute x2, starting transfers between devices, across(): return lax.ppermute(block, 'rows', list(enumerate(partner)))  3.86 us
    all_to_all x1, waiting for transfers between devices, coefficients(): stats = lax.all_to_all(sums, ('section', 'rows'), 0, 0, tiled=True)  3.29 us
    ppermute x1, starting transfers between devices, on_device(): received = lax.ppermute(halo, 'section', ring)  2.99 us
    unnamed x3, local copies, waits for them, and re-layouts  1 us
  transfers between devices with their start and end apart: 4, of which 1 were waited for; matrix products, arithmetic and copies ran while one was open for 0% of the time, Pallas kernels for 5%

profile of v13, /device:TPU:0, one launch (start us, length us, event | category | flops | bytes accessed | tf_op | source)
XLA Modules:
  0.0 39.8 jit_solution(16234891289169946520)
XLA Ops:
  0.0 1.1 %shard_map.109 = (bf16[8,2,64,128]{3,2,1,0:T(8,128)(2,1)S(1)}, bf16[4,2,64,128]{3,2,1,0:T(8,128)(2,1)S(1)}) custom-call(bf16[8,2,64,128]{3,2,1,0:T(8,128)(2,1)} %own_ref.1, bf16[2,2,64,128]{3,2,1,0:T(8,128)(2,1)} %second_cache_ref.1, bf16[2,2,64,128]{3,2,1,0:T(8,128)(2,1)} %first_cache_ref.1), custom_call_target="tpu_custom_call" | custom-call | bytes 1048576 | tf_op jit(solution)/shard_map/pallas_call | solution.py:241
  1.1 3.0 %collective-permute-start = (bf16[4,2,64,128]{3,2,1,0:T(8,128)(2,1)S(1)}, bf16[4,2,64,128]{3,2,1,0:T(8,128)(2,1)S(1)}, u32[]{:S(2)}, u32[]{:S(2)}) collective-permute-start(bf16[4,2,64,128]{3,2,1,0:T(8,128)(2,1)S(1)} %get-tuple-element.13), channel_id=1, source_target_pairs={{0,8},{8,16},{16,24},{24,0},{1,9},{9,17},{17,25},{25,1},{2,10},{10... | collective-permute-start | bytes 393224 | tf_op jit(solution)/shard_map/ppermute | solution.py:299
  4.1 1.9 %shard_map.110 = (f32[32,1,256]{2,1,0:T(1,128)}, f32[6,1,128]{2,1,0:T(1,128)S(1)}, bf16[3,3,3,128,128]{4,3,2,1,0:T(8,128)(2,1)S(1)}) custom-call(bf16[8,2,64,128]{3,2,1,0:T(8,128)(2,1)S(1)} %get-tuple-element.14.own_ref, bf16[3,3,3,128,128]{4,3,2,1,0:T(8,128)(2,1)} %weight_ref.2, f32[1,128]{1,0:T(1,128)} %bitcast.6, f32[1,128]{1,0:T(1,128)} %bitcast.7, ...), custom_call_target="tpu_custom_call" | custom-call | bytes 1048576 | tf_op jit(solution)/shard_map/pallas_call | solution.py:241
  5.9 4.9 %all-to-all-start = ((f32[32,1,256]{2,1,0:T(1,128)}), f32[32,1,256]{2,1,0:T(1,128)S(1)}, u32[]{:S(2)}, u32[]{:S(2)}) async-start(f32[32,1,256]{2,1,0:T(1,128)} %get-tuple-element.15), calls=%async_computation | async-start | bytes 65536 | tf_op jit(solution)/shard_map/all_to_all | solution.py:304
  10.9 0.0 collective-permute-done
  10.9 0.7 %collective-permute-start.2 = (bf16[12,2,64,128]{3,2,1,0:T(8,128)(2,1)S(1)}, bf16[12,2,64,128]{3,2,1,0:T(8,128)(2,1)S(1)}, u32[]{:S(2)}, u32[]{:S(2)}) collective-permute-start(bf16[12,2,64,128]{3,2,1,0:T(8,128)(2,1)S(1)} %constant_dynamic-update-slice_fusion.own_ref), channel_id=1, source_target_pairs={{0,0},{1,2},{2,1},{3,4},{4,3},{5,6},{6,5},{7,7},{8,8},{9,10},{10,9... | collective-permute-start | bytes 1179656 | tf_op jit(solution)/shard_map/ppermute | solution.py:275
  11.6 3.2 %collective-permute-start.1 = (bf16[12,2,64,128]{3,2,1,0:T(8,128)(2,1)S(1)}, bf16[12,2,64,128]{3,2,1,0:T(8,128)(2,1)S(1)}, u32[]{:S(2)}, u32[]{:S(2)}) collective-permute-start(bf16[12,2,64,128]{3,2,1,0:T(8,128)(2,1)S(1)} %constant_dynamic-update-slice_fusion.own_ref), channel_id=1, source_target_pairs={{0,1},{1,0},{2,3},{3,2},{4,5},{5,4},{6,7},{7,6},{8,9},{9,8},{10,11... | collective-permute-start | bytes 1179656 | tf_op jit(solution)/shard_map/ppermute | solution.py:275
  14.8 3.3 %all-to-all-done.stats_ref = f32[32,1,256]{2,1,0:T(1,128)S(1)} async-done(((f32[32,1,256]{2,1,0:T(1,128)}), f32[32,1,256]{2,1,0:T(1,128)S(1)}, u32[]{:S(2)}, u32[]{:S(2)}) %all-to-all-start) | async-done | bytes 32800 | tf_op jit(solution)/shard_map/all_to_all | solution.py:304
  18.1 0.2 shard_map.111.affine_ref
  18.3 0.0 collective-permute-done.2.far_ref
  18.3 0.0 collective-permute-done.1.near_ref
  18.3 3.4 %shard_map.112 = (bf16[10,4,64,128]{3,2,1,0:T(8,128)(2,1)S(1)}, f32[32,1,256]{2,1,0:T(1,128)S(1)}) custom-call(bf16[12,2,64,128]{3,2,1,0:T(8,128)(2,1)S(1)} %constant_dynamic-update-slice_fusion.own_ref, bf16[12,2,64,128]{3,2,1,0:T(8,128)(2,1)S(1)} %collective-permute-done.1.near_ref, bf16[12,2,64,128]{3,2,1,0:T(8,128)(2,1)S(1)} %collective-permute-done.2.far_ref, ...), custom_call_target="tpu_custom_call" | custom-call | flops 1000000000 | bytes 1048576 | tf_op jit(solution)/shard_map/pallas_call | solution.py:241
  21.7 14.6 %all_to_all.10.stats_ref = f32[32,1,256]{2,1,0:T(1,128)S(1)} all-to-all(f32[32,1,256]{2,1,0:T(1,128)S(1)} %get-tuple-element.20), channel_id=1, replica_groups=mesh['section'=4,'rows'=8] {'section','rows'}, dimensions={0} | all-to-all | bytes 65536 | tf_op jit(solution)/shard_map/all_to_all | solution.py:304
  36.3 0.0 copy-start
  36.3 0.2 shard_map.113.affine_ref
  36.5 1.0 %copy-done = bf16[3,3,3,128,128]{4,3,2,1,0:T(8,128)(2,1)S(1)} copy-done((bf16[3,3,3,128,128]{4,3,2,1,0:T(8,128)(2,1)S(1)}, bf16[3,3,3,128,128]{4,3,2,1,0:T(8,128)(2,1)}, u32[]{:S(2)}) %copy-start) | copy-done | bytes 884760
  37.5 2.3 %shard_map.114 = bf16[8,2,64,128]{3,2,1,0:T(8,128)(2,1)} custom-call(bf16[10,4,64,128]{3,2,1,0:T(8,128)(2,1)S(1)} %get-tuple-element.19.middle_ref, f32[4,1,128]{2,1,0:T(1,128)S(1)} %shard_map.113.affine_ref, f32[6,1,128]{2,1,0:T(1,128)S(1)} %get-tuple-element.17.vectors_ref, bf16[3,3,3,128,128]{4,3,2,1,0:T(8,128)(2,1)S(1)} %copy-done, ...), custom_call_target="tpu_custom_call" | custom-call | flops 1000000000 | bytes 1048576 | tf_op jit(solution)/shard_map/pallas_call | solution.py:241
  (2 shorter events, 0.1 us)
Async XLA Ops:
  1.1 9.8 %collective-permute-start = (bf16[4,2,64,128]{3,2,1,0:T(8,128)(2,1)S(1)}, bf16[4,2,64,128]{3,2,1,0:T(8,128)(2,1)S(1)}, u32[]{:S(2)}, u32[]{:S(2)}) collective-permute-start(bf16[4,2,64,128]{3,2,1,0:T(8,128)(2,1)S(1)} %get-tuple-element.13), channel_id=1, source_target_pairs={{0,8},{8,16},{16,24},{24,0},{1,9},{9,17},{17,25},{25,1},{2,10},{10... | collective-permute-start | bytes 393224 | tf_op jit(solution)/shard_map/ppermute | solution.py:299
  5.9 12.2 %all-to-all-start = ((f32[32,1,256]{2,1,0:T(1,128)}), f32[32,1,256]{2,1,0:T(1,128)S(1)}, u32[]{:S(2)}, u32[]{:S(2)}) async-start(f32[32,1,256]{2,1,0:T(1,128)} %get-tuple-element.15), calls=%async_computation | async-start | bytes 65536 | tf_op jit(solution)/shard_map/all_to_all | solution.py:304
  10.9 7.3 %collective-permute-start.2 = (bf16[12,2,64,128]{3,2,1,0:T(8,128)(2,1)S(1)}, bf16[12,2,64,128]{3,2,1,0:T(8,128)(2,1)S(1)}, u32[]{:S(2)}, u32[]{:S(2)}) collective-permute-start(bf16[12,2,64,128]{3,2,1,0:T(8,128)(2,1)S(1)} %constant_dynamic-update-slice_fusion.own_ref), channel_id=1, source_target_pairs={{0,0},{1,2},{2,1},{3,4},{4,3},{5,6},{6,5},{7,7},{8,8},{9,10},{10,9... | collective-permute-start | bytes 1179656 | tf_op jit(solution)/shard_map/ppermute | solution.py:275
  11.6 6.7 %collective-permute-start.1 = (bf16[12,2,64,128]{3,2,1,0:T(8,128)(2,1)S(1)}, bf16[12,2,64,128]{3,2,1,0:T(8,128)(2,1)S(1)}, u32[]{:S(2)}, u32[]{:S(2)}) collective-permute-start(bf16[12,2,64,128]{3,2,1,0:T(8,128)(2,1)S(1)} %constant_dynamic-update-slice_fusion.own_ref), channel_id=1, source_target_pairs={{0,1},{1,0},{2,3},{3,2},{4,5},{5,4},{6,7},{7,6},{8,9},{9,8},{10,11... | collective-permute-start | bytes 1179656 | tf_op jit(solution)/shard_map/ppermute | solution.py:275
  36.3 1.2 %copy-start = (bf16[3,3,3,128,128]{4,3,2,1,0:T(8,128)(2,1)S(1)}, bf16[3,3,3,128,128]{4,3,2,1,0:T(8,128)(2,1)}, u32[]{:S(2)}) copy-start(bf16[3,3,3,128,128]{4,3,2,1,0:T(8,128)(2,1)} %weight_ref.3) | copy-start | bytes 2654212

commit v14 on v13

--- a/solution.py
+++ b/solution.py
@@ -24,12 +24,12 @@
         total = total + jnp.sum(away, axis=0, keepdims=True)
         squares = squares + jnp.sum(away * away, axis=0, keepdims=True)
     shift = total * (1.0 / cells)
-    return jnp.concatenate([pivot + shift, squares - total * shift], axis=1)
+    return jnp.concatenate([pivot + shift, squares - total * shift], axis=0)
 
 
 def affine(stats, cells, scale, shift):
-    devices, channels = stats.shape[0], scale.shape[-1]
-    means, squares = stats[:, :channels], stats[:, channels:]
+    devices, _, channels = stats.shape
+    means, squares = stats[:, 0], stats[:, 1]
     mean = jnp.sum(means, axis=0, keepdims=True) * (1.0 / devices)
     away = means - mean
     square = jnp.sum(squares + cells * (away * away), axis=0, keepdims=True)
@@ -138,7 +138,8 @@
     channels = own_ref.shape[-1]
     blocks = [own_ref[frame].astype(jnp.float32) for frame in range(own_ref.shape[0])]
     packed = moments([block.reshape(-1, channels) for block in blocks])
-    stats_ref[...] = jnp.broadcast_to(packed[None], stats_ref.shape)
+    for device in range(stats_ref.shape[0]):
+        stats_ref[device] = packed
     for load in loads:
         load.wait()
 
@@ -148,15 +149,17 @@
     scale, shift = vectors_ref[which], vectors_ref[which + 1]
     for index, span in enumerate((section, jnp.maximum(section - 1, 0))):
         stats = stats_ref[pl.ds(span * row_count, row_count)]
-        slope, offset = affine(stats.reshape(row_count, stats.shape[-1]), cells, scale, shift)
+        slope, offset = affine(stats, cells, scale, shift)
         affine_ref[2 * index] = slope
         affine_ref[2 * index + 1] = offset
 
 
 def first_kernel(
-    row_count, own_ref, near_ref, far_ref, affine_ref, vectors_ref, weight_ref, middle_ref,
-    sums_ref, field
+    row_count, own_ref, near_ref, far_ref, affine_ref, vectors_ref, weight_ref, next_ref,
+    middle_ref, sums_ref, next_copy, field, sem
 ):
+    load = pltpu.make_async_copy(next_ref, next_copy, sem)
+    load.start()
     section, row_at = lax.axis_index("section"), lax.axis_index("rows")
     frames, lines, columns, channels = own_ref.shape
     inner = frames - SPAN_HALO
@@ -199,7 +202,10 @@
             middle_ref[2:, line] = rounded[2:]
             if 1 <= line <= lines:
                 kept.append(rounded[2:].astype(jnp.float32).reshape(-1, channels))
-    sums_ref[...] = jnp.broadcast_to(moments(kept)[None], sums_ref.shape)
+    packed = moments(kept)
+    for device in range(sums_ref.shape[0]):
+        sums_ref[device] = packed
+    load.wait()
 
 
 def second_kernel(
@@ -265,7 +271,7 @@
     frames, lines, columns, channels = activations.shape
     sections, row_count = lax.axis_size("section"), lax.axis_size("rows")
     everyone = sections * row_count
-    stats_shape = jax.ShapeDtypeStruct((everyone, 1, 2 * channels), jnp.float32)
+    stats_shape = jax.ShapeDtypeStruct((everyone, 2, channels), jnp.float32)
     vectors = (norm1_scale, norm1_shift, conv1_bias, norm2_scale, norm2_shift, conv2_bias)
 
     near = [i ^ 1 for i in range(row_count)]
@@ -310,24 +316,29 @@
             flops=10**11,
         )
 
-    middle, sums = call(
+    middle, sums, weight = call(
         functools.partial(first_kernel, row_count),
         (
             jax.ShapeDtypeStruct((frames + 2, lines + 2, columns, channels), jnp.bfloat16),
             stats_shape,
+            jax.ShapeDtypeStruct(conv2_weight.shape, jnp.bfloat16),
         ),
-        [pltpu.VMEM((frames + SPAN_HALO, 3 * lines, columns, channels), jnp.bfloat16)],
+        [
+            pltpu.VMEM((frames + SPAN_HALO, 3 * lines, columns, channels), jnp.bfloat16),
+            pltpu.SemaphoreType.DMA,
+        ],
         (
             joined, across(joined, near), across(joined, far), coefficients(sums, 0), packed,
-            weight,
+            weight, conv2_weight,
         ),
+        in_place=(6,),
         flops=10**9,
     )
     return call(
         functools.partial(second_kernel, row_count),
         jax.ShapeDtypeStruct(activations.shape, jnp.bfloat16),
         [pltpu.VMEM((frames + 2, lines + 2, columns, channels), jnp.bfloat16)],
-        (middle, coefficients(sums, 3), packed, conv2_weight, own),
+        (middle, coefficients(sums, 3), packed, weight, own),
         flops=10**9,
     )
 

time: 40 us -> 39 us (0.975)
  local copies, waits for them, and re-layouts: 1.04 us -> 0.05 us
    unnamed x3 -> x1, local copies, waits for them, and re-layouts: 1 us -> 0.01 us
where the time goes in v14:
time: 39 us; the launch traced here: 38.8 us
  blocking collectives  14.6 us (37%)
  starting transfers between devices  11.8 us (30%)
  Pallas kernels  9 us (23%)
  waiting for transfers between devices  3.3 us (8%)
    all_to_all x1, blocking collectives, coefficients(): stats = lax.all_to_all(sums, ('section', 'rows'), 0, 0, tiled=True)  14.6 us
    pallas_call x6, Pallas kernels, call(): pl.pallas_call(kernel, out_shape=out_shape, in_specs=specs, out_specs=jax...  9 us
    all_to_all x1, starting transfers between devices, coefficients(): stats = lax.all_to_all(sums, ('section', 'rows'), 0, 0, tiled=True)  4.92 us
    ppermute x2, starting transfers between devices, across(): return lax.ppermute(block, 'rows', list(enumerate(partner)))  3.86 us
    all_to_all x1, waiting for transfers between devices, coefficients(): stats = lax.all_to_all(sums, ('section', 'rows'), 0, 0, tiled=True)  3.29 us
    ppermute x1, starting transfers between devices, on_device(): received = lax.ppermute(halo, 'section', ring)  2.99 us
  transfers between devices with their start and end apart: 4, of which 1 were waited for; matrix products, arithmetic and copies ran while one was open for 0% of the time, Pallas kernels for 5%

profile of v14, /device:TPU:0, one launch (start us, length us, event | category | flops | bytes accessed | tf_op | source)
XLA Modules:
  0.0 38.8 jit_solution(4989305248442841013)
XLA Ops:
  0.0 1.1 %shard_map.109 = (bf16[8,2,64,128]{3,2,1,0:T(8,128)(2,1)S(1)}, bf16[4,2,64,128]{3,2,1,0:T(8,128)(2,1)S(1)}) custom-call(bf16[8,2,64,128]{3,2,1,0:T(8,128)(2,1)} %own_ref.1, bf16[2,2,64,128]{3,2,1,0:T(8,128)(2,1)} %second_cache_ref.1, bf16[2,2,64,128]{3,2,1,0:T(8,128)(2,1)} %first_cache_ref.1), custom_call_target="tpu_custom_call" | custom-call | bytes 1048576 | tf_op jit(solution)/shard_map/pallas_call | solution.py:247
  1.1 3.0 %collective-permute-start = (bf16[4,2,64,128]{3,2,1,0:T(8,128)(2,1)S(1)}, bf16[4,2,64,128]{3,2,1,0:T(8,128)(2,1)S(1)}, u32[]{:S(2)}, u32[]{:S(2)}) collective-permute-start(bf16[4,2,64,128]{3,2,1,0:T(8,128)(2,1)S(1)} %get-tuple-element.14), channel_id=1, source_target_pairs={{0,8},{8,16},{16,24},{24,0},{1,9},{9,17},{17,25},{25,1},{2,10},{10... | collective-permute-start | bytes 393224 | tf_op jit(solution)/shard_map/ppermute | solution.py:305
  4.1 1.9 %shard_map.110 = (f32[32,2,128]{2,1,0:T(2,128)}, f32[6,1,128]{2,1,0:T(1,128)S(1)}, bf16[3,3,3,128,128]{4,3,2,1,0:T(8,128)(2,1)S(1)}) custom-call(bf16[8,2,64,128]{3,2,1,0:T(8,128)(2,1)S(1)} %get-tuple-element.15.own_ref, bf16[3,3,3,128,128]{4,3,2,1,0:T(8,128)(2,1)} %weight_ref.1, f32[1,128]{1,0:T(1,128)} %bitcast.6, f32[1,128]{1,0:T(1,128)} %bitcast.7, ...), custom_call_target="tpu_custom_call" | custom-call | bytes 1048576 | tf_op jit(solution)/shard_map/pallas_call | solution.py:247
  5.9 4.9 %all-to-all-start = ((f32[32,2,128]{2,1,0:T(2,128)}), f32[32,2,128]{2,1,0:T(2,128)S(1)}, u32[]{:S(2)}, u32[]{:S(2)}) async-start(f32[32,2,128]{2,1,0:T(2,128)} %get-tuple-element.16), calls=%async_computation | async-start | bytes 65536 | tf_op jit(solution)/shard_map/all_to_all | solution.py:310
  10.9 0.0 collective-permute-done
  10.9 0.7 %collective-permute-start.2 = (bf16[12,2,64,128]{3,2,1,0:T(8,128)(2,1)S(1)}, bf16[12,2,64,128]{3,2,1,0:T(8,128)(2,1)S(1)}, u32[]{:S(2)}, u32[]{:S(2)}) collective-permute-start(bf16[12,2,64,128]{3,2,1,0:T(8,128)(2,1)S(1)} %constant_dynamic-update-slice_fusion.own_ref), channel_id=1, source_target_pairs={{0,0},{1,2},{2,1},{3,4},{4,3},{5,6},{6,5},{7,7},{8,8},{9,10},{10,9... | collective-permute-start | bytes 1179656 | tf_op jit(solution)/shard_map/ppermute | solution.py:281
  11.6 3.2 %collective-permute-start.1 = (bf16[12,2,64,128]{3,2,1,0:T(8,128)(2,1)S(1)}, bf16[12,2,64,128]{3,2,1,0:T(8,128)(2,1)S(1)}, u32[]{:S(2)}, u32[]{:S(2)}) collective-permute-start(bf16[12,2,64,128]{3,2,1,0:T(8,128)(2,1)S(1)} %constant_dynamic-update-slice_fusion.own_ref), channel_id=1, source_target_pairs={{0,1},{1,0},{2,3},{3,2},{4,5},{5,4},{6,7},{7,6},{8,9},{9,8},{10,11... | collective-permute-start | bytes 1179656 | tf_op jit(solution)/shard_map/ppermute | solution.py:281
  14.8 3.3 %all-to-all-done.stats_ref = f32[32,2,128]{2,1,0:T(2,128)S(1)} async-done(((f32[32,2,128]{2,1,0:T(2,128)}), f32[32,2,128]{2,1,0:T(2,128)S(1)}, u32[]{:S(2)}, u32[]{:S(2)}) %all-to-all-start) | async-done | bytes 32800 | tf_op jit(solution)/shard_map/all_to_all | solution.py:310
  18.1 0.2 shard_map.111.affine_ref
  18.3 0.0 collective-permute-done.2.far_ref
  18.3 0.0 collective-permute-done.1.near_ref
  18.3 3.4 %shard_map.112 = (bf16[10,4,64,128]{3,2,1,0:T(8,128)(2,1)S(1)}, f32[32,2,128]{2,1,0:T(2,128)S(1)}, bf16[3,3,3,128,128]{4,3,2,1,0:T(8,128)(2,1)S(1)}) custom-call(bf16[12,2,64,128]{3,2,1,0:T(8,128)(2,1)S(1)} %constant_dynamic-update-slice_fusion.own_ref, bf16[12,2,64,128]{3,2,1,0:T(8,128)(2,1)S(1)} %collective-permute-done.1.near_ref, ...), custom_call_target="tpu_custom_call" | custom-call | flops 1000000000 | bytes 1048576 | tf_op jit(solution)/shard_map/pallas_call | solution.py:247
  21.7 14.6 %all_to_all.10.stats_ref = f32[32,2,128]{2,1,0:T(2,128)S(1)} all-to-all(f32[32,2,128]{2,1,0:T(2,128)S(1)} %get-tuple-element.21), channel_id=1, replica_groups=mesh['section'=4,'rows'=8] {'section','rows'}, dimensions={0} | all-to-all | bytes 65536 | tf_op jit(solution)/shard_map/all_to_all | solution.py:310
  36.3 0.2 shard_map.113.affine_ref
  36.5 2.3 %shard_map.114 = bf16[8,2,64,128]{3,2,1,0:T(8,128)(2,1)} custom-call(bf16[10,4,64,128]{3,2,1,0:T(8,128)(2,1)S(1)} %get-tuple-element.20.middle_ref, f32[4,1,128]{2,1,0:T(1,128)S(1)} %shard_map.113.affine_ref, f32[6,1,128]{2,1,0:T(1,128)S(1)} %get-tuple-element.18.vectors_ref, bf16[3,3,3,128,128]{4,3,2,1,0:T(8,128)(2,1)S(1)} %get-tuple-element.22.weight_ref, ...), custom_call_target="tpu_custom_call" | custom-call | flops 1000000000 | bytes 1048576 | tf_op jit(solution)/shard_map/pallas_call | solution.py:247
  (2 shorter events, 0.1 us)
Async XLA Ops:
  1.1 9.8 %collective-permute-start = (bf16[4,2,64,128]{3,2,1,0:T(8,128)(2,1)S(1)}, bf16[4,2,64,128]{3,2,1,0:T(8,128)(2,1)S(1)}, u32[]{:S(2)}, u32[]{:S(2)}) collective-permute-start(bf16[4,2,64,128]{3,2,1,0:T(8,128)(2,1)S(1)} %get-tuple-element.14), channel_id=1, source_target_pairs={{0,8},{8,16},{16,24},{24,0},{1,9},{9,17},{17,25},{25,1},{2,10},{10... | collective-permute-start | bytes 393224 | tf_op jit(solution)/shard_map/ppermute | solution.py:305
  5.9 12.2 %all-to-all-start = ((f32[32,2,128]{2,1,0:T(2,128)}), f32[32,2,128]{2,1,0:T(2,128)S(1)}, u32[]{:S(2)}, u32[]{:S(2)}) async-start(f32[32,2,128]{2,1,0:T(2,128)} %get-tuple-element.16), calls=%async_computation | async-start | bytes 65536 | tf_op jit(solution)/shard_map/all_to_all | solution.py:310
  10.9 7.3 %collective-permute-start.2 = (bf16[12,2,64,128]{3,2,1,0:T(8,128)(2,1)S(1)}, bf16[12,2,64,128]{3,2,1,0:T(8,128)(2,1)S(1)}, u32[]{:S(2)}, u32[]{:S(2)}) collective-permute-start(bf16[12,2,64,128]{3,2,1,0:T(8,128)(2,1)S(1)} %constant_dynamic-update-slice_fusion.own_ref), channel_id=1, source_target_pairs={{0,0},{1,2},{2,1},{3,4},{4,3},{5,6},{6,5},{7,7},{8,8},{9,10},{10,9... | collective-permute-start | bytes 1179656 | tf_op jit(solution)/shard_map/ppermute | solution.py:281
  11.6 6.7 %collective-permute-start.1 = (bf16[12,2,64,128]{3,2,1,0:T(8,128)(2,1)S(1)}, bf16[12,2,64,128]{3,2,1,0:T(8,128)(2,1)S(1)}, u32[]{:S(2)}, u32[]{:S(2)}) collective-permute-start(bf16[12,2,64,128]{3,2,1,0:T(8,128)(2,1)S(1)} %constant_dynamic-update-slice_fusion.own_ref), channel_id=1, source_target_pairs={{0,1},{1,0},{2,3},{3,2},{4,5},{5,4},{6,7},{7,6},{8,9},{9,8},{10,11... | collective-permute-start | bytes 1179656 | tf_op jit(solution)/shard_map/ppermute | solution.py:281

commit v15 on v14

--- a/solution.py
+++ b/solution.py
@@ -144,7 +144,8 @@
         load.wait()
 
 
-def affine_kernel(row_count, cells, which, stats_ref, vectors_ref, affine_ref):
+def affine_kernel(row_count, cells, which, stats_ref, vectors_ref, *rest):
+    affine_ref = rest[-1]
     section = lax.axis_index("section")
     scale, shift = vectors_ref[which], vectors_ref[which + 1]
     for index, span in enumerate((section, jnp.maximum(section - 1, 0))):
@@ -155,14 +156,13 @@
 
 
 def first_kernel(
-    row_count, own_ref, near_ref, far_ref, affine_ref, vectors_ref, weight_ref, next_ref,
-    middle_ref, sums_ref, next_copy, field, sem
+    row_count, own_ref, near_ref, far_ref, halo_ref, halo_near_ref, halo_far_ref, affine_ref,
+    vectors_ref, weight_ref, next_ref, middle_ref, sums_ref, next_copy, field, sem
 ):
     load = pltpu.make_async_copy(next_ref, next_copy, sem)
     load.start()
     section, row_at = lax.axis_index("section"), lax.axis_index("rows")
-    frames, lines, columns, channels = own_ref.shape
-    inner = frames - SPAN_HALO
+    inner, lines, columns, channels = own_ref.shape
     slope, offset, slope_before, offset_before = (affine_ref[row] for row in range(4))
     even = row_at % 2 == 0
     at_start = section == 0
@@ -170,11 +170,11 @@
     def fill(line):
         side, local = divmod(line, lines)
         if side == 1:
-            block = own_ref[:, local]
+            halo, body = halo_ref[:, local], own_ref[:, local]
         else:
             near_side = even if side == 2 else jnp.logical_not(even)
-            block = jnp.where(near_side, near_ref[:, local], far_ref[:, local])
-        halo, body = block[:SPAN_HALO], block[SPAN_HALO:]
+            halo = jnp.where(near_side, halo_near_ref[:, local], halo_far_ref[:, local])
+            body = jnp.where(near_side, near_ref[:, local], far_ref[:, local])
         behind = activate(halo, slope_before, offset_before).astype(jnp.bfloat16)
         behind = jnp.where(at_start, halo, behind)
         ahead = activate(body, slope, offset).astype(jnp.bfloat16)
@@ -235,11 +235,13 @@
             out_ref[:, line] = (result + own_ref[:, line].astype(jnp.float32)).astype(jnp.bfloat16)
 
 
-def call(kernel, out_shape, scratch, operands, in_place=(), flops=0):
+def call(kernel, out_shape, scratch, operands, in_place=(), unread=(), flops=0):
     vmem = pl.BlockSpec(memory_space=pltpu.VMEM)
     specs = [vmem] * len(operands)
     for index in in_place:
         specs[index] = pl.BlockSpec(memory_space=pltpu.HBM)
+    for index in unread:
+        specs[index] = pl.BlockSpec(memory_space=pl.ANY)
     operands = [
         pltpu.with_memory_space_constraint(operand, pltpu.HBM) if index in in_place else operand
         for index, operand in enumerate(operands)
@@ -301,18 +303,21 @@
         [pltpu.SemaphoreType.DMA((1 + len(vectors),))],
         (own, conv1_weight) + tuple(vector.reshape(1, channels) for vector in vectors),
         in_place=range(1, 2 + len(vectors)),
+        flops=10**11,
     )
     received = lax.ppermute(halo, "section", ring)
     received, _ = lax.optimization_barrier((received, sums))
-    joined = jnp.concatenate([received, own], axis=0)
-
-    def coefficients(sums, which):
+    beside = [across(activations, near), across(activations, far)]
+    behind = [received, across(received, near), across(received, far)]
+
+    def coefficients(sums, which, *after):
         stats = lax.all_to_all(sums, ("section", "rows"), 0, 0, tiled=True)
         return call(
             functools.partial(affine_kernel, row_count, frames * lines * columns, which),
             jax.ShapeDtypeStruct((4, 1, channels), jnp.float32),
             [],
-            (stats, packed),
+            (stats, packed, *after),
+            unread=range(2, 2 + len(after)),
             flops=10**11,
         )
 
@@ -328,10 +333,10 @@
             pltpu.SemaphoreType.DMA,
         ],
         (
-            joined, across(joined, near), across(joined, far), coefficients(sums, 0), packed,
-            weight, conv2_weight,
+            own, *beside, *behind, coefficients(sums, 0, *beside), packed, weight,
+            conv2_weight,
         ),
-        in_place=(6,),
+        in_place=(9,),
         flops=10**9,
     )
     return call(

time: 39 us -> 38.8 us (level)
  blocking collectives: 14.6 us -> 11.7 us
  starting transfers between devices: 11.8 us -> 14.4 us
    ppermute x2 -> x4, starting transfers between devices: 3.86 us -> 8.97 us  [across(): return lax.ppermute(block, 'rows', list(enumerate(partner)))]
    all_to_all x1, blocking collectives: 14.6 us -> 11.7 us  [coefficients(): stats = lax.all_to_all(sums, ('section', 'rows'), 0, 0, tiled=True)]
    ppermute x1, starting transfers between devices: 2.99 us -> 1.54 us  [on_device(): received = lax.ppermute(halo, 'section', ring)]
    all_to_all x1, starting transfers between devices: 4.92 us -> 3.91 us  [coefficients(): stats = lax.all_to_all(sums, ('section', 'rows'), 0, 0, tiled=True)]
  transfers between devices with their start and end apart: 4 -> 6, of which waited for: 1 -> 1; matrix products, arithmetic and copies ran while one was open for 0% -> 0% of each run, Pallas kernels for 5% -> 8%
where the time goes in v15:
time: 38.8 us; the launch traced here: 38.6 us
  starting transfers between devices  14.4 us (37%)
  blocking collectives  11.7 us (30%)
  Pallas kernels  9 us (23%)
  waiting for transfers between devices  3.37 us (9%)
    all_to_all x1, blocking collectives, coefficients(): stats = lax.all_to_all(sums, ('section', 'rows'), 0, 0, tiled=True)  11.7 us
    pallas_call x6, Pallas kernels, call(): pl.pallas_call(kernel, out_shape=out_shape, in_specs=specs, out_specs=jax...  9 us
    ppermute x4, starting transfers between devices, across(): return lax.ppermute(block, 'rows', list(enumerate(partner)))  8.97 us
    all_to_all x1, starting transfers between devices, coefficients(): stats = lax.all_to_all(sums, ('section', 'rows'), 0, 0, tiled=True)  3.91 us
    all_to_all x1, waiting for transfers between devices, coefficients(): stats = lax.all_to_all(sums, ('section', 'rows'), 0, 0, tiled=True)  3.36 us
    ppermute x1, starting transfers between devices, on_device(): received = lax.ppermute(halo, 'section', ring)  1.54 us
  transfers between devices with their start and end apart: 6, of which 1 were waited for; matrix products, arithmetic and copies ran while one was open for 0% of the time, Pallas kernels for 8%

profile of v15, /device:TPU:0, one launch (start us, length us, event | category | flops | bytes accessed | tf_op | source)
XLA Modules:
  0.0 38.6 jit_solution(9561391052476735713)
XLA Ops:
  0.0 1.6 %collective-permute-start.1 = (bf16[8,2,64,128]{3,2,1,0:T(8,128)(2,1)}, bf16[8,2,64,128]{3,2,1,0:T(8,128)(2,1)S(1)}, u32[]{:S(2)}, u32[]{:S(2)}) collective-permute-start(bf16[8,2,64,128]{3,2,1,0:T(8,128)(2,1)} %own_ref.1), channel_id=1, source_target_pairs={{0,0},{1,2},{2,1},{3,4},{4,3},{5,6},{6,5},{7,7},{8,8},{9,10},{10,9... | collective-permute-start | bytes 786440 | tf_op jit(solution)/shard_map/ppermute | solution.py:283
  1.6 3.5 %collective-permute-start = (bf16[8,2,64,128]{3,2,1,0:T(8,128)(2,1)}, bf16[8,2,64,128]{3,2,1,0:T(8,128)(2,1)S(1)}, u32[]{:S(2)}, u32[]{:S(2)}) collective-permute-start(bf16[8,2,64,128]{3,2,1,0:T(8,128)(2,1)} %own_ref.1), channel_id=1, source_target_pairs={{0,1},{1,0},{2,3},{3,2},{4,5},{5,4},{6,7},{7,6},{8,9},{9,8},{10,11... | collective-permute-start | bytes 786440 | tf_op jit(solution)/shard_map/ppermute | solution.py:283
  5.1 1.1 %shard_map.109 = (bf16[8,2,64,128]{3,2,1,0:T(8,128)(2,1)S(1)}, bf16[4,2,64,128]{3,2,1,0:T(8,128)(2,1)S(1)}) custom-call(bf16[8,2,64,128]{3,2,1,0:T(8,128)(2,1)} %own_ref.1, bf16[2,2,64,128]{3,2,1,0:T(8,128)(2,1)} %second_cache_ref.1, bf16[2,2,64,128]{3,2,1,0:T(8,128)(2,1)} %first_cache_ref.1), custom_call_target="tpu_custom_call" | custom-call | bytes 1048576 | tf_op jit(solution)/shard_map/pallas_call | solution.py:249
  6.2 1.5 %collective-permute-start.2 = (bf16[4,2,64,128]{3,2,1,0:T(8,128)(2,1)S(1)}, bf16[4,2,64,128]{3,2,1,0:T(8,128)(2,1)S(1)}, u32[]{:S(2)}, u32[]{:S(2)}) collective-permute-start(bf16[4,2,64,128]{3,2,1,0:T(8,128)(2,1)S(1)} %get-tuple-element.15), channel_id=1, source_target_pairs={{0,8},{8,16},{16,24},{24,0},{1,9},{9,17},{17,25},{25,1},{2,10},{10... | collective-permute-start | bytes 393224 | tf_op jit(solution)/shard_map/ppermute | solution.py:308
  7.7 1.9 %shard_map.110 = (f32[32,2,128]{2,1,0:T(2,128)}, f32[6,1,128]{2,1,0:T(1,128)S(1)}, bf16[3,3,3,128,128]{4,3,2,1,0:T(8,128)(2,1)S(1)}) custom-call(bf16[8,2,64,128]{3,2,1,0:T(8,128)(2,1)S(1)} %get-tuple-element.14.own_ref, bf16[3,3,3,128,128]{4,3,2,1,0:T(8,128)(2,1)} %weight_ref.1, f32[1,128]{1,0:T(1,128)} %bitcast.6, f32[1,128]{1,0:T(1,128)} %bitcast.7, ...), custom_call_target="tpu_custom_call" | custom-call | flops 99999997952 | bytes 1048576 | tf_op jit(solution)/shard_map/pallas_call | solution.py:249
  9.6 3.9 %all-to-all-start = ((f32[32,2,128]{2,1,0:T(2,128)}), f32[32,2,128]{2,1,0:T(2,128)S(1)}, u32[]{:S(2)}, u32[]{:S(2)}) async-start(f32[32,2,128]{2,1,0:T(2,128)} %get-tuple-element.16), calls=%async_computation | async-start | bytes 65536 | tf_op jit(solution)/shard_map/all_to_all | solution.py:314
  13.5 0.0 collective-permute-done.2.halo_ref
  13.5 0.7 %collective-permute-start.4 = (bf16[4,2,64,128]{3,2,1,0:T(8,128)(2,1)S(1)}, bf16[4,2,64,128]{3,2,1,0:T(8,128)(2,1)S(1)}, u32[]{:S(2)}, u32[]{:S(2)}) collective-permute-start(bf16[4,2,64,128]{3,2,1,0:T(8,128)(2,1)S(1)} %collective-permute-done.2.halo_ref), channel_id=1, source_target_pairs={{0,0},{1,2},{2,1},{3,4},{4,3},{5,6},{6,5},{7,7},{8,8},{9,10},{10,9... | collective-permute-start | bytes 393224 | tf_op jit(solution)/shard_map/ppermute | solution.py:283
  14.2 3.2 %collective-permute-start.3 = (bf16[4,2,64,128]{3,2,1,0:T(8,128)(2,1)S(1)}, bf16[4,2,64,128]{3,2,1,0:T(8,128)(2,1)S(1)}, u32[]{:S(2)}, u32[]{:S(2)}) collective-permute-start(bf16[4,2,64,128]{3,2,1,0:T(8,128)(2,1)S(1)} %collective-permute-done.2.halo_ref), channel_id=1, source_target_pairs={{0,1},{1,0},{2,3},{3,2},{4,5},{5,4},{6,7},{7,6},{8,9},{9,8},{10,11... | collective-permute-start | bytes 393224 | tf_op jit(solution)/shard_map/ppermute | solution.py:283
  17.4 3.4 %all-to-all-done.stats_ref = f32[32,2,128]{2,1,0:T(2,128)S(1)} async-done(((f32[32,2,128]{2,1,0:T(2,128)}), f32[32,2,128]{2,1,0:T(2,128)S(1)}, u32[]{:S(2)}, u32[]{:S(2)}) %all-to-all-start) | async-done | bytes 32800 | tf_op jit(solution)/shard_map/all_to_all | solution.py:314
  20.7 0.0 collective-permute-done.1.rest_1_.far_ref
  20.7 0.0 collective-permute-done.rest_0_.near_ref
  20.8 0.2 shard_map.111.affine_ref
  20.9 0.0 collective-permute-done.4.halo_far_ref
  20.9 0.0 collective-permute-done.3.halo_near_ref
  21.0 3.4 %shard_map.112 = (bf16[10,4,64,128]{3,2,1,0:T(8,128)(2,1)S(1)}, f32[32,2,128]{2,1,0:T(2,128)S(1)}, bf16[3,3,3,128,128]{4,3,2,1,0:T(8,128)(2,1)S(1)}) custom-call(bf16[8,2,64,128]{3,2,1,0:T(8,128)(2,1)S(1)} %get-tuple-element.14.own_ref, bf16[8,2,64,128]{3,2,1,0:T(8,128)(2,1)S(1)} %collective-permute-done.rest_0_.near_ref, ...), custom_call_target="tpu_custom_call" | custom-call | flops 1000000000 | bytes 1048576 | tf_op jit(solution)/shard_map/pallas_call | solution.py:249
  24.4 11.7 %all_to_all.10.stats_ref = f32[32,2,128]{2,1,0:T(2,128)S(1)} all-to-all(f32[32,2,128]{2,1,0:T(2,128)S(1)} %get-tuple-element.21), channel_id=1, replica_groups=mesh['section'=4,'rows'=8] {'section','rows'}, dimensions={0} | all-to-all | bytes 65536 | tf_op jit(solution)/shard_map/all_to_all | solution.py:314
  36.1 0.2 shard_map.113.affine_ref
  36.3 2.3 %shard_map.114 = bf16[8,2,64,128]{3,2,1,0:T(8,128)(2,1)} custom-call(bf16[10,4,64,128]{3,2,1,0:T(8,128)(2,1)S(1)} %get-tuple-element.20.middle_ref, f32[4,1,128]{2,1,0:T(1,128)S(1)} %shard_map.113.affine_ref, f32[6,1,128]{2,1,0:T(1,128)S(1)} %get-tuple-element.18.vectors_ref, bf16[3,3,3,128,128]{4,3,2,1,0:T(8,128)(2,1)S(1)} %get-tuple-element.22.weight_ref, ...), custom_call_target="tpu_custom_call" | custom-call | flops 1000000000 | bytes 1048576 | tf_op jit(solution)/shard_map/pallas_call | solution.py:249
Async XLA Ops:
  0.0 20.7 %collective-permute-start.1 = (bf16[8,2,64,128]{3,2,1,0:T(8,128)(2,1)}, bf16[8,2,64,128]{3,2,1,0:T(8,128)(2,1)S(1)}, u32[]{:S(2)}, u32[]{:S(2)}) collective-permute-start(bf16[8,2,64,128]{3,2,1,0:T(8,128)(2,1)} %own_ref.1), channel_id=1, source_target_pairs={{0,0},{1,2},{2,1},{3,4},{4,3},{5,6},{6,5},{7,7},{8,8},{9,10},{10,9... | collective-permute-start | bytes 786440 | tf_op jit(solution)/shard_map/ppermute | solution.py:283
  1.6 19.2 %collective-permute-start = (bf16[8,2,64,128]{3,2,1,0:T(8,128)(2,1)}, bf16[8,2,64,128]{3,2,1,0:T(8,128)(2,1)S(1)}, u32[]{:S(2)}, u32[]{:S(2)}) collective-permute-start(bf16[8,2,64,128]{3,2,1,0:T(8,128)(2,1)} %own_ref.1), channel_id=1, source_target_pairs={{0,1},{1,0},{2,3},{3,2},{4,5},{5,4},{6,7},{7,6},{8,9},{9,8},{10,11... | collective-permute-start | bytes 786440 | tf_op jit(solution)/shard_map/ppermute | solution.py:283
  6.2 7.3 %collective-permute-start.2 = (bf16[4,2,64,128]{3,2,1,0:T(8,128)(2,1)S(1)}, bf16[4,2,64,128]{3,2,1,0:T(8,128)(2,1)S(1)}, u32[]{:S(2)}, u32[]{:S(2)}) collective-permute-start(bf16[4,2,64,128]{3,2,1,0:T(8,128)(2,1)S(1)} %get-tuple-element.15), channel_id=1, source_target_pairs={{0,8},{8,16},{16,24},{24,0},{1,9},{9,17},{17,25},{25,1},{2,10},{10... | collective-permute-start | bytes 393224 | tf_op jit(solution)/shard_map/ppermute | solution.py:308
  9.6 11.2 %all-to-all-start = ((f32[32,2,128]{2,1,0:T(2,128)}), f32[32,2,128]{2,1,0:T(2,128)S(1)}, u32[]{:S(2)}, u32[]{:S(2)}) async-start(f32[32,2,128]{2,1,0:T(2,128)} %get-tuple-element.16), calls=%async_computation | async-start | bytes 65536 | tf_op jit(solution)/shard_map/all_to_all | solution.py:314
  13.5 7.4 %collective-permute-start.4 = (bf16[4,2,64,128]{3,2,1,0:T(8,128)(2,1)S(1)}, bf16[4,2,64,128]{3,2,1,0:T(8,128)(2,1)S(1)}, u32[]{:S(2)}, u32[]{:S(2)}) collective-permute-start(bf16[4,2,64,128]{3,2,1,0:T(8,128)(2,1)S(1)} %collective-permute-done.2.halo_ref), channel_id=1, source_target_pairs={{0,0},{1,2},{2,1},{3,4},{4,3},{5,6},{6,5},{7,7},{8,8},{9,10},{10,9... | collective-permute-start | bytes 393224 | tf_op jit(solution)/shard_map/ppermute | solution.py:283
  14.2 6.8 %collective-permute-start.3 = (bf16[4,2,64,128]{3,2,1,0:T(8,128)(2,1)S(1)}, bf16[4,2,64,128]{3,2,1,0:T(8,128)(2,1)S(1)}, u32[]{:S(2)}, u32[]{:S(2)}) collective-permute-start(bf16[4,2,64,128]{3,2,1,0:T(8,128)(2,1)S(1)} %collective-permute-done.2.halo_ref), channel_id=1, source_target_pairs={{0,1},{1,0},{2,3},{3,2},{4,5},{5,4},{6,7},{7,6},{8,9},{9,8},{10,11... | collective-permute-start | bytes 393224 | tf_op jit(solution)/shard_map/ppermute | solution.py:283

commit v16 on v15

--- a/solution.py
+++ b/solution.py
@@ -138,8 +138,7 @@
     channels = own_ref.shape[-1]
     blocks = [own_ref[frame].astype(jnp.float32) for frame in range(own_ref.shape[0])]
     packed = moments([block.reshape(-1, channels) for block in blocks])
-    for device in range(stats_ref.shape[0]):
-        stats_ref[device] = packed
+    stats_ref[0] = packed
     for load in loads:
         load.wait()
 
@@ -149,7 +148,10 @@
     section = lax.axis_index("section")
     scale, shift = vectors_ref[which], vectors_ref[which + 1]
     for index, span in enumerate((section, jnp.maximum(section - 1, 0))):
-        stats = stats_ref[pl.ds(span * row_count, row_count)]
+        if stats_ref.shape[1] == 4:
+            stats = stats_ref[:, 2 * index : 2 * index + 2]
+        else:
+            stats = stats_ref[pl.ds(span * row_count, row_count)]
         slope, offset = affine(stats, cells, scale, shift)
         affine_ref[2 * index] = slope
         affine_ref[2 * index + 1] = offset
@@ -296,7 +298,7 @@
     sums, packed, weight = call(
         stats_kernel,
         (
-            stats_shape,
+            jax.ShapeDtypeStruct((1, 2, channels), jnp.float32),
             jax.ShapeDtypeStruct((len(vectors), 1, channels), jnp.float32),
             jax.ShapeDtypeStruct(conv1_weight.shape, jnp.bfloat16),
         ),
@@ -310,8 +312,11 @@
     beside = [across(activations, near), across(activations, far)]
     behind = [received, across(received, near), across(received, far)]
 
-    def coefficients(sums, which, *after):
-        stats = lax.all_to_all(sums, ("section", "rows"), 0, 0, tiled=True)
+    both = jnp.concatenate([sums, lax.ppermute(sums, "section", ring)], axis=1)
+    both = jnp.broadcast_to(both, (row_count,) + both.shape[1:])
+
+    def coefficients(sums, axes, which, *after):
+        stats = lax.all_to_all(sums, axes, 0, 0, tiled=True)
         return call(
             functools.partial(affine_kernel, row_count, frames * lines * columns, which),
             jax.ShapeDtypeStruct((4, 1, channels), jnp.float32),
@@ -333,7 +338,7 @@
             pltpu.SemaphoreType.DMA,
         ],
         (
-            own, *beside, *behind, coefficients(sums, 0, *beside), packed, weight,
+            own, *beside, *behind, coefficients(both, "rows", 0, *beside), packed, weight,
             conv2_weight,
         ),
         in_place=(9,),
@@ -343,7 +348,7 @@
         functools.partial(second_kernel, row_count),
         jax.ShapeDtypeStruct(activations.shape, jnp.bfloat16),
         [pltpu.VMEM((frames + 2, lines + 2, columns, channels), jnp.bfloat16)],
-        (middle, coefficients(sums, 3), packed, weight, own),
+        (middle, coefficients(sums, ("section", "rows"), 3), packed, weight, own),
         flops=10**9,
     )
 

time: 38.8 us -> 41.1 us (1.059)
  starting transfers between devices: 14.4 us -> 16.1 us
  blocking collectives: 11.7 us -> 12.6 us
  local copies, waits for them, and re-layouts: 0 us -> 0.61 us
  Pallas kernels: 9 us -> 8.39 us
    all_to_all x1, waiting for transfers between devices: 3.36 us -> 1.62 us  [coefficients(): stats = lax.all_to_all(sums, axes, 0, 0, tiled=True)]
    ppermute x0 -> x1, starting transfers between devices: none -> 1.54 us  [on_device(): both = jnp.concatenate([sums, lax.ppermute(sums, 'section', ring)], axis=1)]
    ppermute x0 -> x1, waiting for transfers between devices: none -> 1.48 us  [on_device(): both = jnp.concatenate([sums, lax.ppermute(sums, 'section', ring)], axis=1)]
    all_to_all x1, blocking collectives: 11.7 us -> 12.6 us  [coefficients(): stats = lax.all_to_all(sums, axes, 0, 0, tiled=True)]
    pallas_call x6, Pallas kernels: 9 us -> 8.39 us  [call(): pl.pallas_call(kernel, out_shape=out_shape, in_specs=specs, out_specs=jax...]
    broadcast_in_dim x0 -> x1, local copies, waits for them, and re-layouts: none -> 0.61 us  [on_device(): both = jnp.broadcast_to(both, (row_count,) + both.shape[1:])]
  transfers between devices with their start and end apart: 6 -> 7, of which waited for: 1 -> 2; matrix products, arithmetic and copies ran while one was open for 0% -> 2% of each run, Pallas kernels for 8% -> 6%
where the time goes in v16:
time: 41.1 us; the launch traced here: 40.9 us
  starting transfers between devices  16.1 us (39%)
  blocking collectives  12.6 us (31%)
  Pallas kernels  8.39 us (20%)
  waiting for transfers between devices  3.12 us (8%)
  local copies, waits for them, and re-layouts  0.61 us (1%)
    all_to_all x1, blocking collectives, coefficients(): stats = lax.all_to_all(sums, axes, 0, 0, tiled=True)  12.6 us
    ppermute x4, starting transfers between devices, across(): return lax.ppermute(block, 'rows', list(enumerate(partner)))  9.2 us
    pallas_call x6, Pallas kernels, call(): pl.pallas_call(kernel, out_shape=out_shape, in_specs=specs, out_specs=jax...  8.39 us
    all_to_all x1, starting transfers between devices, coefficients(): stats = lax.all_to_all(sums, axes, 0, 0, tiled=True)  3.87 us
    all_to_all x1, waiting for transfers between devices, coefficients(): stats = lax.all_to_all(sums, axes, 0, 0, tiled=True)  1.62 us
    ppermute x1, starting transfers between devices, on_device(): both = jnp.concatenate([sums, lax.ppermute(sums, 'section', ring)], axis=1)  1.54 us
    ppermute x1, starting transfers between devices, on_device(): received = lax.ppermute(halo, 'section', ring)  1.49 us
    ppermute x1, waiting for transfers between devices, on_device(): both = jnp.concatenate([sums, lax.ppermute(sums, 'section', ring)], axis=1)  1.48 us
  transfers between devices with their start and end apart: 7, of which 2 were waited for; matrix products, arithmetic and copies ran while one was open for 2% of the time, Pallas kernels for 6%

profile of v16, /device:TPU:0, one launch (start us, length us, event | category | flops | bytes accessed | tf_op | source)
XLA Modules:
  0.0 40.9 jit_solution(2873571365352251124)
XLA Ops:
  0.0 1.6 %collective-permute-start.1 = (bf16[8,2,64,128]{3,2,1,0:T(8,128)(2,1)}, bf16[8,2,64,128]{3,2,1,0:T(8,128)(2,1)S(1)}, u32[]{:S(2)}, u32[]{:S(2)}) collective-permute-start(bf16[8,2,64,128]{3,2,1,0:T(8,128)(2,1)} %own_ref.1), channel_id=1, source_target_pairs={{0,0},{1,2},{2,1},{3,4},{4,3},{5,6},{6,5},{7,7},{8,8},{9,10},{10,9... | collective-permute-start | bytes 786440 | tf_op jit(solution)/shard_map/ppermute | solution.py:285
  1.6 3.5 %collective-permute-start = (bf16[8,2,64,128]{3,2,1,0:T(8,128)(2,1)}, bf16[8,2,64,128]{3,2,1,0:T(8,128)(2,1)S(1)}, u32[]{:S(2)}, u32[]{:S(2)}) collective-permute-start(bf16[8,2,64,128]{3,2,1,0:T(8,128)(2,1)} %own_ref.1), channel_id=1, source_target_pairs={{0,1},{1,0},{2,3},{3,2},{4,5},{5,4},{6,7},{7,6},{8,9},{9,8},{10,11... | collective-permute-start | bytes 786440 | tf_op jit(solution)/shard_map/ppermute | solution.py:285
  5.1 1.1 %shard_map.109 = (bf16[8,2,64,128]{3,2,1,0:T(8,128)(2,1)S(1)}, bf16[4,2,64,128]{3,2,1,0:T(8,128)(2,1)S(1)}) custom-call(bf16[8,2,64,128]{3,2,1,0:T(8,128)(2,1)} %own_ref.1, bf16[2,2,64,128]{3,2,1,0:T(8,128)(2,1)} %second_cache_ref.1, bf16[2,2,64,128]{3,2,1,0:T(8,128)(2,1)} %first_cache_ref.1), custom_call_target="tpu_custom_call" | custom-call | bytes 1048576 | tf_op jit(solution)/shard_map/pallas_call | solution.py:251
  6.2 1.2 %shard_map.110 = (f32[1,2,128]{2,1,0:T(2,128)S(1)}, f32[6,1,128]{2,1,0:T(1,128)S(1)}, bf16[3,3,3,128,128]{4,3,2,1,0:T(8,128)(2,1)S(1)}) custom-call(bf16[8,2,64,128]{3,2,1,0:T(8,128)(2,1)S(1)} %get-tuple-element.14.own_ref, bf16[3,3,3,128,128]{4,3,2,1,0:T(8,128)(2,1)} %weight_ref.1, f32[1,128]{1,0:T(1,128)} %bitcast.8, f32[1,128]{1,0:T(1,128)} %bitcast.9, ...), custom_call_target="tpu_custom_call" | custom-call | flops 99999997952 | bytes 1048576 | tf_op jit(solution)/shard_map/pallas_call | solution.py:251
  7.4 1.5 %collective-permute-start.5 = (f32[1,2,128]{2,1,0:T(2,128)S(1)}, f32[1,2,128]{2,1,0:T(2,128)S(1)}, u32[]{:S(2)}, u32[]{:S(2)}) collective-permute-start(f32[1,2,128]{2,1,0:T(2,128)S(1)} %get-tuple-element.16), channel_id=1, source_target_pairs={{0,8},{8,16},{16,24},{24,0},{1,9},{9,17},{17,25},{25,1},{2,10},{10... | collective-permute-start | bytes 3080 | tf_op jit(solution)/shard_map/ppermute | solution.py:315
  9.0 1.5 %collective-permute-start.2 = (bf16[4,2,64,128]{3,2,1,0:T(8,128)(2,1)S(1)}, bf16[4,2,64,128]{3,2,1,0:T(8,128)(2,1)S(1)}, u32[]{:S(2)}, u32[]{:S(2)}) collective-permute-start(bf16[4,2,64,128]{3,2,1,0:T(8,128)(2,1)S(1)} %get-tuple-element.15), channel_id=1, source_target_pairs={{0,8},{8,16},{16,24},{24,0},{1,9},{9,17},{17,25},{25,1},{2,10},{10... | collective-permute-start | bytes 393224 | tf_op jit(solution)/shard_map/ppermute | solution.py:310
  10.5 1.5 %collective-permute-done.5 = f32[1,2,128]{2,1,0:T(2,128)S(1)} collective-permute-done((f32[1,2,128]{2,1,0:T(2,128)S(1)}, f32[1,2,128]{2,1,0:T(2,128)S(1)}, u32[]{:S(2)}, u32[]{:S(2)}) %collective-permute-start.5) | collective-permute-done | bytes 1056 | tf_op jit(solution)/shard_map/ppermute | solution.py:315
  12.0 0.6 %broadcast_in_dim.8 = f32[8,4,128]{2,1,0:T(4,128)} broadcast(f32[4,128]{1,0:T(4,128)S(1)} %maximum_bitcast_fusion), dimensions={1,2} | broadcast | bytes 18432 | tf_op jit(solution)/shard_map/broadcast_in_dim | solution.py:316
  12.6 3.9 %all-to-all-start = ((f32[8,4,128]{2,1,0:T(4,128)}), f32[8,4,128]{2,1,0:T(4,128)S(1)}, u32[]{:S(2)}, u32[]{:S(2)}) async-start(f32[8,4,128]{2,1,0:T(4,128)} %broadcast_in_dim.8), calls=%async_computation | async-start | bytes 32768 | tf_op jit(solution)/shard_map/all_to_all | solution.py:319
  16.4 0.0 collective-permute-done.2.halo_ref
  16.4 0.7 %collective-permute-start.4 = (bf16[4,2,64,128]{3,2,1,0:T(8,128)(2,1)S(1)}, bf16[4,2,64,128]{3,2,1,0:T(8,128)(2,1)S(1)}, u32[]{:S(2)}, u32[]{:S(2)}) collective-permute-start(bf16[4,2,64,128]{3,2,1,0:T(8,128)(2,1)S(1)} %collective-permute-done.2.halo_ref), channel_id=1, source_target_pairs={{0,0},{1,2},{2,1},{3,4},{4,3},{5,6},{6,5},{7,7},{8,8},{9,10},{10,9... | collective-permute-start | bytes 393224 | tf_op jit(solution)/shard_map/ppermute | solution.py:285
  17.1 3.4 %collective-permute-start.3 = (bf16[4,2,64,128]{3,2,1,0:T(8,128)(2,1)S(1)}, bf16[4,2,64,128]{3,2,1,0:T(8,128)(2,1)S(1)}, u32[]{:S(2)}, u32[]{:S(2)}) collective-permute-start(bf16[4,2,64,128]{3,2,1,0:T(8,128)(2,1)S(1)} %collective-permute-done.2.halo_ref), channel_id=1, source_target_pairs={{0,1},{1,0},{2,3},{3,2},{4,5},{5,4},{6,7},{7,6},{8,9},{9,8},{10,11... | collective-permute-start | bytes 393224 | tf_op jit(solution)/shard_map/ppermute | solution.py:285
  20.6 1.6 %all-to-all-done.stats_ref = f32[8,4,128]{2,1,0:T(4,128)S(1)} async-done(((f32[8,4,128]{2,1,0:T(4,128)}), f32[8,4,128]{2,1,0:T(4,128)S(1)}, u32[]{:S(2)}, u32[]{:S(2)}) %all-to-all-start) | async-done | bytes 16416 | tf_op jit(solution)/shard_map/all_to_all | solution.py:319
  22.2 0.0 collective-permute-done.1.rest_1_.far_ref
  22.2 0.0 collective-permute-done.rest_0_.near_ref
  22.2 0.2 shard_map.111.affine_ref
  22.4 0.0 collective-permute-done.4.halo_far_ref
  22.4 0.0 collective-permute-done.3.halo_near_ref
  22.4 3.4 %shard_map.112 = (bf16[10,4,64,128]{3,2,1,0:T(8,128)(2,1)S(1)}, f32[32,2,128]{2,1,0:T(2,128)S(1)}, bf16[3,3,3,128,128]{4,3,2,1,0:T(8,128)(2,1)S(1)}) custom-call(bf16[8,2,64,128]{3,2,1,0:T(8,128)(2,1)S(1)} %get-tuple-element.14.own_ref, bf16[8,2,64,128]{3,2,1,0:T(8,128)(2,1)S(1)} %collective-permute-done.rest_0_.near_ref, ...), custom_call_target="tpu_custom_call" | custom-call | flops 1000000000 | bytes 1048576 | tf_op jit(solution)/shard_map/pallas_call | solution.py:251
  25.8 12.6 %all_to_all.10.stats_ref = f32[32,2,128]{2,1,0:T(2,128)S(1)} all-to-all(f32[32,2,128]{2,1,0:T(2,128)S(1)} %get-tuple-element.21), channel_id=1, replica_groups=mesh['section'=4,'rows'=8] {'section','rows'}, dimensions={0} | all-to-all | bytes 65536 | tf_op jit(solution)/shard_map/all_to_all | solution.py:319
  38.4 0.2 shard_map.113.affine_ref
  38.5 2.3 %shard_map.114 = bf16[8,2,64,128]{3,2,1,0:T(8,128)(2,1)} custom-call(bf16[10,4,64,128]{3,2,1,0:T(8,128)(2,1)S(1)} %get-tuple-element.20.middle_ref, f32[4,1,128]{2,1,0:T(1,128)S(1)} %shard_map.113.affine_ref, f32[6,1,128]{2,1,0:T(1,128)S(1)} %get-tuple-element.18.vectors_ref, bf16[3,3,3,128,128]{4,3,2,1,0:T(8,128)(2,1)S(1)} %get-tuple-element.22.weight_ref, ...), custom_call_target="tpu_custom_call" | custom-call | flops 1000000000 | bytes 1048576 | tf_op jit(solution)/shard_map/pallas_call | solution.py:251
  (1 shorter events, 0.0 us)
Async XLA Ops:
  0.0 22.2 %collective-permute-start.1 = (bf16[8,2,64,128]{3,2,1,0:T(8,128)(2,1)}, bf16[8,2,64,128]{3,2,1,0:T(8,128)(2,1)S(1)}, u32[]{:S(2)}, u32[]{:S(2)}) collective-permute-start(bf16[8,2,64,128]{3,2,1,0:T(8,128)(2,1)} %own_ref.1), channel_id=1, source_target_pairs={{0,0},{1,2},{2,1},{3,4},{4,3},{5,6},{6,5},{7,7},{8,8},{9,10},{10,9... | collective-permute-start | bytes 786440 | tf_op jit(solution)/shard_map/ppermute | solution.py:285
  1.6 20.6 %collective-permute-start = (bf16[8,2,64,128]{3,2,1,0:T(8,128)(2,1)}, bf16[8,2,64,128]{3,2,1,0:T(8,128)(2,1)S(1)}, u32[]{:S(2)}, u32[]{:S(2)}) collective-permute-start(bf16[8,2,64,128]{3,2,1,0:T(8,128)(2,1)} %own_ref.1), channel_id=1, source_target_pairs={{0,1},{1,0},{2,3},{3,2},{4,5},{5,4},{6,7},{7,6},{8,9},{9,8},{10,11... | collective-permute-start | bytes 786440 | tf_op jit(solution)/shard_map/ppermute | solution.py:285
  7.4 4.5 %collective-permute-start.5 = (f32[1,2,128]{2,1,0:T(2,128)S(1)}, f32[1,2,128]{2,1,0:T(2,128)S(1)}, u32[]{:S(2)}, u32[]{:S(2)}) collective-permute-start(f32[1,2,128]{2,1,0:T(2,128)S(1)} %get-tuple-element.16), channel_id=1, source_target_pairs={{0,8},{8,16},{16,24},{24,0},{1,9},{9,17},{17,25},{25,1},{2,10},{10... | collective-permute-start | bytes 3080 | tf_op jit(solution)/shard_map/ppermute | solution.py:315
  9.0 7.5 %collective-permute-start.2 = (bf16[4,2,64,128]{3,2,1,0:T(8,128)(2,1)S(1)}, bf16[4,2,64,128]{3,2,1,0:T(8,128)(2,1)S(1)}, u32[]{:S(2)}, u32[]{:S(2)}) collective-permute-start(bf16[4,2,64,128]{3,2,1,0:T(8,128)(2,1)S(1)} %get-tuple-element.15), channel_id=1, source_target_pairs={{0,8},{8,16},{16,24},{24,0},{1,9},{9,17},{17,25},{25,1},{2,10},{10... | collective-permute-start | bytes 393224 | tf_op jit(solution)/shard_map/ppermute | solution.py:310
  12.6 9.6 %all-to-all-start = ((f32[8,4,128]{2,1,0:T(4,128)}), f32[8,4,128]{2,1,0:T(4,128)S(1)}, u32[]{:S(2)}, u32[]{:S(2)}) async-start(f32[8,4,128]{2,1,0:T(4,128)} %broadcast_in_dim.8), calls=%async_computation | async-start | bytes 32768 | tf_op jit(solution)/shard_map/all_to_all | solution.py:319
  16.4 5.9 %collective-permute-start.4 = (bf16[4,2,64,128]{3,2,1,0:T(8,128)(2,1)S(1)}, bf16[4,2,64,128]{3,2,1,0:T(8,128)(2,1)S(1)}, u32[]{:S(2)}, u32[]{:S(2)}) collective-permute-start(bf16[4,2,64,128]{3,2,1,0:T(8,128)(2,1)S(1)} %collective-permute-done.2.halo_ref), channel_id=1, source_target_pairs={{0,0},{1,2},{2,1},{3,4},{4,3},{5,6},{6,5},{7,7},{8,8},{9,10},{10,9... | collective-permute-start | bytes 393224 | tf_op jit(solution)/shard_map/ppermute | solution.py:285
  17.1 5.2 %collective-permute-start.3 = (bf16[4,2,64,128]{3,2,1,0:T(8,128)(2,1)S(1)}, bf16[4,2,64,128]{3,2,1,0:T(8,128)(2,1)S(1)}, u32[]{:S(2)}, u32[]{:S(2)}) collective-permute-start(bf16[4,2,64,128]{3,2,1,0:T(8,128)(2,1)S(1)} %collective-permute-done.2.halo_ref), channel_id=1, source_target_pairs={{0,1},{1,0},{2,3},{3,2},{4,5},{5,4},{6,7},{7,6},{8,9},{9,8},{10,11... | collective-permute-start | bytes 393224 | tf_op jit(solution)/shard_map/ppermute | solution.py:285

commit v17 on v13

--- a/solution.py
+++ b/solution.py
@@ -24,12 +24,12 @@
         total = total + jnp.sum(away, axis=0, keepdims=True)
         squares = squares + jnp.sum(away * away, axis=0, keepdims=True)
     shift = total * (1.0 / cells)
-    return jnp.concatenate([pivot + shift, squares - total * shift], axis=1)
+    return jnp.concatenate([pivot + shift, squares - total * shift], axis=0)
 
 
 def affine(stats, cells, scale, shift):
-    devices, channels = stats.shape[0], scale.shape[-1]
-    means, squares = stats[:, :channels], stats[:, channels:]
+    devices, _, channels = stats.shape
+    means, squares = stats[:, 0], stats[:, 1]
     mean = jnp.sum(means, axis=0, keepdims=True) * (1.0 / devices)
     away = means - mean
     square = jnp.sum(squares + cells * (away * away), axis=0, keepdims=True)
@@ -57,37 +57,57 @@
 
 def pair_conv(field, row, frames, weight_ref):
     columns, channels = field.shape[2], field.shape[3]
-    pieces, blocks = [], []
+    cells = frames * columns
     nothing = jnp.zeros((channels, channels), jnp.bfloat16)
-    for frame_tap in range(3):
-        for line in range(4):
-            piece = field[frame_tap : frame_tap + frames, row + line]
-            pieces.append(piece.reshape(frames * columns, channels))
-            blocks.append(
+
+    def piece(frame_tap, line):
+        return field[frame_tap : frame_tap + frames, row + line].reshape(cells, channels)
+
+    def dot(pieces, blocks):
+        return jnp.dot(pieces, blocks, preferred_element_type=jnp.float32)
+
+    taps = [(frame_tap, row_tap) for frame_tap in range(3) for row_tap in range(3)]
+    early = dot(
+        jnp.concatenate(
+            [
+                jnp.concatenate([piece(tap, out + row_tap) for tap, row_tap in taps], axis=1)
+                for out in range(2)
+            ],
+            axis=0,
+        ),
+        jnp.concatenate(
+            [
+                jnp.concatenate([weight_ref[tap, row_tap, 0], weight_ref[tap, row_tap, 1]], axis=1)
+                for tap, row_tap in taps
+            ],
+            axis=0,
+        ),
+    )
+    lines = [(frame_tap, line) for frame_tap in range(3) for line in range(4)]
+    late = dot(
+        jnp.concatenate([piece(tap, line) for tap, line in lines], axis=1),
+        jnp.concatenate(
+            [
                 jnp.concatenate(
                     [
-                        weight_ref[frame_tap, line - out, col_tap]
-                        if 0 <= line - out <= 2
-                        else nothing
-                        for col_tap in range(3)
+                        weight_ref[tap, line - out, 2] if 0 <= line - out <= 2 else nothing
                         for out in range(2)
                     ],
                     axis=1,
                 )
-            )
-    product = jnp.dot(
-        jnp.concatenate(pieces, axis=1),
-        jnp.concatenate(blocks, axis=0),
-        preferred_element_type=jnp.float32,
-    )
-    cells = frames * columns
+                for tap, line in lines
+            ],
+            axis=0,
+        ),
+    )
     column = lax.broadcasted_iota(jnp.int32, (cells, channels), 0) % columns
     results = []
     for out in range(2):
-        left, centre, right = (
-            product[:, (2 * tap + out) * channels : (2 * tap + out + 1) * channels]
-            for tap in range(3)
+        left, centre = (
+            early[out * cells : (out + 1) * cells, tap * channels : (tap + 1) * channels]
+            for tap in range(2)
         )
+        right = late[:, out * channels : (out + 1) * channels]
         left = jnp.where(column == 0, 0.0, pltpu.roll(left, 1, 0))
         right = jnp.where(column == columns - 1, 0.0, pltpu.roll(right, cells - 1, 0))
         results.append(left + centre + right)
@@ -137,30 +157,23 @@
         load.start()
     channels = own_ref.shape[-1]
     blocks = [own_ref[frame].astype(jnp.float32) for frame in range(own_ref.shape[0])]
-    packed = moments([block.reshape(-1, channels) for block in blocks])
-    stats_ref[...] = jnp.broadcast_to(packed[None], stats_ref.shape)
+    stats_ref[0] = moments([block.reshape(-1, channels) for block in blocks])
     for load in loads:
         load.wait()
 
 
-def affine_kernel(row_count, cells, which, stats_ref, vectors_ref, affine_ref):
-    section = lax.axis_index("section")
-    scale, shift = vectors_ref[which], vectors_ref[which + 1]
-    for index, span in enumerate((section, jnp.maximum(section - 1, 0))):
-        stats = stats_ref[pl.ds(span * row_count, row_count)]
-        slope, offset = affine(stats.reshape(row_count, stats.shape[-1]), cells, scale, shift)
-        affine_ref[2 * index] = slope
-        affine_ref[2 * index + 1] = offset
-
-
 def first_kernel(
-    row_count, own_ref, near_ref, far_ref, affine_ref, vectors_ref, weight_ref, middle_ref,
+    row_count, own_ref, near_ref, far_ref, stats_ref, vectors_ref, weight_ref, middle_ref,
     sums_ref, field
 ):
     section, row_at = lax.axis_index("section"), lax.axis_index("rows")
     frames, lines, columns, channels = own_ref.shape
     inner = frames - SPAN_HALO
-    slope, offset, slope_before, offset_before = (affine_ref[row] for row in range(4))
+    cells = inner * lines * columns
+    scale, shift = vectors_ref[0], vectors_ref[1]
+    mine, before = stats_ref[:, :2], stats_ref[:, 2:]
+    slope, offset = affine(mine, cells, scale, shift)
+    slope_before, offset_before = affine(before, cells, scale, shift)
     even = row_at % 2 == 0
     at_start = section == 0
 
@@ -199,15 +212,22 @@
             middle_ref[2:, line] = rounded[2:]
             if 1 <= line <= lines:
                 kept.append(rounded[2:].astype(jnp.float32).reshape(-1, channels))
-    sums_ref[...] = jnp.broadcast_to(moments(kept)[None], sums_ref.shape)
+    packed = moments(kept)
+    for device in range(sums_ref.shape[0]):
+        sums_ref[device] = packed
 
 
 def second_kernel(
-    row_count, middle_ref, affine_ref, vectors_ref, weight_ref, own_ref, out_ref, field
+    row_count, middle_ref, stats_ref, vectors_ref, weight_ref, own_ref, out_ref, field
 ):
     section, row_at = lax.axis_index("section"), lax.axis_index("rows")
     frames, lines, columns, channels = own_ref.shape
-    slope, offset, slope_before, offset_before = (affine_ref[row] for row in range(4))
+    cells = frames * lines * columns
+    scale, shift = vectors_ref[3], vectors_ref[4]
+    mine = stats_ref[pl.ds(section * row_count, row_count)]
+    before = stats_ref[pl.ds(jnp.maximum(section - 1, 0) * row_count, row_count)]
+    slope, offset = affine(mine, cells, scale, shift)
+    slope_before, offset_before = affine(before, cells, scale, shift)
     at_start = section == 0
     for line in range(lines + 2):
         halo, body = middle_ref[:2, line], middle_ref[2:, line]
@@ -265,7 +285,7 @@
     frames, lines, columns, channels = activations.shape
     sections, row_count = lax.axis_size("section"), lax.axis_size("rows")
     everyone = sections * row_count
-    stats_shape = jax.ShapeDtypeStruct((everyone, 1, 2 * channels), jnp.float32)
+    stats_shape = jax.ShapeDtypeStruct((everyone, 2, channels), jnp.float32)
     vectors = (norm1_scale, norm1_shift, conv1_bias, norm2_scale, norm2_shift, conv2_bias)
 
     near = [i ^ 1 for i in range(row_count)]
@@ -288,7 +308,7 @@
     sums, packed, weight = call(
         stats_kernel,
         (
-            stats_shape,
+            jax.ShapeDtypeStruct((1, 2, channels), jnp.float32),
             jax.ShapeDtypeStruct((len(vectors), 1, channels), jnp.float32),
             jax.ShapeDtypeStruct(conv1_weight.shape, jnp.bfloat16),
         ),
@@ -297,37 +317,28 @@
         in_place=range(1, 2 + len(vectors)),
     )
     received = lax.ppermute(halo, "section", ring)
-    received, _ = lax.optimization_barrier((received, sums))
+    passed = lax.ppermute(sums, "section", ring)
+    received, sums, passed = lax.optimization_barrier((received, sums, passed))
     joined = jnp.concatenate([received, own], axis=0)
-
-    def coefficients(sums, which):
-        stats = lax.all_to_all(sums, ("section", "rows"), 0, 0, tiled=True)
-        return call(
-            functools.partial(affine_kernel, row_count, frames * lines * columns, which),
-            jax.ShapeDtypeStruct((4, 1, channels), jnp.float32),
-            [],
-            (stats, packed),
-            flops=10**11,
-        )
-
-    middle, sums = call(
+    both = jnp.concatenate([sums, passed], axis=1)
+    both = jnp.broadcast_to(both, (row_count,) + both.shape[1:])
+    stats = lax.all_to_all(both, "rows", 0, 0, tiled=True)
+    middle, sums_two = call(
         functools.partial(first_kernel, row_count),
         (
             jax.ShapeDtypeStruct((frames + 2, lines + 2, columns, channels), jnp.bfloat16),
             stats_shape,
         ),
         [pltpu.VMEM((frames + SPAN_HALO, 3 * lines, columns, channels), jnp.bfloat16)],
-        (
-            joined, across(joined, near), across(joined, far), coefficients(sums, 0), packed,
-            weight,
-        ),
+        (joined, across(joined, near), across(joined, far), stats, packed, weight),
         flops=10**9,
     )
+    stats_two = lax.all_to_all(sums_two, ("section", "rows"), 0, 0, tiled=True)
     return call(
         functools.partial(second_kernel, row_count),
         jax.ShapeDtypeStruct(activations.shape, jnp.bfloat16),
         [pltpu.VMEM((frames + 2, lines + 2, columns, channels), jnp.bfloat16)],
-        (middle, coefficients(sums, 3), packed, conv2_weight, own),
+        (middle, stats_two, packed, conv2_weight, own),
         flops=10**9,
     )
 

time: 40 us -> 37.6 us (0.940)
  blocking collectives: 14.6 us -> 18.3 us
  starting transfers between devices: 11.8 us -> 8.2 us
  Pallas kernels: 8.98 us -> 7.85 us
  local copies, waits for them, and re-layouts: 1.04 us -> 0.06 us
    all_to_all x1 -> x0, starting transfers between devices: 4.92 us -> none  [coefficients(): stats = lax.all_to_all(sums, ('section', 'rows'), 0, 0, tiled=True)]
    all_to_all x1 -> x2, blocking collectives: 14.6 us -> 18.3 us  [the longest x1 9.31 us: on_device(): stats = lax.all_to_all(both, 'rows', 0, 0, tiled=True)]
    all_to_all x1 -> x0, waiting for transfers between devices: 3.29 us -> none  [coefficients(): stats = lax.all_to_all(sums, ('section', 'rows'), 0, 0, tiled=True)]
    ppermute x0 -> x1, waiting for transfers between devices: none -> 2.98 us  [on_device(): passed = lax.ppermute(sums, 'section', ring)]
    ppermute x0 -> x1, starting transfers between devices: none -> 1.54 us  [on_device(): passed = lax.ppermute(sums, 'section', ring)]
    pallas_call x6 -> x4, Pallas kernels: 8.98 us -> 7.85 us  [call(): pl.pallas_call(kernel, out_shape=out_shape, in_specs=specs, out_specs=jax...]
    unnamed x3, local copies, waits for them, and re-layouts: 1 us -> 0.01 us
  transfers between devices with their start and end apart: 4 -> 4, of which waited for: 1 -> 1; matrix products, arithmetic and copies ran while one was open for 0% -> 0% of each run, Pallas kernels for 5% -> 3%
where the time goes in v17:
time: 37.6 us; the launch traced here: 37.4 us
  blocking collectives  18.3 us (49%)
  starting transfers between devices  8.2 us (22%)
  Pallas kernels  7.85 us (21%)
  waiting for transfers between devices  2.98 us (8%)
    all_to_all x1, blocking collectives, on_device(): stats = lax.all_to_all(both, 'rows', 0, 0, tiled=True)  9.31 us
    all_to_all x1, blocking collectives, on_device(): stats_two = lax.all_to_all(sums_two, ('section', 'rows'), 0, 0, tiled=True)  8.97 us
    pallas_call x4, Pallas kernels, call(): pl.pallas_call(kernel, out_shape=out_shape, in_specs=specs, out_specs=jax...  7.85 us
    ppermute x2, starting transfers between devices, across(): return lax.ppermute(block, 'rows', list(enumerate(partner)))  3.67 us
    ppermute x1, starting transfers between devices, on_device(): received = lax.ppermute(halo, 'section', ring)  2.99 us
    ppermute x1, waiting for transfers between devices, on_device(): passed = lax.ppermute(sums, 'section', ring)  2.98 us
    ppermute x1, starting transfers between devices, on_device(): passed = lax.ppermute(sums, 'section', ring)  1.54 us
  transfers between devices with their start and end apart: 4, of which 1 were waited for; matrix products, arithmetic and copies ran while one was open for 0% of the time, Pallas kernels for 3%

profile of v17, /device:TPU:0, one launch (start us, length us, event | category | flops | bytes accessed | tf_op | source)
XLA Modules:
  0.0 37.4 jit_solution(7404728271111681830)
XLA Ops:
  0.0 1.1 %shard_map.109 = (bf16[8,2,64,128]{3,2,1,0:T(8,128)(2,1)S(1)}, bf16[4,2,64,128]{3,2,1,0:T(8,128)(2,1)S(1)}) custom-call(bf16[8,2,64,128]{3,2,1,0:T(8,128)(2,1)} %own_ref.1, bf16[2,2,64,128]{3,2,1,0:T(8,128)(2,1)} %second_cache_ref.1, bf16[2,2,64,128]{3,2,1,0:T(8,128)(2,1)} %first_cache_ref.1), custom_call_target="tpu_custom_call" | custom-call | bytes 1048576 | tf_op jit(solution)/shard_map/pallas_call | solution.py:261
  1.1 3.0 %collective-permute-start = (bf16[4,2,64,128]{3,2,1,0:T(8,128)(2,1)S(1)}, bf16[4,2,64,128]{3,2,1,0:T(8,128)(2,1)S(1)}, u32[]{:S(2)}, u32[]{:S(2)}) collective-permute-start(bf16[4,2,64,128]{3,2,1,0:T(8,128)(2,1)S(1)} %get-tuple-element.15), channel_id=1, source_target_pairs={{0,8},{8,16},{16,24},{24,0},{1,9},{9,17},{17,25},{25,1},{2,10},{10... | collective-permute-start | bytes 393224 | tf_op jit(solution)/shard_map/ppermute | solution.py:319
  4.1 1.2 %shard_map.110 = (f32[1,2,128]{2,1,0:T(2,128)S(1)}, f32[6,1,128]{2,1,0:T(1,128)S(1)}, bf16[3,3,3,128,128]{4,3,2,1,0:T(8,128)(2,1)S(1)}) custom-call(bf16[8,2,64,128]{3,2,1,0:T(8,128)(2,1)S(1)} %get-tuple-element.16.own_ref, bf16[3,3,3,128,128]{4,3,2,1,0:T(8,128)(2,1)} %weight_ref.2, f32[1,128]{1,0:T(1,128)} %bitcast.8, f32[1,128]{1,0:T(1,128)} %bitcast.9, ...), custom_call_target="tpu_custom_call" | custom-call | bytes 1048576 | tf_op jit(solution)/shard_map/pallas_call | solution.py:261
  5.3 1.5 %collective-permute-start.1 = (f32[1,2,128]{2,1,0:T(2,128)S(1)}, f32[1,2,128]{2,1,0:T(2,128)S(1)}, u32[]{:S(2)}, u32[]{:S(2)}) collective-permute-start(f32[1,2,128]{2,1,0:T(2,128)S(1)} %get-tuple-element.19), channel_id=1, source_target_pairs={{0,8},{8,16},{16,24},{24,0},{1,9},{9,17},{17,25},{25,1},{2,10},{10... | collective-permute-start | bytes 3080 | tf_op jit(solution)/shard_map/ppermute | solution.py:320
  6.9 3.0 %collective-permute-done.1 = f32[1,2,128]{2,1,0:T(2,128)S(1)} collective-permute-done((f32[1,2,128]{2,1,0:T(2,128)S(1)}, f32[1,2,128]{2,1,0:T(2,128)S(1)}, u32[]{:S(2)}, u32[]{:S(2)}) %collective-permute-start.1) | collective-permute-done | bytes 1056 | tf_op jit(solution)/shard_map/ppermute | solution.py:320
  9.8 0.0 collective-permute-done
  9.9 0.7 %collective-permute-start.3 = (bf16[12,2,64,128]{3,2,1,0:T(8,128)(2,1)S(1)}, bf16[12,2,64,128]{3,2,1,0:T(8,128)(2,1)S(1)}, u32[]{:S(2)}, u32[]{:S(2)}) collective-permute-start(bf16[12,2,64,128]{3,2,1,0:T(8,128)(2,1)S(1)} %constant_dynamic-update-slice_fusion.own_ref), channel_id=1, source_target_pairs={{0,0},{1,2},{2,1},{3,4},{4,3},{5,6},{6,5},{7,7},{8,8},{9,10},{10,9... | collective-permute-start | bytes 1179656 | tf_op jit(solution)/shard_map/ppermute | solution.py:295
  10.6 3.0 %collective-permute-start.2 = (bf16[12,2,64,128]{3,2,1,0:T(8,128)(2,1)S(1)}, bf16[12,2,64,128]{3,2,1,0:T(8,128)(2,1)S(1)}, u32[]{:S(2)}, u32[]{:S(2)}) collective-permute-start(bf16[12,2,64,128]{3,2,1,0:T(8,128)(2,1)S(1)} %constant_dynamic-update-slice_fusion.own_ref), channel_id=1, source_target_pairs={{0,1},{1,0},{2,3},{3,2},{4,5},{5,4},{6,7},{7,6},{8,9},{9,8},{10,11... | collective-permute-start | bytes 1179656 | tf_op jit(solution)/shard_map/ppermute | solution.py:295
  13.6 9.3 %all_to_all.10.stats_ref = f32[8,4,128]{2,1,0:T(4,128)S(1)} all-to-all(f32[8,4,128]{2,1,0:T(4,128)S(1)} %broadcast_in_dim.8), channel_id=1, replica_groups=mesh['section'=4,'rows'=8] {'rows'}, dimensions={0} | all-to-all | bytes 32768 | tf_op jit(solution)/shard_map/all_to_all | solution.py:325
  22.9 0.0 collective-permute-done.3.far_ref
  22.9 0.0 collective-permute-done.2.near_ref
  22.9 0.0 copy-start
  22.9 3.3 %shard_map.111 = (bf16[10,4,64,128]{3,2,1,0:T(8,128)(2,1)S(1)}, f32[32,2,128]{2,1,0:T(2,128)S(1)}) custom-call(bf16[12,2,64,128]{3,2,1,0:T(8,128)(2,1)S(1)} %constant_dynamic-update-slice_fusion.own_ref, bf16[12,2,64,128]{3,2,1,0:T(8,128)(2,1)S(1)} %collective-permute-done.2.near_ref, bf16[12,2,64,128]{3,2,1,0:T(8,128)(2,1)S(1)} %collective-permute-done.3.far_ref, ...), custom_call_target="tpu_custom_call" | custom-call | flops 1000000000 | bytes 1048576 | tf_op jit(solution)/shard_map/pallas_call | solution.py:261
  26.2 9.0 %all_to_all.11.stats_ref = f32[32,2,128]{2,1,0:T(2,128)S(1)} all-to-all(f32[32,2,128]{2,1,0:T(2,128)S(1)} %get-tuple-element.24), channel_id=1, replica_groups=mesh['section'=4,'rows'=8] {'section','rows'}, dimensions={0} | all-to-all | bytes 65536 | tf_op jit(solution)/shard_map/all_to_all | solution.py:336
  35.2 0.0 copy-done
  35.2 2.3 %shard_map.112 = bf16[8,2,64,128]{3,2,1,0:T(8,128)(2,1)} custom-call(bf16[10,4,64,128]{3,2,1,0:T(8,128)(2,1)S(1)} %get-tuple-element.23.middle_ref, f32[32,2,128]{2,1,0:T(2,128)S(1)} %all_to_all.11.stats_ref, f32[6,1,128]{2,1,0:T(1,128)S(1)} %get-tuple-element.21.vectors_ref, bf16[3,3,3,128,128]{4,3,2,1,0:T(8,128)(2,1)S(1)} %copy-done, ...), custom_call_target="tpu_custom_call" | custom-call | flops 1000000000 | bytes 1048576 | tf_op jit(solution)/shard_map/pallas_call | solution.py:261
  (4 shorter events, 0.1 us)
Async XLA Ops:
  1.1 8.8 %collective-permute-start = (bf16[4,2,64,128]{3,2,1,0:T(8,128)(2,1)S(1)}, bf16[4,2,64,128]{3,2,1,0:T(8,128)(2,1)S(1)}, u32[]{:S(2)}, u32[]{:S(2)}) collective-permute-start(bf16[4,2,64,128]{3,2,1,0:T(8,128)(2,1)S(1)} %get-tuple-element.15), channel_id=1, source_target_pairs={{0,8},{8,16},{16,24},{24,0},{1,9},{9,17},{17,25},{25,1},{2,10},{10... | collective-permute-start | bytes 393224 | tf_op jit(solution)/shard_map/ppermute | solution.py:319
  5.3 4.5 %collective-permute-start.1 = (f32[1,2,128]{2,1,0:T(2,128)S(1)}, f32[1,2,128]{2,1,0:T(2,128)S(1)}, u32[]{:S(2)}, u32[]{:S(2)}) collective-permute-start(f32[1,2,128]{2,1,0:T(2,128)S(1)} %get-tuple-element.19), channel_id=1, source_target_pairs={{0,8},{8,16},{16,24},{24,0},{1,9},{9,17},{17,25},{25,1},{2,10},{10... | collective-permute-start | bytes 3080 | tf_op jit(solution)/shard_map/ppermute | solution.py:320
  9.9 13.0 %collective-permute-start.3 = (bf16[12,2,64,128]{3,2,1,0:T(8,128)(2,1)S(1)}, bf16[12,2,64,128]{3,2,1,0:T(8,128)(2,1)S(1)}, u32[]{:S(2)}, u32[]{:S(2)}) collective-permute-start(bf16[12,2,64,128]{3,2,1,0:T(8,128)(2,1)S(1)} %constant_dynamic-update-slice_fusion.own_ref), channel_id=1, source_target_pairs={{0,0},{1,2},{2,1},{3,4},{4,3},{5,6},{6,5},{7,7},{8,8},{9,10},{10,9... | collective-permute-start | bytes 1179656 | tf_op jit(solution)/shard_map/ppermute | solution.py:295
  10.6 12.3 %collective-permute-start.2 = (bf16[12,2,64,128]{3,2,1,0:T(8,128)(2,1)S(1)}, bf16[12,2,64,128]{3,2,1,0:T(8,128)(2,1)S(1)}, u32[]{:S(2)}, u32[]{:S(2)}) collective-permute-start(bf16[12,2,64,128]{3,2,1,0:T(8,128)(2,1)S(1)} %constant_dynamic-update-slice_fusion.own_ref), channel_id=1, source_target_pairs={{0,1},{1,0},{2,3},{3,2},{4,5},{5,4},{6,7},{7,6},{8,9},{9,8},{10,11... | collective-permute-start | bytes 1179656 | tf_op jit(solution)/shard_map/ppermute | solution.py:295
  22.9 12.3 %copy-start = (bf16[3,3,3,128,128]{4,3,2,1,0:T(8,128)(2,1)S(1)}, bf16[3,3,3,128,128]{4,3,2,1,0:T(8,128)(2,1)}, u32[]{:S(2)}) copy-start(bf16[3,3,3,128,128]{4,3,2,1,0:T(8,128)(2,1)} %weight_ref.3) | copy-start | bytes 2654212

commit v18 on v17

--- a/solution.py
+++ b/solution.py
@@ -163,7 +163,7 @@
 
 
 def first_kernel(
-    row_count, own_ref, near_ref, far_ref, stats_ref, vectors_ref, weight_ref, middle_ref,
+    row_count, own_ref, far_ref, near_ref, stats_ref, vectors_ref, weight_ref, middle_ref,
     sums_ref, field
 ):
     section, row_at = lax.axis_index("section"), lax.axis_index("rows")
@@ -320,6 +320,8 @@
     passed = lax.ppermute(sums, "section", ring)
     received, sums, passed = lax.optimization_barrier((received, sums, passed))
     joined = jnp.concatenate([received, own], axis=0)
+    from_far = across(joined, far)
+    from_near = across(joined, near)
     both = jnp.concatenate([sums, passed], axis=1)
     both = jnp.broadcast_to(both, (row_count,) + both.shape[1:])
     stats = lax.all_to_all(both, "rows", 0, 0, tiled=True)
@@ -330,7 +332,7 @@
             stats_shape,
         ),
         [pltpu.VMEM((frames + SPAN_HALO, 3 * lines, columns, channels), jnp.bfloat16)],
-        (joined, across(joined, near), across(joined, far), stats, packed, weight),
+        (joined, from_far, from_near, stats, packed, weight),
         flops=10**9,
     )
     stats_two = lax.all_to_all(sums_two, ("section", "rows"), 0, 0, tiled=True)

time: 37.6 us -> 37.5 us (level)
  starting transfers between devices: 8.2 us -> 5.29 us
  blocking collectives: 18.3 us -> 21.1 us
    ppermute x2, starting transfers between devices: 3.67 us -> 0.76 us  [across(): return lax.ppermute(block, 'rows', list(enumerate(partner)))]
    all_to_all x1, blocking collectives: 9.31 us -> 12.1 us  [on_device(): stats = lax.all_to_all(both, 'rows', 0, 0, tiled=True)]
where the time goes in v18:
time: 37.5 us; the launch traced here: 37.3 us
  blocking collectives  21.1 us (56%)
  Pallas kernels  7.85 us (21%)
  starting transfers between devices  5.29 us (14%)
  waiting for transfers between devices  2.98 us (8%)
    all_to_all x1, blocking collectives, on_device(): stats = lax.all_to_all(both, 'rows', 0, 0, tiled=True)  12.1 us
    all_to_all x1, blocking collectives, on_device(): stats_two = lax.all_to_all(sums_two, ('section', 'rows'), 0, 0, tiled=True)  8.98 us
    pallas_call x4, Pallas kernels, call(): pl.pallas_call(kernel, out_shape=out_shape, in_specs=specs, out_specs=jax...  7.85 us
    ppermute x1, starting transfers between devices, on_device(): received = lax.ppermute(halo, 'section', ring)  2.99 us
    ppermute x1, waiting for transfers between devices, on_device(): passed = lax.ppermute(sums, 'section', ring)  2.98 us
    ppermute x1, starting transfers between devices, on_device(): passed = lax.ppermute(sums, 'section', ring)  1.54 us
    ppermute x2, starting transfers between devices, across(): return lax.ppermute(block, 'rows', list(enumerate(partner)))  0.76 us
  transfers between devices with their start and end apart: 4, of which 1 were waited for; matrix products, arithmetic and copies ran while one was open for 0% of the time, Pallas kernels for 3%

profile of v18, /device:TPU:0, one launch (start us, length us, event | category | flops | bytes accessed | tf_op | source)
XLA Modules:
  0.0 37.3 jit_solution(16115163603047069011)
XLA Ops:
  0.0 1.1 %shard_map.109 = (bf16[8,2,64,128]{3,2,1,0:T(8,128)(2,1)S(1)}, bf16[4,2,64,128]{3,2,1,0:T(8,128)(2,1)S(1)}) custom-call(bf16[8,2,64,128]{3,2,1,0:T(8,128)(2,1)} %own_ref.1, bf16[2,2,64,128]{3,2,1,0:T(8,128)(2,1)} %second_cache_ref.1, bf16[2,2,64,128]{3,2,1,0:T(8,128)(2,1)} %first_cache_ref.1), custom_call_target="tpu_custom_call" | custom-call | bytes 1048576 | tf_op jit(solution)/shard_map/pallas_call | solution.py:261
  1.1 3.0 %collective-permute-start = (bf16[4,2,64,128]{3,2,1,0:T(8,128)(2,1)S(1)}, bf16[4,2,64,128]{3,2,1,0:T(8,128)(2,1)S(1)}, u32[]{:S(2)}, u32[]{:S(2)}) collective-permute-start(bf16[4,2,64,128]{3,2,1,0:T(8,128)(2,1)S(1)} %get-tuple-element.15), channel_id=1, source_target_pairs={{0,8},{8,16},{16,24},{24,0},{1,9},{9,17},{17,25},{25,1},{2,10},{10... | collective-permute-start | bytes 393224 | tf_op jit(solution)/shard_map/ppermute | solution.py:319
  4.1 1.2 %shard_map.110 = (f32[1,2,128]{2,1,0:T(2,128)S(1)}, f32[6,1,128]{2,1,0:T(1,128)S(1)}, bf16[3,3,3,128,128]{4,3,2,1,0:T(8,128)(2,1)S(1)}) custom-call(bf16[8,2,64,128]{3,2,1,0:T(8,128)(2,1)S(1)} %get-tuple-element.16.own_ref, bf16[3,3,3,128,128]{4,3,2,1,0:T(8,128)(2,1)} %weight_ref.2, f32[1,128]{1,0:T(1,128)} %bitcast.8, f32[1,128]{1,0:T(1,128)} %bitcast.9, ...), custom_call_target="tpu_custom_call" | custom-call | bytes 1048576 | tf_op jit(solution)/shard_map/pallas_call | solution.py:261
  5.3 1.5 %collective-permute-start.1 = (f32[1,2,128]{2,1,0:T(2,128)S(1)}, f32[1,2,128]{2,1,0:T(2,128)S(1)}, u32[]{:S(2)}, u32[]{:S(2)}) collective-permute-start(f32[1,2,128]{2,1,0:T(2,128)S(1)} %get-tuple-element.19), channel_id=1, source_target_pairs={{0,8},{8,16},{16,24},{24,0},{1,9},{9,17},{17,25},{25,1},{2,10},{10... | collective-permute-start | bytes 3080 | tf_op jit(solution)/shard_map/ppermute | solution.py:320
  6.9 3.0 %collective-permute-done.1 = f32[1,2,128]{2,1,0:T(2,128)S(1)} collective-permute-done((f32[1,2,128]{2,1,0:T(2,128)S(1)}, f32[1,2,128]{2,1,0:T(2,128)S(1)}, u32[]{:S(2)}, u32[]{:S(2)}) %collective-permute-start.1) | collective-permute-done | bytes 1056 | tf_op jit(solution)/shard_map/ppermute | solution.py:320
  9.8 0.0 collective-permute-done
  9.9 0.1 collective-permute-start.3
  10.0 0.7 %collective-permute-start.2 = (bf16[12,2,64,128]{3,2,1,0:T(8,128)(2,1)S(1)}, bf16[12,2,64,128]{3,2,1,0:T(8,128)(2,1)S(1)}, u32[]{:S(2)}, u32[]{:S(2)}) collective-permute-start(bf16[12,2,64,128]{3,2,1,0:T(8,128)(2,1)S(1)} %constant_dynamic-update-slice_fusion.own_ref), channel_id=1, source_target_pairs={{0,0},{1,2},{2,1},{3,4},{4,3},{5,6},{6,5},{7,7},{8,8},{9,10},{10,9... | collective-permute-start | bytes 1179656 | tf_op jit(solution)/shard_map/ppermute | solution.py:295
  10.7 12.1 %all_to_all.10.stats_ref = f32[8,4,128]{2,1,0:T(4,128)S(1)} all-to-all(f32[8,4,128]{2,1,0:T(4,128)S(1)} %broadcast_in_dim.8), channel_id=1, replica_groups=mesh['section'=4,'rows'=8] {'rows'}, dimensions={0} | all-to-all | bytes 32768 | tf_op jit(solution)/shard_map/all_to_all | solution.py:327
  22.8 0.0 collective-permute-done.3.near_ref
  22.8 0.0 collective-permute-done.2.far_ref
  22.8 0.0 copy-start
  22.8 3.3 %shard_map.111 = (bf16[10,4,64,128]{3,2,1,0:T(8,128)(2,1)S(1)}, f32[32,2,128]{2,1,0:T(2,128)S(1)}) custom-call(bf16[12,2,64,128]{3,2,1,0:T(8,128)(2,1)S(1)} %constant_dynamic-update-slice_fusion.own_ref, bf16[12,2,64,128]{3,2,1,0:T(8,128)(2,1)S(1)} %collective-permute-done.2.far_ref, bf16[12,2,64,128]{3,2,1,0:T(8,128)(2,1)S(1)} %collective-permute-done.3.near_ref, ...), custom_call_target="tpu_custom_call" | custom-call | flops 1000000000 | bytes 1048576 | tf_op jit(solution)/shard_map/pallas_call | solution.py:261
  26.1 9.0 %all_to_all.11.stats_ref = f32[32,2,128]{2,1,0:T(2,128)S(1)} all-to-all(f32[32,2,128]{2,1,0:T(2,128)S(1)} %get-tuple-element.24), channel_id=1, replica_groups=mesh['section'=4,'rows'=8] {'section','rows'}, dimensions={0} | all-to-all | bytes 65536 | tf_op jit(solution)/shard_map/all_to_all | solution.py:338
  35.1 0.0 copy-done
  35.1 2.3 %shard_map.112 = bf16[8,2,64,128]{3,2,1,0:T(8,128)(2,1)} custom-call(bf16[10,4,64,128]{3,2,1,0:T(8,128)(2,1)S(1)} %get-tuple-element.23.middle_ref, f32[32,2,128]{2,1,0:T(2,128)S(1)} %all_to_all.11.stats_ref, f32[6,1,128]{2,1,0:T(1,128)S(1)} %get-tuple-element.21.vectors_ref, bf16[3,3,3,128,128]{4,3,2,1,0:T(8,128)(2,1)S(1)} %copy-done, ...), custom_call_target="tpu_custom_call" | custom-call | flops 1000000000 | bytes 1048576 | tf_op jit(solution)/shard_map/pallas_call | solution.py:261
  (4 shorter events, 0.1 us)
Async XLA Ops:
  1.1 8.8 %collective-permute-start = (bf16[4,2,64,128]{3,2,1,0:T(8,128)(2,1)S(1)}, bf16[4,2,64,128]{3,2,1,0:T(8,128)(2,1)S(1)}, u32[]{:S(2)}, u32[]{:S(2)}) collective-permute-start(bf16[4,2,64,128]{3,2,1,0:T(8,128)(2,1)S(1)} %get-tuple-element.15), channel_id=1, source_target_pairs={{0,8},{8,16},{16,24},{24,0},{1,9},{9,17},{17,25},{25,1},{2,10},{10... | collective-permute-start | bytes 393224 | tf_op jit(solution)/shard_map/ppermute | solution.py:319
  5.3 4.5 %collective-permute-start.1 = (f32[1,2,128]{2,1,0:T(2,128)S(1)}, f32[1,2,128]{2,1,0:T(2,128)S(1)}, u32[]{:S(2)}, u32[]{:S(2)}) collective-permute-start(f32[1,2,128]{2,1,0:T(2,128)S(1)} %get-tuple-element.19), channel_id=1, source_target_pairs={{0,8},{8,16},{16,24},{24,0},{1,9},{9,17},{17,25},{25,1},{2,10},{10... | collective-permute-start | bytes 3080 | tf_op jit(solution)/shard_map/ppermute | solution.py:320
  9.9 12.9 %collective-permute-start.3 = (bf16[12,2,64,128]{3,2,1,0:T(8,128)(2,1)S(1)}, bf16[12,2,64,128]{3,2,1,0:T(8,128)(2,1)S(1)}, u32[]{:S(2)}, u32[]{:S(2)}) collective-permute-start(bf16[12,2,64,128]{3,2,1,0:T(8,128)(2,1)S(1)} %constant_dynamic-update-slice_fusion.own_ref), channel_id=1, source_target_pairs={{0,1},{1,0},{2,3},{3,2},{4,5},{5,4},{6,7},{7,6},{8,9},{9,8},{10,11... | collective-permute-start | bytes 1179656 | tf_op jit(solution)/shard_map/ppermute | solution.py:295
  10.0 12.8 %collective-permute-start.2 = (bf16[12,2,64,128]{3,2,1,0:T(8,128)(2,1)S(1)}, bf16[12,2,64,128]{3,2,1,0:T(8,128)(2,1)S(1)}, u32[]{:S(2)}, u32[]{:S(2)}) collective-permute-start(bf16[12,2,64,128]{3,2,1,0:T(8,128)(2,1)S(1)} %constant_dynamic-update-slice_fusion.own_ref), channel_id=1, source_target_pairs={{0,0},{1,2},{2,1},{3,4},{4,3},{5,6},{6,5},{7,7},{8,8},{9,10},{10,9... | collective-permute-start | bytes 1179656 | tf_op jit(solution)/shard_map/ppermute | solution.py:295
  22.8 12.3 %copy-start = (bf16[3,3,3,128,128]{4,3,2,1,0:T(8,128)(2,1)S(1)}, bf16[3,3,3,128,128]{4,3,2,1,0:T(8,128)(2,1)}, u32[]{:S(2)}) copy-start(bf16[3,3,3,128,128]{4,3,2,1,0:T(8,128)(2,1)} %weight_ref.3) | copy-start | bytes 2654212

commit v19 on v18

--- a/solution.py
+++ b/solution.py
@@ -55,13 +55,14 @@
     return half + half * jnp.tanh(half)
 
 
-def pair_conv(field, row, frames, weight_ref):
+def pair_conv(field, row, begin, frames, weight_ref):
     columns, channels = field.shape[2], field.shape[3]
     cells = frames * columns
     nothing = jnp.zeros((channels, channels), jnp.bfloat16)
 
     def piece(frame_tap, line):
-        return field[frame_tap : frame_tap + frames, row + line].reshape(cells, channels)
+        first = begin + frame_tap
+        return field[first : first + frames, row + line].reshape(cells, channels)
 
     def dot(pieces, blocks):
         return jnp.dot(pieces, blocks, preferred_element_type=jnp.float32)
@@ -203,7 +204,7 @@
         for line in range(ready, 2 * pair + 4):
             fill(line)
         ready = 2 * pair + 4
-        results = pair_conv(field, 2 * pair, inner + 2, weight_ref)
+        results = pair_conv(field, 2 * pair, 0, inner + 2, weight_ref)
         for out in range(2):
             line = 2 * pair + out
             rounded = (results[out] + bias).astype(jnp.bfloat16)
@@ -218,7 +219,8 @@
 
 
 def second_kernel(
-    row_count, middle_ref, stats_ref, vectors_ref, weight_ref, own_ref, out_ref, field
+    row_count, middle_ref, stats_ref, vectors_ref, weight_ref, own_ref, out_ref, field, ready,
+    sems
 ):
     section, row_at = lax.axis_index("section"), lax.axis_index("rows")
     frames, lines, columns, channels = own_ref.shape
@@ -229,28 +231,43 @@
     slope, offset = affine(mine, cells, scale, shift)
     slope_before, offset_before = affine(before, cells, scale, shift)
     at_start = section == 0
-    for line in range(lines + 2):
-        halo, body = middle_ref[:2, line], middle_ref[2:, line]
-        behind = activate(halo, slope_before, offset_before).astype(jnp.bfloat16)
-        behind = jnp.where(at_start, halo, behind)
-        ahead = activate(body, slope, offset).astype(jnp.bfloat16)
-        if line == 0 or line == lines + 1:
-            outside = row_at == 0 if line == 0 else row_at == row_count - 1
-            behind = jnp.where(outside, jnp.zeros_like(behind), behind)
-            ahead = jnp.where(outside, jnp.zeros_like(ahead), ahead)
-        field[:2, line] = behind
-        field[2:, line] = ahead
-    bias = vectors_ref[5]
-    for pair in range(lines // 2):
-        results = pair_conv(field, 2 * pair, frames, weight_ref)
-        for out in range(2):
-            line = 2 * pair + out
-            result = (results[out] + bias).reshape(frames, columns, channels)
-            out_ref[:, line] = (result + own_ref[:, line].astype(jnp.float32)).astype(jnp.bfloat16)
-
-
-def call(kernel, out_shape, scratch, operands, in_place=(), flops=0):
+    half = frames // 2
+    copies = []
+    for begin in range(0, frames, half):
+        filled = 0 if begin == 0 else begin + 2
+        for line in range(lines + 2):
+            ahead = middle_ref[filled : begin + half + 2, line]
+            if begin == 0:
+                behind = activate(ahead[:2], slope_before, offset_before).astype(jnp.bfloat16)
+                behind = jnp.where(at_start, ahead[:2], behind)
+                ahead = activate(ahead[2:], slope, offset).astype(jnp.bfloat16)
+                ahead = jnp.concatenate([behind, ahead], axis=0)
+            else:
+                ahead = activate(ahead, slope, offset).astype(jnp.bfloat16)
+            if line == 0 or line == lines + 1:
+                outside = row_at == 0 if line == 0 else row_at == row_count - 1
+                ahead = jnp.where(outside, jnp.zeros_like(ahead), ahead)
+            field[filled : begin + half + 2, line] = ahead
+        span = slice(begin, begin + half)
+        for pair in range(lines // 2):
+            results = pair_conv(field, 2 * pair, begin, half, weight_ref)
+            for out in range(2):
+                line = 2 * pair + out
+                result = (results[out] + vectors_ref[5]).reshape(half, columns, channels)
+                result = result + own_ref[span, line].astype(jnp.float32)
+                ready[span, line] = result.astype(jnp.bfloat16)
+        copy = pltpu.make_async_copy(
+            ready.at[span], out_ref.at[span], sems.at[begin // half]
+        )
+        copy.start()
+        copies.append(copy)
+    for copy in copies:
+        copy.wait()
+
+
+def call(kernel, out_shape, scratch, operands, in_place=(), out_in_place=False, flops=0):
     vmem = pl.BlockSpec(memory_space=pltpu.VMEM)
+    out_spec = pl.BlockSpec(memory_space=pltpu.HBM) if out_in_place else vmem
     specs = [vmem] * len(operands)
     for index in in_place:
         specs[index] = pl.BlockSpec(memory_space=pltpu.HBM)
@@ -262,7 +279,7 @@
         kernel,
         out_shape=out_shape,
         in_specs=specs,
-        out_specs=jax.tree.map(lambda _: vmem, out_shape),
+        out_specs=jax.tree.map(lambda _: out_spec, out_shape),
         scratch_shapes=scratch,
         compiler_params=pltpu.CompilerParams(vmem_limit_bytes=40 * 2**20),
         cost_estimate=pl.CostEstimate(flops=flops, bytes_accessed=2**20, transcendentals=0),
@@ -339,8 +356,13 @@
     return call(
         functools.partial(second_kernel, row_count),
         jax.ShapeDtypeStruct(activations.shape, jnp.bfloat16),
-        [pltpu.VMEM((frames + 2, lines + 2, columns, channels), jnp.bfloat16)],
+        [
+            pltpu.VMEM((frames + 2, lines + 2, columns, channels), jnp.bfloat16),
+            pltpu.VMEM(activations.shape, jnp.bfloat16),
+            pltpu.SemaphoreType.DMA((2,)),
+        ],
         (middle, stats_two, packed, conv2_weight, own),
+        out_in_place=True,
         flops=10**9,
     )
 

time: 37.5 us -> 37.4 us (level)
  no operation moved by 1% of the time
where the time goes in v19:
time: 37.4 us; the launch traced here: 37.2 us
  blocking collectives  21.1 us (56%)
  Pallas kernels  7.73 us (21%)
  starting transfers between devices  5.29 us (14%)
  waiting for transfers between devices  2.98 us (8%)
    all_to_all x1, blocking collectives, on_device(): stats = lax.all_to_all(both, 'rows', 0, 0, tiled=True)  12.1 us
    all_to_all x1, blocking collectives, on_device(): stats_two = lax.all_to_all(sums_two, ('section', 'rows'), 0, 0, tiled=True)  8.98 us
    pallas_call x4, Pallas kernels, call(): pl.pallas_call(kernel, out_shape=out_shape, in_specs=specs, out_specs=jax...  7.73 us
    ppermute x1, starting transfers between devices, on_device(): received = lax.ppermute(halo, 'section', ring)  2.99 us
    ppermute x1, waiting for transfers between devices, on_device(): passed = lax.ppermute(sums, 'section', ring)  2.98 us
    ppermute x1, starting transfers between devices, on_device(): passed = lax.ppermute(sums, 'section', ring)  1.54 us
    ppermute x2, starting transfers between devices, across(): return lax.ppermute(block, 'rows', list(enumerate(partner)))  0.76 us
  transfers between devices with their start and end apart: 4, of which 1 were waited for; matrix products, arithmetic and copies ran while one was open for 0% of the time, Pallas kernels for 3%

profile of v19, /device:TPU:0, one launch (start us, length us, event | category | flops | bytes accessed | tf_op | source)
XLA Modules:
  0.0 37.2 jit_solution(2337051306198986712)
XLA Ops:
  0.0 1.1 %shard_map.109 = (bf16[8,2,64,128]{3,2,1,0:T(8,128)(2,1)S(1)}, bf16[4,2,64,128]{3,2,1,0:T(8,128)(2,1)S(1)}) custom-call(bf16[8,2,64,128]{3,2,1,0:T(8,128)(2,1)} %own_ref.1, bf16[2,2,64,128]{3,2,1,0:T(8,128)(2,1)} %second_cache_ref.1, bf16[2,2,64,128]{3,2,1,0:T(8,128)(2,1)} %first_cache_ref.1), custom_call_target="tpu_custom_call" | custom-call | bytes 1048576 | tf_op jit(solution)/shard_map/pallas_call | solution.py:278
  1.1 3.0 %collective-permute-start = (bf16[4,2,64,128]{3,2,1,0:T(8,128)(2,1)S(1)}, bf16[4,2,64,128]{3,2,1,0:T(8,128)(2,1)S(1)}, u32[]{:S(2)}, u32[]{:S(2)}) collective-permute-start(bf16[4,2,64,128]{3,2,1,0:T(8,128)(2,1)S(1)} %get-tuple-element.15), channel_id=1, source_target_pairs={{0,8},{8,16},{16,24},{24,0},{1,9},{9,17},{17,25},{25,1},{2,10},{10... | collective-permute-start | bytes 393224 | tf_op jit(solution)/shard_map/ppermute | solution.py:336
  4.1 1.2 %shard_map.110 = (f32[1,2,128]{2,1,0:T(2,128)S(1)}, f32[6,1,128]{2,1,0:T(1,128)S(1)}, bf16[3,3,3,128,128]{4,3,2,1,0:T(8,128)(2,1)S(1)}) custom-call(bf16[8,2,64,128]{3,2,1,0:T(8,128)(2,1)S(1)} %get-tuple-element.16.own_ref, bf16[3,3,3,128,128]{4,3,2,1,0:T(8,128)(2,1)} %weight_ref.2, f32[1,128]{1,0:T(1,128)} %bitcast.8, f32[1,128]{1,0:T(1,128)} %bitcast.9, ...), custom_call_target="tpu_custom_call" | custom-call | bytes 1048576 | tf_op jit(solution)/shard_map/pallas_call | solution.py:278
  5.3 1.5 %collective-permute-start.1 = (f32[1,2,128]{2,1,0:T(2,128)S(1)}, f32[1,2,128]{2,1,0:T(2,128)S(1)}, u32[]{:S(2)}, u32[]{:S(2)}) collective-permute-start(f32[1,2,128]{2,1,0:T(2,128)S(1)} %get-tuple-element.19), channel_id=1, source_target_pairs={{0,8},{8,16},{16,24},{24,0},{1,9},{9,17},{17,25},{25,1},{2,10},{10... | collective-permute-start | bytes 3080 | tf_op jit(solution)/shard_map/ppermute | solution.py:337
  6.9 3.0 %collective-permute-done.1 = f32[1,2,128]{2,1,0:T(2,128)S(1)} collective-permute-done((f32[1,2,128]{2,1,0:T(2,128)S(1)}, f32[1,2,128]{2,1,0:T(2,128)S(1)}, u32[]{:S(2)}, u32[]{:S(2)}) %collective-permute-start.1) | collective-permute-done | bytes 1056 | tf_op jit(solution)/shard_map/ppermute | solution.py:337
  9.8 0.0 collective-permute-done
  9.9 0.1 collective-permute-start.3
  10.0 0.7 %collective-permute-start.2 = (bf16[12,2,64,128]{3,2,1,0:T(8,128)(2,1)S(1)}, bf16[12,2,64,128]{3,2,1,0:T(8,128)(2,1)S(1)}, u32[]{:S(2)}, u32[]{:S(2)}) collective-permute-start(bf16[12,2,64,128]{3,2,1,0:T(8,128)(2,1)S(1)} %constant_dynamic-update-slice_fusion.own_ref), channel_id=1, source_target_pairs={{0,0},{1,2},{2,1},{3,4},{4,3},{5,6},{6,5},{7,7},{8,8},{9,10},{10,9... | collective-permute-start | bytes 1179656 | tf_op jit(solution)/shard_map/ppermute | solution.py:312
  10.7 12.1 %all_to_all.10.stats_ref = f32[8,4,128]{2,1,0:T(4,128)S(1)} all-to-all(f32[8,4,128]{2,1,0:T(4,128)S(1)} %broadcast_in_dim.8), channel_id=1, replica_groups=mesh['section'=4,'rows'=8] {'rows'}, dimensions={0} | all-to-all | bytes 32768 | tf_op jit(solution)/shard_map/all_to_all | solution.py:344
  22.8 0.0 collective-permute-done.3.near_ref
  22.8 0.0 collective-permute-done.2.far_ref
  22.8 0.0 copy-start
  22.8 3.3 %shard_map.111 = (bf16[10,4,64,128]{3,2,1,0:T(8,128)(2,1)S(1)}, f32[32,2,128]{2,1,0:T(2,128)S(1)}) custom-call(bf16[12,2,64,128]{3,2,1,0:T(8,128)(2,1)S(1)} %constant_dynamic-update-slice_fusion.own_ref, bf16[12,2,64,128]{3,2,1,0:T(8,128)(2,1)S(1)} %collective-permute-done.2.far_ref, bf16[12,2,64,128]{3,2,1,0:T(8,128)(2,1)S(1)} %collective-permute-done.3.near_ref, ...), custom_call_target="tpu_custom_call" | custom-call | flops 1000000000 | bytes 1048576 | tf_op jit(solution)/shard_map/pallas_call | solution.py:278
  26.1 9.0 %all_to_all.11.stats_ref = f32[32,2,128]{2,1,0:T(2,128)S(1)} all-to-all(f32[32,2,128]{2,1,0:T(2,128)S(1)} %get-tuple-element.24), channel_id=1, replica_groups=mesh['section'=4,'rows'=8] {'section','rows'}, dimensions={0} | all-to-all | bytes 65536 | tf_op jit(solution)/shard_map/all_to_all | solution.py:355
  35.1 0.0 copy-done
  35.1 2.1 %shard_map.112 = bf16[8,2,64,128]{3,2,1,0:T(8,128)(2,1)} custom-call(bf16[10,4,64,128]{3,2,1,0:T(8,128)(2,1)S(1)} %get-tuple-element.23.middle_ref, f32[32,2,128]{2,1,0:T(2,128)S(1)} %all_to_all.11.stats_ref, f32[6,1,128]{2,1,0:T(1,128)S(1)} %get-tuple-element.21.vectors_ref, bf16[3,3,3,128,128]{4,3,2,1,0:T(8,128)(2,1)S(1)} %copy-done, ...), custom_call_target="tpu_custom_call" | custom-call | flops 1000000000 | bytes 1048576 | tf_op jit(solution)/shard_map/pallas_call | solution.py:278
  (4 shorter events, 0.1 us)
Async XLA Ops:
  1.1 8.8 %collective-permute-start = (bf16[4,2,64,128]{3,2,1,0:T(8,128)(2,1)S(1)}, bf16[4,2,64,128]{3,2,1,0:T(8,128)(2,1)S(1)}, u32[]{:S(2)}, u32[]{:S(2)}) collective-permute-start(bf16[4,2,64,128]{3,2,1,0:T(8,128)(2,1)S(1)} %get-tuple-element.15), channel_id=1, source_target_pairs={{0,8},{8,16},{16,24},{24,0},{1,9},{9,17},{17,25},{25,1},{2,10},{10... | collective-permute-start | bytes 393224 | tf_op jit(solution)/shard_map/ppermute | solution.py:336
  5.3 4.5 %collective-permute-start.1 = (f32[1,2,128]{2,1,0:T(2,128)S(1)}, f32[1,2,128]{2,1,0:T(2,128)S(1)}, u32[]{:S(2)}, u32[]{:S(2)}) collective-permute-start(f32[1,2,128]{2,1,0:T(2,128)S(1)} %get-tuple-element.19), channel_id=1, source_target_pairs={{0,8},{8,16},{16,24},{24,0},{1,9},{9,17},{17,25},{25,1},{2,10},{10... | collective-permute-start | bytes 3080 | tf_op jit(solution)/shard_map/ppermute | solution.py:337
  9.9 12.9 %collective-permute-start.3 = (bf16[12,2,64,128]{3,2,1,0:T(8,128)(2,1)S(1)}, bf16[12,2,64,128]{3,2,1,0:T(8,128)(2,1)S(1)}, u32[]{:S(2)}, u32[]{:S(2)}) collective-permute-start(bf16[12,2,64,128]{3,2,1,0:T(8,128)(2,1)S(1)} %constant_dynamic-update-slice_fusion.own_ref), channel_id=1, source_target_pairs={{0,1},{1,0},{2,3},{3,2},{4,5},{5,4},{6,7},{7,6},{8,9},{9,8},{10,11... | collective-permute-start | bytes 1179656 | tf_op jit(solution)/shard_map/ppermute | solution.py:312
  10.0 12.8 %collective-permute-start.2 = (bf16[12,2,64,128]{3,2,1,0:T(8,128)(2,1)S(1)}, bf16[12,2,64,128]{3,2,1,0:T(8,128)(2,1)S(1)}, u32[]{:S(2)}, u32[]{:S(2)}) collective-permute-start(bf16[12,2,64,128]{3,2,1,0:T(8,128)(2,1)S(1)} %constant_dynamic-update-slice_fusion.own_ref), channel_id=1, source_target_pairs={{0,0},{1,2},{2,1},{3,4},{4,3},{5,6},{6,5},{7,7},{8,8},{9,10},{10,9... | collective-permute-start | bytes 1179656 | tf_op jit(solution)/shard_map/ppermute | solution.py:312
  22.8 12.3 %copy-start = (bf16[3,3,3,128,128]{4,3,2,1,0:T(8,128)(2,1)S(1)}, bf16[3,3,3,128,128]{4,3,2,1,0:T(8,128)(2,1)}, u32[]{:S(2)}) copy-start(bf16[3,3,3,128,128]{4,3,2,1,0:T(8,128)(2,1)} %weight_ref.3) | copy-start | bytes 2654212

commit v20 on v19

--- a/solution.py
+++ b/solution.py
@@ -55,14 +55,13 @@
     return half + half * jnp.tanh(half)
 
 
-def pair_conv(field, row, begin, frames, weight_ref):
-    columns, channels = field.shape[2], field.shape[3]
+def pair_conv(lines, frames, weight_ref):
+    columns, channels = lines[0].shape[1:]
     cells = frames * columns
     nothing = jnp.zeros((channels, channels), jnp.bfloat16)
 
     def piece(frame_tap, line):
-        first = begin + frame_tap
-        return field[first : first + frames, row + line].reshape(cells, channels)
+        return lines[line][frame_tap : frame_tap + frames].reshape(cells, channels)
 
     def dot(pieces, blocks):
         return jnp.dot(pieces, blocks, preferred_element_type=jnp.float32)
@@ -84,9 +83,9 @@
             axis=0,
         ),
     )
-    lines = [(frame_tap, line) for frame_tap in range(3) for line in range(4)]
+    spread = [(frame_tap, line) for frame_tap in range(3) for line in range(4)]
     late = dot(
-        jnp.concatenate([piece(tap, line) for tap, line in lines], axis=1),
+        jnp.concatenate([piece(tap, line) for tap, line in spread], axis=1),
         jnp.concatenate(
             [
                 jnp.concatenate(
@@ -96,7 +95,7 @@
                     ],
                     axis=1,
                 )
-                for tap, line in lines
+                for tap, line in spread
             ],
             axis=0,
         ),
@@ -165,7 +164,7 @@
 
 def first_kernel(
     row_count, own_ref, far_ref, near_ref, stats_ref, vectors_ref, weight_ref, middle_ref,
-    sums_ref, field
+    sums_ref, *field
 ):
     section, row_at = lax.axis_index("section"), lax.axis_index("rows")
     frames, lines, columns, channels = own_ref.shape
@@ -193,8 +192,8 @@
             outside = row_at == 0 if side == 0 else row_at == row_count - 1
             behind = jnp.where(outside, jnp.zeros_like(behind), behind)
             ahead = jnp.where(outside, jnp.zeros_like(ahead), ahead)
-        field[:SPAN_HALO, line] = behind
-        field[SPAN_HALO:, line] = ahead
+        field[line][:SPAN_HALO] = behind
+        field[line][SPAN_HALO:] = ahead
 
     bias = vectors_ref[2]
     kept = []
@@ -204,12 +203,14 @@
         for line in range(ready, 2 * pair + 4):
             fill(line)
         ready = 2 * pair + 4
-        results = pair_conv(field, 2 * pair, 0, inner + 2, weight_ref)
+        results = pair_conv(field[2 * pair : 2 * pair + 4], inner + 2, weight_ref)
         for out in range(2):
             line = 2 * pair + out
             rounded = (results[out] + bias).astype(jnp.bfloat16)
             rounded = rounded.reshape(inner + 2, columns, channels)
-            middle_ref[:2, line] = jnp.where(at_start, field[:spare, line + lines - 1], rounded[:2])
+            middle_ref[:2, line] = jnp.where(
+                at_start, field[line + lines - 1][:spare], rounded[:2]
+            )
             middle_ref[2:, line] = rounded[2:]
             if 1 <= line <= lines:
                 kept.append(rounded[2:].astype(jnp.float32).reshape(-1, channels))
@@ -219,8 +220,8 @@
 
 
 def second_kernel(
-    row_count, middle_ref, stats_ref, vectors_ref, weight_ref, own_ref, out_ref, field, ready,
-    sems
+    row_count, middle_ref, stats_ref, vectors_ref, weight_ref, own_ref, out_ref, ready, sems,
+    *field
 ):
     section, row_at = lax.axis_index("section"), lax.axis_index("rows")
     frames, lines, columns, channels = own_ref.shape
@@ -234,9 +235,9 @@
     half = frames // 2
     copies = []
     for begin in range(0, frames, half):
-        filled = 0 if begin == 0 else begin + 2
+        parts = field[(begin // half) * (lines + 2) :]
         for line in range(lines + 2):
-            ahead = middle_ref[filled : begin + half + 2, line]
+            ahead = middle_ref[begin : begin + half + 2, line]
             if begin == 0:
                 behind = activate(ahead[:2], slope_before, offset_before).astype(jnp.bfloat16)
                 behind = jnp.where(at_start, ahead[:2], behind)
@@ -247,10 +248,10 @@
             if line == 0 or line == lines + 1:
                 outside = row_at == 0 if line == 0 else row_at == row_count - 1
                 ahead = jnp.where(outside, jnp.zeros_like(ahead), ahead)
-            field[filled : begin + half + 2, line] = ahead
+            parts[line][...] = ahead
         span = slice(begin, begin + half)
         for pair in range(lines // 2):
-            results = pair_conv(field, 2 * pair, begin, half, weight_ref)
+            results = pair_conv(parts[2 * pair : 2 * pair + 4], half, weight_ref)
             for out in range(2):
                 line = 2 * pair + out
                 result = (results[out] + vectors_ref[5]).reshape(half, columns, channels)
@@ -348,7 +349,7 @@
             jax.ShapeDtypeStruct((frames + 2, lines + 2, columns, channels), jnp.bfloat16),
             stats_shape,
         ),
-        [pltpu.VMEM((frames + SPAN_HALO, 3 * lines, columns, channels), jnp.bfloat16)],
+        [pltpu.VMEM((frames + SPAN_HALO, columns, channels), jnp.bfloat16)] * (3 * lines),
         (joined, from_far, from_near, stats, packed, weight),
         flops=10**9,
     )
@@ -357,10 +358,10 @@
         functools.partial(second_kernel, row_count),
         jax.ShapeDtypeStruct(activations.shape, jnp.bfloat16),
         [
-            pltpu.VMEM((frames + 2, lines + 2, columns, channels), jnp.bfloat16),
             pltpu.VMEM(activations.shape, jnp.bfloat16),
             pltpu.SemaphoreType.DMA((2,)),
-        ],
+        ]
+        + [pltpu.VMEM((frames // 2 + 2, columns, channels), jnp.bfloat16)] * (2 * lines + 4),
         (middle, stats_two, packed, conv2_weight, own),
         out_in_place=True,
         flops=10**9,

time: 37.4 us -> 37.4 us (level)
  no operation moved by 1% of the time
where the time goes in v20:
time: 37.4 us; the launch traced here: 37.2 us
  blocking collectives  21.1 us (56%)
  Pallas kernels  7.75 us (21%)
  starting transfers between devices  5.29 us (14%)
  waiting for transfers between devices  2.98 us (8%)
    all_to_all x1, blocking collectives, on_device(): stats = lax.all_to_all(both, 'rows', 0, 0, tiled=True)  12.1 us
    all_to_all x1, blocking collectives, on_device(): stats_two = lax.all_to_all(sums_two, ('section', 'rows'), 0, 0, tiled=True)  8.98 us
    pallas_call x4, Pallas kernels, call(): pl.pallas_call(kernel, out_shape=out_shape, in_specs=specs, out_specs=jax...  7.75 us
    ppermute x1, starting transfers between devices, on_device(): received = lax.ppermute(halo, 'section', ring)  2.99 us
    ppermute x1, waiting for transfers between devices, on_device(): passed = lax.ppermute(sums, 'section', ring)  2.98 us
    ppermute x1, starting transfers between devices, on_device(): passed = lax.ppermute(sums, 'section', ring)  1.54 us
    ppermute x2, starting transfers between devices, across(): return lax.ppermute(block, 'rows', list(enumerate(partner)))  0.76 us
  transfers between devices with their start and end apart: 4, of which 1 were waited for; matrix products, arithmetic and copies ran while one was open for 0% of the time, Pallas kernels for 3%

profile of v20, /device:TPU:0, one launch (start us, length us, event | category | flops | bytes accessed | tf_op | source)
XLA Modules:
  0.0 37.2 jit_solution(5558980047816357391)
XLA Ops:
  0.0 1.1 %shard_map.109 = (bf16[8,2,64,128]{3,2,1,0:T(8,128)(2,1)S(1)}, bf16[4,2,64,128]{3,2,1,0:T(8,128)(2,1)S(1)}) custom-call(bf16[8,2,64,128]{3,2,1,0:T(8,128)(2,1)} %own_ref.1, bf16[2,2,64,128]{3,2,1,0:T(8,128)(2,1)} %second_cache_ref.1, bf16[2,2,64,128]{3,2,1,0:T(8,128)(2,1)} %first_cache_ref.1), custom_call_target="tpu_custom_call" | custom-call | bytes 1048576 | tf_op jit(solution)/shard_map/pallas_call | solution.py:279
  1.1 3.0 %collective-permute-start = (bf16[4,2,64,128]{3,2,1,0:T(8,128)(2,1)S(1)}, bf16[4,2,64,128]{3,2,1,0:T(8,128)(2,1)S(1)}, u32[]{:S(2)}, u32[]{:S(2)}) collective-permute-start(bf16[4,2,64,128]{3,2,1,0:T(8,128)(2,1)S(1)} %get-tuple-element.15), channel_id=1, source_target_pairs={{0,8},{8,16},{16,24},{24,0},{1,9},{9,17},{17,25},{25,1},{2,10},{10... | collective-permute-start | bytes 393224 | tf_op jit(solution)/shard_map/ppermute | solution.py:337
  4.1 1.2 %shard_map.110 = (f32[1,2,128]{2,1,0:T(2,128)S(1)}, f32[6,1,128]{2,1,0:T(1,128)S(1)}, bf16[3,3,3,128,128]{4,3,2,1,0:T(8,128)(2,1)S(1)}) custom-call(bf16[8,2,64,128]{3,2,1,0:T(8,128)(2,1)S(1)} %get-tuple-element.16.own_ref, bf16[3,3,3,128,128]{4,3,2,1,0:T(8,128)(2,1)} %weight_ref.2, f32[1,128]{1,0:T(1,128)} %bitcast.8, f32[1,128]{1,0:T(1,128)} %bitcast.9, ...), custom_call_target="tpu_custom_call" | custom-call | bytes 1048576 | tf_op jit(solution)/shard_map/pallas_call | solution.py:279
  5.3 1.5 %collective-permute-start.1 = (f32[1,2,128]{2,1,0:T(2,128)S(1)}, f32[1,2,128]{2,1,0:T(2,128)S(1)}, u32[]{:S(2)}, u32[]{:S(2)}) collective-permute-start(f32[1,2,128]{2,1,0:T(2,128)S(1)} %get-tuple-element.19), channel_id=1, source_target_pairs={{0,8},{8,16},{16,24},{24,0},{1,9},{9,17},{17,25},{25,1},{2,10},{10... | collective-permute-start | bytes 3080 | tf_op jit(solution)/shard_map/ppermute | solution.py:338
  6.9 3.0 %collective-permute-done.1 = f32[1,2,128]{2,1,0:T(2,128)S(1)} collective-permute-done((f32[1,2,128]{2,1,0:T(2,128)S(1)}, f32[1,2,128]{2,1,0:T(2,128)S(1)}, u32[]{:S(2)}, u32[]{:S(2)}) %collective-permute-start.1) | collective-permute-done | bytes 1056 | tf_op jit(solution)/shard_map/ppermute | solution.py:338
  9.8 0.0 collective-permute-done
  9.9 0.1 collective-permute-start.3
  10.0 0.7 %collective-permute-start.2 = (bf16[12,2,64,128]{3,2,1,0:T(8,128)(2,1)S(1)}, bf16[12,2,64,128]{3,2,1,0:T(8,128)(2,1)S(1)}, u32[]{:S(2)}, u32[]{:S(2)}) collective-permute-start(bf16[12,2,64,128]{3,2,1,0:T(8,128)(2,1)S(1)} %constant_dynamic-update-slice_fusion.own_ref), channel_id=1, source_target_pairs={{0,0},{1,2},{2,1},{3,4},{4,3},{5,6},{6,5},{7,7},{8,8},{9,10},{10,9... | collective-permute-start | bytes 1179656 | tf_op jit(solution)/shard_map/ppermute | solution.py:313
  10.7 12.1 %all_to_all.10.stats_ref = f32[8,4,128]{2,1,0:T(4,128)S(1)} all-to-all(f32[8,4,128]{2,1,0:T(4,128)S(1)} %broadcast_in_dim.8), channel_id=1, replica_groups=mesh['section'=4,'rows'=8] {'rows'}, dimensions={0} | all-to-all | bytes 32768 | tf_op jit(solution)/shard_map/all_to_all | solution.py:345
  22.8 0.0 collective-permute-done.3.near_ref
  22.8 0.0 collective-permute-done.2.far_ref
  22.8 0.0 copy-start
  22.8 3.3 %shard_map.111 = (bf16[10,4,64,128]{3,2,1,0:T(8,128)(2,1)S(1)}, f32[32,2,128]{2,1,0:T(2,128)S(1)}) custom-call(bf16[12,2,64,128]{3,2,1,0:T(8,128)(2,1)S(1)} %constant_dynamic-update-slice_fusion.own_ref, bf16[12,2,64,128]{3,2,1,0:T(8,128)(2,1)S(1)} %collective-permute-done.2.far_ref, bf16[12,2,64,128]{3,2,1,0:T(8,128)(2,1)S(1)} %collective-permute-done.3.near_ref, ...), custom_call_target="tpu_custom_call" | custom-call | flops 1000000000 | bytes 1048576 | tf_op jit(solution)/shard_map/pallas_call | solution.py:279
  26.1 9.0 %all_to_all.11.stats_ref = f32[32,2,128]{2,1,0:T(2,128)S(1)} all-to-all(f32[32,2,128]{2,1,0:T(2,128)S(1)} %get-tuple-element.24), channel_id=1, replica_groups=mesh['section'=4,'rows'=8] {'section','rows'}, dimensions={0} | all-to-all | bytes 65536 | tf_op jit(solution)/shard_map/all_to_all | solution.py:356
  35.1 0.0 copy-done
  35.1 2.2 %shard_map.112 = bf16[8,2,64,128]{3,2,1,0:T(8,128)(2,1)} custom-call(bf16[10,4,64,128]{3,2,1,0:T(8,128)(2,1)S(1)} %get-tuple-element.23.middle_ref, f32[32,2,128]{2,1,0:T(2,128)S(1)} %all_to_all.11.stats_ref, f32[6,1,128]{2,1,0:T(1,128)S(1)} %get-tuple-element.21.vectors_ref, bf16[3,3,3,128,128]{4,3,2,1,0:T(8,128)(2,1)S(1)} %copy-done, ...), custom_call_target="tpu_custom_call" | custom-call | flops 1000000000 | bytes 1048576 | tf_op jit(solution)/shard_map/pallas_call | solution.py:279
  (4 shorter events, 0.1 us)
Async XLA Ops:
  1.1 8.8 %collective-permute-start = (bf16[4,2,64,128]{3,2,1,0:T(8,128)(2,1)S(1)}, bf16[4,2,64,128]{3,2,1,0:T(8,128)(2,1)S(1)}, u32[]{:S(2)}, u32[]{:S(2)}) collective-permute-start(bf16[4,2,64,128]{3,2,1,0:T(8,128)(2,1)S(1)} %get-tuple-element.15), channel_id=1, source_target_pairs={{0,8},{8,16},{16,24},{24,0},{1,9},{9,17},{17,25},{25,1},{2,10},{10... | collective-permute-start | bytes 393224 | tf_op jit(solution)/shard_map/ppermute | solution.py:337
  5.3 4.5 %collective-permute-start.1 = (f32[1,2,128]{2,1,0:T(2,128)S(1)}, f32[1,2,128]{2,1,0:T(2,128)S(1)}, u32[]{:S(2)}, u32[]{:S(2)}) collective-permute-start(f32[1,2,128]{2,1,0:T(2,128)S(1)} %get-tuple-element.19), channel_id=1, source_target_pairs={{0,8},{8,16},{16,24},{24,0},{1,9},{9,17},{17,25},{25,1},{2,10},{10... | collective-permute-start | bytes 3080 | tf_op jit(solution)/shard_map/ppermute | solution.py:338
  9.9 12.9 %collective-permute-start.3 = (bf16[12,2,64,128]{3,2,1,0:T(8,128)(2,1)S(1)}, bf16[12,2,64,128]{3,2,1,0:T(8,128)(2,1)S(1)}, u32[]{:S(2)}, u32[]{:S(2)}) collective-permute-start(bf16[12,2,64,128]{3,2,1,0:T(8,128)(2,1)S(1)} %constant_dynamic-update-slice_fusion.own_ref), channel_id=1, source_target_pairs={{0,1},{1,0},{2,3},{3,2},{4,5},{5,4},{6,7},{7,6},{8,9},{9,8},{10,11... | collective-permute-start | bytes 1179656 | tf_op jit(solution)/shard_map/ppermute | solution.py:313
  10.0 12.8 %collective-permute-start.2 = (bf16[12,2,64,128]{3,2,1,0:T(8,128)(2,1)S(1)}, bf16[12,2,64,128]{3,2,1,0:T(8,128)(2,1)S(1)}, u32[]{:S(2)}, u32[]{:S(2)}) collective-permute-start(bf16[12,2,64,128]{3,2,1,0:T(8,128)(2,1)S(1)} %constant_dynamic-update-slice_fusion.own_ref), channel_id=1, source_target_pairs={{0,0},{1,2},{2,1},{3,4},{4,3},{5,6},{6,5},{7,7},{8,8},{9,10},{10,9... | collective-permute-start | bytes 1179656 | tf_op jit(solution)/shard_map/ppermute | solution.py:313
  22.8 12.3 %copy-start = (bf16[3,3,3,128,128]{4,3,2,1,0:T(8,128)(2,1)S(1)}, bf16[3,3,3,128,128]{4,3,2,1,0:T(8,128)(2,1)}, u32[]{:S(2)}) copy-start(bf16[3,3,3,128,128]{4,3,2,1,0:T(8,128)(2,1)} %weight_ref.3) | copy-start | bytes 2654212

commit v21 on v19

--- a/solution.py
+++ b/solution.py
@@ -164,12 +164,11 @@
 
 
 def first_kernel(
-    row_count, own_ref, far_ref, near_ref, stats_ref, vectors_ref, weight_ref, middle_ref,
-    sums_ref, field
+    row_count, halo_ref, own_ref, near_ref, far_ref, stats_ref, vectors_ref, weight_ref,
+    middle_ref, sums_ref, field
 ):
     section, row_at = lax.axis_index("section"), lax.axis_index("rows")
-    frames, lines, columns, channels = own_ref.shape
-    inner = frames - SPAN_HALO
+    inner, lines, columns, channels = own_ref.shape
     cells = inner * lines * columns
     scale, shift = vectors_ref[0], vectors_ref[1]
     mine, before = stats_ref[:, :2], stats_ref[:, 2:]
@@ -181,11 +180,11 @@
     def fill(line):
         side, local = divmod(line, lines)
         if side == 1:
-            block = own_ref[:, local]
+            halo, body = halo_ref[:, local], own_ref[:, local]
         else:
             near_side = even if side == 2 else jnp.logical_not(even)
             block = jnp.where(near_side, near_ref[:, local], far_ref[:, local])
-        halo, body = block[:SPAN_HALO], block[SPAN_HALO:]
+            halo, body = block[:SPAN_HALO], block[SPAN_HALO:]
         behind = activate(halo, slope_before, offset_before).astype(jnp.bfloat16)
         behind = jnp.where(at_start, halo, behind)
         ahead = activate(body, slope, offset).astype(jnp.bfloat16)
@@ -306,7 +305,8 @@
     vectors = (norm1_scale, norm1_shift, conv1_bias, norm2_scale, norm2_shift, conv2_bias)
 
     near = [i ^ 1 for i in range(row_count)]
-    far = [0] + [i + 1 if i % 2 else i - 1 for i in range(1, row_count - 1)] + [row_count - 1]
+    far = [i + 2 if i % 2 == 0 else i - 2 for i in range(row_count)]
+    far[row_count - 2], far[1] = row_count - 1, 0
 
     def across(block, partner):
         return lax.ppermute(block, "rows", list(enumerate(partner)))
@@ -336,9 +336,8 @@
     received = lax.ppermute(halo, "section", ring)
     passed = lax.ppermute(sums, "section", ring)
     received, sums, passed = lax.optimization_barrier((received, sums, passed))
-    joined = jnp.concatenate([received, own], axis=0)
-    from_far = across(joined, far)
-    from_near = across(joined, near)
+    from_near = jnp.concatenate([across(received, near), across(own, near)], axis=0)
+    from_far = across(from_near, far)
     both = jnp.concatenate([sums, passed], axis=1)
     both = jnp.broadcast_to(both, (row_count,) + both.shape[1:])
     stats = lax.all_to_all(both, "rows", 0, 0, tiled=True)
@@ -349,7 +348,7 @@
             stats_shape,
         ),
         [pltpu.VMEM((frames + SPAN_HALO, 3 * lines, columns, channels), jnp.bfloat16)],
-        (joined, from_far, from_near, stats, packed, weight),
+        (received, own, from_near, from_far, stats, packed, weight),
         flops=10**9,
     )
     stats_two = lax.all_to_all(sums_two, ("section", "rows"), 0, 0, tiled=True)

time: 37.4 us -> 36.9 us (0.987)
  blocking collectives: 21.1 us -> 18.4 us
  waiting for transfers between devices: 2.98 us -> 4.33 us
  starting transfers between devices: 5.29 us -> 6.13 us
    all_to_all x1, blocking collectives: 12.1 us -> 9.31 us  [on_device(): stats = lax.all_to_all(both, 'rows', 0, 0, tiled=True)]
    ppermute x2 -> x3, waiting for transfers between devices: 0.01 us -> 1.35 us  [across(): return lax.ppermute(block, 'rows', list(enumerate(partner)))]
    ppermute x2 -> x3, starting transfers between devices: 0.76 us -> 1.6 us  [across(): return lax.ppermute(block, 'rows', list(enumerate(partner)))]
  transfers between devices with their start and end apart: 4 -> 5, of which waited for: 1 -> 2; matrix products, arithmetic and copies ran while one was open for 0% -> 0% of each run, Pallas kernels for 3% -> 3%
where the time goes in v21:
time: 36.9 us; the launch traced here: 36.7 us
  blocking collectives  18.4 us (50%)
  Pallas kernels  7.73 us (21%)
  starting transfers between devices  6.13 us (17%)
  waiting for transfers between devices  4.33 us (12%)
    all_to_all x1, blocking collectives, on_device(): stats = lax.all_to_all(both, 'rows', 0, 0, tiled=True)  9.31 us
    all_to_all x1, blocking collectives, on_device(): stats_two = lax.all_to_all(sums_two, ('section', 'rows'), 0, 0, tiled=True)  9.09 us
    pallas_call x4, Pallas kernels, call(): pl.pallas_call(kernel, out_shape=out_shape, in_specs=specs, out_specs=jax...  7.73 us
    ppermute x1, starting transfers between devices, on_device(): received = lax.ppermute(halo, 'section', ring)  2.99 us
    ppermute x1, waiting for transfers between devices, on_device(): passed = lax.ppermute(sums, 'section', ring)  2.98 us
    ppermute x3, starting transfers between devices, across(): return lax.ppermute(block, 'rows', list(enumerate(partner)))  1.6 us
    ppermute x1, starting transfers between devices, on_device(): passed = lax.ppermute(sums, 'section', ring)  1.54 us
    ppermute x3, waiting for transfers between devices, across(): return lax.ppermute(block, 'rows', list(enumerate(partner)))  1.35 us
  transfers between devices with their start and end apart: 5, of which 2 were waited for; matrix products, arithmetic and copies ran while one was open for 0% of the time, Pallas kernels for 3%

profile of v21, /device:TPU:0, one launch (start us, length us, event | category | flops | bytes accessed | tf_op | source)
XLA Modules:
  0.0 36.7 jit_solution(10527451751458755430)
XLA Ops:
  0.0 1.1 %shard_map.109 = (bf16[8,2,64,128]{3,2,1,0:T(8,128)(2,1)S(1)}, bf16[4,2,64,128]{3,2,1,0:T(8,128)(2,1)S(1)}) custom-call(bf16[8,2,64,128]{3,2,1,0:T(8,128)(2,1)} %own_ref.1, bf16[2,2,64,128]{3,2,1,0:T(8,128)(2,1)} %second_cache_ref.1, bf16[2,2,64,128]{3,2,1,0:T(8,128)(2,1)} %first_cache_ref.1), custom_call_target="tpu_custom_call" | custom-call | bytes 1048576 | tf_op jit(solution)/shard_map/pallas_call | solution.py:277
  1.1 3.0 %collective-permute-start = (bf16[4,2,64,128]{3,2,1,0:T(8,128)(2,1)S(1)}, bf16[4,2,64,128]{3,2,1,0:T(8,128)(2,1)S(1)}, u32[]{:S(2)}, u32[]{:S(2)}) collective-permute-start(bf16[4,2,64,128]{3,2,1,0:T(8,128)(2,1)S(1)} %get-tuple-element.15), channel_id=1, source_target_pairs={{0,8},{8,16},{16,24},{24,0},{1,9},{9,17},{17,25},{25,1},{2,10},{10... | collective-permute-start | bytes 393224 | tf_op jit(solution)/shard_map/ppermute | solution.py:336
  4.1 0.0 collective-permute-start.3
  4.1 1.2 %shard_map.110 = (f32[1,2,128]{2,1,0:T(2,128)S(1)}, f32[6,1,128]{2,1,0:T(1,128)S(1)}, bf16[3,3,3,128,128]{4,3,2,1,0:T(8,128)(2,1)S(1)}) custom-call(bf16[8,2,64,128]{3,2,1,0:T(8,128)(2,1)S(1)} %get-tuple-element.16.own_ref, bf16[3,3,3,128,128]{4,3,2,1,0:T(8,128)(2,1)} %weight_ref.2, f32[1,128]{1,0:T(1,128)} %bitcast.8, f32[1,128]{1,0:T(1,128)} %bitcast.9, ...), custom_call_target="tpu_custom_call" | custom-call | bytes 1048576 | tf_op jit(solution)/shard_map/pallas_call | solution.py:277
  5.3 1.5 %collective-permute-start.1 = (f32[1,2,128]{2,1,0:T(2,128)S(1)}, f32[1,2,128]{2,1,0:T(2,128)S(1)}, u32[]{:S(2)}, u32[]{:S(2)}) collective-permute-start(f32[1,2,128]{2,1,0:T(2,128)S(1)} %get-tuple-element.19), channel_id=1, source_target_pairs={{0,8},{8,16},{16,24},{24,0},{1,9},{9,17},{17,25},{25,1},{2,10},{10... | collective-permute-start | bytes 3080 | tf_op jit(solution)/shard_map/ppermute | solution.py:337
  6.9 3.0 %collective-permute-done.1 = f32[1,2,128]{2,1,0:T(2,128)S(1)} collective-permute-done((f32[1,2,128]{2,1,0:T(2,128)S(1)}, f32[1,2,128]{2,1,0:T(2,128)S(1)}, u32[]{:S(2)}, u32[]{:S(2)}) %collective-permute-start.1) | collective-permute-done | bytes 1056 | tf_op jit(solution)/shard_map/ppermute | solution.py:337
  9.8 0.0 collective-permute-done.halo_ref
  9.8 0.0 collective-permute-start.2
  9.8 1.3 %collective-permute-done.2 = bf16[4,2,64,128]{3,2,1,0:T(8,128)(2,1)S(1)} collective-permute-done((bf16[4,2,64,128]{3,2,1,0:T(8,128)(2,1)S(1)}, bf16[4,2,64,128]{3,2,1,0:T(8,128)(2,1)S(1)}, u32[]{:S(2)}, u32[]{:S(2)}) %collective-permute-start.2) | collective-permute-done | bytes 131104 | tf_op jit(solution)/shard_map/ppermute | solution.py:312
  11.2 0.0 collective-permute-done.3
  11.3 1.6 %collective-permute-start.4 = (bf16[12,2,64,128]{3,2,1,0:T(8,128)(2,1)S(1)}, bf16[12,2,64,128]{3,2,1,0:T(8,128)(2,1)S(1)}, u32[]{:S(2)}, u32[]{:S(2)}) collective-permute-start(bf16[12,2,64,128]{3,2,1,0:T(8,128)(2,1)S(1)} %constant_dynamic-update-slice_fusion.near_ref), channel_id=1, source_target_pairs={{0,2},{1,0},{2,4},{3,1},{4,6},{5,3},{6,7},{7,5},{8,10},{9,8},{10,1... | collective-permute-start | bytes 1179656 | tf_op jit(solution)/shard_map/ppermute | solution.py:312
  12.9 9.3 %all_to_all.10.stats_ref = f32[8,4,128]{2,1,0:T(4,128)S(1)} all-to-all(f32[8,4,128]{2,1,0:T(4,128)S(1)} %broadcast_in_dim.8), channel_id=1, replica_groups=mesh['section'=4,'rows'=8] {'rows'}, dimensions={0} | all-to-all | bytes 32768 | tf_op jit(solution)/shard_map/all_to_all | solution.py:343
  22.2 0.0 collective-permute-done.4.far_ref
  22.2 0.0 copy-start
  22.2 3.3 %shard_map.111 = (bf16[10,4,64,128]{3,2,1,0:T(8,128)(2,1)S(1)}, f32[32,2,128]{2,1,0:T(2,128)S(1)}) custom-call(bf16[4,2,64,128]{3,2,1,0:T(8,128)(2,1)S(1)} %collective-permute-done.halo_ref, bf16[8,2,64,128]{3,2,1,0:T(8,128)(2,1)S(1)} %get-tuple-element.16.own_ref, bf16[12,2,64,128]{3,2,1,0:T(8,128)(2,1)S(1)} %constant_dynamic-update-slice_fusion.near_ref, ...), custom_call_target="tpu_custom_call" | custom-call | flops 1000000000 | bytes 1048576 | tf_op jit(solution)/shard_map/pallas_call | solution.py:277
  25.5 9.1 %all_to_all.11.stats_ref = f32[32,2,128]{2,1,0:T(2,128)S(1)} all-to-all(f32[32,2,128]{2,1,0:T(2,128)S(1)} %get-tuple-element.24), channel_id=1, replica_groups=mesh['section'=4,'rows'=8] {'section','rows'}, dimensions={0} | all-to-all | bytes 65536 | tf_op jit(solution)/shard_map/all_to_all | solution.py:354
  34.6 0.0 copy-done
  34.6 2.2 %shard_map.112 = bf16[8,2,64,128]{3,2,1,0:T(8,128)(2,1)} custom-call(bf16[10,4,64,128]{3,2,1,0:T(8,128)(2,1)S(1)} %get-tuple-element.23.middle_ref, f32[32,2,128]{2,1,0:T(2,128)S(1)} %all_to_all.11.stats_ref, f32[6,1,128]{2,1,0:T(1,128)S(1)} %get-tuple-element.21.vectors_ref, bf16[3,3,3,128,128]{4,3,2,1,0:T(8,128)(2,1)S(1)} %copy-done, ...), custom_call_target="tpu_custom_call" | custom-call | flops 1000000000 | bytes 1048576 | tf_op jit(solution)/shard_map/pallas_call | solution.py:277
  (4 shorter events, 0.1 us)
Async XLA Ops:
  1.1 8.8 %collective-permute-start = (bf16[4,2,64,128]{3,2,1,0:T(8,128)(2,1)S(1)}, bf16[4,2,64,128]{3,2,1,0:T(8,128)(2,1)S(1)}, u32[]{:S(2)}, u32[]{:S(2)}) collective-permute-start(bf16[4,2,64,128]{3,2,1,0:T(8,128)(2,1)S(1)} %get-tuple-element.15), channel_id=1, source_target_pairs={{0,8},{8,16},{16,24},{24,0},{1,9},{9,17},{17,25},{25,1},{2,10},{10... | collective-permute-start | bytes 393224 | tf_op jit(solution)/shard_map/ppermute | solution.py:336
  4.1 7.1 %collective-permute-start.3 = (bf16[8,2,64,128]{3,2,1,0:T(8,128)(2,1)S(1)}, bf16[8,2,64,128]{3,2,1,0:T(8,128)(2,1)S(1)}, u32[]{:S(2)}, u32[]{:S(2)}) collective-permute-start(bf16[8,2,64,128]{3,2,1,0:T(8,128)(2,1)S(1)} %get-tuple-element.16.own_ref), channel_id=1, source_target_pairs={{0,1},{1,0},{2,3},{3,2},{4,5},{5,4},{6,7},{7,6},{8,9},{9,8},{10,11... | collective-permute-start | bytes 786440 | tf_op jit(solution)/shard_map/ppermute | solution.py:312
  5.3 4.5 %collective-permute-start.1 = (f32[1,2,128]{2,1,0:T(2,128)S(1)}, f32[1,2,128]{2,1,0:T(2,128)S(1)}, u32[]{:S(2)}, u32[]{:S(2)}) collective-permute-start(f32[1,2,128]{2,1,0:T(2,128)S(1)} %get-tuple-element.19), channel_id=1, source_target_pairs={{0,8},{8,16},{16,24},{24,0},{1,9},{9,17},{17,25},{25,1},{2,10},{10... | collective-permute-start | bytes 3080 | tf_op jit(solution)/shard_map/ppermute | solution.py:337
  9.8 1.3 %collective-permute-start.2 = (bf16[4,2,64,128]{3,2,1,0:T(8,128)(2,1)S(1)}, bf16[4,2,64,128]{3,2,1,0:T(8,128)(2,1)S(1)}, u32[]{:S(2)}, u32[]{:S(2)}) collective-permute-start(bf16[4,2,64,128]{3,2,1,0:T(8,128)(2,1)S(1)} %collective-permute-done.halo_ref), channel_id=1, source_target_pairs={{0,1},{1,0},{2,3},{3,2},{4,5},{5,4},{6,7},{7,6},{8,9},{9,8},{10,11... | collective-permute-start | bytes 393224 | tf_op jit(solution)/shard_map/ppermute | solution.py:312
  11.3 10.9 %collective-permute-start.4 = (bf16[12,2,64,128]{3,2,1,0:T(8,128)(2,1)S(1)}, bf16[12,2,64,128]{3,2,1,0:T(8,128)(2,1)S(1)}, u32[]{:S(2)}, u32[]{:S(2)}) collective-permute-start(bf16[12,2,64,128]{3,2,1,0:T(8,128)(2,1)S(1)} %constant_dynamic-update-slice_fusion.near_ref), channel_id=1, source_target_pairs={{0,2},{1,0},{2,4},{3,1},{4,6},{5,3},{6,7},{7,5},{8,10},{9,8},{10,1... | collective-permute-start | bytes 1179656 | tf_op jit(solution)/shard_map/ppermute | solution.py:312
  22.2 12.4 %copy-start = (bf16[3,3,3,128,128]{4,3,2,1,0:T(8,128)(2,1)S(1)}, bf16[3,3,3,128,128]{4,3,2,1,0:T(8,128)(2,1)}, u32[]{:S(2)}) copy-start(bf16[3,3,3,128,128]{4,3,2,1,0:T(8,128)(2,1)} %weight_ref.3) | copy-start | bytes 2654212

commit v22 on v21

--- a/solution.py
+++ b/solution.py
@@ -164,8 +164,8 @@
 
 
 def first_kernel(
-    row_count, halo_ref, own_ref, near_ref, far_ref, stats_ref, vectors_ref, weight_ref,
-    middle_ref, sums_ref, field
+    row_count, own_ref, near_ref, far_ref, halo_ref, halo_near_ref, halo_far_ref, stats_ref,
+    vectors_ref, weight_ref, middle_ref, sums_ref, field
 ):
     section, row_at = lax.axis_index("section"), lax.axis_index("rows")
     inner, lines, columns, channels = own_ref.shape
@@ -183,8 +183,8 @@
             halo, body = halo_ref[:, local], own_ref[:, local]
         else:
             near_side = even if side == 2 else jnp.logical_not(even)
-            block = jnp.where(near_side, near_ref[:, local], far_ref[:, local])
-            halo, body = block[:SPAN_HALO], block[SPAN_HALO:]
+            halo = jnp.where(near_side, halo_near_ref[:, local], halo_far_ref[:, local])
+            body = jnp.where(near_side, near_ref[:, local], far_ref[:, local])
         behind = activate(halo, slope_before, offset_before).astype(jnp.bfloat16)
         behind = jnp.where(at_start, halo, behind)
         ahead = activate(body, slope, offset).astype(jnp.bfloat16)
@@ -334,10 +334,12 @@
         in_place=range(1, 2 + len(vectors)),
     )
     received = lax.ppermute(halo, "section", ring)
+    bodies = [own, across(own, near)]
+    bodies.append(across(bodies[1], far))
     passed = lax.ppermute(sums, "section", ring)
     received, sums, passed = lax.optimization_barrier((received, sums, passed))
-    from_near = jnp.concatenate([across(received, near), across(own, near)], axis=0)
-    from_far = across(from_near, far)
+    halos = [received, across(received, near)]
+    halos.append(across(halos[1], far))
     both = jnp.concatenate([sums, passed], axis=1)
     both = jnp.broadcast_to(both, (row_count,) + both.shape[1:])
     stats = lax.all_to_all(both, "rows", 0, 0, tiled=True)
@@ -348,7 +350,7 @@
             stats_shape,
         ),
         [pltpu.VMEM((frames + SPAN_HALO, 3 * lines, columns, channels), jnp.bfloat16)],
-        (received, own, from_near, from_far, stats, packed, weight),
+        (*bodies, *halos, stats, packed, weight),
         flops=10**9,
     )
     stats_two = lax.all_to_all(sums_two, ("section", "rows"), 0, 0, tiled=True)

time: 36.9 us -> 36.8 us (level)
  starting transfers between devices: 6.13 us -> 7.79 us
  waiting for transfers between devices: 4.33 us -> 2.99 us
  blocking collectives: 18.4 us -> 18 us
    ppermute x3 -> x4, starting transfers between devices: 1.6 us -> 3.69 us  [across(): return lax.ppermute(block, 'rows', list(enumerate(partner)))]
    ppermute x3 -> x4, waiting for transfers between devices: 1.35 us -> 0.01 us  [across(): return lax.ppermute(block, 'rows', list(enumerate(partner)))]
    ppermute x1, starting transfers between devices: 2.99 us -> 2.55 us  [on_device(): received = lax.ppermute(halo, 'section', ring)]
  transfers between devices with their start and end apart: 5 -> 6, of which waited for: 2 -> 1; matrix products, arithmetic and copies ran while one was open for 0% -> 0% of each run, Pallas kernels for 3% -> 3%
where the time goes in v22:
time: 36.8 us; the launch traced here: 36.6 us
  blocking collectives  18 us (49%)
  starting transfers between devices  7.79 us (21%)
  Pallas kernels  7.75 us (21%)
  waiting for transfers between devices  2.99 us (8%)
    all_to_all x1, blocking collectives, on_device(): stats = lax.all_to_all(both, 'rows', 0, 0, tiled=True)  9.06 us
    all_to_all x1, blocking collectives, on_device(): stats_two = lax.all_to_all(sums_two, ('section', 'rows'), 0, 0, tiled=True)  8.97 us
    pallas_call x4, Pallas kernels, call(): pl.pallas_call(kernel, out_shape=out_shape, in_specs=specs, out_specs=jax...  7.75 us
    ppermute x4, starting transfers between devices, across(): return lax.ppermute(block, 'rows', list(enumerate(partner)))  3.69 us
    ppermute x1, waiting for transfers between devices, on_device(): passed = lax.ppermute(sums, 'section', ring)  2.98 us
    ppermute x1, starting transfers between devices, on_device(): received = lax.ppermute(halo, 'section', ring)  2.55 us
    ppermute x1, starting transfers between devices, on_device(): passed = lax.ppermute(sums, 'section', ring)  1.54 us
  transfers between devices with their start and end apart: 6, of which 1 were waited for; matrix products, arithmetic and copies ran while one was open for 0% of the time, Pallas kernels for 3%

profile of v22, /device:TPU:0, one launch (start us, length us, event | category | flops | bytes accessed | tf_op | source)
XLA Modules:
  0.0 36.6 jit_solution(6221004506136355495)
XLA Ops:
  0.0 1.1 %shard_map.109 = (bf16[8,2,64,128]{3,2,1,0:T(8,128)(2,1)S(1)}, bf16[4,2,64,128]{3,2,1,0:T(8,128)(2,1)S(1)}) custom-call(bf16[8,2,64,128]{3,2,1,0:T(8,128)(2,1)} %own_ref.1, bf16[2,2,64,128]{3,2,1,0:T(8,128)(2,1)} %second_cache_ref.1, bf16[2,2,64,128]{3,2,1,0:T(8,128)(2,1)} %first_cache_ref.1), custom_call_target="tpu_custom_call" | custom-call | bytes 1048576 | tf_op jit(solution)/shard_map/pallas_call | solution.py:277
  1.1 0.5 %collective-permute-start = (bf16[8,2,64,128]{3,2,1,0:T(8,128)(2,1)S(1)}, bf16[8,2,64,128]{3,2,1,0:T(8,128)(2,1)S(1)}, u32[]{:S(2)}, u32[]{:S(2)}) collective-permute-start(bf16[8,2,64,128]{3,2,1,0:T(8,128)(2,1)S(1)} %get-tuple-element.15.own_ref), channel_id=1, source_target_pairs={{0,1},{1,0},{2,3},{3,2},{4,5},{5,4},{6,7},{7,6},{8,9},{9,8},{10,11... | collective-permute-start | bytes 786440 | tf_op jit(solution)/shard_map/ppermute | solution.py:312
  1.6 2.6 %collective-permute-start.2 = (bf16[4,2,64,128]{3,2,1,0:T(8,128)(2,1)S(1)}, bf16[4,2,64,128]{3,2,1,0:T(8,128)(2,1)S(1)}, u32[]{:S(2)}, u32[]{:S(2)}) collective-permute-start(bf16[4,2,64,128]{3,2,1,0:T(8,128)(2,1)S(1)} %get-tuple-element.16), channel_id=1, source_target_pairs={{0,8},{8,16},{16,24},{24,0},{1,9},{9,17},{17,25},{25,1},{2,10},{10... | collective-permute-start | bytes 393224 | tf_op jit(solution)/shard_map/ppermute | solution.py:336
  4.1 1.2 %shard_map.110 = (f32[1,2,128]{2,1,0:T(2,128)S(1)}, f32[6,1,128]{2,1,0:T(1,128)S(1)}, bf16[3,3,3,128,128]{4,3,2,1,0:T(8,128)(2,1)S(1)}) custom-call(bf16[8,2,64,128]{3,2,1,0:T(8,128)(2,1)S(1)} %get-tuple-element.15.own_ref, bf16[3,3,3,128,128]{4,3,2,1,0:T(8,128)(2,1)} %weight_ref.2, f32[1,128]{1,0:T(1,128)} %bitcast.8, f32[1,128]{1,0:T(1,128)} %bitcast.9, ...), custom_call_target="tpu_custom_call" | custom-call | bytes 1048576 | tf_op jit(solution)/shard_map/pallas_call | solution.py:277
  5.4 1.5 %collective-permute-start.3 = (f32[1,2,128]{2,1,0:T(2,128)S(1)}, f32[1,2,128]{2,1,0:T(2,128)S(1)}, u32[]{:S(2)}, u32[]{:S(2)}) collective-permute-start(f32[1,2,128]{2,1,0:T(2,128)S(1)} %get-tuple-element.19), channel_id=1, source_target_pairs={{0,8},{8,16},{16,24},{24,0},{1,9},{9,17},{17,25},{25,1},{2,10},{10... | collective-permute-start | bytes 3080 | tf_op jit(solution)/shard_map/ppermute | solution.py:339
  6.9 3.0 %collective-permute-done.3 = f32[1,2,128]{2,1,0:T(2,128)S(1)} collective-permute-done((f32[1,2,128]{2,1,0:T(2,128)S(1)}, f32[1,2,128]{2,1,0:T(2,128)S(1)}, u32[]{:S(2)}, u32[]{:S(2)}) %collective-permute-start.3) | collective-permute-done | bytes 1056 | tf_op jit(solution)/shard_map/ppermute | solution.py:339
  9.9 0.0 collective-permute-done.2.halo_ref
  9.9 0.0 collective-permute-start.4
  9.9 0.0 collective-permute-done.near_ref
  9.9 1.6 %collective-permute-start.1 = (bf16[8,2,64,128]{3,2,1,0:T(8,128)(2,1)S(1)}, bf16[8,2,64,128]{3,2,1,0:T(8,128)(2,1)S(1)}, u32[]{:S(2)}, u32[]{:S(2)}) collective-permute-start(bf16[8,2,64,128]{3,2,1,0:T(8,128)(2,1)S(1)} %collective-permute-done.near_ref), channel_id=1, source_target_pairs={{0,2},{1,0},{2,4},{3,1},{4,6},{5,3},{6,7},{7,5},{8,10},{9,8},{10,1... | collective-permute-start | bytes 786440 | tf_op jit(solution)/shard_map/ppermute | solution.py:312
  11.5 0.0 collective-permute-done.4.halo_near_ref
  11.5 1.6 %collective-permute-start.5 = (bf16[4,2,64,128]{3,2,1,0:T(8,128)(2,1)S(1)}, bf16[4,2,64,128]{3,2,1,0:T(8,128)(2,1)S(1)}, u32[]{:S(2)}, u32[]{:S(2)}) collective-permute-start(bf16[4,2,64,128]{3,2,1,0:T(8,128)(2,1)S(1)} %collective-permute-done.4.halo_near_ref), channel_id=1, source_target_pairs={{0,2},{1,0},{2,4},{3,1},{4,6},{5,3},{6,7},{7,5},{8,10},{9,8},{10,1... | collective-permute-start | bytes 393224 | tf_op jit(solution)/shard_map/ppermute | solution.py:312
  13.1 9.1 %all_to_all.10.stats_ref = f32[8,4,128]{2,1,0:T(4,128)S(1)} all-to-all(f32[8,4,128]{2,1,0:T(4,128)S(1)} %broadcast_in_dim.8), channel_id=1, replica_groups=mesh['section'=4,'rows'=8] {'rows'}, dimensions={0} | all-to-all | bytes 32768 | tf_op jit(solution)/shard_map/all_to_all | solution.py:345
  22.2 0.0 collective-permute-done.5.halo_far_ref
  22.2 0.0 collective-permute-done.1.far_ref
  22.2 0.0 copy-start
  22.2 3.3 %shard_map.111 = (bf16[10,4,64,128]{3,2,1,0:T(8,128)(2,1)S(1)}, f32[32,2,128]{2,1,0:T(2,128)S(1)}) custom-call(bf16[8,2,64,128]{3,2,1,0:T(8,128)(2,1)S(1)} %get-tuple-element.15.own_ref, bf16[8,2,64,128]{3,2,1,0:T(8,128)(2,1)S(1)} %collective-permute-done.near_ref, bf16[8,2,64,128]{3,2,1,0:T(8,128)(2,1)S(1)} %collective-permute-done.1.far_ref, ...), custom_call_target="tpu_custom_call" | custom-call | flops 1000000000 | bytes 1048576 | tf_op jit(solution)/shard_map/pallas_call | solution.py:277
  25.5 9.0 %all_to_all.11.stats_ref = f32[32,2,128]{2,1,0:T(2,128)S(1)} all-to-all(f32[32,2,128]{2,1,0:T(2,128)S(1)} %get-tuple-element.24), channel_id=1, replica_groups=mesh['section'=4,'rows'=8] {'section','rows'}, dimensions={0} | all-to-all | bytes 65536 | tf_op jit(solution)/shard_map/all_to_all | solution.py:356
  34.5 0.0 copy-done
  34.5 2.2 %shard_map.112 = bf16[8,2,64,128]{3,2,1,0:T(8,128)(2,1)} custom-call(bf16[10,4,64,128]{3,2,1,0:T(8,128)(2,1)S(1)} %get-tuple-element.23.middle_ref, f32[32,2,128]{2,1,0:T(2,128)S(1)} %all_to_all.11.stats_ref, f32[6,1,128]{2,1,0:T(1,128)S(1)} %get-tuple-element.21.vectors_ref, bf16[3,3,3,128,128]{4,3,2,1,0:T(8,128)(2,1)S(1)} %copy-done, ...), custom_call_target="tpu_custom_call" | custom-call | flops 1000000000 | bytes 1048576 | tf_op jit(solution)/shard_map/pallas_call | solution.py:277
  (2 shorter events, 0.0 us)
Async XLA Ops:
  1.1 8.8 %collective-permute-start = (bf16[8,2,64,128]{3,2,1,0:T(8,128)(2,1)S(1)}, bf16[8,2,64,128]{3,2,1,0:T(8,128)(2,1)S(1)}, u32[]{:S(2)}, u32[]{:S(2)}) collective-permute-start(bf16[8,2,64,128]{3,2,1,0:T(8,128)(2,1)S(1)} %get-tuple-element.15.own_ref), channel_id=1, source_target_pairs={{0,1},{1,0},{2,3},{3,2},{4,5},{5,4},{6,7},{7,6},{8,9},{9,8},{10,11... | collective-permute-start | bytes 786440 | tf_op jit(solution)/shard_map/ppermute | solution.py:312
  1.6 8.3 %collective-permute-start.2 = (bf16[4,2,64,128]{3,2,1,0:T(8,128)(2,1)S(1)}, bf16[4,2,64,128]{3,2,1,0:T(8,128)(2,1)S(1)}, u32[]{:S(2)}, u32[]{:S(2)}) collective-permute-start(bf16[4,2,64,128]{3,2,1,0:T(8,128)(2,1)S(1)} %get-tuple-element.16), channel_id=1, source_target_pairs={{0,8},{8,16},{16,24},{24,0},{1,9},{9,17},{17,25},{25,1},{2,10},{10... | collective-permute-start | bytes 393224 | tf_op jit(solution)/shard_map/ppermute | solution.py:336
  5.4 4.5 %collective-permute-start.3 = (f32[1,2,128]{2,1,0:T(2,128)S(1)}, f32[1,2,128]{2,1,0:T(2,128)S(1)}, u32[]{:S(2)}, u32[]{:S(2)}) collective-permute-start(f32[1,2,128]{2,1,0:T(2,128)S(1)} %get-tuple-element.19), channel_id=1, source_target_pairs={{0,8},{8,16},{16,24},{24,0},{1,9},{9,17},{17,25},{25,1},{2,10},{10... | collective-permute-start | bytes 3080 | tf_op jit(solution)/shard_map/ppermute | solution.py:339
  9.9 1.6 %collective-permute-start.4 = (bf16[4,2,64,128]{3,2,1,0:T(8,128)(2,1)S(1)}, bf16[4,2,64,128]{3,2,1,0:T(8,128)(2,1)S(1)}, u32[]{:S(2)}, u32[]{:S(2)}) collective-permute-start(bf16[4,2,64,128]{3,2,1,0:T(8,128)(2,1)S(1)} %collective-permute-done.2.halo_ref), channel_id=1, source_target_pairs={{0,1},{1,0},{2,3},{3,2},{4,5},{5,4},{6,7},{7,6},{8,9},{9,8},{10,11... | collective-permute-start | bytes 393224 | tf_op jit(solution)/shard_map/ppermute | solution.py:312
  9.9 12.3 %collective-permute-start.1 = (bf16[8,2,64,128]{3,2,1,0:T(8,128)(2,1)S(1)}, bf16[8,2,64,128]{3,2,1,0:T(8,128)(2,1)S(1)}, u32[]{:S(2)}, u32[]{:S(2)}) collective-permute-start(bf16[8,2,64,128]{3,2,1,0:T(8,128)(2,1)S(1)} %collective-permute-done.near_ref), channel_id=1, source_target_pairs={{0,2},{1,0},{2,4},{3,1},{4,6},{5,3},{6,7},{7,5},{8,10},{9,8},{10,1... | collective-permute-start | bytes 786440 | tf_op jit(solution)/shard_map/ppermute | solution.py:312
  11.5 10.7 %collective-permute-start.5 = (bf16[4,2,64,128]{3,2,1,0:T(8,128)(2,1)S(1)}, bf16[4,2,64,128]{3,2,1,0:T(8,128)(2,1)S(1)}, u32[]{:S(2)}, u32[]{:S(2)}) collective-permute-start(bf16[4,2,64,128]{3,2,1,0:T(8,128)(2,1)S(1)} %collective-permute-done.4.halo_near_ref), channel_id=1, source_target_pairs={{0,2},{1,0},{2,4},{3,1},{4,6},{5,3},{6,7},{7,5},{8,10},{9,8},{10,1... | collective-permute-start | bytes 393224 | tf_op jit(solution)/shard_map/ppermute | solution.py:312
  22.2 12.3 %copy-start = (bf16[3,3,3,128,128]{4,3,2,1,0:T(8,128)(2,1)S(1)}, bf16[3,3,3,128,128]{4,3,2,1,0:T(8,128)(2,1)}, u32[]{:S(2)}) copy-start(bf16[3,3,3,128,128]{4,3,2,1,0:T(8,128)(2,1)} %weight_ref.3) | copy-start | bytes 2654212

commit v23 on v21

--- a/solution.py
+++ b/solution.py
@@ -115,49 +115,41 @@
     return results
 
 
-def copy_kernel(sections, own_ref, second_cache_ref, first_cache_ref, copied, halo_ref, sems):
+def copy_kernel(sections, own_ref, second_cache_ref, first_cache_ref, halo_ref, sems):
     last = lax.axis_index("section") == sections - 1
     frames = own_ref.shape[0]
     spare = SPAN_HALO - 2
     tail = pltpu.make_async_copy(own_ref.at[frames - SPAN_HALO :], halo_ref, sems.at[0])
     older = pltpu.make_async_copy(second_cache_ref, halo_ref.at[:spare], sems.at[1])
     newer = pltpu.make_async_copy(first_cache_ref, halo_ref.at[spare:], sems.at[2])
-    load = pltpu.make_async_copy(own_ref, copied, sems.at[3])
 
     @pl.when(last)
     def _():
         older.start()
         newer.start()
+        older.wait()
+        newer.wait()
 
     @pl.when(jnp.logical_not(last))
     def _():
         tail.start()
-
-    load.start()
-
-    @pl.when(last)
-    def _():
-        older.wait()
-        newer.wait()
-
-    @pl.when(jnp.logical_not(last))
-    def _():
         tail.wait()
 
-    load.wait()
-
 
 def stats_kernel(own_ref, weight_ref, *rest):
-    *vector_refs, stats_ref, vectors_ref, weight_copy, sems = rest
-    loads = [pltpu.make_async_copy(weight_ref, weight_copy, sems.at[0])]
+    *vector_refs, stats_ref, vectors_ref, copied, weight_copy, sems = rest
+    first = pltpu.make_async_copy(own_ref, copied, sems.at[0])
+    first.start()
+    loads = [pltpu.make_async_copy(weight_ref, weight_copy, sems.at[1])]
     loads += [
-        pltpu.make_async_copy(vector_ref, vectors_ref.at[index], sems.at[1 + index])
+        pltpu.make_async_copy(vector_ref, vectors_ref.at[index], sems.at[2 + index])
         for index, vector_ref in enumerate(vector_refs)
     ]
     for load in loads:
         load.start()
+    first.wait()
     channels = own_ref.shape[-1]
-    blocks = [own_ref[frame].astype(jnp.float32) for frame in range(own_ref.shape[0])]
+    blocks = [copied[frame].astype(jnp.float32) for frame in range(own_ref.shape[0])]
     stats_ref[0] = moments([block.reshape(-1, channels) for block in blocks])
     for load in loads:
         load.wait()
@@ -225,8 +217,8 @@
     frames, lines, columns, channels = own_ref.shape
     cells = frames * lines * columns
     scale, shift = vectors_ref[3], vectors_ref[4]
-    mine = stats_ref[pl.ds(section * row_count, row_count)]
-    before = stats_ref[pl.ds(jnp.maximum(section - 1, 0) * row_count, row_count)]
+    mine = stats_ref[:, section]
+    before = stats_ref[:, jnp.maximum(section - 1, 0)]
     slope, offset = affine(mine, cells, scale, shift)
     slope_before, offset_before = affine(before, cells, scale, shift)
     at_start = section == 0
@@ -312,31 +304,29 @@
         return lax.ppermute(block, "rows", list(enumerate(partner)))
 
     ring = [(at, (at + 1) % sections) for at in range(sections)]
-    own, halo = call(
+    halo = call(
         functools.partial(copy_kernel, sections),
-        (
-            jax.ShapeDtypeStruct(activations.shape, jnp.bfloat16),
-            jax.ShapeDtypeStruct((SPAN_HALO, lines, columns, channels), jnp.bfloat16),
-        ),
-        [pltpu.SemaphoreType.DMA((4,))],
+        jax.ShapeDtypeStruct((SPAN_HALO, lines, columns, channels), jnp.bfloat16),
+        [pltpu.SemaphoreType.DMA((3,))],
         (activations, second_cache, first_cache),
         in_place=range(3),
     )
-    sums, packed, weight = call(
+    sums, packed, own, weight = call(
         stats_kernel,
         (
             jax.ShapeDtypeStruct((1, 2, channels), jnp.float32),
             jax.ShapeDtypeStruct((len(vectors), 1, channels), jnp.float32),
+            jax.ShapeDtypeStruct(activations.shape, jnp.bfloat16),
             jax.ShapeDtypeStruct(conv1_weight.shape, jnp.bfloat16),
         ),
-        [pltpu.SemaphoreType.DMA((1 + len(vectors),))],
-        (own, conv1_weight) + tuple(vector.reshape(1, channels) for vector in vectors),
-        in_place=range(1, 2 + len(vectors)),
+        [pltpu.SemaphoreType.DMA((2 + len(vectors),))],
+        (activations, conv1_weight) + tuple(vector.reshape(1, channels) for vector in vectors),
+        in_place=range(2 + len(vectors)),
     )
     received = lax.ppermute(halo, "section", ring)
     passed = lax.ppermute(sums, "section", ring)
     received, sums, passed = lax.optimization_barrier((received, sums, passed))
-    from_near = jnp.concatenate([across(received, near), across(own, near)], axis=0)
+    from_near = jnp.concatenate([across(received, near), across(activations, near)], axis=0)
     from_far = across(from_near, far)
     both = jnp.concatenate([sums, passed], axis=1)
     both = jnp.broadcast_to(both, (row_count,) + both.shape[1:])
@@ -351,7 +341,8 @@
         (received, own, from_near, from_far, stats, packed, weight),
         flops=10**9,
     )
-    stats_two = lax.all_to_all(sums_two, ("section", "rows"), 0, 0, tiled=True)
+    stats_two = lax.all_to_all(sums_two, ("rows", "section"), 0, 0, tiled=True)
+    stats_two = stats_two.reshape(row_count, sections, 2, channels)
     return call(
         functools.partial(second_kernel, row_count),
         jax.ShapeDtypeStruct(activations.shape, jnp.bfloat16),

time: 36.9 us -> 37 us (level)
  transfers between devices with their start and end apart: 5 -> 5, of which waited for: 2 -> 2; matrix products, arithmetic and copies ran while one was open for 0% -> 0% of each run, Pallas kernels for 3% -> 4%
where the time goes in v23:
time: 37 us; the launch traced here: 36.8 us
  blocking collectives  18.4 us (50%)
  Pallas kernels  7.79 us (21%)
  starting transfers between devices  6.13 us (17%)
  waiting for transfers between devices  4.33 us (12%)
    all_to_all x1, blocking collectives, on_device(): stats = lax.all_to_all(both, 'rows', 0, 0, tiled=True)  9.31 us
    all_to_all x1, blocking collectives, on_device(): stats_two = lax.all_to_all(sums_two, ('rows', 'section'), 0, 0, tiled=True)  9.1 us
    pallas_call x4, Pallas kernels, call(): pl.pallas_call(kernel, out_shape=out_shape, in_specs=specs, out_specs=jax...  7.79 us
    ppermute x1, starting transfers between devices, on_device(): received = lax.ppermute(halo, 'section', ring)  2.99 us
    ppermute x1, waiting for transfers between devices, on_device(): passed = lax.ppermute(sums, 'section', ring)  2.98 us
    ppermute x3, starting transfers between devices, across(): return lax.ppermute(block, 'rows', list(enumerate(partner)))  1.6 us
    ppermute x1, starting transfers between devices, on_device(): passed = lax.ppermute(sums, 'section', ring)  1.54 us
    ppermute x3, waiting for transfers between devices, across(): return lax.ppermute(block, 'rows', list(enumerate(partner)))  1.35 us
  transfers between devices with their start and end apart: 5, of which 2 were waited for; matrix products, arithmetic and copies ran while one was open for 0% of the time, Pallas kernels for 4%

profile of v23, /device:TPU:0, one launch (start us, length us, event | category | flops | bytes accessed | tf_op | source)
XLA Modules:
  0.0 36.8 jit_solution(7236804916465056304)
XLA Ops:
  0.0 0.0 copy-start.1
  0.0 1.0 %shard_map.109 = bf16[4,2,64,128]{3,2,1,0:T(8,128)(2,1)S(1)} custom-call(bf16[8,2,64,128]{3,2,1,0:T(8,128)(2,1)} %own_ref.3, bf16[2,2,64,128]{3,2,1,0:T(8,128)(2,1)} %second_cache_ref.1, bf16[2,2,64,128]{3,2,1,0:T(8,128)(2,1)} %first_cache_ref.1), custom_call_target="tpu_custom_call" | custom-call | bytes 1048576 | tf_op jit(solution)/shard_map/pallas_call | solution.py:269
  1.0 3.0 %collective-permute-start = (bf16[4,2,64,128]{3,2,1,0:T(8,128)(2,1)S(1)}, bf16[4,2,64,128]{3,2,1,0:T(8,128)(2,1)S(1)}, u32[]{:S(2)}, u32[]{:S(2)}) collective-permute-start(bf16[4,2,64,128]{3,2,1,0:T(8,128)(2,1)S(1)} %shard_map.109), channel_id=1, source_target_pairs={{0,8},{8,16},{16,24},{24,0},{1,9},{9,17},{17,25},{25,1},{2,10},{10... | collective-permute-start | bytes 393224 | tf_op jit(solution)/shard_map/ppermute | solution.py:326
  4.0 0.0 copy-done.1
  4.0 0.0 collective-permute-start.3
  4.0 1.4 %shard_map.110 = (f32[1,2,128]{2,1,0:T(2,128)S(1)}, f32[6,1,128]{2,1,0:T(1,128)S(1)}, bf16[8,2,64,128]{3,2,1,0:T(8,128)(2,1)S(1)}, bf16[3,3,3,128,128]{4,3,2,1,0:T(8,128)(2,1)S(1)}) custom-call(bf16[8,2,64,128]{3,2,1,0:T(8,128)(2,1)} %own_ref.3, bf16[3,3,3,128,128]{4,3,2,1,0:T(8,128)(2,1)} %weight_ref.2, f32[1,128]{1,0:T(1,128)} %bitcast.10, ...), custom_call_target="tpu_custom_call" | custom-call | bytes 1048576 | tf_op jit(solution)/shard_map/pallas_call | solution.py:269
  5.4 1.5 %collective-permute-start.1 = (f32[1,2,128]{2,1,0:T(2,128)S(1)}, f32[1,2,128]{2,1,0:T(2,128)S(1)}, u32[]{:S(2)}, u32[]{:S(2)}) collective-permute-start(f32[1,2,128]{2,1,0:T(2,128)S(1)} %get-tuple-element.17), channel_id=1, source_target_pairs={{0,8},{8,16},{16,24},{24,0},{1,9},{9,17},{17,25},{25,1},{2,10},{10... | collective-permute-start | bytes 3080 | tf_op jit(solution)/shard_map/ppermute | solution.py:327
  6.9 3.0 %collective-permute-done.1 = f32[1,2,128]{2,1,0:T(2,128)S(1)} collective-permute-done((f32[1,2,128]{2,1,0:T(2,128)S(1)}, f32[1,2,128]{2,1,0:T(2,128)S(1)}, u32[]{:S(2)}, u32[]{:S(2)}) %collective-permute-start.1) | collective-permute-done | bytes 1056 | tf_op jit(solution)/shard_map/ppermute | solution.py:327
  9.9 0.0 collective-permute-done.halo_ref
  9.9 0.0 collective-permute-start.2
  9.9 1.3 %collective-permute-done.2 = bf16[4,2,64,128]{3,2,1,0:T(8,128)(2,1)S(1)} collective-permute-done((bf16[4,2,64,128]{3,2,1,0:T(8,128)(2,1)S(1)}, bf16[4,2,64,128]{3,2,1,0:T(8,128)(2,1)S(1)}, u32[]{:S(2)}, u32[]{:S(2)}) %collective-permute-start.2) | collective-permute-done | bytes 131104 | tf_op jit(solution)/shard_map/ppermute | solution.py:304
  11.3 0.0 collective-permute-done.3
  11.3 1.6 %collective-permute-start.4 = (bf16[12,2,64,128]{3,2,1,0:T(8,128)(2,1)S(1)}, bf16[12,2,64,128]{3,2,1,0:T(8,128)(2,1)S(1)}, u32[]{:S(2)}, u32[]{:S(2)}) collective-permute-start(bf16[12,2,64,128]{3,2,1,0:T(8,128)(2,1)S(1)} %constant_dynamic-update-slice_fusion.near_ref), channel_id=1, source_target_pairs={{0,2},{1,0},{2,4},{3,1},{4,6},{5,3},{6,7},{7,5},{8,10},{9,8},{10,1... | collective-permute-start | bytes 1179656 | tf_op jit(solution)/shard_map/ppermute | solution.py:304
  12.9 9.3 %all_to_all.10.stats_ref = f32[8,4,128]{2,1,0:T(4,128)S(1)} all-to-all(f32[8,4,128]{2,1,0:T(4,128)S(1)} %broadcast_in_dim.8), channel_id=1, replica_groups=mesh['section'=4,'rows'=8] {'rows'}, dimensions={0} | all-to-all | bytes 32768 | tf_op jit(solution)/shard_map/all_to_all | solution.py:333
  22.2 0.0 collective-permute-done.4.far_ref
  22.2 0.0 copy-start
  22.2 3.3 %shard_map.111 = (bf16[10,4,64,128]{3,2,1,0:T(8,128)(2,1)S(1)}, f32[32,2,128]{2,1,0:T(2,128)S(1)}) custom-call(bf16[4,2,64,128]{3,2,1,0:T(8,128)(2,1)S(1)} %collective-permute-done.halo_ref, bf16[8,2,64,128]{3,2,1,0:T(8,128)(2,1)S(1)} %get-tuple-element.16.own_ref, bf16[12,2,64,128]{3,2,1,0:T(8,128)(2,1)S(1)} %constant_dynamic-update-slice_fusion.near_ref, ...), custom_call_target="tpu_custom_call" | custom-call | flops 1000000000 | bytes 1048576 | tf_op jit(solution)/shard_map/pallas_call | solution.py:269
  25.5 9.1 %all_to_all.11 = f32[32,2,128]{2,1,0:T(2,128)S(1)} all-to-all(f32[32,2,128]{2,1,0:T(2,128)S(1)} %get-tuple-element.22), channel_id=1, replica_groups=mesh['section'=4,'rows'=8] {'rows','section'}, dimensions={0} | all-to-all | bytes 65536 | tf_op jit(solution)/shard_map/all_to_all | solution.py:344
  34.6 0.0 copy-done
  34.6 2.2 %shard_map.112 = bf16[8,2,64,128]{3,2,1,0:T(8,128)(2,1)} custom-call(bf16[10,4,64,128]{3,2,1,0:T(8,128)(2,1)S(1)} %get-tuple-element.21.middle_ref, f32[8,4,2,128]{3,2,1,0:T(2,128)S(1)} %bitcast.9, f32[6,1,128]{2,1,0:T(1,128)S(1)} %get-tuple-element.19.vectors_ref, bf16[3,3,3,128,128]{4,3,2,1,0:T(8,128)(2,1)S(1)} %copy-done, ...), custom_call_target="tpu_custom_call" | custom-call | flops 1000000000 | bytes 1048576 | tf_op jit(solution)/shard_map/pallas_call | solution.py:269
  (4 shorter events, 0.1 us)
Async XLA Ops:
  0.0 4.0 %copy-start.1 = (bf16[8,2,64,128]{3,2,1,0:T(8,128)(2,1)S(1)}, bf16[8,2,64,128]{3,2,1,0:T(8,128)(2,1)}, u32[]{:S(2)}) copy-start(bf16[8,2,64,128]{3,2,1,0:T(8,128)(2,1)} %own_ref.3) | copy-start | bytes 786436
  1.0 8.9 %collective-permute-start = (bf16[4,2,64,128]{3,2,1,0:T(8,128)(2,1)S(1)}, bf16[4,2,64,128]{3,2,1,0:T(8,128)(2,1)S(1)}, u32[]{:S(2)}, u32[]{:S(2)}) collective-permute-start(bf16[4,2,64,128]{3,2,1,0:T(8,128)(2,1)S(1)} %shard_map.109), channel_id=1, source_target_pairs={{0,8},{8,16},{16,24},{24,0},{1,9},{9,17},{17,25},{25,1},{2,10},{10... | collective-permute-start | bytes 393224 | tf_op jit(solution)/shard_map/ppermute | solution.py:326
  4.0 7.3 %collective-permute-start.3 = (bf16[8,2,64,128]{3,2,1,0:T(8,128)(2,1)S(1)}, bf16[8,2,64,128]{3,2,1,0:T(8,128)(2,1)S(1)}, u32[]{:S(2)}, u32[]{:S(2)}) collective-permute-start(bf16[8,2,64,128]{3,2,1,0:T(8,128)(2,1)S(1)} %copy-done.1), channel_id=1, source_target_pairs={{0,1},{1,0},{2,3},{3,2},{4,5},{5,4},{6,7},{7,6},{8,9},{9,8},{10,11... | collective-permute-start | bytes 786440 | tf_op jit(solution)/shard_map/ppermute | solution.py:304
  5.4 4.5 %collective-permute-start.1 = (f32[1,2,128]{2,1,0:T(2,128)S(1)}, f32[1,2,128]{2,1,0:T(2,128)S(1)}, u32[]{:S(2)}, u32[]{:S(2)}) collective-permute-start(f32[1,2,128]{2,1,0:T(2,128)S(1)} %get-tuple-element.17), channel_id=1, source_target_pairs={{0,8},{8,16},{16,24},{24,0},{1,9},{9,17},{17,25},{25,1},{2,10},{10... | collective-permute-start | bytes 3080 | tf_op jit(solution)/shard_map/ppermute | solution.py:327
  9.9 1.3 %collective-permute-start.2 = (bf16[4,2,64,128]{3,2,1,0:T(8,128)(2,1)S(1)}, bf16[4,2,64,128]{3,2,1,0:T(8,128)(2,1)S(1)}, u32[]{:S(2)}, u32[]{:S(2)}) collective-permute-start(bf16[4,2,64,128]{3,2,1,0:T(8,128)(2,1)S(1)} %collective-permute-done.halo_ref), channel_id=1, source_target_pairs={{0,1},{1,0},{2,3},{3,2},{4,5},{5,4},{6,7},{7,6},{8,9},{9,8},{10,11... | collective-permute-start | bytes 393224 | tf_op jit(solution)/shard_map/ppermute | solution.py:304
  11.3 10.9 %collective-permute-start.4 = (bf16[12,2,64,128]{3,2,1,0:T(8,128)(2,1)S(1)}, bf16[12,2,64,128]{3,2,1,0:T(8,128)(2,1)S(1)}, u32[]{:S(2)}, u32[]{:S(2)}) collective-permute-start(bf16[12,2,64,128]{3,2,1,0:T(8,128)(2,1)S(1)} %constant_dynamic-update-slice_fusion.near_ref), channel_id=1, source_target_pairs={{0,2},{1,0},{2,4},{3,1},{4,6},{5,3},{6,7},{7,5},{8,10},{9,8},{10,1... | collective-permute-start | bytes 1179656 | tf_op jit(solution)/shard_map/ppermute | solution.py:304
  22.2 12.4 %copy-start = (bf16[3,3,3,128,128]{4,3,2,1,0:T(8,128)(2,1)S(1)}, bf16[3,3,3,128,128]{4,3,2,1,0:T(8,128)(2,1)}, u32[]{:S(2)}) copy-start(bf16[3,3,3,128,128]{4,3,2,1,0:T(8,128)(2,1)} %weight_ref.3) | copy-start | bytes 2654212

commit v24 on v22

--- a/solution.py
+++ b/solution.py
@@ -158,22 +158,30 @@
         load.start()
     channels = own_ref.shape[-1]
     blocks = [own_ref[frame].astype(jnp.float32) for frame in range(own_ref.shape[0])]
-    stats_ref[0] = moments([block.reshape(-1, channels) for block in blocks])
+    packed = moments([block.reshape(-1, channels) for block in blocks])
+    for device in range(stats_ref.shape[0]):
+        stats_ref[device] = packed
     for load in loads:
         load.wait()
 
 
+def affine_kernel(row_count, cells, which, stats_ref, vectors_ref, affine_ref):
+    section = lax.axis_index("section")
+    scale, shift = vectors_ref[which], vectors_ref[which + 1]
+    for index, span in enumerate((section, jnp.maximum(section - 1, 0))):
+        stats = stats_ref[pl.ds(span * row_count, row_count)]
+        slope, offset = affine(stats, cells, scale, shift)
+        affine_ref[2 * index] = slope
+        affine_ref[2 * index + 1] = offset
+
+
 def first_kernel(
-    row_count, own_ref, near_ref, far_ref, halo_ref, halo_near_ref, halo_far_ref, stats_ref,
+    row_count, own_ref, near_ref, far_ref, halo_ref, halo_near_ref, halo_far_ref, affine_ref,
     vectors_ref, weight_ref, middle_ref, sums_ref, field
 ):
     section, row_at = lax.axis_index("section"), lax.axis_index("rows")
     inner, lines, columns, channels = own_ref.shape
-    cells = inner * lines * columns
-    scale, shift = vectors_ref[0], vectors_ref[1]
-    mine, before = stats_ref[:, :2], stats_ref[:, 2:]
-    slope, offset = affine(mine, cells, scale, shift)
-    slope_before, offset_before = affine(before, cells, scale, shift)
+    slope, offset, slope_before, offset_before = (affine_ref[row] for row in range(4))
     even = row_at % 2 == 0
     at_start = section == 0
 
@@ -325,7 +333,7 @@
     sums, packed, weight = call(
         stats_kernel,
         (
-            jax.ShapeDtypeStruct((1, 2, channels), jnp.float32),
+            stats_shape,
             jax.ShapeDtypeStruct((len(vectors), 1, channels), jnp.float32),
             jax.ShapeDtypeStruct(conv1_weight.shape, jnp.bfloat16),
         ),
@@ -336,13 +344,17 @@
     received = lax.ppermute(halo, "section", ring)
     bodies = [own, across(own, near)]
     bodies.append(across(bodies[1], far))
-    passed = lax.ppermute(sums, "section", ring)
-    received, sums, passed = lax.optimization_barrier((received, sums, passed))
+    received, _ = lax.optimization_barrier((received, sums))
     halos = [received, across(received, near)]
     halos.append(across(halos[1], far))
-    both = jnp.concatenate([sums, passed], axis=1)
-    both = jnp.broadcast_to(both, (row_count,) + both.shape[1:])
-    stats = lax.all_to_all(both, "rows", 0, 0, tiled=True)
+    stats = lax.all_to_all(sums, ("section", "rows"), 0, 0, tiled=True)
+    coefficients = call(
+        functools.partial(affine_kernel, row_count, frames * lines * columns, 0),
+        jax.ShapeDtypeStruct((4, 1, channels), jnp.float32),
+        [],
+        (stats, packed),
+        flops=10**11,
+    )
     middle, sums_two = call(
         functools.partial(first_kernel, row_count),
         (
@@ -350,7 +362,7 @@
             stats_shape,
         ),
         [pltpu.VMEM((frames + SPAN_HALO, 3 * lines, columns, channels), jnp.bfloat16)],
-        (*bodies, *halos, stats, packed, weight),
+        (*bodies, *halos, coefficients, packed, weight),
         flops=10**9,
     )
     stats_two = lax.all_to_all(sums_two, ("section", "rows"), 0, 0, tiled=True)

time: 36.8 us -> 39.9 us (1.084)
  blocking collectives: 18 us -> 13.2 us
  starting transfers between devices: 7.79 us -> 11.5 us
  waiting for transfers between devices: 2.99 us -> 6.64 us
  Pallas kernels: 7.75 us -> 8.34 us
    all_to_all x1 -> x0, blocking collectives: 9.06 us -> none  [on_device(): stats = lax.all_to_all(both, 'rows', 0, 0, tiled=True)]
    all_to_all x0 -> x1, starting transfers between devices: none -> 5.26 us  [on_device(): stats = lax.all_to_all(sums, ('section', 'rows'), 0, 0, tiled=True)]
    all_to_all x1, blocking collectives: 8.97 us -> 13.2 us  [on_device(): stats_two = lax.all_to_all(sums_two, ('section', 'rows'), 0, 0, tiled=True)]
    all_to_all x0 -> x1, waiting for transfers between devices: none -> 4.05 us  [on_device(): stats = lax.all_to_all(sums, ('section', 'rows'), 0, 0, tiled=True)]
    ppermute x1 -> x0, waiting for transfers between devices: 2.98 us -> none  [on_device(): passed = lax.ppermute(sums, 'section', ring)]
    ppermute x1, waiting for transfers between devices: 0.01 us -> 2.58 us  [on_device(): received = lax.ppermute(halo, 'section', ring)]
    ppermute x1 -> x0, starting transfers between devices: 1.54 us -> none  [on_device(): passed = lax.ppermute(sums, 'section', ring)]
    pallas_call x4 -> x5, Pallas kernels: 7.75 us -> 8.34 us  [call(): pl.pallas_call(kernel, out_shape=out_shape, in_specs=specs, out_specs=jax...]
  transfers between devices with their start and end apart: 6 -> 6, of which waited for: 1 -> 2; matrix products, arithmetic and copies ran while one was open for 0% -> 0% of each run, Pallas kernels for 3% -> 5%
where the time goes in v24:
time: 39.9 us; the launch traced here: 39.7 us
  blocking collectives  13.2 us (33%)
  starting transfers between devices  11.5 us (29%)
  Pallas kernels  8.34 us (21%)
  waiting for transfers between devices  6.64 us (17%)
    all_to_all x1, blocking collectives, on_device(): stats_two = lax.all_to_all(sums_two, ('section', 'rows'), 0, 0, tiled=True)  13.2 us
    pallas_call x5, Pallas kernels, call(): pl.pallas_call(kernel, out_shape=out_shape, in_specs=specs, out_specs=jax...  8.34 us
    all_to_all x1, starting transfers between devices, on_device(): stats = lax.all_to_all(sums, ('section', 'rows'), 0, 0, tiled=True)  5.26 us
    all_to_all x1, waiting for transfers between devices, on_device(): stats = lax.all_to_all(sums, ('section', 'rows'), 0, 0, tiled=True)  4.05 us
    ppermute x4, starting transfers between devices, across(): return lax.ppermute(block, 'rows', list(enumerate(partner)))  3.26 us
    ppermute x1, starting transfers between devices, on_device(): received = lax.ppermute(halo, 'section', ring)  2.99 us
    ppermute x1, waiting for transfers between devices, on_device(): received = lax.ppermute(halo, 'section', ring)  2.58 us
  transfers between devices with their start and end apart: 6, of which 2 were waited for; matrix products, arithmetic and copies ran while one was open for 0% of the time, Pallas kernels for 5%

profile of v24, /device:TPU:0, one launch (start us, length us, event | category | flops | bytes accessed | tf_op | source)
XLA Modules:
  0.0 39.7 jit_solution(3630405351922909410)
XLA Ops:
  0.0 1.1 %shard_map.109 = (bf16[8,2,64,128]{3,2,1,0:T(8,128)(2,1)S(1)}, bf16[4,2,64,128]{3,2,1,0:T(8,128)(2,1)S(1)}) custom-call(bf16[8,2,64,128]{3,2,1,0:T(8,128)(2,1)} %own_ref.1, bf16[2,2,64,128]{3,2,1,0:T(8,128)(2,1)} %second_cache_ref.1, bf16[2,2,64,128]{3,2,1,0:T(8,128)(2,1)} %first_cache_ref.1), custom_call_target="tpu_custom_call" | custom-call | bytes 1048576 | tf_op jit(solution)/shard_map/pallas_call | solution.py:285
  1.1 3.0 %collective-permute-start.2 = (bf16[4,2,64,128]{3,2,1,0:T(8,128)(2,1)S(1)}, bf16[4,2,64,128]{3,2,1,0:T(8,128)(2,1)S(1)}, u32[]{:S(2)}, u32[]{:S(2)}) collective-permute-start(bf16[4,2,64,128]{3,2,1,0:T(8,128)(2,1)S(1)} %get-tuple-element.14), channel_id=1, source_target_pairs={{0,8},{8,16},{16,24},{24,0},{1,9},{9,17},{17,25},{25,1},{2,10},{10... | collective-permute-start | bytes 393224 | tf_op jit(solution)/shard_map/ppermute | solution.py:344
  4.1 0.0 collective-permute-start
  4.1 1.9 %shard_map.110 = (f32[32,2,128]{2,1,0:T(2,128)}, f32[6,1,128]{2,1,0:T(1,128)S(1)}, bf16[3,3,3,128,128]{4,3,2,1,0:T(8,128)(2,1)S(1)}) custom-call(bf16[8,2,64,128]{3,2,1,0:T(8,128)(2,1)S(1)} %get-tuple-element.13.own_ref, bf16[3,3,3,128,128]{4,3,2,1,0:T(8,128)(2,1)} %weight_ref.2, f32[1,128]{1,0:T(1,128)} %bitcast.6, f32[1,128]{1,0:T(1,128)} %bitcast.7, ...), custom_call_target="tpu_custom_call" | custom-call | bytes 1048576 | tf_op jit(solution)/shard_map/pallas_call | solution.py:285
  5.9 2.6 %collective-permute-done.2.halo_ref = bf16[4,2,64,128]{3,2,1,0:T(8,128)(2,1)S(1)} collective-permute-done((bf16[4,2,64,128]{3,2,1,0:T(8,128)(2,1)S(1)}, bf16[4,2,64,128]{3,2,1,0:T(8,128)(2,1)S(1)}, u32[]{:S(2)}, u32[]{:S(2)}) %collective-permute-start.2) | collective-permute-done | bytes 131104 | tf_op jit(solution)/shard_map/ppermute | solution.py:344
  8.5 0.0 collective-permute-start.3
  8.5 5.3 %all-to-all-start = ((f32[32,2,128]{2,1,0:T(2,128)}), f32[32,2,128]{2,1,0:T(2,128)S(1)}, u32[]{:S(2)}, u32[]{:S(2)}) async-start(f32[32,2,128]{2,1,0:T(2,128)} %get-tuple-element.15), calls=%async_computation | async-start | bytes 65536 | tf_op jit(solution)/shard_map/all_to_all | solution.py:350
  13.8 0.0 collective-permute-done.near_ref
  13.8 1.8 %collective-permute-start.1 = (bf16[8,2,64,128]{3,2,1,0:T(8,128)(2,1)S(1)}, bf16[8,2,64,128]{3,2,1,0:T(8,128)(2,1)S(1)}, u32[]{:S(2)}, u32[]{:S(2)}) collective-permute-start(bf16[8,2,64,128]{3,2,1,0:T(8,128)(2,1)S(1)} %collective-permute-done.near_ref), channel_id=1, source_target_pairs={{0,2},{1,0},{2,4},{3,1},{4,6},{5,3},{6,7},{7,5},{8,10},{9,8},{10,1... | collective-permute-start | bytes 786440 | tf_op jit(solution)/shard_map/ppermute | solution.py:320
  15.6 0.0 collective-permute-done.3.halo_near_ref
  15.6 1.5 %collective-permute-start.4 = (bf16[4,2,64,128]{3,2,1,0:T(8,128)(2,1)S(1)}, bf16[4,2,64,128]{3,2,1,0:T(8,128)(2,1)S(1)}, u32[]{:S(2)}, u32[]{:S(2)}) collective-permute-start(bf16[4,2,64,128]{3,2,1,0:T(8,128)(2,1)S(1)} %collective-permute-done.3.halo_near_ref), channel_id=1, source_target_pairs={{0,2},{1,0},{2,4},{3,1},{4,6},{5,3},{6,7},{7,5},{8,10},{9,8},{10,1... | collective-permute-start | bytes 393224 | tf_op jit(solution)/shard_map/ppermute | solution.py:320
  17.0 4.0 %all-to-all-done.stats_ref = f32[32,2,128]{2,1,0:T(2,128)S(1)} async-done(((f32[32,2,128]{2,1,0:T(2,128)}), f32[32,2,128]{2,1,0:T(2,128)S(1)}, u32[]{:S(2)}, u32[]{:S(2)}) %all-to-all-start) | async-done | bytes 32800 | tf_op jit(solution)/shard_map/all_to_all | solution.py:350
  21.1 0.2 shard_map.111.affine_ref
  21.3 0.0 collective-permute-done.4.halo_far_ref
  21.3 0.0 collective-permute-done.1.far_ref
  21.3 0.0 copy-start
  21.3 3.1 %shard_map.112 = (bf16[10,4,64,128]{3,2,1,0:T(8,128)(2,1)S(1)}, f32[32,2,128]{2,1,0:T(2,128)S(1)}) custom-call(bf16[8,2,64,128]{3,2,1,0:T(8,128)(2,1)S(1)} %get-tuple-element.13.own_ref, bf16[8,2,64,128]{3,2,1,0:T(8,128)(2,1)S(1)} %collective-permute-done.near_ref, bf16[8,2,64,128]{3,2,1,0:T(8,128)(2,1)S(1)} %collective-permute-done.1.far_ref, ...), custom_call_target="tpu_custom_call" | custom-call | flops 1000000000 | bytes 1048576 | tf_op jit(solution)/shard_map/pallas_call | solution.py:285
  24.4 13.2 %all_to_all.10.stats_ref = f32[32,2,128]{2,1,0:T(2,128)S(1)} all-to-all(f32[32,2,128]{2,1,0:T(2,128)S(1)} %get-tuple-element.20), channel_id=1, replica_groups=mesh['section'=4,'rows'=8] {'section','rows'}, dimensions={0} | all-to-all | bytes 65536 | tf_op jit(solution)/shard_map/all_to_all | solution.py:368
  37.6 0.0 copy-done
  37.6 2.1 %shard_map.113 = bf16[8,2,64,128]{3,2,1,0:T(8,128)(2,1)} custom-call(bf16[10,4,64,128]{3,2,1,0:T(8,128)(2,1)S(1)} %get-tuple-element.19.middle_ref, f32[32,2,128]{2,1,0:T(2,128)S(1)} %all_to_all.10.stats_ref, f32[6,1,128]{2,1,0:T(1,128)S(1)} %get-tuple-element.17.vectors_ref, bf16[3,3,3,128,128]{4,3,2,1,0:T(8,128)(2,1)S(1)} %copy-done, ...), custom_call_target="tpu_custom_call" | custom-call | flops 1000000000 | bytes 1048576 | tf_op jit(solution)/shard_map/pallas_call | solution.py:285
Async XLA Ops:
  1.1 7.4 %collective-permute-start.2 = (bf16[4,2,64,128]{3,2,1,0:T(8,128)(2,1)S(1)}, bf16[4,2,64,128]{3,2,1,0:T(8,128)(2,1)S(1)}, u32[]{:S(2)}, u32[]{:S(2)}) collective-permute-start(bf16[4,2,64,128]{3,2,1,0:T(8,128)(2,1)S(1)} %get-tuple-element.14), channel_id=1, source_target_pairs={{0,8},{8,16},{16,24},{24,0},{1,9},{9,17},{17,25},{25,1},{2,10},{10... | collective-permute-start | bytes 393224 | tf_op jit(solution)/shard_map/ppermute | solution.py:344
  4.1 9.7 %collective-permute-start = (bf16[8,2,64,128]{3,2,1,0:T(8,128)(2,1)S(1)}, bf16[8,2,64,128]{3,2,1,0:T(8,128)(2,1)S(1)}, u32[]{:S(2)}, u32[]{:S(2)}) collective-permute-start(bf16[8,2,64,128]{3,2,1,0:T(8,128)(2,1)S(1)} %get-tuple-element.13.own_ref), channel_id=1, source_target_pairs={{0,1},{1,0},{2,3},{3,2},{4,5},{5,4},{6,7},{7,6},{8,9},{9,8},{10,11... | collective-permute-start | bytes 786440 | tf_op jit(solution)/shard_map/ppermute | solution.py:320
  8.5 7.1 %collective-permute-start.3 = (bf16[4,2,64,128]{3,2,1,0:T(8,128)(2,1)S(1)}, bf16[4,2,64,128]{3,2,1,0:T(8,128)(2,1)S(1)}, u32[]{:S(2)}, u32[]{:S(2)}) collective-permute-start(bf16[4,2,64,128]{3,2,1,0:T(8,128)(2,1)S(1)} %collective-permute-done.2.halo_ref), channel_id=1, source_target_pairs={{0,1},{1,0},{2,3},{3,2},{4,5},{5,4},{6,7},{7,6},{8,9},{9,8},{10,11... | collective-permute-start | bytes 393224 | tf_op jit(solution)/shard_map/ppermute | solution.py:320
  8.5 12.6 %all-to-all-start = ((f32[32,2,128]{2,1,0:T(2,128)}), f32[32,2,128]{2,1,0:T(2,128)S(1)}, u32[]{:S(2)}, u32[]{:S(2)}) async-start(f32[32,2,128]{2,1,0:T(2,128)} %get-tuple-element.15), calls=%async_computation | async-start | bytes 65536 | tf_op jit(solution)/shard_map/all_to_all | solution.py:350
  13.8 7.5 %collective-permute-start.1 = (bf16[8,2,64,128]{3,2,1,0:T(8,128)(2,1)S(1)}, bf16[8,2,64,128]{3,2,1,0:T(8,128)(2,1)S(1)}, u32[]{:S(2)}, u32[]{:S(2)}) collective-permute-start(bf16[8,2,64,128]{3,2,1,0:T(8,128)(2,1)S(1)} %collective-permute-done.near_ref), channel_id=1, source_target_pairs={{0,2},{1,0},{2,4},{3,1},{4,6},{5,3},{6,7},{7,5},{8,10},{9,8},{10,1... | collective-permute-start | bytes 786440 | tf_op jit(solution)/shard_map/ppermute | solution.py:320
  15.6 5.7 %collective-permute-start.4 = (bf16[4,2,64,128]{3,2,1,0:T(8,128)(2,1)S(1)}, bf16[4,2,64,128]{3,2,1,0:T(8,128)(2,1)S(1)}, u32[]{:S(2)}, u32[]{:S(2)}) collective-permute-start(bf16[4,2,64,128]{3,2,1,0:T(8,128)(2,1)S(1)} %collective-permute-done.3.halo_near_ref), channel_id=1, source_target_pairs={{0,2},{1,0},{2,4},{3,1},{4,6},{5,3},{6,7},{7,5},{8,10},{9,8},{10,1... | collective-permute-start | bytes 393224 | tf_op jit(solution)/shard_map/ppermute | solution.py:320
  21.3 16.3 %copy-start = (bf16[3,3,3,128,128]{4,3,2,1,0:T(8,128)(2,1)S(1)}, bf16[3,3,3,128,128]{4,3,2,1,0:T(8,128)(2,1)}, u32[]{:S(2)}) copy-start(bf16[3,3,3,128,128]{4,3,2,1,0:T(8,128)(2,1)} %weight_ref.3) | copy-start | bytes 2654212

commit v25 on v22

--- a/solution.py
+++ b/solution.py
@@ -337,7 +337,7 @@
     bodies = [own, across(own, near)]
     bodies.append(across(bodies[1], far))
     passed = lax.ppermute(sums, "section", ring)
-    received, sums, passed = lax.optimization_barrier((received, sums, passed))
+    received, _ = lax.optimization_barrier((received, sums))
     halos = [received, across(received, near)]
     halos.append(across(halos[1], far))
     both = jnp.concatenate([sums, passed], axis=1)

time: 36.8 us -> 39.4 us (1.071)
  waiting for transfers between devices: 2.99 us -> 6.11 us
  starting transfers between devices: 7.79 us -> 7.02 us
    ppermute x1, waiting for transfers between devices: 0.01 us -> 3.81 us  [on_device(): received = lax.ppermute(halo, 'section', ring)]
    ppermute x1, starting transfers between devices: 1.54 us -> 0.59 us  [on_device(): passed = lax.ppermute(sums, 'section', ring)]
    ppermute x1, waiting for transfers between devices: 2.98 us -> 2.29 us  [on_device(): passed = lax.ppermute(sums, 'section', ring)]
  transfers between devices with their start and end apart: 6 -> 6, of which waited for: 1 -> 2; matrix products, arithmetic and copies ran while one was open for 0% -> 0% of each run, Pallas kernels for 3% -> 3%
where the time goes in v25:
time: 39.4 us; the launch traced here: 39.2 us
  blocking collectives  18.3 us (46%)
  Pallas kernels  7.75 us (20%)
  starting transfers between devices  7.02 us (18%)
  waiting for transfers between devices  6.11 us (16%)
    all_to_all x1, blocking collectives, on_device(): stats = lax.all_to_all(both, 'rows', 0, 0, tiled=True)  9.31 us
    all_to_all x1, blocking collectives, on_device(): stats_two = lax.all_to_all(sums_two, ('section', 'rows'), 0, 0, tiled=True)  8.98 us
    pallas_call x4, Pallas kernels, call(): pl.pallas_call(kernel, out_shape=out_shape, in_specs=specs, out_specs=jax...  7.75 us
    ppermute x4, starting transfers between devices, across(): return lax.ppermute(block, 'rows', list(enumerate(partner)))  3.87 us
    ppermute x1, waiting for transfers between devices, on_device(): received = lax.ppermute(halo, 'section', ring)  3.81 us
    ppermute x1, starting transfers between devices, on_device(): received = lax.ppermute(halo, 'section', ring)  2.55 us
    ppermute x1, waiting for transfers between devices, on_device(): passed = lax.ppermute(sums, 'section', ring)  2.29 us
  transfers between devices with their start and end apart: 6, of which 2 were waited for; matrix products, arithmetic and copies ran while one was open for 0% of the time, Pallas kernels for 3%

profile of v25, /device:TPU:0, one launch (start us, length us, event | category | flops | bytes accessed | tf_op | source)
XLA Modules:
  0.0 39.2 jit_solution(8890507723514593095)
XLA Ops:
  0.0 1.1 %shard_map.109 = (bf16[8,2,64,128]{3,2,1,0:T(8,128)(2,1)S(1)}, bf16[4,2,64,128]{3,2,1,0:T(8,128)(2,1)S(1)}) custom-call(bf16[8,2,64,128]{3,2,1,0:T(8,128)(2,1)} %own_ref.1, bf16[2,2,64,128]{3,2,1,0:T(8,128)(2,1)} %second_cache_ref.1, bf16[2,2,64,128]{3,2,1,0:T(8,128)(2,1)} %first_cache_ref.1), custom_call_target="tpu_custom_call" | custom-call | bytes 1048576 | tf_op jit(solution)/shard_map/pallas_call | solution.py:277
  1.1 0.5 %collective-permute-start = (bf16[8,2,64,128]{3,2,1,0:T(8,128)(2,1)S(1)}, bf16[8,2,64,128]{3,2,1,0:T(8,128)(2,1)S(1)}, u32[]{:S(2)}, u32[]{:S(2)}) collective-permute-start(bf16[8,2,64,128]{3,2,1,0:T(8,128)(2,1)S(1)} %get-tuple-element.13.own_ref), channel_id=1, source_target_pairs={{0,1},{1,0},{2,3},{3,2},{4,5},{5,4},{6,7},{7,6},{8,9},{9,8},{10,11... | collective-permute-start | bytes 786440 | tf_op jit(solution)/shard_map/ppermute | solution.py:312
  1.6 2.6 %collective-permute-start.2 = (bf16[4,2,64,128]{3,2,1,0:T(8,128)(2,1)S(1)}, bf16[4,2,64,128]{3,2,1,0:T(8,128)(2,1)S(1)}, u32[]{:S(2)}, u32[]{:S(2)}) collective-permute-start(bf16[4,2,64,128]{3,2,1,0:T(8,128)(2,1)S(1)} %get-tuple-element.14), channel_id=1, source_target_pairs={{0,8},{8,16},{16,24},{24,0},{1,9},{9,17},{17,25},{25,1},{2,10},{10... | collective-permute-start | bytes 393224 | tf_op jit(solution)/shard_map/ppermute | solution.py:336
  4.1 1.2 %shard_map.110 = (f32[1,2,128]{2,1,0:T(2,128)S(1)}, f32[6,1,128]{2,1,0:T(1,128)S(1)}, bf16[3,3,3,128,128]{4,3,2,1,0:T(8,128)(2,1)S(1)}) custom-call(bf16[8,2,64,128]{3,2,1,0:T(8,128)(2,1)S(1)} %get-tuple-element.13.own_ref, bf16[3,3,3,128,128]{4,3,2,1,0:T(8,128)(2,1)} %weight_ref.2, f32[1,128]{1,0:T(1,128)} %bitcast.8, f32[1,128]{1,0:T(1,128)} %bitcast.9, ...), custom_call_target="tpu_custom_call" | custom-call | bytes 1048576 | tf_op jit(solution)/shard_map/pallas_call | solution.py:277
  5.4 3.8 %collective-permute-done.2.halo_ref = bf16[4,2,64,128]{3,2,1,0:T(8,128)(2,1)S(1)} collective-permute-done((bf16[4,2,64,128]{3,2,1,0:T(8,128)(2,1)S(1)}, bf16[4,2,64,128]{3,2,1,0:T(8,128)(2,1)S(1)}, u32[]{:S(2)}, u32[]{:S(2)}) %collective-permute-start.2) | collective-permute-done | bytes 131104 | tf_op jit(solution)/shard_map/ppermute | solution.py:336
  9.2 0.0 collective-permute-start.3
  9.2 0.0 collective-permute-done.near_ref
  9.2 1.8 %collective-permute-start.1 = (bf16[8,2,64,128]{3,2,1,0:T(8,128)(2,1)S(1)}, bf16[8,2,64,128]{3,2,1,0:T(8,128)(2,1)S(1)}, u32[]{:S(2)}, u32[]{:S(2)}) collective-permute-start(bf16[8,2,64,128]{3,2,1,0:T(8,128)(2,1)S(1)} %collective-permute-done.near_ref), channel_id=1, source_target_pairs={{0,2},{1,0},{2,4},{3,1},{4,6},{5,3},{6,7},{7,5},{8,10},{9,8},{10,1... | collective-permute-start | bytes 786440 | tf_op jit(solution)/shard_map/ppermute | solution.py:312
  11.0 0.6 %collective-permute-start.5 = (f32[1,2,128]{2,1,0:T(2,128)S(1)}, f32[1,2,128]{2,1,0:T(2,128)S(1)}, u32[]{:S(2)}, u32[]{:S(2)}) collective-permute-start(f32[1,2,128]{2,1,0:T(2,128)S(1)} %get-tuple-element.15), channel_id=1, source_target_pairs={{0,8},{8,16},{16,24},{24,0},{1,9},{9,17},{17,25},{25,1},{2,10},{10... | collective-permute-start | bytes 3080 | tf_op jit(solution)/shard_map/ppermute | solution.py:339
  11.6 0.0 collective-permute-done.3.halo_near_ref
  11.6 1.6 %collective-permute-start.4 = (bf16[4,2,64,128]{3,2,1,0:T(8,128)(2,1)S(1)}, bf16[4,2,64,128]{3,2,1,0:T(8,128)(2,1)S(1)}, u32[]{:S(2)}, u32[]{:S(2)}) collective-permute-start(bf16[4,2,64,128]{3,2,1,0:T(8,128)(2,1)S(1)} %collective-permute-done.3.halo_near_ref), channel_id=1, source_target_pairs={{0,2},{1,0},{2,4},{3,1},{4,6},{5,3},{6,7},{7,5},{8,10},{9,8},{10,1... | collective-permute-start | bytes 393224 | tf_op jit(solution)/shard_map/ppermute | solution.py:312
  13.2 2.3 %collective-permute-done.5 = f32[1,2,128]{2,1,0:T(2,128)S(1)} collective-permute-done((f32[1,2,128]{2,1,0:T(2,128)S(1)}, f32[1,2,128]{2,1,0:T(2,128)S(1)}, u32[]{:S(2)}, u32[]{:S(2)}) %collective-permute-start.5) | collective-permute-done | bytes 1056 | tf_op jit(solution)/shard_map/ppermute | solution.py:339
  15.5 9.3 %all_to_all.10.stats_ref = f32[8,4,128]{2,1,0:T(4,128)S(1)} all-to-all(f32[8,4,128]{2,1,0:T(4,128)S(1)} %broadcast_in_dim.8), channel_id=1, replica_groups=mesh['section'=4,'rows'=8] {'rows'}, dimensions={0} | all-to-all | bytes 32768 | tf_op jit(solution)/shard_map/all_to_all | solution.py:345
  24.8 0.0 collective-permute-done.4.halo_far_ref
  24.8 0.0 collective-permute-done.1.far_ref
  24.8 0.0 copy-start
  24.8 3.3 %shard_map.111 = (bf16[10,4,64,128]{3,2,1,0:T(8,128)(2,1)S(1)}, f32[32,2,128]{2,1,0:T(2,128)S(1)}) custom-call(bf16[8,2,64,128]{3,2,1,0:T(8,128)(2,1)S(1)} %get-tuple-element.13.own_ref, bf16[8,2,64,128]{3,2,1,0:T(8,128)(2,1)S(1)} %collective-permute-done.near_ref, bf16[8,2,64,128]{3,2,1,0:T(8,128)(2,1)S(1)} %collective-permute-done.1.far_ref, ...), custom_call_target="tpu_custom_call" | custom-call | flops 1000000000 | bytes 1048576 | tf_op jit(solution)/shard_map/pallas_call | solution.py:277
  28.1 9.0 %all_to_all.11.stats_ref = f32[32,2,128]{2,1,0:T(2,128)S(1)} all-to-all(f32[32,2,128]{2,1,0:T(2,128)S(1)} %get-tuple-element.20), channel_id=1, replica_groups=mesh['section'=4,'rows'=8] {'section','rows'}, dimensions={0} | all-to-all | bytes 65536 | tf_op jit(solution)/shard_map/all_to_all | solution.py:356
  37.1 0.0 copy-done
  37.1 2.1 %shard_map.112 = bf16[8,2,64,128]{3,2,1,0:T(8,128)(2,1)} custom-call(bf16[10,4,64,128]{3,2,1,0:T(8,128)(2,1)S(1)} %get-tuple-element.19.middle_ref, f32[32,2,128]{2,1,0:T(2,128)S(1)} %all_to_all.11.stats_ref, f32[6,1,128]{2,1,0:T(1,128)S(1)} %get-tuple-element.17.vectors_ref, bf16[3,3,3,128,128]{4,3,2,1,0:T(8,128)(2,1)S(1)} %copy-done, ...), custom_call_target="tpu_custom_call" | custom-call | flops 1000000000 | bytes 1048576 | tf_op jit(solution)/shard_map/pallas_call | solution.py:277
  (2 shorter events, 0.0 us)
Async XLA Ops:
  1.1 8.1 %collective-permute-start = (bf16[8,2,64,128]{3,2,1,0:T(8,128)(2,1)S(1)}, bf16[8,2,64,128]{3,2,1,0:T(8,128)(2,1)S(1)}, u32[]{:S(2)}, u32[]{:S(2)}) collective-permute-start(bf16[8,2,64,128]{3,2,1,0:T(8,128)(2,1)S(1)} %get-tuple-element.13.own_ref), channel_id=1, source_target_pairs={{0,1},{1,0},{2,3},{3,2},{4,5},{5,4},{6,7},{7,6},{8,9},{9,8},{10,11... | collective-permute-start | bytes 786440 | tf_op jit(solution)/shard_map/ppermute | solution.py:312
  1.6 7.6 %collective-permute-start.2 = (bf16[4,2,64,128]{3,2,1,0:T(8,128)(2,1)S(1)}, bf16[4,2,64,128]{3,2,1,0:T(8,128)(2,1)S(1)}, u32[]{:S(2)}, u32[]{:S(2)}) collective-permute-start(bf16[4,2,64,128]{3,2,1,0:T(8,128)(2,1)S(1)} %get-tuple-element.14), channel_id=1, source_target_pairs={{0,8},{8,16},{16,24},{24,0},{1,9},{9,17},{17,25},{25,1},{2,10},{10... | collective-permute-start | bytes 393224 | tf_op jit(solution)/shard_map/ppermute | solution.py:336
  9.2 2.4 %collective-permute-start.3 = (bf16[4,2,64,128]{3,2,1,0:T(8,128)(2,1)S(1)}, bf16[4,2,64,128]{3,2,1,0:T(8,128)(2,1)S(1)}, u32[]{:S(2)}, u32[]{:S(2)}) collective-permute-start(bf16[4,2,64,128]{3,2,1,0:T(8,128)(2,1)S(1)} %collective-permute-done.2.halo_ref), channel_id=1, source_target_pairs={{0,1},{1,0},{2,3},{3,2},{4,5},{5,4},{6,7},{7,6},{8,9},{9,8},{10,11... | collective-permute-start | bytes 393224 | tf_op jit(solution)/shard_map/ppermute | solution.py:312
  9.2 15.6 %collective-permute-start.1 = (bf16[8,2,64,128]{3,2,1,0:T(8,128)(2,1)S(1)}, bf16[8,2,64,128]{3,2,1,0:T(8,128)(2,1)S(1)}, u32[]{:S(2)}, u32[]{:S(2)}) collective-permute-start(bf16[8,2,64,128]{3,2,1,0:T(8,128)(2,1)S(1)} %collective-permute-done.near_ref), channel_id=1, source_target_pairs={{0,2},{1,0},{2,4},{3,1},{4,6},{5,3},{6,7},{7,5},{8,10},{9,8},{10,1... | collective-permute-start | bytes 786440 | tf_op jit(solution)/shard_map/ppermute | solution.py:312
  11.0 4.5 %collective-permute-start.5 = (f32[1,2,128]{2,1,0:T(2,128)S(1)}, f32[1,2,128]{2,1,0:T(2,128)S(1)}, u32[]{:S(2)}, u32[]{:S(2)}) collective-permute-start(f32[1,2,128]{2,1,0:T(2,128)S(1)} %get-tuple-element.15), channel_id=1, source_target_pairs={{0,8},{8,16},{16,24},{24,0},{1,9},{9,17},{17,25},{25,1},{2,10},{10... | collective-permute-start | bytes 3080 | tf_op jit(solution)/shard_map/ppermute | solution.py:339
  11.6 13.2 %collective-permute-start.4 = (bf16[4,2,64,128]{3,2,1,0:T(8,128)(2,1)S(1)}, bf16[4,2,64,128]{3,2,1,0:T(8,128)(2,1)S(1)}, u32[]{:S(2)}, u32[]{:S(2)}) collective-permute-start(bf16[4,2,64,128]{3,2,1,0:T(8,128)(2,1)S(1)} %collective-permute-done.3.halo_near_ref), channel_id=1, source_target_pairs={{0,2},{1,0},{2,4},{3,1},{4,6},{5,3},{6,7},{7,5},{8,10},{9,8},{10,1... | collective-permute-start | bytes 393224 | tf_op jit(solution)/shard_map/ppermute | solution.py:312
  24.8 12.3 %copy-start = (bf16[3,3,3,128,128]{4,3,2,1,0:T(8,128)(2,1)S(1)}, bf16[3,3,3,128,128]{4,3,2,1,0:T(8,128)(2,1)}, u32[]{:S(2)}) copy-start(bf16[3,3,3,128,128]{4,3,2,1,0:T(8,128)(2,1)} %weight_ref.3) | copy-start | bytes 2654212

commit v26 on v19

--- a/solution.py
+++ b/solution.py
@@ -335,7 +335,7 @@
     )
     received = lax.ppermute(halo, "section", ring)
     passed = lax.ppermute(sums, "section", ring)
-    received, sums, passed = lax.optimization_barrier((received, sums, passed))
+    received, _ = lax.optimization_barrier((received, sums))
     joined = jnp.concatenate([received, own], axis=0)
     from_far = across(joined, far)
     from_near = across(joined, near)

time: 37.4 us -> 40.8 us (1.091)
  waiting for transfers between devices: 2.98 us -> 6.89 us
  starting transfers between devices: 5.29 us -> 4.59 us
    ppermute x1, waiting for transfers between devices: 0.01 us -> 3.2 us  [on_device(): received = lax.ppermute(halo, 'section', ring)]
    ppermute x1, starting transfers between devices: 1.54 us -> 0.84 us  [on_device(): passed = lax.ppermute(sums, 'section', ring)]
    ppermute x1, waiting for transfers between devices: 2.98 us -> 3.68 us  [on_device(): passed = lax.ppermute(sums, 'section', ring)]
  transfers between devices with their start and end apart: 4 -> 4, of which waited for: 1 -> 2; matrix products, arithmetic and copies ran while one was open for 0% -> 0% of each run, Pallas kernels for 3% -> 3%
where the time goes in v26:
time: 40.8 us; the launch traced here: 40.6 us
  blocking collectives  21.3 us (52%)
  Pallas kernels  7.74 us (19%)
  waiting for transfers between devices  6.89 us (17%)
  starting transfers between devices  4.59 us (11%)
    all_to_all x1, blocking collectives, on_device(): stats = lax.all_to_all(both, 'rows', 0, 0, tiled=True)  12.3 us
    all_to_all x1, blocking collectives, on_device(): stats_two = lax.all_to_all(sums_two, ('section', 'rows'), 0, 0, tiled=True)  8.98 us
    pallas_call x4, Pallas kernels, call(): pl.pallas_call(kernel, out_shape=out_shape, in_specs=specs, out_specs=jax...  7.74 us
    ppermute x1, waiting for transfers between devices, on_device(): passed = lax.ppermute(sums, 'section', ring)  3.68 us
    ppermute x1, waiting for transfers between devices, on_device(): received = lax.ppermute(halo, 'section', ring)  3.2 us
    ppermute x1, starting transfers between devices, on_device(): received = lax.ppermute(halo, 'section', ring)  2.99 us
    ppermute x1, starting transfers between devices, on_device(): passed = lax.ppermute(sums, 'section', ring)  0.84 us
  transfers between devices with their start and end apart: 4, of which 2 were waited for; matrix products, arithmetic and copies ran while one was open for 0% of the time, Pallas kernels for 3%

profile of v26, /device:TPU:0, one launch (start us, length us, event | category | flops | bytes accessed | tf_op | source)
XLA Modules:
  0.0 40.6 jit_solution(15034133548409184033)
XLA Ops:
  0.0 1.1 %shard_map.109 = (bf16[8,2,64,128]{3,2,1,0:T(8,128)(2,1)S(1)}, bf16[4,2,64,128]{3,2,1,0:T(8,128)(2,1)S(1)}) custom-call(bf16[8,2,64,128]{3,2,1,0:T(8,128)(2,1)} %own_ref.1, bf16[2,2,64,128]{3,2,1,0:T(8,128)(2,1)} %second_cache_ref.1, bf16[2,2,64,128]{3,2,1,0:T(8,128)(2,1)} %first_cache_ref.1), custom_call_target="tpu_custom_call" | custom-call | bytes 1048576 | tf_op jit(solution)/shard_map/pallas_call | solution.py:278
  1.1 3.0 %collective-permute-start = (bf16[4,2,64,128]{3,2,1,0:T(8,128)(2,1)S(1)}, bf16[4,2,64,128]{3,2,1,0:T(8,128)(2,1)S(1)}, u32[]{:S(2)}, u32[]{:S(2)}) collective-permute-start(bf16[4,2,64,128]{3,2,1,0:T(8,128)(2,1)S(1)} %get-tuple-element.13), channel_id=1, source_target_pairs={{0,8},{8,16},{16,24},{24,0},{1,9},{9,17},{17,25},{25,1},{2,10},{10... | collective-permute-start | bytes 393224 | tf_op jit(solution)/shard_map/ppermute | solution.py:336
  4.1 1.2 %shard_map.110 = (f32[1,2,128]{2,1,0:T(2,128)S(1)}, f32[6,1,128]{2,1,0:T(1,128)S(1)}, bf16[3,3,3,128,128]{4,3,2,1,0:T(8,128)(2,1)S(1)}) custom-call(bf16[8,2,64,128]{3,2,1,0:T(8,128)(2,1)S(1)} %get-tuple-element.14.own_ref, bf16[3,3,3,128,128]{4,3,2,1,0:T(8,128)(2,1)} %weight_ref.2, f32[1,128]{1,0:T(1,128)} %bitcast.8, f32[1,128]{1,0:T(1,128)} %bitcast.9, ...), custom_call_target="tpu_custom_call" | custom-call | bytes 1048576 | tf_op jit(solution)/shard_map/pallas_call | solution.py:278
  5.3 3.2 %collective-permute-done = bf16[4,2,64,128]{3,2,1,0:T(8,128)(2,1)S(1)} collective-permute-done((bf16[4,2,64,128]{3,2,1,0:T(8,128)(2,1)S(1)}, bf16[4,2,64,128]{3,2,1,0:T(8,128)(2,1)S(1)}, u32[]{:S(2)}, u32[]{:S(2)}) %collective-permute-start) | collective-permute-done | bytes 131104 | tf_op jit(solution)/shard_map/ppermute | solution.py:336
  8.6 0.1 collective-permute-start.2
  8.7 0.7 %collective-permute-start.1 = (bf16[12,2,64,128]{3,2,1,0:T(8,128)(2,1)S(1)}, bf16[12,2,64,128]{3,2,1,0:T(8,128)(2,1)S(1)}, u32[]{:S(2)}, u32[]{:S(2)}) collective-permute-start(bf16[12,2,64,128]{3,2,1,0:T(8,128)(2,1)S(1)} %constant_dynamic-update-slice_fusion.own_ref), channel_id=1, source_target_pairs={{0,0},{1,2},{2,1},{3,4},{4,3},{5,6},{6,5},{7,7},{8,8},{9,10},{10,9... | collective-permute-start | bytes 1179656 | tf_op jit(solution)/shard_map/ppermute | solution.py:312
  9.3 0.8 %collective-permute-start.3 = (f32[1,2,128]{2,1,0:T(2,128)S(1)}, f32[1,2,128]{2,1,0:T(2,128)S(1)}, u32[]{:S(2)}, u32[]{:S(2)}) collective-permute-start(f32[1,2,128]{2,1,0:T(2,128)S(1)} %get-tuple-element.15), channel_id=1, source_target_pairs={{0,8},{8,16},{16,24},{24,0},{1,9},{9,17},{17,25},{25,1},{2,10},{10... | collective-permute-start | bytes 3080 | tf_op jit(solution)/shard_map/ppermute | solution.py:337
  10.2 3.7 %collective-permute-done.3 = f32[1,2,128]{2,1,0:T(2,128)S(1)} collective-permute-done((f32[1,2,128]{2,1,0:T(2,128)S(1)}, f32[1,2,128]{2,1,0:T(2,128)S(1)}, u32[]{:S(2)}, u32[]{:S(2)}) %collective-permute-start.3) | collective-permute-done | bytes 1056 | tf_op jit(solution)/shard_map/ppermute | solution.py:337
  13.9 12.3 %all_to_all.10.stats_ref = f32[8,4,128]{2,1,0:T(4,128)S(1)} all-to-all(f32[8,4,128]{2,1,0:T(4,128)S(1)} %broadcast_in_dim.8), channel_id=1, replica_groups=mesh['section'=4,'rows'=8] {'rows'}, dimensions={0} | all-to-all | bytes 32768 | tf_op jit(solution)/shard_map/all_to_all | solution.py:344
  26.2 0.0 collective-permute-done.2.near_ref
  26.2 0.0 collective-permute-done.1.far_ref
  26.2 0.0 copy-start
  26.2 3.3 %shard_map.111 = (bf16[10,4,64,128]{3,2,1,0:T(8,128)(2,1)S(1)}, f32[32,2,128]{2,1,0:T(2,128)S(1)}) custom-call(bf16[12,2,64,128]{3,2,1,0:T(8,128)(2,1)S(1)} %constant_dynamic-update-slice_fusion.own_ref, bf16[12,2,64,128]{3,2,1,0:T(8,128)(2,1)S(1)} %collective-permute-done.1.far_ref, bf16[12,2,64,128]{3,2,1,0:T(8,128)(2,1)S(1)} %collective-permute-done.2.near_ref, ...), custom_call_target="tpu_custom_call" | custom-call | flops 1000000000 | bytes 1048576 | tf_op jit(solution)/shard_map/pallas_call | solution.py:278
  29.5 9.0 %all_to_all.11.stats_ref = f32[32,2,128]{2,1,0:T(2,128)S(1)} all-to-all(f32[32,2,128]{2,1,0:T(2,128)S(1)} %get-tuple-element.20), channel_id=1, replica_groups=mesh['section'=4,'rows'=8] {'section','rows'}, dimensions={0} | all-to-all | bytes 65536 | tf_op jit(solution)/shard_map/all_to_all | solution.py:355
  38.4 0.0 copy-done
  38.4 2.2 %shard_map.112 = bf16[8,2,64,128]{3,2,1,0:T(8,128)(2,1)} custom-call(bf16[10,4,64,128]{3,2,1,0:T(8,128)(2,1)S(1)} %get-tuple-element.19.middle_ref, f32[32,2,128]{2,1,0:T(2,128)S(1)} %all_to_all.11.stats_ref, f32[6,1,128]{2,1,0:T(1,128)S(1)} %get-tuple-element.17.vectors_ref, bf16[3,3,3,128,128]{4,3,2,1,0:T(8,128)(2,1)S(1)} %copy-done, ...), custom_call_target="tpu_custom_call" | custom-call | flops 1000000000 | bytes 1048576 | tf_op jit(solution)/shard_map/pallas_call | solution.py:278
  (4 shorter events, 0.1 us)
Async XLA Ops:
  1.1 7.4 %collective-permute-start = (bf16[4,2,64,128]{3,2,1,0:T(8,128)(2,1)S(1)}, bf16[4,2,64,128]{3,2,1,0:T(8,128)(2,1)S(1)}, u32[]{:S(2)}, u32[]{:S(2)}) collective-permute-start(bf16[4,2,64,128]{3,2,1,0:T(8,128)(2,1)S(1)} %get-tuple-element.13), channel_id=1, source_target_pairs={{0,8},{8,16},{16,24},{24,0},{1,9},{9,17},{17,25},{25,1},{2,10},{10... | collective-permute-start | bytes 393224 | tf_op jit(solution)/shard_map/ppermute | solution.py:336
  8.6 17.6 %collective-permute-start.2 = (bf16[12,2,64,128]{3,2,1,0:T(8,128)(2,1)S(1)}, bf16[12,2,64,128]{3,2,1,0:T(8,128)(2,1)S(1)}, u32[]{:S(2)}, u32[]{:S(2)}) collective-permute-start(bf16[12,2,64,128]{3,2,1,0:T(8,128)(2,1)S(1)} %constant_dynamic-update-slice_fusion.own_ref), channel_id=1, source_target_pairs={{0,1},{1,0},{2,3},{3,2},{4,5},{5,4},{6,7},{7,6},{8,9},{9,8},{10,11... | collective-permute-start | bytes 1179656 | tf_op jit(solution)/shard_map/ppermute | solution.py:312
  8.7 17.5 %collective-permute-start.1 = (bf16[12,2,64,128]{3,2,1,0:T(8,128)(2,1)S(1)}, bf16[12,2,64,128]{3,2,1,0:T(8,128)(2,1)S(1)}, u32[]{:S(2)}, u32[]{:S(2)}) collective-permute-start(bf16[12,2,64,128]{3,2,1,0:T(8,128)(2,1)S(1)} %constant_dynamic-update-slice_fusion.own_ref), channel_id=1, source_target_pairs={{0,0},{1,2},{2,1},{3,4},{4,3},{5,6},{6,5},{7,7},{8,8},{9,10},{10,9... | collective-permute-start | bytes 1179656 | tf_op jit(solution)/shard_map/ppermute | solution.py:312
  9.3 4.5 %collective-permute-start.3 = (f32[1,2,128]{2,1,0:T(2,128)S(1)}, f32[1,2,128]{2,1,0:T(2,128)S(1)}, u32[]{:S(2)}, u32[]{:S(2)}) collective-permute-start(f32[1,2,128]{2,1,0:T(2,128)S(1)} %get-tuple-element.15), channel_id=1, source_target_pairs={{0,8},{8,16},{16,24},{24,0},{1,9},{9,17},{17,25},{25,1},{2,10},{10... | collective-permute-start | bytes 3080 | tf_op jit(solution)/shard_map/ppermute | solution.py:337
  26.2 12.3 %copy-start = (bf16[3,3,3,128,128]{4,3,2,1,0:T(8,128)(2,1)S(1)}, bf16[3,3,3,128,128]{4,3,2,1,0:T(8,128)(2,1)}, u32[]{:S(2)}) copy-start(bf16[3,3,3,128,128]{4,3,2,1,0:T(8,128)(2,1)} %weight_ref.3) | copy-start | bytes 2654212

commit v27 on v25

--- a/solution.py
+++ b/solution.py
@@ -164,7 +164,7 @@
 
 
 def first_kernel(
-    row_count, own_ref, near_ref, far_ref, halo_ref, halo_near_ref, halo_far_ref, stats_ref,
+    row_count, own_ref, near_ref, far_ref, halo_ref, halo_far_ref, halo_near_ref, stats_ref,
     vectors_ref, weight_ref, middle_ref, sums_ref, field
 ):
     section, row_at = lax.axis_index("section"), lax.axis_index("rows")
@@ -337,9 +337,8 @@
     bodies = [own, across(own, near)]
     bodies.append(across(bodies[1], far))
     passed = lax.ppermute(sums, "section", ring)
-    received, _ = lax.optimization_barrier((received, sums))
-    halos = [received, across(received, near)]
-    halos.append(across(halos[1], far))
+    pairs = [0] + [i + 1 if i % 2 else i - 1 for i in range(1, row_count - 1)] + [row_count - 1]
+    halos = [received, across(received, pairs), across(received, near)]
     both = jnp.concatenate([sums, passed], axis=1)
     both = jnp.broadcast_to(both, (row_count,) + both.shape[1:])
     stats = lax.all_to_all(both, "rows", 0, 0, tiled=True)

time: 39.4 us -> 36.9 us (0.937)
  waiting for transfers between devices: 6.11 us -> 2.32 us
  blocking collectives: 18.3 us -> 19.7 us
    ppermute x1, waiting for transfers between devices: 3.81 us -> 0.68 us  [on_device(): received = lax.ppermute(halo, 'section', ring)]
    all_to_all x1, blocking collectives: 9.31 us -> 10.7 us  [on_device(): stats = lax.all_to_all(both, 'rows', 0, 0, tiled=True)]
    ppermute x4, starting transfers between devices: 3.87 us -> 2.76 us  [across(): return lax.ppermute(block, 'rows', list(enumerate(partner)))]
    ppermute x1, starting transfers between devices: 0.59 us -> 1.54 us  [on_device(): passed = lax.ppermute(sums, 'section', ring)]
    ppermute x1, waiting for transfers between devices: 2.29 us -> 1.62 us  [on_device(): passed = lax.ppermute(sums, 'section', ring)]
where the time goes in v27:
time: 36.9 us; the launch traced here: 36.7 us
  blocking collectives  19.7 us (53%)
  Pallas kernels  7.75 us (21%)
  starting transfers between devices  6.85 us (19%)
  waiting for transfers between devices  2.32 us (6%)
    all_to_all x1, blocking collectives, on_device(): stats = lax.all_to_all(both, 'rows', 0, 0, tiled=True)  10.7 us
    all_to_all x1, blocking collectives, on_device(): stats_two = lax.all_to_all(sums_two, ('section', 'rows'), 0, 0, tiled=True)  9 us
    pallas_call x4, Pallas kernels, call(): pl.pallas_call(kernel, out_shape=out_shape, in_specs=specs, out_specs=jax...  7.75 us
    ppermute x4, starting transfers between devices, across(): return lax.ppermute(block, 'rows', list(enumerate(partner)))  2.76 us
    ppermute x1, starting transfers between devices, on_device(): received = lax.ppermute(halo, 'section', ring)  2.55 us
    ppermute x1, waiting for transfers between devices, on_device(): passed = lax.ppermute(sums, 'section', ring)  1.62 us
    ppermute x1, starting transfers between devices, on_device(): passed = lax.ppermute(sums, 'section', ring)  1.54 us
  transfers between devices with their start and end apart: 6, of which 2 were waited for; matrix products, arithmetic and copies ran while one was open for 0% of the time, Pallas kernels for 3%

profile of v27, /device:TPU:0, one launch (start us, length us, event | category | flops | bytes accessed | tf_op | source)
XLA Modules:
  0.0 36.7 jit_solution(12756872588556817769)
XLA Ops:
  0.0 1.1 %shard_map.109 = (bf16[8,2,64,128]{3,2,1,0:T(8,128)(2,1)S(1)}, bf16[4,2,64,128]{3,2,1,0:T(8,128)(2,1)S(1)}) custom-call(bf16[8,2,64,128]{3,2,1,0:T(8,128)(2,1)} %own_ref.1, bf16[2,2,64,128]{3,2,1,0:T(8,128)(2,1)} %second_cache_ref.1, bf16[2,2,64,128]{3,2,1,0:T(8,128)(2,1)} %first_cache_ref.1), custom_call_target="tpu_custom_call" | custom-call | bytes 1048576 | tf_op jit(solution)/shard_map/pallas_call | solution.py:277
  1.1 0.5 %collective-permute-start = (bf16[8,2,64,128]{3,2,1,0:T(8,128)(2,1)S(1)}, bf16[8,2,64,128]{3,2,1,0:T(8,128)(2,1)S(1)}, u32[]{:S(2)}, u32[]{:S(2)}) collective-permute-start(bf16[8,2,64,128]{3,2,1,0:T(8,128)(2,1)S(1)} %get-tuple-element.12.own_ref), channel_id=1, source_target_pairs={{0,1},{1,0},{2,3},{3,2},{4,5},{5,4},{6,7},{7,6},{8,9},{9,8},{10,11... | collective-permute-start | bytes 786440 | tf_op jit(solution)/shard_map/ppermute | solution.py:312
  1.6 2.6 %collective-permute-start.2 = (bf16[4,2,64,128]{3,2,1,0:T(8,128)(2,1)S(1)}, bf16[4,2,64,128]{3,2,1,0:T(8,128)(2,1)S(1)}, u32[]{:S(2)}, u32[]{:S(2)}) collective-permute-start(bf16[4,2,64,128]{3,2,1,0:T(8,128)(2,1)S(1)} %get-tuple-element.13), channel_id=1, source_target_pairs={{0,8},{8,16},{16,24},{24,0},{1,9},{9,17},{17,25},{25,1},{2,10},{10... | collective-permute-start | bytes 393224 | tf_op jit(solution)/shard_map/ppermute | solution.py:336
  4.1 0.0 collective-permute-done.near_ref
  4.1 1.6 %collective-permute-start.1 = (bf16[8,2,64,128]{3,2,1,0:T(8,128)(2,1)S(1)}, bf16[8,2,64,128]{3,2,1,0:T(8,128)(2,1)S(1)}, u32[]{:S(2)}, u32[]{:S(2)}) collective-permute-start(bf16[8,2,64,128]{3,2,1,0:T(8,128)(2,1)S(1)} %collective-permute-done.near_ref), channel_id=1, source_target_pairs={{0,2},{1,0},{2,4},{3,1},{4,6},{5,3},{6,7},{7,5},{8,10},{9,8},{10,1... | collective-permute-start | bytes 786440 | tf_op jit(solution)/shard_map/ppermute | solution.py:312
  5.7 1.2 %shard_map.110 = (f32[1,2,128]{2,1,0:T(2,128)S(1)}, f32[6,1,128]{2,1,0:T(1,128)S(1)}, bf16[3,3,3,128,128]{4,3,2,1,0:T(8,128)(2,1)S(1)}) custom-call(bf16[8,2,64,128]{3,2,1,0:T(8,128)(2,1)S(1)} %get-tuple-element.12.own_ref, bf16[3,3,3,128,128]{4,3,2,1,0:T(8,128)(2,1)} %weight_ref.2, f32[1,128]{1,0:T(1,128)} %bitcast.8, f32[1,128]{1,0:T(1,128)} %bitcast.9, ...), custom_call_target="tpu_custom_call" | custom-call | bytes 1048576 | tf_op jit(solution)/shard_map/pallas_call | solution.py:277
  7.0 1.5 %collective-permute-start.5 = (f32[1,2,128]{2,1,0:T(2,128)S(1)}, f32[1,2,128]{2,1,0:T(2,128)S(1)}, u32[]{:S(2)}, u32[]{:S(2)}) collective-permute-start(f32[1,2,128]{2,1,0:T(2,128)S(1)} %get-tuple-element.14), channel_id=1, source_target_pairs={{0,8},{8,16},{16,24},{24,0},{1,9},{9,17},{17,25},{25,1},{2,10},{10... | collective-permute-start | bytes 3080 | tf_op jit(solution)/shard_map/ppermute | solution.py:339
  8.5 0.7 %collective-permute-done.2.halo_ref = bf16[4,2,64,128]{3,2,1,0:T(8,128)(2,1)S(1)} collective-permute-done((bf16[4,2,64,128]{3,2,1,0:T(8,128)(2,1)S(1)}, bf16[4,2,64,128]{3,2,1,0:T(8,128)(2,1)S(1)}, u32[]{:S(2)}, u32[]{:S(2)}) %collective-permute-start.2) | collective-permute-done | bytes 131104 | tf_op jit(solution)/shard_map/ppermute | solution.py:336
  9.2 0.0 collective-permute-start.4
  9.2 0.7 %collective-permute-start.3 = (bf16[4,2,64,128]{3,2,1,0:T(8,128)(2,1)S(1)}, bf16[4,2,64,128]{3,2,1,0:T(8,128)(2,1)S(1)}, u32[]{:S(2)}, u32[]{:S(2)}) collective-permute-start(bf16[4,2,64,128]{3,2,1,0:T(8,128)(2,1)S(1)} %collective-permute-done.2.halo_ref), channel_id=1, source_target_pairs={{0,0},{1,2},{2,1},{3,4},{4,3},{5,6},{6,5},{7,7},{8,8},{9,10},{10,9... | collective-permute-start | bytes 393224 | tf_op jit(solution)/shard_map/ppermute | solution.py:312
  9.9 1.6 %collective-permute-done.5 = f32[1,2,128]{2,1,0:T(2,128)S(1)} collective-permute-done((f32[1,2,128]{2,1,0:T(2,128)S(1)}, f32[1,2,128]{2,1,0:T(2,128)S(1)}, u32[]{:S(2)}, u32[]{:S(2)}) %collective-permute-start.5) | collective-permute-done | bytes 1056 | tf_op jit(solution)/shard_map/ppermute | solution.py:339
  11.5 10.7 %all_to_all.10.stats_ref = f32[8,4,128]{2,1,0:T(4,128)S(1)} all-to-all(f32[8,4,128]{2,1,0:T(4,128)S(1)} %broadcast_in_dim.8), channel_id=1, replica_groups=mesh['section'=4,'rows'=8] {'rows'}, dimensions={0} | all-to-all | bytes 32768 | tf_op jit(solution)/shard_map/all_to_all | solution.py:344
  22.2 0.0 collective-permute-done.4.halo_near_ref
  22.2 0.0 collective-permute-done.3.halo_far_ref
  22.3 0.0 collective-permute-done.1.far_ref
  22.3 0.0 copy-start
  22.3 3.3 %shard_map.111 = (bf16[10,4,64,128]{3,2,1,0:T(8,128)(2,1)S(1)}, f32[32,2,128]{2,1,0:T(2,128)S(1)}) custom-call(bf16[8,2,64,128]{3,2,1,0:T(8,128)(2,1)S(1)} %get-tuple-element.12.own_ref, bf16[8,2,64,128]{3,2,1,0:T(8,128)(2,1)S(1)} %collective-permute-done.near_ref, bf16[8,2,64,128]{3,2,1,0:T(8,128)(2,1)S(1)} %collective-permute-done.1.far_ref, ...), custom_call_target="tpu_custom_call" | custom-call | flops 1000000000 | bytes 1048576 | tf_op jit(solution)/shard_map/pallas_call | solution.py:277
  25.6 9.0 %all_to_all.11.stats_ref = f32[32,2,128]{2,1,0:T(2,128)S(1)} all-to-all(f32[32,2,128]{2,1,0:T(2,128)S(1)} %get-tuple-element.18), channel_id=1, replica_groups=mesh['section'=4,'rows'=8] {'section','rows'}, dimensions={0} | all-to-all | bytes 65536 | tf_op jit(solution)/shard_map/all_to_all | solution.py:355
  34.6 0.0 copy-done
  34.6 2.2 %shard_map.112 = bf16[8,2,64,128]{3,2,1,0:T(8,128)(2,1)} custom-call(bf16[10,4,64,128]{3,2,1,0:T(8,128)(2,1)S(1)} %get-tuple-element.17.middle_ref, f32[32,2,128]{2,1,0:T(2,128)S(1)} %all_to_all.11.stats_ref, f32[6,1,128]{2,1,0:T(1,128)S(1)} %get-tuple-element.15.vectors_ref, bf16[3,3,3,128,128]{4,3,2,1,0:T(8,128)(2,1)S(1)} %copy-done, ...), custom_call_target="tpu_custom_call" | custom-call | flops 1000000000 | bytes 1048576 | tf_op jit(solution)/shard_map/pallas_call | solution.py:277
  (2 shorter events, 0.0 us)
Async XLA Ops:
  1.1 3.1 %collective-permute-start = (bf16[8,2,64,128]{3,2,1,0:T(8,128)(2,1)S(1)}, bf16[8,2,64,128]{3,2,1,0:T(8,128)(2,1)S(1)}, u32[]{:S(2)}, u32[]{:S(2)}) collective-permute-start(bf16[8,2,64,128]{3,2,1,0:T(8,128)(2,1)S(1)} %get-tuple-element.12.own_ref), channel_id=1, source_target_pairs={{0,1},{1,0},{2,3},{3,2},{4,5},{5,4},{6,7},{7,6},{8,9},{9,8},{10,11... | collective-permute-start | bytes 786440 | tf_op jit(solution)/shard_map/ppermute | solution.py:312
  1.6 7.6 %collective-permute-start.2 = (bf16[4,2,64,128]{3,2,1,0:T(8,128)(2,1)S(1)}, bf16[4,2,64,128]{3,2,1,0:T(8,128)(2,1)S(1)}, u32[]{:S(2)}, u32[]{:S(2)}) collective-permute-start(bf16[4,2,64,128]{3,2,1,0:T(8,128)(2,1)S(1)} %get-tuple-element.13), channel_id=1, source_target_pairs={{0,8},{8,16},{16,24},{24,0},{1,9},{9,17},{17,25},{25,1},{2,10},{10... | collective-permute-start | bytes 393224 | tf_op jit(solution)/shard_map/ppermute | solution.py:336
  4.1 18.1 %collective-permute-start.1 = (bf16[8,2,64,128]{3,2,1,0:T(8,128)(2,1)S(1)}, bf16[8,2,64,128]{3,2,1,0:T(8,128)(2,1)S(1)}, u32[]{:S(2)}, u32[]{:S(2)}) collective-permute-start(bf16[8,2,64,128]{3,2,1,0:T(8,128)(2,1)S(1)} %collective-permute-done.near_ref), channel_id=1, source_target_pairs={{0,2},{1,0},{2,4},{3,1},{4,6},{5,3},{6,7},{7,5},{8,10},{9,8},{10,1... | collective-permute-start | bytes 786440 | tf_op jit(solution)/shard_map/ppermute | solution.py:312
  7.0 4.5 %collective-permute-start.5 = (f32[1,2,128]{2,1,0:T(2,128)S(1)}, f32[1,2,128]{2,1,0:T(2,128)S(1)}, u32[]{:S(2)}, u32[]{:S(2)}) collective-permute-start(f32[1,2,128]{2,1,0:T(2,128)S(1)} %get-tuple-element.14), channel_id=1, source_target_pairs={{0,8},{8,16},{16,24},{24,0},{1,9},{9,17},{17,25},{25,1},{2,10},{10... | collective-permute-start | bytes 3080 | tf_op jit(solution)/shard_map/ppermute | solution.py:339
  9.2 13.0 %collective-permute-start.4 = (bf16[4,2,64,128]{3,2,1,0:T(8,128)(2,1)S(1)}, bf16[4,2,64,128]{3,2,1,0:T(8,128)(2,1)S(1)}, u32[]{:S(2)}, u32[]{:S(2)}) collective-permute-start(bf16[4,2,64,128]{3,2,1,0:T(8,128)(2,1)S(1)} %collective-permute-done.2.halo_ref), channel_id=1, source_target_pairs={{0,1},{1,0},{2,3},{3,2},{4,5},{5,4},{6,7},{7,6},{8,9},{9,8},{10,11... | collective-permute-start | bytes 393224 | tf_op jit(solution)/shard_map/ppermute | solution.py:312
  9.2 13.0 %collective-permute-start.3 = (bf16[4,2,64,128]{3,2,1,0:T(8,128)(2,1)S(1)}, bf16[4,2,64,128]{3,2,1,0:T(8,128)(2,1)S(1)}, u32[]{:S(2)}, u32[]{:S(2)}) collective-permute-start(bf16[4,2,64,128]{3,2,1,0:T(8,128)(2,1)S(1)} %collective-permute-done.2.halo_ref), channel_id=1, source_target_pairs={{0,0},{1,2},{2,1},{3,4},{4,3},{5,6},{6,5},{7,7},{8,8},{9,10},{10,9... | collective-permute-start | bytes 393224 | tf_op jit(solution)/shard_map/ppermute | solution.py:312
  22.3 12.3 %copy-start = (bf16[3,3,3,128,128]{4,3,2,1,0:T(8,128)(2,1)S(1)}, bf16[3,3,3,128,128]{4,3,2,1,0:T(8,128)(2,1)}, u32[]{:S(2)}) copy-start(bf16[3,3,3,128,128]{4,3,2,1,0:T(8,128)(2,1)} %weight_ref.3) | copy-start | bytes 2654212

commit v28 on v21

--- a/solution.py
+++ b/solution.py
@@ -101,7 +101,8 @@
             axis=0,
         ),
     )
-    column = lax.broadcasted_iota(jnp.int32, (cells, channels), 0) % columns
+    column = lax.broadcasted_iota(jnp.int32, (frames, columns, channels), 1)
+    column = column.reshape(cells, channels)
     results = []
     for out in range(2):
         left, centre = (

time: 36.9 us -> 36.9 us (level)
  no operation moved by 1% of the time
where the time goes in v28:
time: 36.9 us; the launch traced here: 36.7 us
  blocking collectives  18.4 us (50%)
  Pallas kernels  7.72 us (21%)
  starting transfers between devices  6.13 us (17%)
  waiting for transfers between devices  4.33 us (12%)
    all_to_all x1, blocking collectives, on_device(): stats = lax.all_to_all(both, 'rows', 0, 0, tiled=True)  9.31 us
    all_to_all x1, blocking collectives, on_device(): stats_two = lax.all_to_all(sums_two, ('section', 'rows'), 0, 0, tiled=True)  9.09 us
    pallas_call x4, Pallas kernels, call(): pl.pallas_call(kernel, out_shape=out_shape, in_specs=specs, out_specs=jax...  7.72 us
    ppermute x1, starting transfers between devices, on_device(): received = lax.ppermute(halo, 'section', ring)  2.99 us
    ppermute x1, waiting for transfers between devices, on_device(): passed = lax.ppermute(sums, 'section', ring)  2.98 us
    ppermute x3, starting transfers between devices, across(): return lax.ppermute(block, 'rows', list(enumerate(partner)))  1.6 us
    ppermute x1, starting transfers between devices, on_device(): passed = lax.ppermute(sums, 'section', ring)  1.54 us
    ppermute x3, waiting for transfers between devices, across(): return lax.ppermute(block, 'rows', list(enumerate(partner)))  1.35 us
  transfers between devices with their start and end apart: 5, of which 2 were waited for; matrix products, arithmetic and copies ran while one was open for 0% of the time, Pallas kernels for 3%

profile of v28, /device:TPU:0, one launch (start us, length us, event | category | flops | bytes accessed | tf_op | source)
XLA Modules:
  0.0 36.7 jit_solution(2927883754658380648)
XLA Ops:
  0.0 1.1 %shard_map.109 = (bf16[8,2,64,128]{3,2,1,0:T(8,128)(2,1)S(1)}, bf16[4,2,64,128]{3,2,1,0:T(8,128)(2,1)S(1)}) custom-call(bf16[8,2,64,128]{3,2,1,0:T(8,128)(2,1)} %own_ref.1, bf16[2,2,64,128]{3,2,1,0:T(8,128)(2,1)} %second_cache_ref.1, bf16[2,2,64,128]{3,2,1,0:T(8,128)(2,1)} %first_cache_ref.1), custom_call_target="tpu_custom_call" | custom-call | bytes 1048576 | tf_op jit(solution)/shard_map/pallas_call | solution.py:278
  1.1 3.0 %collective-permute-start = (bf16[4,2,64,128]{3,2,1,0:T(8,128)(2,1)S(1)}, bf16[4,2,64,128]{3,2,1,0:T(8,128)(2,1)S(1)}, u32[]{:S(2)}, u32[]{:S(2)}) collective-permute-start(bf16[4,2,64,128]{3,2,1,0:T(8,128)(2,1)S(1)} %get-tuple-element.15), channel_id=1, source_target_pairs={{0,8},{8,16},{16,24},{24,0},{1,9},{9,17},{17,25},{25,1},{2,10},{10... | collective-permute-start | bytes 393224 | tf_op jit(solution)/shard_map/ppermute | solution.py:337
  4.1 0.0 collective-permute-start.3
  4.1 1.2 %shard_map.110 = (f32[1,2,128]{2,1,0:T(2,128)S(1)}, f32[6,1,128]{2,1,0:T(1,128)S(1)}, bf16[3,3,3,128,128]{4,3,2,1,0:T(8,128)(2,1)S(1)}) custom-call(bf16[8,2,64,128]{3,2,1,0:T(8,128)(2,1)S(1)} %get-tuple-element.16.own_ref, bf16[3,3,3,128,128]{4,3,2,1,0:T(8,128)(2,1)} %weight_ref.2, f32[1,128]{1,0:T(1,128)} %bitcast.8, f32[1,128]{1,0:T(1,128)} %bitcast.9, ...), custom_call_target="tpu_custom_call" | custom-call | bytes 1048576 | tf_op jit(solution)/shard_map/pallas_call | solution.py:278
  5.3 1.5 %collective-permute-start.1 = (f32[1,2,128]{2,1,0:T(2,128)S(1)}, f32[1,2,128]{2,1,0:T(2,128)S(1)}, u32[]{:S(2)}, u32[]{:S(2)}) collective-permute-start(f32[1,2,128]{2,1,0:T(2,128)S(1)} %get-tuple-element.19), channel_id=1, source_target_pairs={{0,8},{8,16},{16,24},{24,0},{1,9},{9,17},{17,25},{25,1},{2,10},{10... | collective-permute-start | bytes 3080 | tf_op jit(solution)/shard_map/ppermute | solution.py:338
  6.9 3.0 %collective-permute-done.1 = f32[1,2,128]{2,1,0:T(2,128)S(1)} collective-permute-done((f32[1,2,128]{2,1,0:T(2,128)S(1)}, f32[1,2,128]{2,1,0:T(2,128)S(1)}, u32[]{:S(2)}, u32[]{:S(2)}) %collective-permute-start.1) | collective-permute-done | bytes 1056 | tf_op jit(solution)/shard_map/ppermute | solution.py:338
  9.8 0.0 collective-permute-done.halo_ref
  9.8 0.0 collective-permute-start.2
  9.8 1.3 %collective-permute-done.2 = bf16[4,2,64,128]{3,2,1,0:T(8,128)(2,1)S(1)} collective-permute-done((bf16[4,2,64,128]{3,2,1,0:T(8,128)(2,1)S(1)}, bf16[4,2,64,128]{3,2,1,0:T(8,128)(2,1)S(1)}, u32[]{:S(2)}, u32[]{:S(2)}) %collective-permute-start.2) | collective-permute-done | bytes 131104 | tf_op jit(solution)/shard_map/ppermute | solution.py:313
  11.2 0.0 collective-permute-done.3
  11.3 1.6 %collective-permute-start.4 = (bf16[12,2,64,128]{3,2,1,0:T(8,128)(2,1)S(1)}, bf16[12,2,64,128]{3,2,1,0:T(8,128)(2,1)S(1)}, u32[]{:S(2)}, u32[]{:S(2)}) collective-permute-start(bf16[12,2,64,128]{3,2,1,0:T(8,128)(2,1)S(1)} %constant_dynamic-update-slice_fusion.near_ref), channel_id=1, source_target_pairs={{0,2},{1,0},{2,4},{3,1},{4,6},{5,3},{6,7},{7,5},{8,10},{9,8},{10,1... | collective-permute-start | bytes 1179656 | tf_op jit(solution)/shard_map/ppermute | solution.py:313
  12.9 9.3 %all_to_all.10.stats_ref = f32[8,4,128]{2,1,0:T(4,128)S(1)} all-to-all(f32[8,4,128]{2,1,0:T(4,128)S(1)} %broadcast_in_dim.8), channel_id=1, replica_groups=mesh['section'=4,'rows'=8] {'rows'}, dimensions={0} | all-to-all | bytes 32768 | tf_op jit(solution)/shard_map/all_to_all | solution.py:344
  22.2 0.0 collective-permute-done.4.far_ref
  22.2 0.0 copy-start
  22.2 3.3 %shard_map.111 = (bf16[10,4,64,128]{3,2,1,0:T(8,128)(2,1)S(1)}, f32[32,2,128]{2,1,0:T(2,128)S(1)}) custom-call(bf16[4,2,64,128]{3,2,1,0:T(8,128)(2,1)S(1)} %collective-permute-done.halo_ref, bf16[8,2,64,128]{3,2,1,0:T(8,128)(2,1)S(1)} %get-tuple-element.16.own_ref, bf16[12,2,64,128]{3,2,1,0:T(8,128)(2,1)S(1)} %constant_dynamic-update-slice_fusion.near_ref, ...), custom_call_target="tpu_custom_call" | custom-call | flops 1000000000 | bytes 1048576 | tf_op jit(solution)/shard_map/pallas_call | solution.py:278
  25.5 9.1 %all_to_all.11.stats_ref = f32[32,2,128]{2,1,0:T(2,128)S(1)} all-to-all(f32[32,2,128]{2,1,0:T(2,128)S(1)} %get-tuple-element.24), channel_id=1, replica_groups=mesh['section'=4,'rows'=8] {'section','rows'}, dimensions={0} | all-to-all | bytes 65536 | tf_op jit(solution)/shard_map/all_to_all | solution.py:355
  34.6 0.0 copy-done
  34.6 2.1 %shard_map.112 = bf16[8,2,64,128]{3,2,1,0:T(8,128)(2,1)} custom-call(bf16[10,4,64,128]{3,2,1,0:T(8,128)(2,1)S(1)} %get-tuple-element.23.middle_ref, f32[32,2,128]{2,1,0:T(2,128)S(1)} %all_to_all.11.stats_ref, f32[6,1,128]{2,1,0:T(1,128)S(1)} %get-tuple-element.21.vectors_ref, bf16[3,3,3,128,128]{4,3,2,1,0:T(8,128)(2,1)S(1)} %copy-done, ...), custom_call_target="tpu_custom_call" | custom-call | flops 1000000000 | bytes 1048576 | tf_op jit(solution)/shard_map/pallas_call | solution.py:278
  (4 shorter events, 0.1 us)
Async XLA Ops:
  1.1 8.8 %collective-permute-start = (bf16[4,2,64,128]{3,2,1,0:T(8,128)(2,1)S(1)}, bf16[4,2,64,128]{3,2,1,0:T(8,128)(2,1)S(1)}, u32[]{:S(2)}, u32[]{:S(2)}) collective-permute-start(bf16[4,2,64,128]{3,2,1,0:T(8,128)(2,1)S(1)} %get-tuple-element.15), channel_id=1, source_target_pairs={{0,8},{8,16},{16,24},{24,0},{1,9},{9,17},{17,25},{25,1},{2,10},{10... | collective-permute-start | bytes 393224 | tf_op jit(solution)/shard_map/ppermute | solution.py:337
  4.1 7.1 %collective-permute-start.3 = (bf16[8,2,64,128]{3,2,1,0:T(8,128)(2,1)S(1)}, bf16[8,2,64,128]{3,2,1,0:T(8,128)(2,1)S(1)}, u32[]{:S(2)}, u32[]{:S(2)}) collective-permute-start(bf16[8,2,64,128]{3,2,1,0:T(8,128)(2,1)S(1)} %get-tuple-element.16.own_ref), channel_id=1, source_target_pairs={{0,1},{1,0},{2,3},{3,2},{4,5},{5,4},{6,7},{7,6},{8,9},{9,8},{10,11... | collective-permute-start | bytes 786440 | tf_op jit(solution)/shard_map/ppermute | solution.py:313
  5.3 4.5 %collective-permute-start.1 = (f32[1,2,128]{2,1,0:T(2,128)S(1)}, f32[1,2,128]{2,1,0:T(2,128)S(1)}, u32[]{:S(2)}, u32[]{:S(2)}) collective-permute-start(f32[1,2,128]{2,1,0:T(2,128)S(1)} %get-tuple-element.19), channel_id=1, source_target_pairs={{0,8},{8,16},{16,24},{24,0},{1,9},{9,17},{17,25},{25,1},{2,10},{10... | collective-permute-start | bytes 3080 | tf_op jit(solution)/shard_map/ppermute | solution.py:338
  9.8 1.3 %collective-permute-start.2 = (bf16[4,2,64,128]{3,2,1,0:T(8,128)(2,1)S(1)}, bf16[4,2,64,128]{3,2,1,0:T(8,128)(2,1)S(1)}, u32[]{:S(2)}, u32[]{:S(2)}) collective-permute-start(bf16[4,2,64,128]{3,2,1,0:T(8,128)(2,1)S(1)} %collective-permute-done.halo_ref), channel_id=1, source_target_pairs={{0,1},{1,0},{2,3},{3,2},{4,5},{5,4},{6,7},{7,6},{8,9},{9,8},{10,11... | collective-permute-start | bytes 393224 | tf_op jit(solution)/shard_map/ppermute | solution.py:313
  11.3 10.9 %collective-permute-start.4 = (bf16[12,2,64,128]{3,2,1,0:T(8,128)(2,1)S(1)}, bf16[12,2,64,128]{3,2,1,0:T(8,128)(2,1)S(1)}, u32[]{:S(2)}, u32[]{:S(2)}) collective-permute-start(bf16[12,2,64,128]{3,2,1,0:T(8,128)(2,1)S(1)} %constant_dynamic-update-slice_fusion.near_ref), channel_id=1, source_target_pairs={{0,2},{1,0},{2,4},{3,1},{4,6},{5,3},{6,7},{7,5},{8,10},{9,8},{10,1... | collective-permute-start | bytes 1179656 | tf_op jit(solution)/shard_map/ppermute | solution.py:313
  22.2 12.4 %copy-start = (bf16[3,3,3,128,128]{4,3,2,1,0:T(8,128)(2,1)S(1)}, bf16[3,3,3,128,128]{4,3,2,1,0:T(8,128)(2,1)}, u32[]{:S(2)}) copy-start(bf16[3,3,3,128,128]{4,3,2,1,0:T(8,128)(2,1)} %weight_ref.3) | copy-start | bytes 2654212

commit v29 on v28

--- a/solution.py
+++ b/solution.py
@@ -55,7 +55,7 @@
     return half + half * jnp.tanh(half)
 
 
-def pair_conv(field, row, begin, frames, weight_ref):
+def pair_conv(field, row, begin, frames, weight_ref, prepare):
     columns, channels = field.shape[2], field.shape[3]
     cells = frames * columns
     nothing = jnp.zeros((channels, channels), jnp.bfloat16)
@@ -68,22 +68,18 @@
         return jnp.dot(pieces, blocks, preferred_element_type=jnp.float32)
 
     taps = [(frame_tap, row_tap) for frame_tap in range(3) for row_tap in range(3)]
-    early = dot(
-        jnp.concatenate(
-            [
-                jnp.concatenate([piece(tap, out + row_tap) for tap, row_tap in taps], axis=1)
-                for out in range(2)
-            ],
-            axis=0,
-        ),
-        jnp.concatenate(
-            [
-                jnp.concatenate([weight_ref[tap, row_tap, 0], weight_ref[tap, row_tap, 1]], axis=1)
-                for tap, row_tap in taps
-            ],
-            axis=0,
-        ),
-    )
+    early_weight = jnp.concatenate(
+        [
+            jnp.concatenate([weight_ref[tap, row_tap, 0], weight_ref[tap, row_tap, 1]], axis=1)
+            for tap, row_tap in taps
+        ],
+        axis=0,
+    )
+    early = []
+    for out in range(2):
+        prepare(row + out + 2)
+        pieces = [piece(tap, out + row_tap) for tap, row_tap in taps]
+        early.append(dot(jnp.concatenate(pieces, axis=1), early_weight))
     lines = [(frame_tap, line) for frame_tap in range(3) for line in range(4)]
     late = dot(
         jnp.concatenate([piece(tap, line) for tap, line in lines], axis=1),
@@ -106,8 +102,7 @@
     results = []
     for out in range(2):
         left, centre = (
-            early[out * cells : (out + 1) * cells, tap * channels : (tap + 1) * channels]
-            for tap in range(2)
+            early[out][:, tap * channels : (tap + 1) * channels] for tap in range(2)
         )
         right = late[:, out * channels : (out + 1) * channels]
         left = jnp.where(column == 0, 0.0, pltpu.roll(left, 1, 0))
@@ -199,12 +194,15 @@
     bias = vectors_ref[2]
     kept = []
     spare = SPAN_HALO - 2
-    ready = 0
+    filled = []
+
+    def prepare(last):
+        while len(filled) <= last:
+            fill(len(filled))
+            filled.append(last)
+
     for pair in range((lines + 2) // 2):
-        for line in range(ready, 2 * pair + 4):
-            fill(line)
-        ready = 2 * pair + 4
-        results = pair_conv(field, 2 * pair, 0, inner + 2, weight_ref)
+        results = pair_conv(field, 2 * pair, 0, inner + 2, weight_ref, prepare)
         for out in range(2):
             line = 2 * pair + out
             rounded = (results[out] + bias).astype(jnp.bfloat16)
@@ -234,9 +232,10 @@
     half = frames // 2
     copies = []
     for begin in range(0, frames, half):
-        filled = 0 if begin == 0 else begin + 2
-        for line in range(lines + 2):
-            ahead = middle_ref[filled : begin + half + 2, line]
+        start = 0 if begin == 0 else begin + 2
+
+        def fill(line):
+            ahead = middle_ref[start : begin + half + 2, line]
             if begin == 0:
                 behind = activate(ahead[:2], slope_before, offset_before).astype(jnp.bfloat16)
                 behind = jnp.where(at_start, ahead[:2], behind)
@@ -247,10 +246,18 @@
             if line == 0 or line == lines + 1:
                 outside = row_at == 0 if line == 0 else row_at == row_count - 1
                 ahead = jnp.where(outside, jnp.zeros_like(ahead), ahead)
-            field[filled : begin + half + 2, line] = ahead
+            field[start : begin + half + 2, line] = ahead
+
+        filled = []
+
+        def prepare(last):
+            while len(filled) <= last:
+                fill(len(filled))
+                filled.append(last)
+
         span = slice(begin, begin + half)
         for pair in range(lines // 2):
-            results = pair_conv(field, 2 * pair, begin, half, weight_ref)
+            results = pair_conv(field, 2 * pair, begin, half, weight_ref, prepare)
             for out in range(2):
                 line = 2 * pair + out
                 result = (results[out] + vectors_ref[5]).reshape(half, columns, channels)

time: 36.9 us -> 37 us (level)
  no operation moved by 1% of the time
where the time goes in v29:
time: 37 us; the launch traced here: 36.8 us
  blocking collectives  18.4 us (50%)
  Pallas kernels  7.8 us (21%)
  starting transfers between devices  6.13 us (17%)
  waiting for transfers between devices  4.33 us (12%)
    all_to_all x1, blocking collectives, on_device(): stats = lax.all_to_all(both, 'rows', 0, 0, tiled=True)  9.31 us
    all_to_all x1, blocking collectives, on_device(): stats_two = lax.all_to_all(sums_two, ('section', 'rows'), 0, 0, tiled=True)  9.1 us
    pallas_call x4, Pallas kernels, call(): pl.pallas_call(kernel, out_shape=out_shape, in_specs=specs, out_specs=jax...  7.8 us
    ppermute x1, starting transfers between devices, on_device(): received = lax.ppermute(halo, 'section', ring)  2.99 us
    ppermute x1, waiting for transfers between devices, on_device(): passed = lax.ppermute(sums, 'section', ring)  2.98 us
    ppermute x3, starting transfers between devices, across(): return lax.ppermute(block, 'rows', list(enumerate(partner)))  1.6 us
    ppermute x1, starting transfers between devices, on_device(): passed = lax.ppermute(sums, 'section', ring)  1.54 us
    ppermute x3, waiting for transfers between devices, across(): return lax.ppermute(block, 'rows', list(enumerate(partner)))  1.35 us
  transfers between devices with their start and end apart: 5, of which 2 were waited for; matrix products, arithmetic and copies ran while one was open for 0% of the time, Pallas kernels for 3%

profile of v29, /device:TPU:0, one launch (start us, length us, event | category | flops | bytes accessed | tf_op | source)
XLA Modules:
  0.0 36.8 jit_solution(11703419475458414562)
XLA Ops:
  0.0 1.1 %shard_map.109 = (bf16[8,2,64,128]{3,2,1,0:T(8,128)(2,1)S(1)}, bf16[4,2,64,128]{3,2,1,0:T(8,128)(2,1)S(1)}) custom-call(bf16[8,2,64,128]{3,2,1,0:T(8,128)(2,1)} %own_ref.1, bf16[2,2,64,128]{3,2,1,0:T(8,128)(2,1)} %second_cache_ref.1, bf16[2,2,64,128]{3,2,1,0:T(8,128)(2,1)} %first_cache_ref.1), custom_call_target="tpu_custom_call" | custom-call | bytes 1048576 | tf_op jit(solution)/shard_map/pallas_call | solution.py:285
  1.1 3.0 %collective-permute-start = (bf16[4,2,64,128]{3,2,1,0:T(8,128)(2,1)S(1)}, bf16[4,2,64,128]{3,2,1,0:T(8,128)(2,1)S(1)}, u32[]{:S(2)}, u32[]{:S(2)}) collective-permute-start(bf16[4,2,64,128]{3,2,1,0:T(8,128)(2,1)S(1)} %get-tuple-element.15), channel_id=1, source_target_pairs={{0,8},{8,16},{16,24},{24,0},{1,9},{9,17},{17,25},{25,1},{2,10},{10... | collective-permute-start | bytes 393224 | tf_op jit(solution)/shard_map/ppermute | solution.py:344
  4.1 0.0 collective-permute-start.3
  4.1 1.2 %shard_map.110 = (f32[1,2,128]{2,1,0:T(2,128)S(1)}, f32[6,1,128]{2,1,0:T(1,128)S(1)}, bf16[3,3,3,128,128]{4,3,2,1,0:T(8,128)(2,1)S(1)}) custom-call(bf16[8,2,64,128]{3,2,1,0:T(8,128)(2,1)S(1)} %get-tuple-element.16.own_ref, bf16[3,3,3,128,128]{4,3,2,1,0:T(8,128)(2,1)} %weight_ref.2, f32[1,128]{1,0:T(1,128)} %bitcast.8, f32[1,128]{1,0:T(1,128)} %bitcast.9, ...), custom_call_target="tpu_custom_call" | custom-call | bytes 1048576 | tf_op jit(solution)/shard_map/pallas_call | solution.py:285
  5.3 1.5 %collective-permute-start.1 = (f32[1,2,128]{2,1,0:T(2,128)S(1)}, f32[1,2,128]{2,1,0:T(2,128)S(1)}, u32[]{:S(2)}, u32[]{:S(2)}) collective-permute-start(f32[1,2,128]{2,1,0:T(2,128)S(1)} %get-tuple-element.19), channel_id=1, source_target_pairs={{0,8},{8,16},{16,24},{24,0},{1,9},{9,17},{17,25},{25,1},{2,10},{10... | collective-permute-start | bytes 3080 | tf_op jit(solution)/shard_map/ppermute | solution.py:345
  6.9 3.0 %collective-permute-done.1 = f32[1,2,128]{2,1,0:T(2,128)S(1)} collective-permute-done((f32[1,2,128]{2,1,0:T(2,128)S(1)}, f32[1,2,128]{2,1,0:T(2,128)S(1)}, u32[]{:S(2)}, u32[]{:S(2)}) %collective-permute-start.1) | collective-permute-done | bytes 1056 | tf_op jit(solution)/shard_map/ppermute | solution.py:345
  9.8 0.0 collective-permute-done.halo_ref
  9.8 0.0 collective-permute-start.2
  9.8 1.3 %collective-permute-done.2 = bf16[4,2,64,128]{3,2,1,0:T(8,128)(2,1)S(1)} collective-permute-done((bf16[4,2,64,128]{3,2,1,0:T(8,128)(2,1)S(1)}, bf16[4,2,64,128]{3,2,1,0:T(8,128)(2,1)S(1)}, u32[]{:S(2)}, u32[]{:S(2)}) %collective-permute-start.2) | collective-permute-done | bytes 131104 | tf_op jit(solution)/shard_map/ppermute | solution.py:320
  11.2 0.0 collective-permute-done.3
  11.3 1.6 %collective-permute-start.4 = (bf16[12,2,64,128]{3,2,1,0:T(8,128)(2,1)S(1)}, bf16[12,2,64,128]{3,2,1,0:T(8,128)(2,1)S(1)}, u32[]{:S(2)}, u32[]{:S(2)}) collective-permute-start(bf16[12,2,64,128]{3,2,1,0:T(8,128)(2,1)S(1)} %constant_dynamic-update-slice_fusion.near_ref), channel_id=1, source_target_pairs={{0,2},{1,0},{2,4},{3,1},{4,6},{5,3},{6,7},{7,5},{8,10},{9,8},{10,1... | collective-permute-start | bytes 1179656 | tf_op jit(solution)/shard_map/ppermute | solution.py:320
  12.9 9.3 %all_to_all.10.stats_ref = f32[8,4,128]{2,1,0:T(4,128)S(1)} all-to-all(f32[8,4,128]{2,1,0:T(4,128)S(1)} %broadcast_in_dim.8), channel_id=1, replica_groups=mesh['section'=4,'rows'=8] {'rows'}, dimensions={0} | all-to-all | bytes 32768 | tf_op jit(solution)/shard_map/all_to_all | solution.py:351
  22.2 0.0 collective-permute-done.4.far_ref
  22.2 0.0 copy-start
  22.2 3.3 %shard_map.111 = (bf16[10,4,64,128]{3,2,1,0:T(8,128)(2,1)S(1)}, f32[32,2,128]{2,1,0:T(2,128)S(1)}) custom-call(bf16[4,2,64,128]{3,2,1,0:T(8,128)(2,1)S(1)} %collective-permute-done.halo_ref, bf16[8,2,64,128]{3,2,1,0:T(8,128)(2,1)S(1)} %get-tuple-element.16.own_ref, bf16[12,2,64,128]{3,2,1,0:T(8,128)(2,1)S(1)} %constant_dynamic-update-slice_fusion.near_ref, ...), custom_call_target="tpu_custom_call" | custom-call | flops 1000000000 | bytes 1048576 | tf_op jit(solution)/shard_map/pallas_call | solution.py:285
  25.5 9.1 %all_to_all.11.stats_ref = f32[32,2,128]{2,1,0:T(2,128)S(1)} all-to-all(f32[32,2,128]{2,1,0:T(2,128)S(1)} %get-tuple-element.24), channel_id=1, replica_groups=mesh['section'=4,'rows'=8] {'section','rows'}, dimensions={0} | all-to-all | bytes 65536 | tf_op jit(solution)/shard_map/all_to_all | solution.py:362
  34.6 0.0 copy-done
  34.6 2.2 %shard_map.112 = bf16[8,2,64,128]{3,2,1,0:T(8,128)(2,1)} custom-call(bf16[10,4,64,128]{3,2,1,0:T(8,128)(2,1)S(1)} %get-tuple-element.23.middle_ref, f32[32,2,128]{2,1,0:T(2,128)S(1)} %all_to_all.11.stats_ref, f32[6,1,128]{2,1,0:T(1,128)S(1)} %get-tuple-element.21.vectors_ref, bf16[3,3,3,128,128]{4,3,2,1,0:T(8,128)(2,1)S(1)} %copy-done, ...), custom_call_target="tpu_custom_call" | custom-call | flops 1000000000 | bytes 1048576 | tf_op jit(solution)/shard_map/pallas_call | solution.py:285
  (4 shorter events, 0.1 us)
Async XLA Ops:
  1.1 8.8 %collective-permute-start = (bf16[4,2,64,128]{3,2,1,0:T(8,128)(2,1)S(1)}, bf16[4,2,64,128]{3,2,1,0:T(8,128)(2,1)S(1)}, u32[]{:S(2)}, u32[]{:S(2)}) collective-permute-start(bf16[4,2,64,128]{3,2,1,0:T(8,128)(2,1)S(1)} %get-tuple-element.15), channel_id=1, source_target_pairs={{0,8},{8,16},{16,24},{24,0},{1,9},{9,17},{17,25},{25,1},{2,10},{10... | collective-permute-start | bytes 393224 | tf_op jit(solution)/shard_map/ppermute | solution.py:344
  4.1 7.1 %collective-permute-start.3 = (bf16[8,2,64,128]{3,2,1,0:T(8,128)(2,1)S(1)}, bf16[8,2,64,128]{3,2,1,0:T(8,128)(2,1)S(1)}, u32[]{:S(2)}, u32[]{:S(2)}) collective-permute-start(bf16[8,2,64,128]{3,2,1,0:T(8,128)(2,1)S(1)} %get-tuple-element.16.own_ref), channel_id=1, source_target_pairs={{0,1},{1,0},{2,3},{3,2},{4,5},{5,4},{6,7},{7,6},{8,9},{9,8},{10,11... | collective-permute-start | bytes 786440 | tf_op jit(solution)/shard_map/ppermute | solution.py:320
  5.3 4.5 %collective-permute-start.1 = (f32[1,2,128]{2,1,0:T(2,128)S(1)}, f32[1,2,128]{2,1,0:T(2,128)S(1)}, u32[]{:S(2)}, u32[]{:S(2)}) collective-permute-start(f32[1,2,128]{2,1,0:T(2,128)S(1)} %get-tuple-element.19), channel_id=1, source_target_pairs={{0,8},{8,16},{16,24},{24,0},{1,9},{9,17},{17,25},{25,1},{2,10},{10... | collective-permute-start | bytes 3080 | tf_op jit(solution)/shard_map/ppermute | solution.py:345
  9.8 1.3 %collective-permute-start.2 = (bf16[4,2,64,128]{3,2,1,0:T(8,128)(2,1)S(1)}, bf16[4,2,64,128]{3,2,1,0:T(8,128)(2,1)S(1)}, u32[]{:S(2)}, u32[]{:S(2)}) collective-permute-start(bf16[4,2,64,128]{3,2,1,0:T(8,128)(2,1)S(1)} %collective-permute-done.halo_ref), channel_id=1, source_target_pairs={{0,1},{1,0},{2,3},{3,2},{4,5},{5,4},{6,7},{7,6},{8,9},{9,8},{10,11... | collective-permute-start | bytes 393224 | tf_op jit(solution)/shard_map/ppermute | solution.py:320
  11.3 10.9 %collective-permute-start.4 = (bf16[12,2,64,128]{3,2,1,0:T(8,128)(2,1)S(1)}, bf16[12,2,64,128]{3,2,1,0:T(8,128)(2,1)S(1)}, u32[]{:S(2)}, u32[]{:S(2)}) collective-permute-start(bf16[12,2,64,128]{3,2,1,0:T(8,128)(2,1)S(1)} %constant_dynamic-update-slice_fusion.near_ref), channel_id=1, source_target_pairs={{0,2},{1,0},{2,4},{3,1},{4,6},{5,3},{6,7},{7,5},{8,10},{9,8},{10,1... | collective-permute-start | bytes 1179656 | tf_op jit(solution)/shard_map/ppermute | solution.py:320
  22.2 12.4 %copy-start = (bf16[3,3,3,128,128]{4,3,2,1,0:T(8,128)(2,1)S(1)}, bf16[3,3,3,128,128]{4,3,2,1,0:T(8,128)(2,1)}, u32[]{:S(2)}) copy-start(bf16[3,3,3,128,128]{4,3,2,1,0:T(8,128)(2,1)} %weight_ref.3) | copy-start | bytes 2654212

commit v30 on v28

--- a/solution.py
+++ b/solution.py
@@ -1,5 +1,3 @@
-import functools
-
 import functools
 
 import jax
@@ -231,7 +229,7 @@
     slope, offset = affine(mine, cells, scale, shift)
     slope_before, offset_before = affine(before, cells, scale, shift)
     at_start = section == 0
-    half = frames // 2
+    half = frames
     copies = []
     for begin in range(0, frames, half):
         filled = 0 if begin == 0 else begin + 2
@@ -255,12 +253,10 @@
                 line = 2 * pair + out
                 result = (results[out] + vectors_ref[5]).reshape(half, columns, channels)
                 result = result + own_ref[span, line].astype(jnp.float32)
-                ready[span, line] = result.astype(jnp.bfloat16)
-        copy = pltpu.make_async_copy(
-            ready.at[span], out_ref.at[span], sems.at[begin // half]
-        )
-        copy.start()
-        copies.append(copy)
+                ready[line] = result.astype(jnp.bfloat16)
+                copy = pltpu.make_async_copy(ready.at[line], out_ref.at[:, line], sems.at[line])
+                copy.start()
+                copies.append(copy)
     for copy in copies:
         copy.wait()
 
@@ -358,8 +354,8 @@
         jax.ShapeDtypeStruct(activations.shape, jnp.bfloat16),
         [
             pltpu.VMEM((frames + 2, lines + 2, columns, channels), jnp.bfloat16),
-            pltpu.VMEM(activations.shape, jnp.bfloat16),
-            pltpu.SemaphoreType.DMA((2,)),
+            pltpu.VMEM((lines, frames, columns, channels), jnp.bfloat16),
+            pltpu.SemaphoreType.DMA((lines,)),
         ],
         (middle, stats_two, packed, conv2_weight, own),
         out_in_place=True,

time: 36.9 us -> 37 us (level)
  no operation moved by 1% of the time
where the time goes in v30:
time: 37 us; the launch traced here: 36.8 us
  blocking collectives  18.4 us (50%)
  Pallas kernels  7.83 us (21%)
  starting transfers between devices  6.13 us (17%)
  waiting for transfers between devices  4.33 us (12%)
    all_to_all x1, blocking collectives, on_device(): stats = lax.all_to_all(both, 'rows', 0, 0, tiled=True)  9.31 us
    all_to_all x1, blocking collectives, on_device(): stats_two = lax.all_to_all(sums_two, ('section', 'rows'), 0, 0, tiled=True)  9.09 us
    pallas_call x4, Pallas kernels, call(): pl.pallas_call(kernel, out_shape=out_shape, in_specs=specs, out_specs=jax...  7.83 us
    ppermute x1, starting transfers between devices, on_device(): received = lax.ppermute(halo, 'section', ring)  2.99 us
    ppermute x1, waiting for transfers between devices, on_device(): passed = lax.ppermute(sums, 'section', ring)  2.98 us
    ppermute x3, starting transfers between devices, across(): return lax.ppermute(block, 'rows', list(enumerate(partner)))  1.6 us
    ppermute x1, starting transfers between devices, on_device(): passed = lax.ppermute(sums, 'section', ring)  1.54 us
    ppermute x3, waiting for transfers between devices, across(): return lax.ppermute(block, 'rows', list(enumerate(partner)))  1.35 us
  transfers between devices with their start and end apart: 5, of which 2 were waited for; matrix products, arithmetic and copies ran while one was open for 0% of the time, Pallas kernels for 3%

profile of v30, /device:TPU:0, one launch (start us, length us, event | category | flops | bytes accessed | tf_op | source)
XLA Modules:
  0.0 36.8 jit_solution(14680076457985288701)
XLA Ops:
  0.0 1.1 %shard_map.109 = (bf16[8,2,64,128]{3,2,1,0:T(8,128)(2,1)S(1)}, bf16[4,2,64,128]{3,2,1,0:T(8,128)(2,1)S(1)}) custom-call(bf16[8,2,64,128]{3,2,1,0:T(8,128)(2,1)} %own_ref.1, bf16[2,2,64,128]{3,2,1,0:T(8,128)(2,1)} %second_cache_ref.1, bf16[2,2,64,128]{3,2,1,0:T(8,128)(2,1)} %first_cache_ref.1), custom_call_target="tpu_custom_call" | custom-call | bytes 1048576 | tf_op jit(solution)/shard_map/pallas_call | solution.py:274
  1.1 3.0 %collective-permute-start = (bf16[4,2,64,128]{3,2,1,0:T(8,128)(2,1)S(1)}, bf16[4,2,64,128]{3,2,1,0:T(8,128)(2,1)S(1)}, u32[]{:S(2)}, u32[]{:S(2)}) collective-permute-start(bf16[4,2,64,128]{3,2,1,0:T(8,128)(2,1)S(1)} %get-tuple-element.15), channel_id=1, source_target_pairs={{0,8},{8,16},{16,24},{24,0},{1,9},{9,17},{17,25},{25,1},{2,10},{10... | collective-permute-start | bytes 393224 | tf_op jit(solution)/shard_map/ppermute | solution.py:333
  4.1 0.0 collective-permute-start.3
  4.1 1.2 %shard_map.110 = (f32[1,2,128]{2,1,0:T(2,128)S(1)}, f32[6,1,128]{2,1,0:T(1,128)S(1)}, bf16[3,3,3,128,128]{4,3,2,1,0:T(8,128)(2,1)S(1)}) custom-call(bf16[8,2,64,128]{3,2,1,0:T(8,128)(2,1)S(1)} %get-tuple-element.16.own_ref, bf16[3,3,3,128,128]{4,3,2,1,0:T(8,128)(2,1)} %weight_ref.2, f32[1,128]{1,0:T(1,128)} %bitcast.8, f32[1,128]{1,0:T(1,128)} %bitcast.9, ...), custom_call_target="tpu_custom_call" | custom-call | bytes 1048576 | tf_op jit(solution)/shard_map/pallas_call | solution.py:274
  5.3 1.5 %collective-permute-start.1 = (f32[1,2,128]{2,1,0:T(2,128)S(1)}, f32[1,2,128]{2,1,0:T(2,128)S(1)}, u32[]{:S(2)}, u32[]{:S(2)}) collective-permute-start(f32[1,2,128]{2,1,0:T(2,128)S(1)} %get-tuple-element.19), channel_id=1, source_target_pairs={{0,8},{8,16},{16,24},{24,0},{1,9},{9,17},{17,25},{25,1},{2,10},{10... | collective-permute-start | bytes 3080 | tf_op jit(solution)/shard_map/ppermute | solution.py:334
  6.9 3.0 %collective-permute-done.1 = f32[1,2,128]{2,1,0:T(2,128)S(1)} collective-permute-done((f32[1,2,128]{2,1,0:T(2,128)S(1)}, f32[1,2,128]{2,1,0:T(2,128)S(1)}, u32[]{:S(2)}, u32[]{:S(2)}) %collective-permute-start.1) | collective-permute-done | bytes 1056 | tf_op jit(solution)/shard_map/ppermute | solution.py:334
  9.8 0.0 collective-permute-done.halo_ref
  9.8 0.0 collective-permute-start.2
  9.8 1.3 %collective-permute-done.2 = bf16[4,2,64,128]{3,2,1,0:T(8,128)(2,1)S(1)} collective-permute-done((bf16[4,2,64,128]{3,2,1,0:T(8,128)(2,1)S(1)}, bf16[4,2,64,128]{3,2,1,0:T(8,128)(2,1)S(1)}, u32[]{:S(2)}, u32[]{:S(2)}) %collective-permute-start.2) | collective-permute-done | bytes 131104 | tf_op jit(solution)/shard_map/ppermute | solution.py:309
  11.2 0.0 collective-permute-done.3
  11.3 1.6 %collective-permute-start.4 = (bf16[12,2,64,128]{3,2,1,0:T(8,128)(2,1)S(1)}, bf16[12,2,64,128]{3,2,1,0:T(8,128)(2,1)S(1)}, u32[]{:S(2)}, u32[]{:S(2)}) collective-permute-start(bf16[12,2,64,128]{3,2,1,0:T(8,128)(2,1)S(1)} %constant_dynamic-update-slice_fusion.near_ref), channel_id=1, source_target_pairs={{0,2},{1,0},{2,4},{3,1},{4,6},{5,3},{6,7},{7,5},{8,10},{9,8},{10,1... | collective-permute-start | bytes 1179656 | tf_op jit(solution)/shard_map/ppermute | solution.py:309
  12.9 9.3 %all_to_all.10.stats_ref = f32[8,4,128]{2,1,0:T(4,128)S(1)} all-to-all(f32[8,4,128]{2,1,0:T(4,128)S(1)} %broadcast_in_dim.8), channel_id=1, replica_groups=mesh['section'=4,'rows'=8] {'rows'}, dimensions={0} | all-to-all | bytes 32768 | tf_op jit(solution)/shard_map/all_to_all | solution.py:340
  22.2 0.0 collective-permute-done.4.far_ref
  22.2 0.0 copy-start
  22.2 3.3 %shard_map.111 = (bf16[10,4,64,128]{3,2,1,0:T(8,128)(2,1)S(1)}, f32[32,2,128]{2,1,0:T(2,128)S(1)}) custom-call(bf16[4,2,64,128]{3,2,1,0:T(8,128)(2,1)S(1)} %collective-permute-done.halo_ref, bf16[8,2,64,128]{3,2,1,0:T(8,128)(2,1)S(1)} %get-tuple-element.16.own_ref, bf16[12,2,64,128]{3,2,1,0:T(8,128)(2,1)S(1)} %constant_dynamic-update-slice_fusion.near_ref, ...), custom_call_target="tpu_custom_call" | custom-call | flops 1000000000 | bytes 1048576 | tf_op jit(solution)/shard_map/pallas_call | solution.py:274
  25.5 9.1 %all_to_all.11.stats_ref = f32[32,2,128]{2,1,0:T(2,128)S(1)} all-to-all(f32[32,2,128]{2,1,0:T(2,128)S(1)} %get-tuple-element.24), channel_id=1, replica_groups=mesh['section'=4,'rows'=8] {'section','rows'}, dimensions={0} | all-to-all | bytes 65536 | tf_op jit(solution)/shard_map/all_to_all | solution.py:351
  34.6 0.0 copy-done
  34.6 2.3 %shard_map.112 = bf16[8,2,64,128]{3,2,1,0:T(8,128)(2,1)} custom-call(bf16[10,4,64,128]{3,2,1,0:T(8,128)(2,1)S(1)} %get-tuple-element.23.middle_ref, f32[32,2,128]{2,1,0:T(2,128)S(1)} %all_to_all.11.stats_ref, f32[6,1,128]{2,1,0:T(1,128)S(1)} %get-tuple-element.21.vectors_ref, bf16[3,3,3,128,128]{4,3,2,1,0:T(8,128)(2,1)S(1)} %copy-done, ...), custom_call_target="tpu_custom_call" | custom-call | flops 1000000000 | bytes 1048576 | tf_op jit(solution)/shard_map/pallas_call | solution.py:274
  (4 shorter events, 0.1 us)
Async XLA Ops:
  1.1 8.8 %collective-permute-start = (bf16[4,2,64,128]{3,2,1,0:T(8,128)(2,1)S(1)}, bf16[4,2,64,128]{3,2,1,0:T(8,128)(2,1)S(1)}, u32[]{:S(2)}, u32[]{:S(2)}) collective-permute-start(bf16[4,2,64,128]{3,2,1,0:T(8,128)(2,1)S(1)} %get-tuple-element.15), channel_id=1, source_target_pairs={{0,8},{8,16},{16,24},{24,0},{1,9},{9,17},{17,25},{25,1},{2,10},{10... | collective-permute-start | bytes 393224 | tf_op jit(solution)/shard_map/ppermute | solution.py:333
  4.1 7.1 %collective-permute-start.3 = (bf16[8,2,64,128]{3,2,1,0:T(8,128)(2,1)S(1)}, bf16[8,2,64,128]{3,2,1,0:T(8,128)(2,1)S(1)}, u32[]{:S(2)}, u32[]{:S(2)}) collective-permute-start(bf16[8,2,64,128]{3,2,1,0:T(8,128)(2,1)S(1)} %get-tuple-element.16.own_ref), channel_id=1, source_target_pairs={{0,1},{1,0},{2,3},{3,2},{4,5},{5,4},{6,7},{7,6},{8,9},{9,8},{10,11... | collective-permute-start | bytes 786440 | tf_op jit(solution)/shard_map/ppermute | solution.py:309
  5.3 4.5 %collective-permute-start.1 = (f32[1,2,128]{2,1,0:T(2,128)S(1)}, f32[1,2,128]{2,1,0:T(2,128)S(1)}, u32[]{:S(2)}, u32[]{:S(2)}) collective-permute-start(f32[1,2,128]{2,1,0:T(2,128)S(1)} %get-tuple-element.19), channel_id=1, source_target_pairs={{0,8},{8,16},{16,24},{24,0},{1,9},{9,17},{17,25},{25,1},{2,10},{10... | collective-permute-start | bytes 3080 | tf_op jit(solution)/shard_map/ppermute | solution.py:334
  9.8 1.3 %collective-permute-start.2 = (bf16[4,2,64,128]{3,2,1,0:T(8,128)(2,1)S(1)}, bf16[4,2,64,128]{3,2,1,0:T(8,128)(2,1)S(1)}, u32[]{:S(2)}, u32[]{:S(2)}) collective-permute-start(bf16[4,2,64,128]{3,2,1,0:T(8,128)(2,1)S(1)} %collective-permute-done.halo_ref), channel_id=1, source_target_pairs={{0,1},{1,0},{2,3},{3,2},{4,5},{5,4},{6,7},{7,6},{8,9},{9,8},{10,11... | collective-permute-start | bytes 393224 | tf_op jit(solution)/shard_map/ppermute | solution.py:309
  11.3 10.9 %collective-permute-start.4 = (bf16[12,2,64,128]{3,2,1,0:T(8,128)(2,1)S(1)}, bf16[12,2,64,128]{3,2,1,0:T(8,128)(2,1)S(1)}, u32[]{:S(2)}, u32[]{:S(2)}) collective-permute-start(bf16[12,2,64,128]{3,2,1,0:T(8,128)(2,1)S(1)} %constant_dynamic-update-slice_fusion.near_ref), channel_id=1, source_target_pairs={{0,2},{1,0},{2,4},{3,1},{4,6},{5,3},{6,7},{7,5},{8,10},{9,8},{10,1... | collective-permute-start | bytes 1179656 | tf_op jit(solution)/shard_map/ppermute | solution.py:309
  22.2 12.4 %copy-start = (bf16[3,3,3,128,128]{4,3,2,1,0:T(8,128)(2,1)S(1)}, bf16[3,3,3,128,128]{4,3,2,1,0:T(8,128)(2,1)}, u32[]{:S(2)}) copy-start(bf16[3,3,3,128,128]{4,3,2,1,0:T(8,128)(2,1)} %weight_ref.3) | copy-start | bytes 2654212

commit v31 on v28

--- a/solution.py
+++ b/solution.py
@@ -1,5 +1,3 @@
-import functools
-
 import functools
 
 import jax
@@ -204,15 +202,21 @@
         for line in range(ready, 2 * pair + 4):
             fill(line)
         ready = 2 * pair + 4
-        results = pair_conv(field, 2 * pair, 0, inner + 2, weight_ref)
-        for out in range(2):
+        half = (inner + 2) // 2
+        for begin, out in ((begin, out) for begin in (0, half) for out in range(2)):
+            if out == 0:
+                results = pair_conv(field, 2 * pair, begin, half, weight_ref)
             line = 2 * pair + out
             rounded = (results[out] + bias).astype(jnp.bfloat16)
-            rounded = rounded.reshape(inner + 2, columns, channels)
-            middle_ref[:2, line] = jnp.where(at_start, field[:spare, line + lines - 1], rounded[:2])
-            middle_ref[2:, line] = rounded[2:]
+            rounded = rounded.reshape(half, columns, channels)
+            skip = 2 if begin == 0 else 0
+            if begin == 0:
+                middle_ref[:2, line] = jnp.where(
+                    at_start, field[:spare, line + lines - 1], rounded[:2]
+                )
+            middle_ref[begin + skip : begin + half, line] = rounded[skip:]
             if 1 <= line <= lines:
-                kept.append(rounded[2:].astype(jnp.float32).reshape(-1, channels))
+                kept.append(rounded[skip:].astype(jnp.float32).reshape(-1, channels))
     packed = moments(kept)
     for device in range(sums_ref.shape[0]):
         sums_ref[device] = packed

time: 36.9 us -> 36.8 us (level)
  no operation moved by 1% of the time
where the time goes in v31:
time: 36.8 us; the launch traced here: 36.6 us
  blocking collectives  18.4 us (50%)
  Pallas kernels  7.64 us (21%)
  starting transfers between devices  6.13 us (17%)
  waiting for transfers between devices  4.33 us (12%)
    all_to_all x1, blocking collectives, on_device(): stats = lax.all_to_all(both, 'rows', 0, 0, tiled=True)  9.31 us
    all_to_all x1, blocking collectives, on_device(): stats_two = lax.all_to_all(sums_two, ('section', 'rows'), 0, 0, tiled=True)  9.1 us
    pallas_call x4, Pallas kernels, call(): pl.pallas_call(kernel, out_shape=out_shape, in_specs=specs, out_specs=jax...  7.64 us
    ppermute x1, starting transfers between devices, on_device(): received = lax.ppermute(halo, 'section', ring)  2.99 us
    ppermute x1, waiting for transfers between devices, on_device(): passed = lax.ppermute(sums, 'section', ring)  2.98 us
    ppermute x3, starting transfers between devices, across(): return lax.ppermute(block, 'rows', list(enumerate(partner)))  1.6 us
    ppermute x1, starting transfers between devices, on_device(): passed = lax.ppermute(sums, 'section', ring)  1.54 us
    ppermute x3, waiting for transfers between devices, across(): return lax.ppermute(block, 'rows', list(enumerate(partner)))  1.35 us
  transfers between devices with their start and end apart: 5, of which 2 were waited for; matrix products, arithmetic and copies ran while one was open for 0% of the time, Pallas kernels for 3%

profile of v31, /device:TPU:0, one launch (start us, length us, event | category | flops | bytes accessed | tf_op | source)
XLA Modules:
  0.0 36.6 jit_solution(16803100489321522250)
XLA Ops:
  0.0 1.1 %shard_map.109 = (bf16[8,2,64,128]{3,2,1,0:T(8,128)(2,1)S(1)}, bf16[4,2,64,128]{3,2,1,0:T(8,128)(2,1)S(1)}) custom-call(bf16[8,2,64,128]{3,2,1,0:T(8,128)(2,1)} %own_ref.1, bf16[2,2,64,128]{3,2,1,0:T(8,128)(2,1)} %second_cache_ref.1, bf16[2,2,64,128]{3,2,1,0:T(8,128)(2,1)} %first_cache_ref.1), custom_call_target="tpu_custom_call" | custom-call | bytes 1048576 | tf_op jit(solution)/shard_map/pallas_call | solution.py:282
  1.1 3.0 %collective-permute-start = (bf16[4,2,64,128]{3,2,1,0:T(8,128)(2,1)S(1)}, bf16[4,2,64,128]{3,2,1,0:T(8,128)(2,1)S(1)}, u32[]{:S(2)}, u32[]{:S(2)}) collective-permute-start(bf16[4,2,64,128]{3,2,1,0:T(8,128)(2,1)S(1)} %get-tuple-element.15), channel_id=1, source_target_pairs={{0,8},{8,16},{16,24},{24,0},{1,9},{9,17},{17,25},{25,1},{2,10},{10... | collective-permute-start | bytes 393224 | tf_op jit(solution)/shard_map/ppermute | solution.py:341
  4.1 0.0 collective-permute-start.3
  4.1 1.2 %shard_map.110 = (f32[1,2,128]{2,1,0:T(2,128)S(1)}, f32[6,1,128]{2,1,0:T(1,128)S(1)}, bf16[3,3,3,128,128]{4,3,2,1,0:T(8,128)(2,1)S(1)}) custom-call(bf16[8,2,64,128]{3,2,1,0:T(8,128)(2,1)S(1)} %get-tuple-element.16.own_ref, bf16[3,3,3,128,128]{4,3,2,1,0:T(8,128)(2,1)} %weight_ref.2, f32[1,128]{1,0:T(1,128)} %bitcast.8, f32[1,128]{1,0:T(1,128)} %bitcast.9, ...), custom_call_target="tpu_custom_call" | custom-call | bytes 1048576 | tf_op jit(solution)/shard_map/pallas_call | solution.py:282
  5.3 1.5 %collective-permute-start.1 = (f32[1,2,128]{2,1,0:T(2,128)S(1)}, f32[1,2,128]{2,1,0:T(2,128)S(1)}, u32[]{:S(2)}, u32[]{:S(2)}) collective-permute-start(f32[1,2,128]{2,1,0:T(2,128)S(1)} %get-tuple-element.19), channel_id=1, source_target_pairs={{0,8},{8,16},{16,24},{24,0},{1,9},{9,17},{17,25},{25,1},{2,10},{10... | collective-permute-start | bytes 3080 | tf_op jit(solution)/shard_map/ppermute | solution.py:342
  6.9 3.0 %collective-permute-done.1 = f32[1,2,128]{2,1,0:T(2,128)S(1)} collective-permute-done((f32[1,2,128]{2,1,0:T(2,128)S(1)}, f32[1,2,128]{2,1,0:T(2,128)S(1)}, u32[]{:S(2)}, u32[]{:S(2)}) %collective-permute-start.1) | collective-permute-done | bytes 1056 | tf_op jit(solution)/shard_map/ppermute | solution.py:342
  9.8 0.0 collective-permute-done.halo_ref
  9.8 0.0 collective-permute-start.2
  9.8 1.3 %collective-permute-done.2 = bf16[4,2,64,128]{3,2,1,0:T(8,128)(2,1)S(1)} collective-permute-done((bf16[4,2,64,128]{3,2,1,0:T(8,128)(2,1)S(1)}, bf16[4,2,64,128]{3,2,1,0:T(8,128)(2,1)S(1)}, u32[]{:S(2)}, u32[]{:S(2)}) %collective-permute-start.2) | collective-permute-done | bytes 131104 | tf_op jit(solution)/shard_map/ppermute | solution.py:317
  11.2 0.0 collective-permute-done.3
  11.3 1.6 %collective-permute-start.4 = (bf16[12,2,64,128]{3,2,1,0:T(8,128)(2,1)S(1)}, bf16[12,2,64,128]{3,2,1,0:T(8,128)(2,1)S(1)}, u32[]{:S(2)}, u32[]{:S(2)}) collective-permute-start(bf16[12,2,64,128]{3,2,1,0:T(8,128)(2,1)S(1)} %constant_dynamic-update-slice_fusion.near_ref), channel_id=1, source_target_pairs={{0,2},{1,0},{2,4},{3,1},{4,6},{5,3},{6,7},{7,5},{8,10},{9,8},{10,1... | collective-permute-start | bytes 1179656 | tf_op jit(solution)/shard_map/ppermute | solution.py:317
  12.9 9.3 %all_to_all.10.stats_ref = f32[8,4,128]{2,1,0:T(4,128)S(1)} all-to-all(f32[8,4,128]{2,1,0:T(4,128)S(1)} %broadcast_in_dim.8), channel_id=1, replica_groups=mesh['section'=4,'rows'=8] {'rows'}, dimensions={0} | all-to-all | bytes 32768 | tf_op jit(solution)/shard_map/all_to_all | solution.py:348
  22.2 0.0 collective-permute-done.4.far_ref
  22.2 0.0 copy-start
  22.2 3.2 %shard_map.111 = (bf16[10,4,64,128]{3,2,1,0:T(8,128)(2,1)S(1)}, f32[32,2,128]{2,1,0:T(2,128)S(1)}) custom-call(bf16[4,2,64,128]{3,2,1,0:T(8,128)(2,1)S(1)} %collective-permute-done.halo_ref, bf16[8,2,64,128]{3,2,1,0:T(8,128)(2,1)S(1)} %get-tuple-element.16.own_ref, bf16[12,2,64,128]{3,2,1,0:T(8,128)(2,1)S(1)} %constant_dynamic-update-slice_fusion.near_ref, ...), custom_call_target="tpu_custom_call" | custom-call | flops 1000000000 | bytes 1048576 | tf_op jit(solution)/shard_map/pallas_call | solution.py:282
  25.4 9.1 %all_to_all.11.stats_ref = f32[32,2,128]{2,1,0:T(2,128)S(1)} all-to-all(f32[32,2,128]{2,1,0:T(2,128)S(1)} %get-tuple-element.24), channel_id=1, replica_groups=mesh['section'=4,'rows'=8] {'section','rows'}, dimensions={0} | all-to-all | bytes 65536 | tf_op jit(solution)/shard_map/all_to_all | solution.py:359
  34.5 0.0 copy-done
  34.5 2.1 %shard_map.112 = bf16[8,2,64,128]{3,2,1,0:T(8,128)(2,1)} custom-call(bf16[10,4,64,128]{3,2,1,0:T(8,128)(2,1)S(1)} %get-tuple-element.23.middle_ref, f32[32,2,128]{2,1,0:T(2,128)S(1)} %all_to_all.11.stats_ref, f32[6,1,128]{2,1,0:T(1,128)S(1)} %get-tuple-element.21.vectors_ref, bf16[3,3,3,128,128]{4,3,2,1,0:T(8,128)(2,1)S(1)} %copy-done, ...), custom_call_target="tpu_custom_call" | custom-call | flops 1000000000 | bytes 1048576 | tf_op jit(solution)/shard_map/pallas_call | solution.py:282
  (4 shorter events, 0.1 us)
Async XLA Ops:
  1.1 8.8 %collective-permute-start = (bf16[4,2,64,128]{3,2,1,0:T(8,128)(2,1)S(1)}, bf16[4,2,64,128]{3,2,1,0:T(8,128)(2,1)S(1)}, u32[]{:S(2)}, u32[]{:S(2)}) collective-permute-start(bf16[4,2,64,128]{3,2,1,0:T(8,128)(2,1)S(1)} %get-tuple-element.15), channel_id=1, source_target_pairs={{0,8},{8,16},{16,24},{24,0},{1,9},{9,17},{17,25},{25,1},{2,10},{10... | collective-permute-start | bytes 393224 | tf_op jit(solution)/shard_map/ppermute | solution.py:341
  4.1 7.1 %collective-permute-start.3 = (bf16[8,2,64,128]{3,2,1,0:T(8,128)(2,1)S(1)}, bf16[8,2,64,128]{3,2,1,0:T(8,128)(2,1)S(1)}, u32[]{:S(2)}, u32[]{:S(2)}) collective-permute-start(bf16[8,2,64,128]{3,2,1,0:T(8,128)(2,1)S(1)} %get-tuple-element.16.own_ref), channel_id=1, source_target_pairs={{0,1},{1,0},{2,3},{3,2},{4,5},{5,4},{6,7},{7,6},{8,9},{9,8},{10,11... | collective-permute-start | bytes 786440 | tf_op jit(solution)/shard_map/ppermute | solution.py:317
  5.3 4.5 %collective-permute-start.1 = (f32[1,2,128]{2,1,0:T(2,128)S(1)}, f32[1,2,128]{2,1,0:T(2,128)S(1)}, u32[]{:S(2)}, u32[]{:S(2)}) collective-permute-start(f32[1,2,128]{2,1,0:T(2,128)S(1)} %get-tuple-element.19), channel_id=1, source_target_pairs={{0,8},{8,16},{16,24},{24,0},{1,9},{9,17},{17,25},{25,1},{2,10},{10... | collective-permute-start | bytes 3080 | tf_op jit(solution)/shard_map/ppermute | solution.py:342
  9.8 1.3 %collective-permute-start.2 = (bf16[4,2,64,128]{3,2,1,0:T(8,128)(2,1)S(1)}, bf16[4,2,64,128]{3,2,1,0:T(8,128)(2,1)S(1)}, u32[]{:S(2)}, u32[]{:S(2)}) collective-permute-start(bf16[4,2,64,128]{3,2,1,0:T(8,128)(2,1)S(1)} %collective-permute-done.halo_ref), channel_id=1, source_target_pairs={{0,1},{1,0},{2,3},{3,2},{4,5},{5,4},{6,7},{7,6},{8,9},{9,8},{10,11... | collective-permute-start | bytes 393224 | tf_op jit(solution)/shard_map/ppermute | solution.py:317
  11.3 10.9 %collective-permute-start.4 = (bf16[12,2,64,128]{3,2,1,0:T(8,128)(2,1)S(1)}, bf16[12,2,64,128]{3,2,1,0:T(8,128)(2,1)S(1)}, u32[]{:S(2)}, u32[]{:S(2)}) collective-permute-start(bf16[12,2,64,128]{3,2,1,0:T(8,128)(2,1)S(1)} %constant_dynamic-update-slice_fusion.near_ref), channel_id=1, source_target_pairs={{0,2},{1,0},{2,4},{3,1},{4,6},{5,3},{6,7},{7,5},{8,10},{9,8},{10,1... | collective-permute-start | bytes 1179656 | tf_op jit(solution)/shard_map/ppermute | solution.py:317
  22.2 12.3 %copy-start = (bf16[3,3,3,128,128]{4,3,2,1,0:T(8,128)(2,1)S(1)}, bf16[3,3,3,128,128]{4,3,2,1,0:T(8,128)(2,1)}, u32[]{:S(2)}) copy-start(bf16[3,3,3,128,128]{4,3,2,1,0:T(8,128)(2,1)} %weight_ref.3) | copy-start | bytes 2654212
